TPU v7x, 32 devices: a whole 2x2x4 slice. The times are simulated.
32 devices in a mesh: chan: 4 (over z), pix: 8 (over y, x, core).
Axes of the slice: x: 2, y: 2, z: 4, core: 2. Of those that a mesh axis runs over, the one named last changes fastest.
Arguments:
- frames_raw: float32 [16, 256, 5120], P(None, 'chan', 'pix')
- grad_out: float32 [16, 256, 4096], P(None, 'chan', 'pix'), may hold values from -6 to 6
- col_offsets: int32 [4], replicated, may hold values from 0 to 16
- flip_flags: int32 [4], replicated, may hold values from 0 to 1
- owners: int32 [138, 1], replicated, may hold values from 0 to 7; in each aligned block of 138 rows (0 to 137, 138 to 275, ...) at most 26 rows name the same one
- w_expand: float32 [256, 1024], P(None, 'chan'), may hold values from -0.375 to 0.375
- w_dw: float32 [25, 1024], P(None, 'chan'), may hold values from -1.25 to 1.25
- norm_gains: float32 [2, 1024], P(None, 'chan'), may hold values from 0.25 to 1.75
- norm_biases: float32 [2, 1024], P(None, 'chan'), may hold values from -3 to 3
- w_project: float32 [1024, 256], P('chan'), may hold values from -0.5 to 0.5
- squeeze_matrix: float32 [256, 16], P('chan'), may hold values from -1.5 to 1.5
- se_down_bias: float32 [16], replicated, may hold values from -3 to 3
- excite_matrix: float32 [16, 256], P(None, 'chan'), may hold values from -3 to 3
- excite_bias_row: float32 [256], P('chan'), may hold values from -3 to 3
- first_moment: float32 [4, 208, 1024], P('chan', 'pix'), may hold values from -512 to 512
- second_moment: float32 [4, 208, 1024], P('chan', 'pix'), may hold values from 6400 to 25600
Outputs:
- output: float32 [16, 256, 4096], P(None, 'chan', 'pix')
- grad_frames: float32 [16, 256, 5120], P(None, 'chan', 'pix')
- first_new: float32 [4, 208, 1024], P('chan', 'pix')
- second_new: float32 [4, 208, 1024], P('chan', 'pix')
- new_params: float32 [4, 140624], P('chan')
Inputs may be any that keep to these rules, and one draw needn't show every extreme that they name: `owners`: an owner holds at most 26 blocks, a bound that some block reaches.
All inputs are finite; a program needn't handle non-finite values.
Results may differ from a plain program's by a relative error of at most 0.0003.
Values sent between devices are 32-bit elements; how exact they have to be, the bound alone decides.
No kernel may reach another device: no remote copies, remote signals or barrier semaphores. Data moves between devices by JAX's collectives and lax.ppermute only.
A program may use at most 128 MiB of HBM per device.

v0:
```python
from functools import partial
import math

import jax
import jax.numpy as jnp
from jax import lax
from jax.sharding import PartitionSpec as P

K = 5
FRAME_ROWS = 64
FRAME_COLUMNS = 64
CLIP_LEN = 4
MB = 4
STEP = 5
WIN = 80


precise_setting = lax.Precision.HIGHEST
norm_eps = 1e-05
beta_first = 0.5
beta_second = 0.6
adam_eps = 1e-08
weight_decay = 0.1


def with_halo(cells, sides, width):
    for axis, dim in sides:
        count = lax.axis_size(axis)
        ends = count - 1
        head = lax.slice_in_dim(cells, 0, width, axis=dim)
        tail = lax.slice_in_dim(cells, cells.shape[dim] - width, cells.shape[dim], axis=dim)
        cells = jnp.concatenate(
            [
                lax.ppermute(tail, axis, [(i, (i + 1) % count) for i in range(ends)]),
                cells,
                lax.ppermute(head, axis, [((i + 1) % count, i) for i in range(ends)]),
            ],
            axis=dim,
        )
    return cells


def swish_act(values):
    return values * jax.nn.sigmoid(values)


def swish_slope(values):
    sigma_val = jax.nn.sigmoid(values)
    return sigma_val * (1.0 + values * (1.0 - sigma_val))


def crop_band(frame, left_col, flipped, band_rows):
    chan_dev = frame.shape[0]
    square = frame.reshape(chan_dev, band_rows, WIN)
    piece_out = lax.dynamic_slice(
        square, (jnp.int32(0), jnp.int32(0), left_col), (chan_dev, band_rows, FRAME_COLUMNS)
    )
    piece_out = jnp.where(flipped == 1, piece_out[:, :, ::-1], piece_out)
    return piece_out.reshape(chan_dev, band_rows * FRAME_COLUMNS)


def uncrop_band(piece_in, left_col, flipped, band_rows):
    chan_dev = piece_in.shape[0]
    square = piece_in.reshape(chan_dev, band_rows, FRAME_COLUMNS)
    unflipped = jnp.where(flipped == 1, square[:, :, ::-1], square)
    canvas = jnp.zeros((chan_dev, band_rows, WIN), jnp.float32)
    placed = lax.dynamic_update_slice(canvas, unflipped, (jnp.int32(0), jnp.int32(0), left_col))
    return placed.reshape(chan_dev, band_rows * WIN)


def pixel_totals(first_sum, second_sum):
    width = first_sum.shape[1]
    start = lax.axis_index("chan") * width
    empty_row = jnp.zeros((first_sum.shape[0], width * lax.axis_size("chan")), jnp.float32)
    wide_one = lax.dynamic_update_slice_in_dim(empty_row, first_sum, start, 1)
    wide_two = lax.dynamic_update_slice_in_dim(empty_row, second_sum, start, 1)
    total_one, total_two = lax.psum((wide_one, wide_two), ("chan", "pix"))
    return (
        lax.dynamic_slice_in_dim(total_one, start, width, 1),
        lax.dynamic_slice_in_dim(total_two, start, width, 1),
    )


def frame_tally(values):
    total = lax.psum(values, ("chan", "pix"))
    return total


def with_rim(values):
    return with_halo(values, (("pix", 2),), K // 2)


def normalize(hidden, gain_row, bias_row, pixel_count):
    sum_one, sum_two = pixel_totals(
        jnp.sum(hidden, axis=(1, 2, 3)), jnp.sum(hidden * hidden, axis=(1, 2, 3))
    )
    mean_value = sum_one / pixel_count
    mean_square = sum_two / pixel_count
    inverse = lax.rsqrt(mean_square - mean_value * mean_value + norm_eps)
    centered = (hidden - mean_value[:, None, None, None, :]) * inverse[:, None, None, None, :]
    return (centered, inverse, centered * gain_row + bias_row)


def normalize_back(grad_act, centered, inverse, gain_row, pixel_count):
    local_one = jnp.sum(grad_act, axis=(1, 2, 3))
    local_two = jnp.sum(grad_act * centered, axis=(1, 2, 3))
    sum_one, sum_two = pixel_totals(local_one, local_two)
    mean_one = (sum_one / pixel_count)[:, None, None, None, :]
    mean_two = (sum_two / pixel_count)[:, None, None, None, :]
    grad_in = (
        gain_row * inverse[:, None, None, None, :] * (grad_act - mean_one - centered * mean_two)
    )
    return (grad_in, jnp.sum(local_two, axis=0), jnp.sum(local_one, axis=0))


def spread(first_act, w_dw):
    half_width = K // 2
    rimmed = with_rim(first_act)
    padded = jnp.pad(rimmed, ((0, 0), (0, 0), (0, 0), (half_width, half_width), (0, 0)))
    row_count = first_act.shape[2]
    col_count = first_act.shape[3]
    accum_sum = jnp.zeros_like(first_act)
    for row_tap in range(K):
        for col_tap in range(K):
            accum_sum = (
                accum_sum
                + padded[:, :, row_tap : row_tap + row_count, col_tap : col_tap + col_count, :]
                * w_dw[row_tap * K + col_tap]
            )
    return (accum_sum, padded)


def spread_back(grad_spatial, padded, w_dw):
    half_width = K // 2
    rimmed = with_rim(grad_spatial)
    grad_padded = jnp.pad(rimmed, ((0, 0), (0, 0), (0, 0), (half_width, half_width), (0, 0)))
    row_count = grad_spatial.shape[2]
    col_count = grad_spatial.shape[3]
    accum_sum = jnp.zeros_like(grad_spatial)
    kernel_rows = []
    for row_tap in range(K):
        for col_tap in range(K):
            kernel_rows.append(
                jnp.sum(
                    padded[:, :, row_tap : row_tap + row_count, col_tap : col_tap + col_count, :]
                    * grad_spatial,
                    axis=(0, 1, 2, 3),
                )
            )
            row_lo = 2 * half_width - row_tap
            col_lo = 2 * half_width - col_tap
            accum_sum = (
                accum_sum
                + grad_padded[:, :, row_lo : row_lo + row_count, col_lo : col_lo + col_count, :]
                * w_dw[row_tap * K + col_tap]
            )
    return (accum_sum, jnp.stack(kernel_rows))


def run_group(crops, grad_block, weights, band_rows):
    (
        w_expand,
        w_dw,
        norm_gains,
        norm_biases,
        w_project,
        squeeze_matrix,
        se_down_bias,
        excite_matrix,
        excite_bias_row,
    ) = weights
    group_count = crops.shape[0]
    frame_count = crops.shape[1]
    band_area = band_rows * FRAME_COLUMNS
    features = lax.all_gather(crops, "chan", axis=2, tiled=True)
    pixel_count = frame_count * FRAME_ROWS * FRAME_COLUMNS
    expanded = jnp.einsum("gfcp,ce->gfpe", features, w_expand, precision=precise_setting).reshape(
        group_count, frame_count, band_rows, FRAME_COLUMNS, -1
    )
    centered_one, inverse_one, normed_one = normalize(
        expanded, norm_gains[0], norm_biases[0], pixel_count
    )
    first_act = swish_act(normed_one)
    spatial, padded = spread(first_act, w_dw)
    centered_two, inverse_two, normed_two = normalize(
        spatial, norm_gains[1], norm_biases[1], pixel_count
    )
    second_act = swish_act(normed_two)
    second_flat = second_act.reshape(group_count, frame_count, band_area, -1)
    proj_terms = jnp.einsum("gfpe,ec->gfcp", second_flat, w_project, precision=precise_setting)
    projected = lax.psum_scatter(proj_terms, "chan", scatter_dimension=2, tiled=True)
    pooled_portion = jnp.sum(projected, axis=3) / (FRAME_ROWS * FRAME_COLUMNS)
    squeeze_pre = (
        frame_tally(
            jnp.einsum("yxz,zd->yxd", pooled_portion, squeeze_matrix, precision=precise_setting)
        )
        + se_down_bias
    )
    squeezed_features = swish_act(squeeze_pre)
    excite = jax.nn.sigmoid(
        jnp.einsum("zvq,qt->zvt", squeezed_features, excite_matrix, precision=precise_setting)
        + excite_bias_row
    )
    result = crops + projected * excite[:, :, :, None]
    leader = (lax.axis_index("pix") == 0).astype(jnp.float32)
    logit_portion = jnp.sum(grad_block * projected, axis=3) * excite * (1.0 - excite)
    excite_weight_gradient = jnp.einsum(
        "wka,wkv->av", squeezed_features, logit_portion, precision=precise_setting
    )
    g_se_up_bias = jnp.sum(logit_portion, axis=(0, 1))
    squeezed_gradient = frame_tally(
        jnp.einsum("mdp,ep->mde", logit_portion, excite_matrix, precision=precise_setting)
    ) * swish_slope(squeeze_pre)
    squeeze_weight_gradient = jnp.einsum(
        "kjh,kjb->hb", pooled_portion, squeezed_gradient, precision=precise_setting
    )
    g_se_down_bias = jnp.sum(squeezed_gradient, axis=(0, 1)) * leader
    pooled_gradient = jnp.einsum(
        "til,ol->tio", squeezed_gradient, squeeze_matrix, precision=precise_setting
    ) / (FRAME_ROWS * FRAME_COLUMNS)
    grad_proj = grad_block * excite[:, :, :, None] + pooled_gradient[:, :, :, None]
    grad_full = lax.all_gather(grad_proj, "chan", axis=2, tiled=True)
    g_w_project = jnp.einsum("gfpe,gfcp->ec", second_flat, grad_full, precision=precise_setting)
    grad_second = jnp.einsum(
        "gfcp,ec->gfpe", grad_full, w_project, precision=precise_setting
    ).reshape(group_count, frame_count, band_rows, FRAME_COLUMNS, -1) * swish_slope(normed_two)
    grad_spatial, g_gain_two, g_bias_two = normalize_back(
        grad_second, centered_two, inverse_two, norm_gains[1], pixel_count
    )
    grad_first, g_w_dw = spread_back(grad_spatial, padded, w_dw)
    grad_first = grad_first * swish_slope(normed_one)
    grad_expanded, g_gain_one, g_bias_one = normalize_back(
        grad_first, centered_one, inverse_one, norm_gains[0], pixel_count
    )
    expanded_grad_flat = grad_expanded.reshape(group_count, frame_count, band_area, -1)
    g_w_expand = jnp.einsum(
        "gfcp,gfpe->ce", features, expanded_grad_flat, precision=precise_setting
    )
    input_terms = jnp.einsum(
        "gfpe,ce->gfcp", expanded_grad_flat, w_expand, precision=precise_setting
    )
    grad_crops = grad_block + lax.psum_scatter(input_terms, "chan", scatter_dimension=2, tiled=True)
    grads = (
        g_w_expand,
        g_w_dw,
        jnp.stack([g_gain_one, g_gain_two]),
        jnp.stack([g_bias_one, g_bias_two]),
        g_w_project,
        squeeze_weight_gradient,
        g_se_down_bias,
        excite_weight_gradient,
        g_se_up_bias,
    )
    return (result, grad_crops, grads)


def segments(chan_in, hidden_dev, chan_dev, reduced, tap_count, hidden_all):
    seg_sizes = [
        chan_in * hidden_dev,
        tap_count * hidden_dev,
        2 * hidden_dev,
        2 * hidden_dev,
        hidden_dev * chan_in,
        chan_dev * reduced,
        reduced,
        reduced * chan_dev,
        chan_dev,
    ]
    seg_rates = [
        0.5 / math.sqrt(chan_in),
        0.5 / math.sqrt(tap_count),
        0.3,
        0.3,
        0.5 * math.sqrt(8.0 / hidden_all),
        2.0 / math.sqrt(chan_in),
        0.3,
        1.0 / math.sqrt(reduced),
        0.3,
    ]
    return (seg_sizes, seg_rates)


def rate_blocks(seg_sizes, seg_rates, block_count, block_len):
    filled = jnp.concatenate(
        [
            jnp.full((length,), rate_val, jnp.float32)
            for length, rate_val in zip(seg_sizes, seg_rates)
        ]
    )
    return jnp.pad(filled, (0, block_count * block_len - filled.shape[0])).reshape(
        block_count, block_len
    )


def by_columns(values, groups):
    return values.reshape(values.shape[0], groups, -1).transpose(1, 0, 2).reshape(groups, -1)


def group_rows(members, groups):
    (
        w_expand,
        w_dw,
        norm_gains,
        norm_biases,
        w_project,
        squeeze_matrix,
        se_down_bias,
        excite_matrix,
        excite_bias_row,
    ) = members
    pieces = [
        by_columns(w_expand, groups),
        by_columns(w_dw, groups),
        by_columns(norm_gains, groups),
        by_columns(norm_biases, groups),
        w_project.reshape(groups, -1),
        squeeze_matrix.reshape(groups, -1),
        se_down_bias[None, :],
        by_columns(excite_matrix, groups),
        excite_bias_row.reshape(groups, -1),
    ]
    return jnp.concatenate(pieces, axis=1)


def slot_rows(owners, capacity):
    owner_col = owners[:, 0]
    position = jnp.arange(owner_col.shape[0], dtype=jnp.int32)
    earlier = (owner_col[None, :] == owner_col[:, None]) & (position[None, :] < position[:, None])
    return owner_col * capacity + jnp.sum(earlier.astype(jnp.int32), axis=1)


def adam_step(grad_blk, first_old, second_old, weight_old, rate_blk):
    first_next = beta_first * first_old + (1.0 - beta_first) * grad_blk
    second_next = beta_second * second_old + (1.0 - beta_second) * grad_blk * grad_blk
    first_hat = first_next / (1.0 - beta_first**STEP)
    second_hat = second_next / (1.0 - beta_second**STEP)
    weight_next = weight_old * (1.0 - rate_blk * weight_decay) - rate_blk * first_hat / (
        jnp.sqrt(second_hat) + adam_eps
    )
    return (first_next, second_next, weight_next)


def local(
    frames_raw,
    grad_out,
    col_offsets,
    flip_flags,
    owners,
    w_expand,
    w_dw,
    norm_gains,
    norm_biases,
    w_project,
    squeeze_matrix,
    se_down_bias,
    excite_matrix,
    excite_bias_row,
    first_moment,
    second_moment,
):
    left_cols = jnp.repeat(col_offsets, CLIP_LEN)
    flip_each = jnp.repeat(flip_flags, CLIP_LEN)
    frame_count = frames_raw.shape[0]
    chan_dev = frames_raw.shape[1]
    band_rows = frames_raw.shape[2] // WIN
    band_area = band_rows * FRAME_COLUMNS
    crops = jax.vmap(partial(crop_band, band_rows=band_rows))(frames_raw, left_cols, flip_each)
    crops_micro = crops.reshape(MB, frame_count // MB, chan_dev, band_area)
    grad_micro = grad_out.reshape(MB, frame_count // MB, chan_dev, band_area)
    local_weights = (
        w_expand,
        w_dw,
        norm_gains,
        norm_biases,
        w_project,
        squeeze_matrix,
        se_down_bias,
        excite_matrix,
        excite_bias_row,
    )

    def scan_step(total, blocks):
        result, grad_crops_one, grads_one = run_group(
            blocks[0][None], blocks[1][None], local_weights, band_rows
        )
        return (jax.tree.map(jnp.add, total, grads_one), (result[0], grad_crops_one[0]))

    zero_grads = jax.tree.map(jnp.zeros_like, local_weights)
    grads, (results, grad_crops) = lax.scan(scan_step, zero_grads, (crops_micro, grad_micro))
    outputs = results.reshape(frame_count, chan_dev, band_area)
    grad_crops = grad_crops.reshape(frame_count, chan_dev, band_area)
    grad_frames = jax.vmap(partial(uncrop_band, band_rows=band_rows))(
        grad_crops, left_cols, flip_each
    )
    block_len = first_moment.shape[2]
    capacity = first_moment.shape[1]
    group_count = lax.axis_size("chan")
    hidden_dev = w_expand.shape[1]
    seg_sizes, seg_rates = segments(
        w_expand.shape[0],
        hidden_dev,
        chan_dev,
        squeeze_matrix.shape[1],
        w_dw.shape[0],
        hidden_dev * group_count,
    )
    param_count = sum(seg_sizes)
    block_count = (param_count + block_len - 1) // block_len
    slot_index = slot_rows(owners, capacity)
    slot_total = capacity * lax.axis_size("pix")

    def to_slots(rows_in):
        blocks = jnp.pad(rows_in, ((0, 0), (0, block_count * block_len - param_count))).reshape(
            rows_in.shape[0], block_count, block_len
        )
        return (
            jnp.zeros((rows_in.shape[0], slot_total, block_len), jnp.float32)
            .at[:, slot_index]
            .set(blocks)
        )

    slotted = to_slots(group_rows(grads, 1))
    owned_grad = lax.psum_scatter(
        slotted.reshape(slot_total, block_len), "pix", scatter_dimension=0, tiled=True
    )
    start_row = lax.axis_index("pix") * capacity
    owned_weight = lax.dynamic_slice_in_dim(
        to_slots(group_rows(local_weights, 1))[0], start_row, capacity, 0
    )
    rate_table = rate_blocks(seg_sizes, seg_rates, block_count, block_len)
    rate_slots = jnp.zeros((slot_total, block_len), jnp.float32).at[slot_index].set(rate_table)
    owned_rate = lax.dynamic_slice_in_dim(rate_slots, start_row, capacity, 0)
    first_next, second_next, weight_next = adam_step(
        owned_grad, first_moment[0], second_moment[0], owned_weight, owned_rate
    )
    every_block = lax.all_gather(weight_next, "pix", axis=0, tiled=True)
    new_params = every_block[slot_index].reshape(-1)[:param_count][None, :]
    return (outputs, grad_frames, first_next[None], second_next[None], new_params)


def solution(mesh):
    placed = (
        P(None, "chan", "pix"),
        P(None, "chan", "pix"),
        P(),
        P(),
        P(),
        P(None, "chan"),
        P(None, "chan"),
        P(None, "chan"),
        P(None, "chan"),
        P("chan", None),
        P("chan", None),
        P(),
        P(None, "chan"),
        P("chan"),
        P("chan", "pix", None),
        P("chan", "pix", None),
    )
    return jax.shard_map(
        local,
        mesh=mesh,
        in_specs=placed,
        out_specs=(
            P(None, "chan", "pix"),
            P(None, "chan", "pix"),
            P("chan", "pix", None),
            P("chan", "pix", None),
            P("chan", None),
        ),
        check_vma=False,
    )
```

profile of v0, /device:TPU:15, one launch (start us, length us, event | category | flops | bytes accessed | tf_op | source)
XLA Modules:
  0.0 2990.0 jit_solution(12087945137801785778)
XLA Ops:
  27.7 7.2 copy.102
  57.4 2551.2 %while.35 = (s32[]{:T(128)}, f32[256,256]{1,0:T(8,128)}, f32[25,256]{1,0:T(8,128)}, f32[2,256]{1,0:T(2,128)}, f32[2,256]{1,0:T(2,128)}, /*index=5*/f32[256,256]{...) while((s32[]{:T(128)}, f32[256,256]{1,0:T(8,128)}, ...), condition=%wide.region_50.51_spmd.clone, body=%wide.region_0.50_spmd.clone.sunk | while | flops 9797169152 | bytes 363056928 | solution.py:389
  85.1 42.9 %all-gather.4.cloned.1.call-done = f32[1,4,256,512]{3,1,0,2:T(4,128)} async-done(((f32[1,4,64,512]{3,1,0,2:T(4,128)}), f32[1,4,256,512]{3,1,0,2:T(4,128)}) %all-gather.4.cloned.1.call-update) | async-done | bytes 2097168 | tf_op jit(solution)/shard_map/while/body/eval_jaxpr/all_gather | solution.py:175
  134.4 40.2 %all-reduce.20 = (f32[1,1024]{1,0:T(1,128)S(1)}, f32[1,1024]{1,0:T(1,128)S(1)}) all-reduce(f32[1,1024]{1,0:T(1,128)S(1)} %constant_dynamic-update-slice_fusion.28, f32[1,1024]{1,0:T(1,128)S(1)} %constant_dynamic-update-slice_fusion.29), channel_id=1, replica_groups=mesh['chan'=4,'pix'=8] {'chan','pix'}, use_global_device_ids=true, to_apply=%region_2.2 | all-reduce | flops 2048 | bytes 16384 | tf_op jit(solution)/shard_map/while/body/eval_jaxpr/psum | solution.py:77
  184.0 7.1 fusion.191
  192.3 48.2 %all-reduce.21 = (f32[1,1024]{1,0:T(1,128)}, f32[1,1024]{1,0:T(1,128)}) all-reduce(f32[1,1024]{1,0:T(1,128)S(1)} %constant_dynamic-update-slice_fusion.30, f32[1,1024]{1,0:T(1,128)} %constant_dynamic-update-slice_fusion.31), channel_id=1, replica_groups=mesh['chan'=4,'pix'=8] {'chan','pix'}, use_global_device_ids=true, to_apply=%region_6.6 | all-reduce | flops 2048 | bytes 16384 | tf_op jit(solution)/shard_map/while/body/eval_jaxpr/psum | solution.py:77
  254.8 83.3 %all-reduce.29.cloned.1.call-done = f32[1,4,256,512]{3,1,0,2:T(4,128)} async-done(((f32[1,4,256,512]{3,1,0,2:T(4,128)}), f32[1,4,256,512]{3,1,0,2:T(4,128)}) %all-reduce.29.cloned.1.call-update) | async-done | bytes 2097168 | tf_op jit(solution)/shard_map/while
  344.6 40.4 %psum.112 = f32[1,4,16]{2,1,0:T(4,128)} all-reduce(f32[1,4,16]{2,1,0:T(4,128)} %convolution_bitcast_fusion.9), channel_id=1, replica_groups=mesh['chan'=4,'pix'=8] {'chan','pix'}, use_global_device_ids=true, to_apply=%region_11.11 | all-reduce | flops 64 | bytes 512 | tf_op jit(solution)/shard_map/while/body/eval_jaxpr/psum | solution.py:85
  389.7 39.4 %psum.113 = f32[1,4,16]{2,1,0:T(4,128)} all-reduce(f32[1,4,16]{2,1,0:T(4,128)} %convolution_bitcast_fusion.10), channel_id=1, replica_groups=mesh['chan'=4,'pix'=8] {'chan','pix'}, use_global_device_ids=true, to_apply=%region_13.13 | all-reduce | flops 64 | bytes 512 | tf_op jit(solution)/shard_map/while/body/eval_jaxpr/psum | solution.py:85
  439.8 42.4 %all-gather.6.cloned.1.call-done = f32[1,4,256,512]{3,1,0,2:T(4,128)} async-done(((f32[1,4,64,512]{3,1,0,2:T(4,128)}), f32[1,4,256,512]{3,1,0,2:T(4,128)}) %all-gather.6.cloned.1.call-update) | async-done | bytes 2097168 | tf_op jit(solution)/shard_map/while/body/eval_jaxpr/all_gather | solution.py:222
  493.7 40.7 %all-reduce.23 = (f32[1,1024]{1,0:T(1,128)}, f32[1,1024]{1,0:T(1,128)}) all-reduce(f32[1,1024]{1,0:T(1,128)} %constant_dynamic-update-slice_fusion.32, f32[1,1024]{1,0:T(1,128)} %constant_dynamic-update-slice_fusion.33), channel_id=1, replica_groups=mesh['chan'=4,'pix'=8] {'chan','pix'}, use_global_device_ids=true, to_apply=%region_17.17 | all-reduce | flops 2048 | bytes 16384 | tf_op jit(solution)/shard_map/while/body/eval_jaxpr/psum | solution.py:77
  551.1 8.0 fusion.200
  561.4 48.3 %all-reduce.24 = (f32[1,1024]{1,0:T(1,128)}, f32[1,1024]{1,0:T(1,128)}) all-reduce(f32[1,1024]{1,0:T(1,128)} %constant_dynamic-update-slice_fusion.34, f32[1,1024]{1,0:T(1,128)} %constant_dynamic-update-slice_fusion.35), channel_id=1, replica_groups=mesh['chan'=4,'pix'=8] {'chan','pix'}, use_global_device_ids=true, to_apply=%region_21.21 | all-reduce | flops 2048 | bytes 16384 | tf_op jit(solution)/shard_map/while/body/eval_jaxpr/psum | solution.py:77
  644.0 64.6 %all-reduce.31.cloned.1.call-done = f32[1,4,256,512]{3,1,0,2:T(4,128)} async-done(((f32[1,4,256,512]{3,1,0,2:T(4,128)}), f32[1,4,256,512]{3,1,0,2:T(4,128)}) %all-reduce.31.cloned.1.call-update) | async-done | bytes 2097168 | tf_op jit(solution)/shard_map/while
  715.4 42.2 %all-gather.4.cloned.1.call-done = f32[1,4,256,512]{3,1,0,2:T(4,128)} async-done(((f32[1,4,64,512]{3,1,0,2:T(4,128)}), f32[1,4,256,512]{3,1,0,2:T(4,128)}) %all-gather.4.cloned.1.call-update) | async-done | bytes 2097168 | tf_op jit(solution)/shard_map/while/body/eval_jaxpr/all_gather | solution.py:175
  763.9 40.2 %all-reduce.20 = (f32[1,1024]{1,0:T(1,128)S(1)}, f32[1,1024]{1,0:T(1,128)S(1)}) all-reduce(f32[1,1024]{1,0:T(1,128)S(1)} %constant_dynamic-update-slice_fusion.28, f32[1,1024]{1,0:T(1,128)S(1)} %constant_dynamic-update-slice_fusion.29), channel_id=1, replica_groups=mesh['chan'=4,'pix'=8] {'chan','pix'}, use_global_device_ids=true, to_apply=%region_2.2 | all-reduce | flops 2048 | bytes 16384 | tf_op jit(solution)/shard_map/while/body/eval_jaxpr/psum | solution.py:77
  821.8 48.2 %all-reduce.21 = (f32[1,1024]{1,0:T(1,128)}, f32[1,1024]{1,0:T(1,128)}) all-reduce(f32[1,1024]{1,0:T(1,128)S(1)} %constant_dynamic-update-slice_fusion.30, f32[1,1024]{1,0:T(1,128)} %constant_dynamic-update-slice_fusion.31), channel_id=1, replica_groups=mesh['chan'=4,'pix'=8] {'chan','pix'}, use_global_device_ids=true, to_apply=%region_6.6 | all-reduce | flops 2048 | bytes 16384 | tf_op jit(solution)/shard_map/while/body/eval_jaxpr/psum | solution.py:77
  884.4 83.3 %all-reduce.29.cloned.1.call-done = f32[1,4,256,512]{3,1,0,2:T(4,128)} async-done(((f32[1,4,256,512]{3,1,0,2:T(4,128)}), f32[1,4,256,512]{3,1,0,2:T(4,128)}) %all-reduce.29.cloned.1.call-update) | async-done | bytes 2097168 | tf_op jit(solution)/shard_map/while
  974.2 40.4 %psum.112 = f32[1,4,16]{2,1,0:T(4,128)} all-reduce(f32[1,4,16]{2,1,0:T(4,128)} %convolution_bitcast_fusion.9), channel_id=1, replica_groups=mesh['chan'=4,'pix'=8] {'chan','pix'}, use_global_device_ids=true, to_apply=%region_11.11 | all-reduce | flops 64 | bytes 512 | tf_op jit(solution)/shard_map/while/body/eval_jaxpr/psum | solution.py:85
  1019.3 39.4 %psum.113 = f32[1,4,16]{2,1,0:T(4,128)} all-reduce(f32[1,4,16]{2,1,0:T(4,128)} %convolution_bitcast_fusion.10), channel_id=1, replica_groups=mesh['chan'=4,'pix'=8] {'chan','pix'}, use_global_device_ids=true, to_apply=%region_13.13 | all-reduce | flops 64 | bytes 512 | tf_op jit(solution)/shard_map/while/body/eval_jaxpr/psum | solution.py:85
  1069.4 42.4 %all-gather.6.cloned.1.call-done = f32[1,4,256,512]{3,1,0,2:T(4,128)} async-done(((f32[1,4,64,512]{3,1,0,2:T(4,128)}), f32[1,4,256,512]{3,1,0,2:T(4,128)}) %all-gather.6.cloned.1.call-update) | async-done | bytes 2097168 | tf_op jit(solution)/shard_map/while/body/eval_jaxpr/all_gather | solution.py:222
  1123.3 40.7 %all-reduce.23 = (f32[1,1024]{1,0:T(1,128)}, f32[1,1024]{1,0:T(1,128)}) all-reduce(f32[1,1024]{1,0:T(1,128)} %constant_dynamic-update-slice_fusion.32, f32[1,1024]{1,0:T(1,128)} %constant_dynamic-update-slice_fusion.33), channel_id=1, replica_groups=mesh['chan'=4,'pix'=8] {'chan','pix'}, use_global_device_ids=true, to_apply=%region_17.17 | all-reduce | flops 2048 | bytes 16384 | tf_op jit(solution)/shard_map/while/body/eval_jaxpr/psum | solution.py:77
  1180.7 8.0 fusion.200
  1191.0 48.3 %all-reduce.24 = (f32[1,1024]{1,0:T(1,128)}, f32[1,1024]{1,0:T(1,128)}) all-reduce(f32[1,1024]{1,0:T(1,128)} %constant_dynamic-update-slice_fusion.34, f32[1,1024]{1,0:T(1,128)} %constant_dynamic-update-slice_fusion.35), channel_id=1, replica_groups=mesh['chan'=4,'pix'=8] {'chan','pix'}, use_global_device_ids=true, to_apply=%region_21.21 | all-reduce | flops 2048 | bytes 16384 | tf_op jit(solution)/shard_map/while/body/eval_jaxpr/psum | solution.py:77
  1274.3 63.8 %all-reduce.31.cloned.1.call-done = f32[1,4,256,512]{3,1,0,2:T(4,128)} async-done(((f32[1,4,256,512]{3,1,0,2:T(4,128)}), f32[1,4,256,512]{3,1,0,2:T(4,128)}) %all-reduce.31.cloned.1.call-update) | async-done | bytes 2097168 | tf_op jit(solution)/shard_map/while
  1345.0 42.5 %all-gather.4.cloned.1.call-done = f32[1,4,256,512]{3,1,0,2:T(4,128)} async-done(((f32[1,4,64,512]{3,1,0,2:T(4,128)}), f32[1,4,256,512]{3,1,0,2:T(4,128)}) %all-gather.4.cloned.1.call-update) | async-done | bytes 2097168 | tf_op jit(solution)/shard_map/while/body/eval_jaxpr/all_gather | solution.py:175
  1393.8 40.2 %all-reduce.20 = (f32[1,1024]{1,0:T(1,128)S(1)}, f32[1,1024]{1,0:T(1,128)S(1)}) all-reduce(f32[1,1024]{1,0:T(1,128)S(1)} %constant_dynamic-update-slice_fusion.28, f32[1,1024]{1,0:T(1,128)S(1)} %constant_dynamic-update-slice_fusion.29), channel_id=1, replica_groups=mesh['chan'=4,'pix'=8] {'chan','pix'}, use_global_device_ids=true, to_apply=%region_2.2 | all-reduce | flops 2048 | bytes 16384 | tf_op jit(solution)/shard_map/while/body/eval_jaxpr/psum | solution.py:77
  1443.5 7.1 fusion.191
  1451.7 48.2 %all-reduce.21 = (f32[1,1024]{1,0:T(1,128)}, f32[1,1024]{1,0:T(1,128)}) all-reduce(f32[1,1024]{1,0:T(1,128)S(1)} %constant_dynamic-update-slice_fusion.30, f32[1,1024]{1,0:T(1,128)} %constant_dynamic-update-slice_fusion.31), channel_id=1, replica_groups=mesh['chan'=4,'pix'=8] {'chan','pix'}, use_global_device_ids=true, to_apply=%region_6.6 | all-reduce | flops 2048 | bytes 16384 | tf_op jit(solution)/shard_map/while/body/eval_jaxpr/psum | solution.py:77
  1514.3 83.3 %all-reduce.29.cloned.1.call-done = f32[1,4,256,512]{3,1,0,2:T(4,128)} async-done(((f32[1,4,256,512]{3,1,0,2:T(4,128)}), f32[1,4,256,512]{3,1,0,2:T(4,128)}) %all-reduce.29.cloned.1.call-update) | async-done | bytes 2097168 | tf_op jit(solution)/shard_map/while
  1604.1 40.4 %psum.112 = f32[1,4,16]{2,1,0:T(4,128)} all-reduce(f32[1,4,16]{2,1,0:T(4,128)} %convolution_bitcast_fusion.9), channel_id=1, replica_groups=mesh['chan'=4,'pix'=8] {'chan','pix'}, use_global_device_ids=true, to_apply=%region_11.11 | all-reduce | flops 64 | bytes 512 | tf_op jit(solution)/shard_map/while/body/eval_jaxpr/psum | solution.py:85
  1649.2 39.4 %psum.113 = f32[1,4,16]{2,1,0:T(4,128)} all-reduce(f32[1,4,16]{2,1,0:T(4,128)} %convolution_bitcast_fusion.10), channel_id=1, replica_groups=mesh['chan'=4,'pix'=8] {'chan','pix'}, use_global_device_ids=true, to_apply=%region_13.13 | all-reduce | flops 64 | bytes 512 | tf_op jit(solution)/shard_map/while/body/eval_jaxpr/psum | solution.py:85
  1699.3 42.4 %all-gather.6.cloned.1.call-done = f32[1,4,256,512]{3,1,0,2:T(4,128)} async-done(((f32[1,4,64,512]{3,1,0,2:T(4,128)}), f32[1,4,256,512]{3,1,0,2:T(4,128)}) %all-gather.6.cloned.1.call-update) | async-done | bytes 2097168 | tf_op jit(solution)/shard_map/while/body/eval_jaxpr/all_gather | solution.py:222
  1753.1 40.7 %all-reduce.23 = (f32[1,1024]{1,0:T(1,128)}, f32[1,1024]{1,0:T(1,128)}) all-reduce(f32[1,1024]{1,0:T(1,128)} %constant_dynamic-update-slice_fusion.32, f32[1,1024]{1,0:T(1,128)} %constant_dynamic-update-slice_fusion.33), channel_id=1, replica_groups=mesh['chan'=4,'pix'=8] {'chan','pix'}, use_global_device_ids=true, to_apply=%region_17.17 | all-reduce | flops 2048 | bytes 16384 | tf_op jit(solution)/shard_map/while/body/eval_jaxpr/psum | solution.py:77
  1810.5 8.0 fusion.200
  1820.9 48.3 %all-reduce.24 = (f32[1,1024]{1,0:T(1,128)}, f32[1,1024]{1,0:T(1,128)}) all-reduce(f32[1,1024]{1,0:T(1,128)} %constant_dynamic-update-slice_fusion.34, f32[1,1024]{1,0:T(1,128)} %constant_dynamic-update-slice_fusion.35), channel_id=1, replica_groups=mesh['chan'=4,'pix'=8] {'chan','pix'}, use_global_device_ids=true, to_apply=%region_21.21 | all-reduce | flops 2048 | bytes 16384 | tf_op jit(solution)/shard_map/while/body/eval_jaxpr/psum | solution.py:77
  1904.2 63.8 %all-reduce.31.cloned.1.call-done = f32[1,4,256,512]{3,1,0,2:T(4,128)} async-done(((f32[1,4,256,512]{3,1,0,2:T(4,128)}), f32[1,4,256,512]{3,1,0,2:T(4,128)}) %all-reduce.31.cloned.1.call-update) | async-done | bytes 2097168 | tf_op jit(solution)/shard_map/while
  1974.9 42.5 %all-gather.4.cloned.1.call-done = f32[1,4,256,512]{3,1,0,2:T(4,128)} async-done(((f32[1,4,64,512]{3,1,0,2:T(4,128)}), f32[1,4,256,512]{3,1,0,2:T(4,128)}) %all-gather.4.cloned.1.call-update) | async-done | bytes 2097168 | tf_op jit(solution)/shard_map/while/body/eval_jaxpr/all_gather | solution.py:175
  2023.7 40.2 %all-reduce.20 = (f32[1,1024]{1,0:T(1,128)S(1)}, f32[1,1024]{1,0:T(1,128)S(1)}) all-reduce(f32[1,1024]{1,0:T(1,128)S(1)} %constant_dynamic-update-slice_fusion.28, f32[1,1024]{1,0:T(1,128)S(1)} %constant_dynamic-update-slice_fusion.29), channel_id=1, replica_groups=mesh['chan'=4,'pix'=8] {'chan','pix'}, use_global_device_ids=true, to_apply=%region_2.2 | all-reduce | flops 2048 | bytes 16384 | tf_op jit(solution)/shard_map/while/body/eval_jaxpr/psum | solution.py:77
  2073.4 7.1 fusion.191
  2081.6 48.2 %all-reduce.21 = (f32[1,1024]{1,0:T(1,128)}, f32[1,1024]{1,0:T(1,128)}) all-reduce(f32[1,1024]{1,0:T(1,128)S(1)} %constant_dynamic-update-slice_fusion.30, f32[1,1024]{1,0:T(1,128)} %constant_dynamic-update-slice_fusion.31), channel_id=1, replica_groups=mesh['chan'=4,'pix'=8] {'chan','pix'}, use_global_device_ids=true, to_apply=%region_6.6 | all-reduce | flops 2048 | bytes 16384 | tf_op jit(solution)/shard_map/while/body/eval_jaxpr/psum | solution.py:77
  2144.1 83.3 %all-reduce.29.cloned.1.call-done = f32[1,4,256,512]{3,1,0,2:T(4,128)} async-done(((f32[1,4,256,512]{3,1,0,2:T(4,128)}), f32[1,4,256,512]{3,1,0,2:T(4,128)}) %all-reduce.29.cloned.1.call-update) | async-done | bytes 2097168 | tf_op jit(solution)/shard_map/while
  2233.9 40.4 %psum.112 = f32[1,4,16]{2,1,0:T(4,128)} all-reduce(f32[1,4,16]{2,1,0:T(4,128)} %convolution_bitcast_fusion.9), channel_id=1, replica_groups=mesh['chan'=4,'pix'=8] {'chan','pix'}, use_global_device_ids=true, to_apply=%region_11.11 | all-reduce | flops 64 | bytes 512 | tf_op jit(solution)/shard_map/while/body/eval_jaxpr/psum | solution.py:85
  2279.1 39.4 %psum.113 = f32[1,4,16]{2,1,0:T(4,128)} all-reduce(f32[1,4,16]{2,1,0:T(4,128)} %convolution_bitcast_fusion.10), channel_id=1, replica_groups=mesh['chan'=4,'pix'=8] {'chan','pix'}, use_global_device_ids=true, to_apply=%region_13.13 | all-reduce | flops 64 | bytes 512 | tf_op jit(solution)/shard_map/while/body/eval_jaxpr/psum | solution.py:85
  2329.2 42.4 %all-gather.6.cloned.1.call-done = f32[1,4,256,512]{3,1,0,2:T(4,128)} async-done(((f32[1,4,64,512]{3,1,0,2:T(4,128)}), f32[1,4,256,512]{3,1,0,2:T(4,128)}) %all-gather.6.cloned.1.call-update) | async-done | bytes 2097168 | tf_op jit(solution)/shard_map/while/body/eval_jaxpr/all_gather | solution.py:222
  2383.0 40.7 %all-reduce.23 = (f32[1,1024]{1,0:T(1,128)}, f32[1,1024]{1,0:T(1,128)}) all-reduce(f32[1,1024]{1,0:T(1,128)} %constant_dynamic-update-slice_fusion.32, f32[1,1024]{1,0:T(1,128)} %constant_dynamic-update-slice_fusion.33), channel_id=1, replica_groups=mesh['chan'=4,'pix'=8] {'chan','pix'}, use_global_device_ids=true, to_apply=%region_17.17 | all-reduce | flops 2048 | bytes 16384 | tf_op jit(solution)/shard_map/while/body/eval_jaxpr/psum | solution.py:77
  2440.4 8.0 fusion.200
  2450.8 48.3 %all-reduce.24 = (f32[1,1024]{1,0:T(1,128)}, f32[1,1024]{1,0:T(1,128)}) all-reduce(f32[1,1024]{1,0:T(1,128)} %constant_dynamic-update-slice_fusion.34, f32[1,1024]{1,0:T(1,128)} %constant_dynamic-update-slice_fusion.35), channel_id=1, replica_groups=mesh['chan'=4,'pix'=8] {'chan','pix'}, use_global_device_ids=true, to_apply=%region_21.21 | all-reduce | flops 2048 | bytes 16384 | tf_op jit(solution)/shard_map/while/body/eval_jaxpr/psum | solution.py:77
  2534.1 63.8 %all-reduce.31.cloned.1.call-done = f32[1,4,256,512]{3,1,0,2:T(4,128)} async-done(((f32[1,4,256,512]{3,1,0,2:T(4,128)}), f32[1,4,256,512]{3,1,0,2:T(4,128)}) %all-reduce.31.cloned.1.call-update) | async-done | bytes 2097168 | tf_op jit(solution)/shard_map/while
  2635.3 17.7 fusion
  2674.3 273.2 %while.34 = (s32[]{:T(128)}, f32[16,64,8,80]{3,2,1,0:T(8,128)}, s32[16,4]{0,1:T(4,128)S(1)}, f32[16,64,8,64]{1,2,3,0:T(8,128)}, s32[]{:T(128)}, /*index=5*/s32[4]{0:T(128)S(1)}, s32[]{:T(128)}) while((s32[]{:T(128)}, f32[16,64,8,80]{3,2,1,0:T(8,128)}, s32[16,4]{0,1:T(4,128)S(1)}, f32[16,64,8,64]{1,2,3,0:T(8,128)}, s32[]{:T(128)}, ...), condition=%wide.while_cond, body=%wide.while_body.sunk | while | flops 32797 | bytes 1179851 | solution.py:67
  2682.1 11.3 dynamic-update-slice.33
  2701.3 11.3 dynamic-update-slice.33
  2720.5 11.3 dynamic-update-slice.33
  2739.7 11.3 dynamic-update-slice.33
  2801.8 11.3 dynamic-update-slice.33
  2821.0 11.3 dynamic-update-slice.33
  2840.2 11.3 dynamic-update-slice.33
  2859.4 11.3 dynamic-update-slice.33
  2878.6 11.3 dynamic-update-slice.33
  2897.8 11.3 dynamic-update-slice.33
  2917.0 11.3 dynamic-update-slice.33
  2936.2 11.3 dynamic-update-slice.33
  2962.4 16.4 all-gather
  (1375 shorter events, 745.9 us)
Async XLA Ops:
  8.1 32.4 %copy-start.112 = (pred[16]{0:T(512)(128)(4,1)}, pred[16]{0:T(512)(128)(4,1)S(1)}, u32[]{:S(2)}) copy-start(pred[16]{0:T(512)(128)(4,1)S(1)} %eq.30) | copy-start | bytes 52
  80.4 47.6 %all-gather.4.cloned.1.call-start = ((), (), s32[]{:S(2)}) async-start(), calls=%async_computation | async-start | bytes 2621440 | tf_op jit(solution)/shard_map/while/body/eval_jaxpr/all_gather | solution.py:175
  82.3 255.7 %all-reduce.29.cloned.1.call-start = ((), (), s32[]{:S(2)}) async-start(), calls=%async_computation.1 | async-start | bytes 4194304 | tf_op jit(solution)/shard_map/while
  83.7 90.9 %copy-start.72 = (f32[1,256]{1,0:T(1,128)}, f32[1,256]{1,0:T(1,128)S(1)}, u32[]{:S(2)}) copy-start(f32[1,256]{1,0:T(1,128)S(1)} %get-tuple-element.955) | copy-start | bytes 3076 | tf_op jit(solution)/shard_map/while
  85.1 89.6 %copy-start.19 = (f32[1,256]{1,0:T(1,128)}, f32[1,256]{1,0:T(1,128)S(1)}, u32[]{:S(2)}) copy-start(f32[1,256]{1,0:T(1,128)S(1)} %get-tuple-element.956) | copy-start | bytes 3076 | tf_op jit(solution)/shard_map/while
  134.3 41.5 %copy-start.2 = (f32[4,512,256]{2,1,0:T(8,128)}, f32[4,512,256]{2,1,0:T(8,128)S(1)}, u32[]{:S(2)}) copy-start(f32[4,512,256]{2,1,0:T(8,128)S(1)} %get-tuple-element.953) | copy-start | bytes 6291460 | tf_op jit(solution)/shard_map/while
  175.9 7.0 collective-permute-start
  179.4 3.8 collective-permute-start.1
  251.0 231.2 %all-gather.6.cloned.1.call-start = ((), (), s32[]{:S(2)}) async-start(), calls=%async_computation.2 | async-start | bytes 2621440 | tf_op jit(solution)/shard_map/while/body/eval_jaxpr/all_gather | solution.py:222
  436.0 272.5 %all-reduce.31.cloned.1.call-start = ((), (), s32[]{:S(2)}) async-start(), calls=%async_computation.3 | async-start | bytes 4194304 | tf_op jit(solution)/shard_map/while
  542.9 5.7 collective-permute-start.2
  546.5 3.8 collective-permute-start.3
  640.4 68.1 %copy-start.8 = (f32[1,4,64,512]{3,2,1,0:T(8,128)S(1)}, f32[1,4,64,512]{3,2,1,0:T(8,128)}, u32[]{:S(2)}) copy-start(f32[1,4,64,512]{3,2,1,0:T(8,128)} %constant_dynamic-slice_fusion.19) | copy-start | bytes 1572868 | tf_op jit(solution)/shard_map/while
  644.0 66.8 %copy-start.13 = (f32[256,256]{1,0:T(8,128)}, f32[256,256]{1,0:T(8,128)S(1)}, u32[]{:S(2)}) copy-start(f32[256,256]{1,0:T(8,128)S(1)} %fusion.202) | copy-start | bytes 786436 | tf_op jit(solution)/shard_map/while
  710.8 46.8 %all-gather.4.cloned.1.call-start = ((), (), s32[]{:S(2)}) async-start(), calls=%async_computation | async-start | bytes 2621440 | tf_op jit(solution)/shard_map/while/body/eval_jaxpr/all_gather | solution.py:175
  712.7 254.9 %all-reduce.29.cloned.1.call-start = ((), (), s32[]{:S(2)}) async-start(), calls=%async_computation.1 | async-start | bytes 4194304 | tf_op jit(solution)/shard_map/while
  714.1 90.1 %copy-start.72 = (f32[1,256]{1,0:T(1,128)}, f32[1,256]{1,0:T(1,128)S(1)}, u32[]{:S(2)}) copy-start(f32[1,256]{1,0:T(1,128)S(1)} %get-tuple-element.955) | copy-start | bytes 3076 | tf_op jit(solution)/shard_map/while
  715.4 88.8 %copy-start.19 = (f32[1,256]{1,0:T(1,128)}, f32[1,256]{1,0:T(1,128)S(1)}, u32[]{:S(2)}) copy-start(f32[1,256]{1,0:T(1,128)S(1)} %get-tuple-element.956) | copy-start | bytes 3076 | tf_op jit(solution)/shard_map/while
  763.9 41.5 %copy-start.2 = (f32[4,512,256]{2,1,0:T(8,128)}, f32[4,512,256]{2,1,0:T(8,128)S(1)}, u32[]{:S(2)}) copy-start(f32[4,512,256]{2,1,0:T(8,128)S(1)} %get-tuple-element.953) | copy-start | bytes 6291460 | tf_op jit(solution)/shard_map/while
  805.5 7.0 collective-permute-start
  809.0 3.8 collective-permute-start.1
  880.5 231.2 %all-gather.6.cloned.1.call-start = ((), (), s32[]{:S(2)}) async-start(), calls=%async_computation.2 | async-start | bytes 2621440 | tf_op jit(solution)/shard_map/while/body/eval_jaxpr/all_gather | solution.py:222
  1065.6 272.5 %all-reduce.31.cloned.1.call-start = ((), (), s32[]{:S(2)}) async-start(), calls=%async_computation.3 | async-start | bytes 4194304 | tf_op jit(solution)/shard_map/while
  1172.5 5.7 collective-permute-start.2
  1176.1 3.8 collective-permute-start.3
  1270.7 67.4 %copy-start.8 = (f32[1,4,64,512]{3,2,1,0:T(8,128)S(1)}, f32[1,4,64,512]{3,2,1,0:T(8,128)}, u32[]{:S(2)}) copy-start(f32[1,4,64,512]{3,2,1,0:T(8,128)} %constant_dynamic-slice_fusion.19) | copy-start | bytes 1572868 | tf_op jit(solution)/shard_map/while
  1274.3 66.1 %copy-start.13 = (f32[256,256]{1,0:T(8,128)}, f32[256,256]{1,0:T(8,128)S(1)}, u32[]{:S(2)}) copy-start(f32[256,256]{1,0:T(8,128)S(1)} %fusion.202) | copy-start | bytes 786436 | tf_op jit(solution)/shard_map/while
  1340.4 47.1 %all-gather.4.cloned.1.call-start = ((), (), s32[]{:S(2)}) async-start(), calls=%async_computation | async-start | bytes 2621440 | tf_op jit(solution)/shard_map/while/body/eval_jaxpr/all_gather | solution.py:175
  1342.3 255.2 %all-reduce.29.cloned.1.call-start = ((), (), s32[]{:S(2)}) async-start(), calls=%async_computation.1 | async-start | bytes 4194304 | tf_op jit(solution)/shard_map/while
  1343.7 90.4 %copy-start.72 = (f32[1,256]{1,0:T(1,128)}, f32[1,256]{1,0:T(1,128)S(1)}, u32[]{:S(2)}) copy-start(f32[1,256]{1,0:T(1,128)S(1)} %get-tuple-element.955) | copy-start | bytes 3076 | tf_op jit(solution)/shard_map/while
  1345.0 89.1 %copy-start.19 = (f32[1,256]{1,0:T(1,128)}, f32[1,256]{1,0:T(1,128)S(1)}, u32[]{:S(2)}) copy-start(f32[1,256]{1,0:T(1,128)S(1)} %get-tuple-element.956) | copy-start | bytes 3076 | tf_op jit(solution)/shard_map/while
  1393.8 41.5 %copy-start.2 = (f32[4,512,256]{2,1,0:T(8,128)}, f32[4,512,256]{2,1,0:T(8,128)S(1)}, u32[]{:S(2)}) copy-start(f32[4,512,256]{2,1,0:T(8,128)S(1)} %get-tuple-element.953) | copy-start | bytes 6291460 | tf_op jit(solution)/shard_map/while
  1435.4 7.0 collective-permute-start
  1438.9 3.8 collective-permute-start.1
  1510.4 231.2 %all-gather.6.cloned.1.call-start = ((), (), s32[]{:S(2)}) async-start(), calls=%async_computation.2 | async-start | bytes 2621440 | tf_op jit(solution)/shard_map/while/body/eval_jaxpr/all_gather | solution.py:222
  1695.5 272.5 %all-reduce.31.cloned.1.call-start = ((), (), s32[]{:S(2)}) async-start(), calls=%async_computation.3 | async-start | bytes 4194304 | tf_op jit(solution)/shard_map/while
  1802.4 5.7 collective-permute-start.2
  1806.0 3.8 collective-permute-start.3
  1900.6 67.4 %copy-start.8 = (f32[1,4,64,512]{3,2,1,0:T(8,128)S(1)}, f32[1,4,64,512]{3,2,1,0:T(8,128)}, u32[]{:S(2)}) copy-start(f32[1,4,64,512]{3,2,1,0:T(8,128)} %constant_dynamic-slice_fusion.19) | copy-start | bytes 1572868 | tf_op jit(solution)/shard_map/while
  1904.2 66.1 %copy-start.13 = (f32[256,256]{1,0:T(8,128)}, f32[256,256]{1,0:T(8,128)S(1)}, u32[]{:S(2)}) copy-start(f32[256,256]{1,0:T(8,128)S(1)} %fusion.202) | copy-start | bytes 786436 | tf_op jit(solution)/shard_map/while
  1970.3 47.1 %all-gather.4.cloned.1.call-start = ((), (), s32[]{:S(2)}) async-start(), calls=%async_computation | async-start | bytes 2621440 | tf_op jit(solution)/shard_map/while/body/eval_jaxpr/all_gather | solution.py:175
  1972.2 255.3 %all-reduce.29.cloned.1.call-start = ((), (), s32[]{:S(2)}) async-start(), calls=%async_computation.1 | async-start | bytes 4194304 | tf_op jit(solution)/shard_map/while
  1973.5 90.4 %copy-start.72 = (f32[1,256]{1,0:T(1,128)}, f32[1,256]{1,0:T(1,128)S(1)}, u32[]{:S(2)}) copy-start(f32[1,256]{1,0:T(1,128)S(1)} %get-tuple-element.955) | copy-start | bytes 3076 | tf_op jit(solution)/shard_map/while
  1974.9 89.1 %copy-start.19 = (f32[1,256]{1,0:T(1,128)}, f32[1,256]{1,0:T(1,128)S(1)}, u32[]{:S(2)}) copy-start(f32[1,256]{1,0:T(1,128)S(1)} %get-tuple-element.956) | copy-start | bytes 3076 | tf_op jit(solution)/shard_map/while
  2023.7 41.5 %copy-start.2 = (f32[4,512,256]{2,1,0:T(8,128)}, f32[4,512,256]{2,1,0:T(8,128)S(1)}, u32[]{:S(2)}) copy-start(f32[4,512,256]{2,1,0:T(8,128)S(1)} %get-tuple-element.953) | copy-start | bytes 6291460 | tf_op jit(solution)/shard_map/while
  2065.3 7.0 collective-permute-start
  2068.8 3.8 collective-permute-start.1
  2140.3 231.2 %all-gather.6.cloned.1.call-start = ((), (), s32[]{:S(2)}) async-start(), calls=%async_computation.2 | async-start | bytes 2621440 | tf_op jit(solution)/shard_map/while/body/eval_jaxpr/all_gather | solution.py:222
  2325.4 272.5 %all-reduce.31.cloned.1.call-start = ((), (), s32[]{:S(2)}) async-start(), calls=%async_computation.3 | async-start | bytes 4194304 | tf_op jit(solution)/shard_map/while
  2432.3 5.7 collective-permute-start.2
  2435.9 3.8 collective-permute-start.3
  2530.5 67.4 %copy-start.8 = (f32[1,4,64,512]{3,2,1,0:T(8,128)S(1)}, f32[1,4,64,512]{3,2,1,0:T(8,128)}, u32[]{:S(2)}) copy-start(f32[1,4,64,512]{3,2,1,0:T(8,128)} %constant_dynamic-slice_fusion.19) | copy-start | bytes 1572868 | tf_op jit(solution)/shard_map/while
  2534.0 66.1 %copy-start.13 = (f32[256,256]{1,0:T(8,128)}, f32[256,256]{1,0:T(8,128)S(1)}, u32[]{:S(2)}) copy-start(f32[256,256]{1,0:T(8,128)S(1)} %fusion.202) | copy-start | bytes 786436 | tf_op jit(solution)/shard_map/while
  2608.6 11.9 copy-start.104
  2608.6 12.5 copy-start.99
  2608.6 13.8 copy-start.102
  2608.6 13.8 copy-start.105
  2608.7 15.6 copy-start.114
  2608.7 16.9 copy-start.103
  2620.5 13.0 copy-start.111
  2632.6 24.5 copy-start.14
  2653.0 305.7 %collective-permute-start.4 = (f32[32,1024]{1,0:T(8,128)}, f32[32,1024]{1,0:T(8,128)}, u32[]{:S(2)}, u32[]{:S(2)}) collective-permute-start(f32[32,1024]{1,0:T(8,128)} %fusion), channel_id=1, source_target_pairs={{0,1},{1,2},{2,3},{3,4},{4,5},{5,6},{6,7},{8,9},{9,10},{10,11},{11... | collective-permute-start | bytes 393224
  2655.7 303.0 %collective-permute-start.5 = (f32[10,1024]{1,0:T(8,128)}, f32[10,1024]{1,0:T(8,128)}, u32[]{:S(2)}, u32[]{:S(2)}) collective-permute-start(f32[10,1024]{1,0:T(8,128)} %slice.727), channel_id=1, source_target_pairs={{0,2},{1,3},{2,4},{3,5},{4,6},{5,7},{8,10},{9,11},{10,12},{11,13},... | collective-permute-start | bytes 122888
  2952.2 8.5 copy-start.85
  (388 other events, 1134.9 us)
Sparse Core Ops, SparseCore 0:
  82.8 45.1 all-gather.3
  251.1 86.9 all-reduce.28
  436.2 45.9 all-gather.5
  621.9 86.6 all-reduce.30
  712.9 44.6 all-gather.3
  880.7 86.9 all-reduce.28
  1065.8 45.9 all-gather.5
  1251.4 86.6 all-reduce.30
  1342.8 44.6 all-gather.3
  1510.5 86.9 all-reduce.28
  1695.6 45.9 all-gather.5
  1881.3 86.6 all-reduce.30
  1972.7 44.6 all-gather.3
  2140.4 86.9 all-reduce.28
  2325.5 45.9 all-gather.5
  2511.2 86.6 all-reduce.30
where the time goes:
time: 3010 us; the launch traced here: 2990 us
  blocking collectives  1060 us (35%)
  waiting for transfers between devices  935 us (31%)
  local copies, waits for them, and re-layouts  443 us (15%)
  other arithmetic  320 us (11%)
  matrix products  131 us (4%)
  starting transfers between devices  41.7 us (1%)
  loops' own time  40.7 us (1%)
    psum x16, blocking collectives, pixel_totals(): total_one, total_two = lax.psum((wide_one, wide_two), ('chan', 'pix'))  710 us
    while x24, waiting for transfers between devices  589 us
    psum x8, blocking collectives, frame_tally(): total = lax.psum(values, ('chan', 'pix'))  319 us
    scatter x80, local copies, waits for them, and re-layouts  176 us
    all_gather x4, waiting for transfers between devices, run_group(): features = lax.all_gather(crops, 'chan', axis=2, tiled=True)  170 us
    all_gather x4, waiting for transfers between devices, run_group(): grad_full = lax.all_gather(grad_proj, 'chan', axis=2, tiled=True)  169 us
    scatter x32, other arithmetic  96.9 us
  transfers between devices with their start and end apart: 34, of which 24 were waited for; matrix products, arithmetic and copies ran while one was open for 15% of the time, Pallas kernels for 0%

commit v1 on v0

v1 whole, which is shorter than its diff:
```python
from functools import partial
import math

import jax
import jax.numpy as jnp
from jax import lax
from jax.experimental import pallas as pl
from jax.experimental.pallas import tpu as pltpu
from jax.sharding import Mesh, PartitionSpec as P

K = 5
FRAME_ROWS = 64
FRAME_COLUMNS = 64
CLIP_LEN = 4
MB = 4
STEP = 5
WIN = 80
SUB = 8
TAPS = K * K
HALO_IN = 4
HALO_OUT = 2

norm_eps = 1e-05
beta_first = 0.5
beta_second = 0.6
adam_eps = 1e-08
weight_decay = 0.1

F32 = jnp.float32
BF16 = jnp.bfloat16
ALL = ("chan", "hi", "lo")
PIX = ("hi", "lo")
SPREAD = ("chan", "lo")
MIB = 2**20


def params(mib, dims=1):
    return pltpu.CompilerParams(vmem_limit_bytes=mib * MIB, dimension_semantics=("arbitrary",) * dims)


def cost(flops, moved):
    return pl.CostEstimate(flops=int(flops), bytes_accessed=int(moved), transcendentals=0)


def sigmoid(v):
    return 0.5 * jnp.tanh(0.5 * v) + 0.5


def split(v):
    high = v.astype(BF16)
    return high, (v - high.astype(F32)).astype(BF16)


def dot(a, b):
    return jnp.dot(a, b, preferred_element_type=F32)


def dot3(a, b):
    return dot(a[0], b[0]) + (dot(a[0], b[1]) + dot(a[1], b[0]))


def exact_dot(a, b):
    return jnp.dot(a, b, preferred_element_type=F32, precision=lax.Precision.HIGHEST)


def total(refs):
    value = refs[0][...]
    for ref in refs[1:]:
        value = value + ref[...]
    return value


def norm_terms(sums, count, gain, bias):
    mean = sums[0:1] / count
    inverse = lax.rsqrt(sums[1:2] / count - mean * mean + norm_eps)
    scale = gain * inverse
    return mean, inverse, scale, bias - mean * scale


def back_terms(sums, back, count, gain):
    mean = sums[0:1] / count
    inverse = lax.rsqrt(sums[1:2] / count - mean * mean + norm_eps)
    a = gain * inverse
    b = -a * inverse * (back[1:2] / count)
    return a, b, -a * (back[0:1] / count) - b * mean


def exchange(x, stride):
    n = lax.axis_size(ALL)
    return lax.ppermute(x, ALL, [(i, i ^ stride) for i in range(n)])


def shares(x, base, size):
    bits = size.bit_length() - 1
    parts = [x]
    if bits % 2:
        parts = [x, exchange(x, base)]
        base, bits = base * 2, bits - 1
    while bits:
        x = sum(parts[1:], parts[0])
        parts = [x] + [exchange(x, base * k) for k in (1, 2, 3)]
        base, bits = base * 4, bits - 2
    return parts


def deal(x):
    return lax.all_to_all(x, SPREAD, 0, 0, tiled=True)


def edge(x, rows, band, first):
    if rows >= band:
        n = rows // band
        return x[:, :n] if first else x[:, x.shape[1] - n :]
    width = rows * FRAME_COLUMNS
    return x[:, :1, :, :width] if first else x[:, -1:, :, x.shape[3] - width :]


def rims(x, rows, band):
    n = lax.axis_size("hi")
    down = [(i, i + 1) for i in range(n - 1)]
    up = [(i + 1, i) for i in range(n - 1)]
    top = lax.ppermute(edge(x, rows, band, False), "hi", down)
    low = lax.ppermute(edge(x, rows, band, True), "hi", up)
    return top, low


def source_column(p, left, flip):
    row, c, s = p // FRAME_COLUMNS, (p // SUB) % SUB, p % SUB
    j = s * SUB + c
    return row * WIN + left + jnp.where(flip == 1, FRAME_COLUMNS - 1 - j, j)


def plain_place(p):
    row, c, s = p // FRAME_COLUMNS, (p // SUB) % SUB, p % SUB
    return row * FRAME_COLUMNS + s * SUB + c


def pick(x, chosen):
    rows = x.shape[0] * x.shape[1]
    high, low = split(x.reshape(rows, x.shape[2]))
    return (dot(high, chosen) + dot(low, chosen)).reshape(x.shape[0], x.shape[1], chosen.shape[1])


def crop_kernel(left_ref, flip_ref, raw_ref, out_ref):
    k = pl.program_id(0)
    width, area = raw_ref.shape[2], out_ref.shape[2]
    p = lax.broadcasted_iota(jnp.int32, (1, area), 1)
    place = source_column(p, left_ref[k], flip_ref[k])
    q = lax.broadcasted_iota(jnp.int32, (width, area), 0)
    out_ref[...] = pick(raw_ref[...], (q == place).astype(F32).astype(BF16))


def crop(raw, left, flip):
    frames, chans, width = raw.shape
    area = width // WIN * FRAME_COLUMNS
    return pl.pallas_call(
        crop_kernel,
        grid=(frames // CLIP_LEN,),
        in_specs=[
            pl.BlockSpec(memory_space=pltpu.SMEM),
            pl.BlockSpec(memory_space=pltpu.SMEM),
            pl.BlockSpec((CLIP_LEN, chans, width), lambda k: (k, 0, 0)),
        ],
        out_specs=pl.BlockSpec((CLIP_LEN, chans, area), lambda k: (k, 0, 0)),
        out_shape=jax.ShapeDtypeStruct((frames, chans, area), F32),
        compiler_params=params(32),
        cost_estimate=cost(4 * frames * chans * width * area, 4 * frames * chans * (width + area)),
        name="crop",
    )(left, flip, raw)


def order_kernel(x_ref, out_ref):
    area = x_ref.shape[2]
    p = lax.broadcasted_iota(jnp.int32, (1, area), 1)
    q = lax.broadcasted_iota(jnp.int32, (area, area), 0)
    out_ref[...] = pick(x_ref[...], (q == plain_place(p)).astype(F32).astype(BF16))


def order(x):
    frames, chans, area = x.shape
    return pl.pallas_call(
        order_kernel,
        grid=(frames // CLIP_LEN,),
        in_specs=[pl.BlockSpec((CLIP_LEN, chans, area), lambda k: (k, 0, 0))],
        out_specs=pl.BlockSpec((CLIP_LEN, chans, area), lambda k: (k, 0, 0)),
        out_shape=jax.ShapeDtypeStruct((frames, chans, area), F32),
        compiler_params=params(32),
        cost_estimate=cost(4 * frames * chans * area * area, 8 * frames * chans * area),
        name="order",
    )(x)


def restore_kernel(x_ref, out_ref):
    area = x_ref.shape[2]
    p = lax.broadcasted_iota(jnp.int32, (area, 1), 0)
    q = lax.broadcasted_iota(jnp.int32, (area, area), 1)
    out_ref[...] = pick(x_ref[...], (q == plain_place(p)).astype(F32).astype(BF16))


def restore(x):
    frames, chans, area = x.shape
    return pl.pallas_call(
        restore_kernel,
        grid=(frames // CLIP_LEN,),
        in_specs=[pl.BlockSpec((CLIP_LEN, chans, area), lambda k: (k, 0, 0))],
        out_specs=pl.BlockSpec((CLIP_LEN, chans, area), lambda k: (k, 0, 0)),
        out_shape=jax.ShapeDtypeStruct((frames, chans, area), F32),
        compiler_params=params(32),
        cost_estimate=cost(4 * frames * chans * area * area, 8 * frames * chans * area),
        name="restore",
    )(x)


def uncrop_kernel(left_ref, flip_ref, x_ref, out_ref):
    k = pl.program_id(0)
    area, width = x_ref.shape[2], out_ref.shape[2]
    p = lax.broadcasted_iota(jnp.int32, (area, 1), 0)
    place = source_column(p, left_ref[k], flip_ref[k])
    q = lax.broadcasted_iota(jnp.int32, (area, width), 1)
    out_ref[...] = pick(x_ref[...], (q == place).astype(F32).astype(BF16))


def uncrop(x, left, flip):
    frames, chans, area = x.shape
    width = area // FRAME_COLUMNS * WIN
    return pl.pallas_call(
        uncrop_kernel,
        grid=(frames // CLIP_LEN,),
        in_specs=[
            pl.BlockSpec(memory_space=pltpu.SMEM),
            pl.BlockSpec(memory_space=pltpu.SMEM),
            pl.BlockSpec((CLIP_LEN, chans, area), lambda k: (k, 0, 0)),
        ],
        out_specs=pl.BlockSpec((CLIP_LEN, chans, width), lambda k: (k, 0, 0)),
        out_shape=jax.ShapeDtypeStruct((frames, chans, width), F32),
        compiler_params=params(32),
        cost_estimate=cost(4 * frames * chans * width * area, 4 * frames * chans * (width + area)),
        name="uncrop",
    )(left, flip, x)


def chunks(width):
    step = 256 if width % 256 == 0 else width
    return [slice(i, i + step) for i in range(0, width, step)]


def expand_kernel(x_ref, top_ref, low_ref, w_ref, own_ref, halo_ref, sum_ref, w_high, w_low):
    t, n = pl.program_id(0), pl.num_programs(0) - 1
    chan_all, hidden = w_ref.shape

    @pl.when(t == 0)
    def _():
        w_high[...], w_low[...] = split(w_ref[...])
        sum_ref[...] = jnp.zeros_like(sum_ref)

    @pl.when(t < n)
    def _():
        x = split(x_ref[:, 0].reshape(chan_all, x_ref.shape[3]).T)
        for cut in chunks(hidden):
            y = dot3(x, (w_high[:, cut], w_low[:, cut]))
            own_ref[0, :, cut] = y
            sum_ref[0:1, cut] += jnp.sum(y, axis=0, keepdims=True)
            sum_ref[1:2, cut] += jnp.sum(y * y, axis=0, keepdims=True)

    @pl.when(t == n)
    def _():
        width = top_ref.shape[3]
        for side, ref in enumerate((top_ref, low_ref)):
            for k in range(ref.shape[1]):
                x = split(ref[:, k].reshape(chan_all, width).T)
                for cut in chunks(hidden):
                    halo_ref[side, k * width : (k + 1) * width, cut] = dot3(x, (w_high[:, cut], w_low[:, cut]))


def whole(shape):
    return pl.BlockSpec(shape, lambda *_: (0,) * len(shape))


def expand(x, top, low, w):
    nz, bands, chans, area = x.shape
    hidden = w.shape[1]
    halo = HALO_IN * FRAME_COLUMNS
    last = bands - 1
    return pl.pallas_call(
        expand_kernel,
        grid=(bands + 1,),
        in_specs=[
            pl.BlockSpec((nz, 1, chans, area), lambda t: (0, jnp.minimum(t, last), 0, 0)),
            whole(top.shape),
            whole(low.shape),
            whole(w.shape),
        ],
        out_specs=[
            pl.BlockSpec((1, area, hidden), lambda t: (jnp.minimum(t, last), 0, 0)),
            whole((2, halo, hidden)),
            whole((2, hidden)),
        ],
        out_shape=[
            jax.ShapeDtypeStruct((bands, area, hidden), F32),
            jax.ShapeDtypeStruct((2, halo, hidden), F32),
            jax.ShapeDtypeStruct((2, hidden), F32),
        ],
        scratch_shapes=[pltpu.VMEM(w.shape, BF16), pltpu.VMEM(w.shape, BF16)],
        compiler_params=params(40),
        cost_estimate=cost(6 * (bands * area + 2 * halo) * hidden * nz * chans, 4 * bands * area * hidden),
        name="expand",
    )(x, top, low, w)


def fill_sides(pad, row):
    s = lax.broadcasted_iota(jnp.int32, (SUB, 128), 0)
    for k in range(2):
        left = pltpu.roll(pad[row, SUB + k], 1, 0)
        pad[row, k] = jnp.where(s == 0, 0.0, left)
        right = pltpu.roll(pad[row, 2 + k], SUB - 1, 0)
        pad[row, SUB + 2 + k] = jnp.where(s == SUB - 1, 0.0, right)


def clear_rows(pad, start, count):
    for row in range(start, start + count):
        pad[row] = jnp.zeros(pad.shape[1:], F32)


def tap_rows(pad, w_ref, start, count, c, flipped=False):
    acc = [None] * count
    for b in range(K):
        for row in range(count + K - 1):
            value = pad[start + row, c + b]
            for a in range(K):
                o = row - a
                if 0 <= o < count:
                    tap = a * K + b
                    term = value * w_ref[TAPS - 1 - tap if flipped else tap]
                    acc[o] = term if acc[o] is None else acc[o] + term
    return acc


def spread_kernel(parts, count, side_ref, own_ref, halo_ref, gain_ref, bias_ref, w_ref, *rest):
    sums, (out_ref, edge_ref, sum_ref, pad, terms) = rest[:parts], rest[parts:]
    rows = own_ref.shape[0]
    _, _, scale, shift = norm_terms(total(sums), count, gain_ref[0:1], bias_ref[0:1])
    terms[0] = jnp.broadcast_to(scale, (SUB, 128))
    terms[1] = jnp.broadcast_to(shift, (SUB, 128))

    def act(value):
        v = value * terms[0] + terms[1]
        return v * sigmoid(v)

    def own_row(r, _):
        for c in range(SUB):
            pad[r + HALO_IN, c + 2] = act(own_ref[r, c])
        fill_sides(pad, r + HALO_IN)
        return 0

    lax.fori_loop(0, rows, own_row, 0)
    for side, start in ((0, 0), (1, rows + HALO_IN)):

        @pl.when(side_ref[side] == 1)
        def _(side=side, start=start):
            for r in range(HALO_IN):
                for c in range(SUB):
                    pad[start + r, c + 2] = act(halo_ref[side, r, c])
                fill_sides(pad, start + r)

        @pl.when(side_ref[side] == 0)
        def _(start=start):
            clear_rows(pad, start, HALO_IN)

    def group(i, carry):
        one, two = carry
        r = i * SUB
        for c in range(SUB):
            acc = tap_rows(pad, w_ref, r + 2, SUB, c)
            for o in range(SUB):
                out_ref[r + o, c] = acc[o]
                one = one + acc[o]
                two = two + acc[o] * acc[o]
        return one, two

    zero = jnp.zeros((SUB, 128), F32)
    one, two = lax.fori_loop(0, rows // SUB, group, (zero, zero))
    sum_ref[0:1] = jnp.sum(one, axis=0, keepdims=True)
    sum_ref[1:2] = jnp.sum(two, axis=0, keepdims=True)
    for side, start in ((0, 0), (1, rows + 2)):

        @pl.when(side_ref[side] == 1)
        def _(side=side, start=start):
            for c in range(SUB):
                acc = tap_rows(pad, w_ref, start, HALO_OUT, c)
                for o in range(HALO_OUT):
                    edge_ref[side, o, c] = acc[o]

        @pl.when(side_ref[side] == 0)
        def _(side=side):
            edge_ref[side] = jnp.zeros(edge_ref.shape[1:], F32)


def lanes(shape):
    lead = len(shape) - 1
    return pl.BlockSpec(tuple(shape[:-1]) + (128,), lambda e: (0,) * lead + (e,))


def spread(count, side, own, halo, gains, biases, taps, sums):
    rows, hidden = own.shape[0], own.shape[-1]
    arrays = [own, halo, gains, biases, taps, *sums]
    return pl.pallas_call(
        partial(spread_kernel, len(sums), count),
        grid=(hidden // 128,),
        in_specs=[pl.BlockSpec(memory_space=pltpu.SMEM)] + [lanes(a.shape) for a in arrays],
        out_specs=[
            lanes((rows, SUB, SUB, hidden)),
            lanes((2, HALO_OUT, SUB, SUB, hidden)),
            lanes((2, hidden)),
        ],
        out_shape=[
            jax.ShapeDtypeStruct((rows, SUB, SUB, hidden), F32),
            jax.ShapeDtypeStruct((2, HALO_OUT, SUB, SUB, hidden), F32),
            jax.ShapeDtypeStruct((2, hidden), F32),
        ],
        scratch_shapes=[
            pltpu.VMEM((rows + 2 * HALO_IN, SUB + 4, SUB, 128), F32),
            pltpu.VMEM((2, SUB, 128), F32),
        ],
        compiler_params=params(40),
        cost_estimate=cost(rows * 64 * hidden * 800, 8 * rows * 64 * hidden),
        name="spread",
    )(side, *arrays)


def as_row(columns):
    width = columns.shape[1]
    folded = columns[:, 0:128]
    for i in range(128, width, 128):
        folded = folded + columns[:, i : i + 128]
    return jnp.sum(folded.T, axis=0, keepdims=True)


def gather_kernel(parts, count, own_ref, gout_ref, gain_ref, bias_ref, wt_ref, *rest):
    sums, (m_ref, s_ref, se_ref) = rest[:parts], rest[parts:]
    t = pl.program_id(0)
    chan_all, hidden = wt_ref.shape

    @pl.when(t == 0)
    def _():
        m_ref[...] = jnp.zeros_like(m_ref)
        s_ref[...] = jnp.zeros_like(s_ref)

    _, _, scale, shift = norm_terms(total(sums), count, gain_ref[1:2], bias_ref[1:2])
    gout = split(gout_ref[:, 0].reshape(chan_all, gout_ref.shape[3]))
    for cut in chunks(hidden):
        v = own_ref[0, :, cut] * scale[:, cut] + shift[:, cut]
        act = v * sigmoid(v)
        s_ref[0:1, cut] += jnp.sum(act, axis=0, keepdims=True)
        m_ref[:, cut] += dot3(gout, split(act))

    @pl.when(t == pl.num_programs(0) - 1)
    def _():
        wt = wt_ref[...]
        se_ref[0:1] = as_row(s_ref[...] * wt)
        se_ref[1:2] = as_row(m_ref[...] * wt)


def gather(count, own, gout, gains, biases, wt, sums):
    nz, bands, chans, area = gout.shape
    hidden = wt.shape[1]
    chan_all = nz * chans
    return pl.pallas_call(
        partial(gather_kernel, len(sums), count),
        grid=(bands,),
        in_specs=[
            pl.BlockSpec((1, area, hidden), lambda t: (t, 0, 0)),
            pl.BlockSpec((nz, 1, chans, area), lambda t: (0, t, 0, 0)),
            whole(gains.shape),
            whole(biases.shape),
            whole(wt.shape),
        ]
        + [whole(s.shape) for s in sums],
        out_specs=[whole((chan_all, hidden)), whole((1, hidden)), whole((2, chan_all))],
        out_shape=[
            jax.ShapeDtypeStruct((chan_all, hidden), F32),
            jax.ShapeDtypeStruct((1, hidden), F32),
            jax.ShapeDtypeStruct((2, chan_all), F32),
        ],
        compiler_params=params(40),
        cost_estimate=cost(6 * bands * area * hidden * chan_all, 4 * bands * area * hidden),
        name="gather",
    )(own, gout, gains, biases, wt, *sums)


def column(row):
    return jnp.broadcast_to(row, (SUB, row.shape[1])).T[:, 0:1]


def padded_dot(row, matrix):
    return exact_dot(jnp.broadcast_to(row, (SUB, row.shape[1])), matrix)[0:1]


def proj_back_kernel(
    pairs,
    parts,
    count,
    side_ref,
    own_ref,
    halo_ref,
    gout_ref,
    top_ref,
    low_ref,
    gain_ref,
    bias_ref,
    wt_ref,
    sq_ref,
    sqt_ref,
    down_ref,
    ex_ref,
    ext_ref,
    exb_ref,
    *rest,
):
    ses, sums = rest[:pairs], rest[pairs : pairs + parts]
    q_ref, edge_ref, sum_ref, val_ref, w_high, w_low, k_row = rest[pairs + parts :]
    t, n = pl.program_id(0), pl.num_programs(0) - 1
    chan_all, hidden = wt_ref.shape
    reduced = ex_ref.shape[0]

    @pl.when(t == 0)
    def _():
        se = total(ses)
        pooled = se[0:1] / (FRAME_ROWS * FRAME_COLUMNS)
        pre = padded_dot(pooled, sq_ref[...]) + down_ref[...]
        gate = sigmoid(pre)
        squeezed = pre * gate
        excite = sigmoid(padded_dot(squeezed, ex_ref[...]) + exb_ref[...])
        logit = se[1:2] * excite * (1.0 - excite)
        slope = gate * (1.0 + pre * (1.0 - gate))
        grad_sq = padded_dot(logit, ext_ref[...]) * slope
        pool_grad = padded_dot(grad_sq, sqt_ref[...]) / (FRAME_ROWS * FRAME_COLUMNS)
        val_ref[...] = jnp.zeros_like(val_ref)
        val_ref[0:1] = excite
        val_ref[1:2] = pool_grad
        val_ref[2:3] = logit
        val_ref[3:4] = pooled
        val_ref[4:5, 0:reduced] = squeezed
        val_ref[5:6, 0:reduced] = grad_sq
        wt = wt_ref[...]
        w_high[...], w_low[...] = split(wt * column(excite))
        k_row[...] = jnp.sum(wt * column(pool_grad), axis=0, keepdims=True)
        sum_ref[...] = jnp.zeros_like(sum_ref)

    mean, inverse, _, _ = norm_terms(total(sums), count, gain_ref[1:2], bias_ref[1:2])
    gain, bias = gain_ref[1:2], bias_ref[1:2]

    def back(gout, value, cut):
        grad = dot3(gout, (w_high[:, cut], w_low[:, cut])) + k_row[:, cut]
        centered = (value - mean[:, cut]) * inverse[:, cut]
        v = centered * gain[:, cut] + bias[:, cut]
        s = sigmoid(v)
        return grad * (s + v * s * (1.0 - s)), centered

    @pl.when(t < n)
    def _():
        gout = split(gout_ref[:, 0].reshape(chan_all, gout_ref.shape[3]).T)
        for cut in chunks(hidden):
            q, centered = back(gout, own_ref[0, :, cut], cut)
            q_ref[0, :, cut] = q
            sum_ref[0:1, cut] += jnp.sum(q, axis=0, keepdims=True)
            sum_ref[1:2, cut] += jnp.sum(q * centered, axis=0, keepdims=True)

    for side, ref in enumerate((top_ref, low_ref)):

        @pl.when((t == n) & (side_ref[side] == 1))
        def _(side=side, ref=ref):
            width = ref.shape[3]
            for k in range(ref.shape[1]):
                here = slice(k * width, (k + 1) * width)
                gout = split(ref[:, k].reshape(chan_all, width).T)
                for cut in chunks(hidden):
                    edge_ref[side, here, cut] = back(gout, halo_ref[side, here, cut], cut)[0]


def proj_back(count, side, own, halo, gout, top, low, gains, biases, wt, se_weights, ses, sums):
    nz, bands, chans, area = gout.shape
    hidden = wt.shape[1]
    chan_all = nz * chans
    last = bands - 1
    fixed = [top, low, gains, biases, wt, *se_weights, *ses, *sums]
    edge_px = HALO_OUT * FRAME_COLUMNS
    return pl.pallas_call(
        partial(proj_back_kernel, len(ses), len(sums), count),
        grid=(bands + 1,),
        in_specs=[
            pl.BlockSpec(memory_space=pltpu.SMEM),
            pl.BlockSpec((1, area, hidden), lambda t: (jnp.minimum(t, last), 0, 0)),
            whole(halo.shape),
            pl.BlockSpec((nz, 1, chans, area), lambda t: (0, jnp.minimum(t, last), 0, 0)),
        ]
        + [whole(a.shape) for a in fixed],
        out_specs=[
            pl.BlockSpec((1, area, hidden), lambda t: (jnp.minimum(t, last), 0, 0)),
            whole((2, edge_px, hidden)),
            whole((2, hidden)),
            whole((SUB, chan_all)),
        ],
        out_shape=[
            jax.ShapeDtypeStruct((bands, area, hidden), F32),
            jax.ShapeDtypeStruct((2, edge_px, hidden), F32),
            jax.ShapeDtypeStruct((2, hidden), F32),
            jax.ShapeDtypeStruct((SUB, chan_all), F32),
        ],
        scratch_shapes=[
            pltpu.VMEM(wt.shape, BF16),
            pltpu.VMEM(wt.shape, BF16),
            pltpu.VMEM((1, hidden), F32),
        ],
        compiler_params=params(48),
        cost_estimate=cost(6 * (bands * area + 2 * edge_px) * hidden * chan_all, 8 * bands * area * hidden),
        name="proj_back",
    )(side, own, halo, gout, *fixed)


def project_kernel(parts, count, own_ref, x_ref, gain_ref, bias_ref, w_ref, val_ref, m_ref, s_ref, *rest):
    sums, (out_ref, grad_ref, w_high, w_low) = rest[:parts], rest[parts:]
    t = pl.program_id(0)
    nz, _, chans, area = x_ref.shape
    hidden, chan_all = w_ref.shape

    @pl.when(t == 0)
    def _():
        w_high[...], w_low[...] = split(w_ref[...])
        grad_ref[...] = column(val_ref[0:1]) * m_ref[...] + column(val_ref[1:2]) * s_ref[...]

    _, _, scale, shift = norm_terms(total(sums), count, gain_ref[1:2], bias_ref[1:2])
    out = None
    for cut in chunks(hidden):
        v = own_ref[0, :, cut] * scale[:, cut] + shift[:, cut]
        term = dot3(split(v * sigmoid(v)), (w_high[cut], w_low[cut]))
        out = term if out is None else out + term
    out = (out * val_ref[0:1]).T
    out_ref[:, 0] = x_ref[:, 0] + out.reshape(nz, chans, area)


def project(count, own, x, gains, biases, w, values, m, s, sums):
    nz, bands, chans, area = x.shape
    hidden = w.shape[0]
    chan_all = nz * chans
    fixed = [gains, biases, w, values, m, s, *sums]
    return pl.pallas_call(
        partial(project_kernel, len(sums), count),
        grid=(bands,),
        in_specs=[
            pl.BlockSpec((1, area, hidden), lambda t: (t, 0, 0)),
            pl.BlockSpec((nz, 1, chans, area), lambda t: (0, t, 0, 0)),
        ]
        + [whole(a.shape) for a in fixed],
        out_specs=[pl.BlockSpec((nz, 1, chans, area), lambda t: (0, t, 0, 0)), whole(m.shape)],
        out_shape=[
            jax.ShapeDtypeStruct((nz, bands, chans, area), F32),
            jax.ShapeDtypeStruct(m.shape, F32),
        ],
        scratch_shapes=[pltpu.VMEM(w.shape, BF16), pltpu.VMEM(w.shape, BF16)],
        compiler_params=params(40),
        cost_estimate=cost(6 * bands * area * hidden * chan_all, 4 * bands * area * hidden),
        name="project",
    )(own, x, *fixed)


def spread_back_kernel(
    parts,
    count,
    side_ref,
    hid_ref,
    hid_halo_ref,
    own_ref,
    halo_ref,
    q_ref,
    q_halo_ref,
    gain_ref,
    bias_ref,
    w_ref,
    *rest,
):
    sums_one, sums_two, backs = (rest[i * parts : (i + 1) * parts] for i in range(3))
    out_ref, sum_ref, tap_ref, pad, grad, terms = rest[3 * parts :]
    rows = own_ref.shape[0]
    mean, inverse, scale, shift = norm_terms(total(sums_one), count, gain_ref[0:1], bias_ref[0:1])
    a, b, c0 = back_terms(total(sums_two), total(backs), count, gain_ref[1:2])
    for i, row in enumerate((scale, shift, a, b, c0, mean, inverse)):
        terms[i] = jnp.broadcast_to(row, (SUB, 128))

    def act(value):
        v = value * terms[0] + terms[1]
        return v * sigmoid(v)

    def grad_in(q, value):
        return q * terms[2] + (value * terms[3] + terms[4])

    def own_row(r, _):
        for c in range(SUB):
            pad[r + HALO_OUT, c + 2] = act(hid_ref[r, c])
            grad[r + HALO_OUT, c + 2] = grad_in(q_ref[r, c], own_ref[r, c])
        fill_sides(pad, r + HALO_OUT)
        fill_sides(grad, r + HALO_OUT)
        return 0

    lax.fori_loop(0, rows, own_row, 0)
    for side, start, first in ((0, 0, HALO_IN - HALO_OUT), (1, rows + HALO_OUT, 0)):

        @pl.when(side_ref[side] == 1)
        def _(side=side, start=start, first=first):
            for r in range(HALO_OUT):
                for c in range(SUB):
                    pad[start + r, c + 2] = act(hid_halo_ref[side, first + r, c])
                    grad[start + r, c + 2] = grad_in(q_halo_ref[side, r, c], halo_ref[side, r, c])
                fill_sides(pad, start + r)
                fill_sides(grad, start + r)

        @pl.when(side_ref[side] == 0)
        def _(start=start):
            clear_rows(pad, start, HALO_OUT)
            clear_rows(grad, start, HALO_OUT)

    def weight_group(i, acc):
        acc = list(acc)
        r = i // SUB * SUB
        c = i % SUB
        mine = [grad[r + HALO_OUT + o, c + 2] for o in range(SUB)]
        for bb in range(K):
            for row in range(SUB + K - 1):
                value = pad[r + row, c + bb]
                for aa in range(K):
                    o = row - aa
                    if 0 <= o < SUB:
                        acc[aa * K + bb] = acc[aa * K + bb] + value * mine[o]
        return tuple(acc)

    zero = jnp.zeros((SUB, 128), F32)
    acc = lax.fori_loop(0, rows, weight_group, (zero,) * TAPS)
    for tap in range(TAPS):
        tap_ref[tap : tap + 1] = jnp.sum(acc[tap], axis=0, keepdims=True)

    def group(i, carry):
        one, two = carry
        r = i * SUB
        for c in range(SUB):
            acc = tap_rows(grad, w_ref, r, SUB, c, flipped=True)
            for o in range(SUB):
                hidden = hid_ref[r + o, c]
                v = hidden * terms[0] + terms[1]
                s = sigmoid(v)
                value = acc[o] * (s + v * s * (1.0 - s))
                out_ref[r + o, c] = value
                one = one + value
                two = two + value * ((hidden - terms[5]) * terms[6])
        return one, two

    one, two = lax.fori_loop(0, rows // SUB, group, (zero, zero))
    sum_ref[0:1] = jnp.sum(one, axis=0, keepdims=True)
    sum_ref[1:2] = jnp.sum(two, axis=0, keepdims=True)


def spread_back(count, side, hid, hid_halo, own, halo, q, q_halo, gains, biases, taps, sums_one, sums_two, backs):
    rows, hidden = own.shape[0], own.shape[-1]
    arrays = [hid, hid_halo, own, halo, q, q_halo, gains, biases, taps, *sums_one, *sums_two, *backs]
    return pl.pallas_call(
        partial(spread_back_kernel, len(backs), count),
        grid=(hidden // 128,),
        in_specs=[pl.BlockSpec(memory_space=pltpu.SMEM)] + [lanes(a.shape) for a in arrays],
        out_specs=[lanes((rows, SUB, SUB, hidden)), lanes((2, hidden)), lanes((TAPS, hidden))],
        out_shape=[
            jax.ShapeDtypeStruct((rows, SUB, SUB, hidden), F32),
            jax.ShapeDtypeStruct((2, hidden), F32),
            jax.ShapeDtypeStruct((TAPS, hidden), F32),
        ],
        scratch_shapes=[
            pltpu.VMEM((rows + 2 * HALO_OUT, SUB + 4, SUB, 128), F32),
            pltpu.VMEM((rows + 2 * HALO_OUT, SUB + 4, SUB, 128), F32),
            pltpu.VMEM((7, SUB, 128), F32),
        ],
        compiler_params=params(48),
        cost_estimate=cost(rows * 64 * hidden * 1600, 16 * rows * 64 * hidden),
        name="spread_back",
    )(side, *arrays)


def expand_back_kernel(parts, count, q_ref, hid_ref, x_ref, gout_ref, gain_ref, wt_ref, *rest):
    sums, backs = rest[:parts], rest[parts : 2 * parts]
    grad_ref, out_ref, w_high, w_low = rest[2 * parts :]
    t = pl.program_id(0)
    nz, _, chans, area = x_ref.shape
    hidden, chan_all = wt_ref.shape

    @pl.when(t == 0)
    def _():
        w_high[...], w_low[...] = split(wt_ref[...])
        grad_ref[...] = jnp.zeros_like(grad_ref)

    a, b, c = back_terms(total(sums), total(backs), count, gain_ref[0:1])
    x = split(x_ref[:, 0].reshape(chan_all, area))
    out = None
    for cut in chunks(hidden):
        grad = split(q_ref[0, :, cut] * a[:, cut] + (hid_ref[0, :, cut] * b[:, cut] + c[:, cut]))
        grad_ref[:, cut] += dot3(x, grad)
        term = dot3(grad, (w_high[cut], w_low[cut]))
        out = term if out is None else out + term
    out_ref[:, 0] = gout_ref[:, 0] + out.T.reshape(nz, chans, area)


def expand_back(count, q, hid, x, gout, gains, wt, sums, backs):
    nz, bands, chans, area = x.shape
    hidden = wt.shape[0]
    chan_all = nz * chans
    fixed = [gains, wt, *sums, *backs]
    return pl.pallas_call(
        partial(expand_back_kernel, len(sums), count),
        grid=(bands,),
        in_specs=[
            pl.BlockSpec((1, area, hidden), lambda t: (t, 0, 0)),
            pl.BlockSpec((1, area, hidden), lambda t: (t, 0, 0)),
            pl.BlockSpec((nz, 1, chans, area), lambda t: (0, t, 0, 0)),
            pl.BlockSpec((nz, 1, chans, area), lambda t: (0, t, 0, 0)),
        ]
        + [whole(v.shape) for v in fixed],
        out_specs=[whole((chan_all, hidden)), pl.BlockSpec((nz, 1, chans, area), lambda t: (0, t, 0, 0))],
        out_shape=[
            jax.ShapeDtypeStruct((chan_all, hidden), F32),
            jax.ShapeDtypeStruct((nz, bands, chans, area), F32),
        ],
        scratch_shapes=[pltpu.VMEM(wt.shape, BF16), pltpu.VMEM(wt.shape, BF16)],
        compiler_params=params(40),
        cost_estimate=cost(12 * bands * area * hidden * chan_all, 8 * bands * area * hidden),
        name="expand_back",
    )(q, hid, x, gout, *fixed)


def segments(chan_in, hidden_dev, chan_dev, reduced, tap_count, hidden_all):
    seg_sizes = [
        chan_in * hidden_dev,
        tap_count * hidden_dev,
        2 * hidden_dev,
        2 * hidden_dev,
        hidden_dev * chan_in,
        chan_dev * reduced,
        reduced,
        reduced * chan_dev,
        chan_dev,
    ]
    seg_rates = [
        0.5 / math.sqrt(chan_in),
        0.5 / math.sqrt(tap_count),
        0.3,
        0.3,
        0.5 * math.sqrt(8.0 / hidden_all),
        2.0 / math.sqrt(chan_in),
        0.3,
        1.0 / math.sqrt(reduced),
        0.3,
    ]
    return (seg_sizes, seg_rates)


def in_blocks(pieces, block_len):
    flat = jnp.concatenate([piece.reshape(-1) for piece in pieces])
    blocks = -(-flat.shape[0] // block_len)
    return jnp.pad(flat, (0, blocks * block_len - flat.shape[0])).reshape(blocks, block_len)


def thirds(v):
    high = v.astype(BF16)
    rest = v - high.astype(F32)
    mid = rest.astype(BF16)
    return high, mid, (rest - mid.astype(F32)).astype(BF16)


def choose(chosen, v):
    high, mid, low = thirds(v)
    return (dot(chosen, high) + dot(chosen, mid)) + dot(chosen, low)


def adam_kernel(
    bounds,
    rates,
    capacity,
    me_ref,
    row_ref,
    col_ref,
    grad_ref,
    weight_ref,
    first_all_ref,
    second_all_ref,
    first_ref,
    second_ref,
    first_out,
    second_out,
    new_ref,
):
    blocks, length = grad_ref.shape
    slots = first_all_ref.shape[0]
    own_row, own_col = row_ref[...], col_ref[...]
    i = lax.broadcasted_iota(jnp.int32, (blocks, blocks), 0)
    j = lax.broadcasted_iota(jnp.int32, (blocks, blocks), 1)
    same = own_row == own_col
    before = jnp.sum(jnp.where(same & (j < i), 1.0, 0.0), axis=1, keepdims=True)
    slot_col = own_col * capacity + before.astype(jnp.int32)
    behind = jnp.sum(jnp.where(same & (i < j), 1.0, 0.0), axis=0, keepdims=True)
    slot_row = own_row * capacity + behind.astype(jnp.int32)
    grad = grad_ref[...]

    mine = lax.broadcasted_iota(jnp.int32, (capacity, blocks), 0) + me_ref[0] * capacity
    owned = choose((mine == slot_row).astype(F32).astype(BF16), grad)
    first_out[0] = beta_first * first_ref[0] + (1.0 - beta_first) * owned
    second_out[0] = beta_second * second_ref[0] + (1.0 - beta_second) * owned * owned

    pick_slot = lax.broadcasted_iota(jnp.int32, (blocks, slots), 1) == slot_col
    chosen = pick_slot.astype(F32).astype(BF16)
    first = beta_first * choose(chosen, first_all_ref[...]) + (1.0 - beta_first) * grad
    second = beta_second * choose(chosen, second_all_ref[...]) + (1.0 - beta_second) * grad * grad
    first_hat = first / (1.0 - beta_first**STEP)
    second_hat = second / (1.0 - beta_second**STEP)
    place = lax.broadcasted_iota(jnp.int32, (blocks, length), 0) * length + lax.broadcasted_iota(
        jnp.int32, (blocks, length), 1
    )
    rate = jnp.zeros((blocks, length), F32)
    for bound, value in zip(reversed(bounds), reversed(rates)):
        rate = jnp.where(place < bound, jnp.float32(value), rate)
    new = weight_ref[...] * (1.0 - rate * weight_decay) - rate * first_hat / (
        jnp.sqrt(second_hat) + adam_eps
    )
    new_ref[...] = new


def adam(me, owners, grads, weights, first_all, second_all, first, second, bounds, rates):
    capacity = first.shape[1]
    arrays = [owners.reshape(1, -1), owners, grads, weights, first_all, second_all, first, second]
    return pl.pallas_call(
        partial(adam_kernel, bounds, rates, capacity),
        grid=(1,),
        in_specs=[pl.BlockSpec(memory_space=pltpu.SMEM)] + [whole(a.shape) for a in arrays],
        out_specs=[whole(first.shape), whole(second.shape), whole(grads.shape)],
        out_shape=[
            jax.ShapeDtypeStruct(first.shape, F32),
            jax.ShapeDtypeStruct(second.shape, F32),
            jax.ShapeDtypeStruct(grads.shape, F32),
        ],
        compiler_params=params(40),
        cost_estimate=cost(10**8, 4 * 6 * grads.size),
        name="adam",
    )(me, *arrays)


def sum_to_group(rows):
    n_pix = lax.axis_size(PIX)
    nz = lax.axis_size("chan")
    n, hidden = rows.shape
    dealt = lax.all_to_all(rows.reshape(n_pix, n // n_pix, hidden), PIX, 0, 0, tiled=True)
    mine = jnp.sum(dealt, axis=0).reshape(n // n_pix, nz, hidden // nz).transpose(1, 0, 2)
    return jnp.sum(lax.all_to_all(mine, "chan", 0, 0, tiled=True), axis=0)


def local(
    frames_raw,
    grad_out,
    col_offsets,
    flip_flags,
    owners,
    w_expand,
    w_dw,
    norm_gains,
    norm_biases,
    w_project,
    squeeze_matrix,
    se_down_bias,
    excite_matrix,
    excite_bias_row,
    first_moment,
    second_moment,
):
    nz, nhi, nlo = (lax.axis_size(axis) for axis in ALL)
    frames, chans, stored = frames_raw.shape
    band = stored // WIN
    area = band * FRAME_COLUMNS
    rows = nlo * band
    chan_in, hidden_dev = w_expand.shape
    hidden = hidden_dev * nz
    reduced = squeeze_matrix.shape[1]
    group = nz // MB * nhi * nlo
    count = float(frames // MB * FRAME_ROWS * FRAME_COLUMNS)
    hi = lax.axis_index("hi")
    side = jnp.stack([(hi > 0).astype(jnp.int32), (hi < nhi - 1).astype(jnp.int32)])

    crops = crop(frames_raw, col_offsets, flip_flags)
    x = deal(crops).reshape(nz, nlo, chans, area)
    gout = deal(order(grad_out)).reshape(nz, nlo, chans, area)

    w_expand_all = lax.all_gather(w_expand, "chan", axis=1, tiled=True)
    w_project_all = lax.all_gather(w_project, "chan", axis=0, tiled=True)
    hidden_rows = jnp.concatenate([w_dw, norm_gains, norm_biases], axis=0)
    hidden_rows = lax.all_gather(hidden_rows, "chan", axis=1, tiled=True)
    taps = jnp.broadcast_to(hidden_rows[:TAPS, None, :], (TAPS, SUB, hidden))
    gains = hidden_rows[TAPS : TAPS + 2]
    biases = hidden_rows[TAPS + 2 : TAPS + 4]
    se_rows = jnp.concatenate([squeeze_matrix.T, excite_matrix, excite_bias_row[None]], axis=0)
    se_rows = lax.all_gather(se_rows, "chan", axis=0)
    se_rows = se_rows.transpose(1, 0, 2).reshape(2 * reduced + 1, chan_in)
    sq_t, ex_all, ex_bias = se_rows[:reduced], se_rows[reduced : 2 * reduced], se_rows[2 * reduced :]
    se_weights = [sq_t.T, sq_t, se_down_bias[None], ex_all, ex_all.T, ex_bias]
    w_project_t = w_project_all.T
    w_expand_t = w_expand_all.T

    first_all = lax.all_gather(first_moment[0], PIX, axis=0, tiled=True)
    second_all = lax.all_gather(second_moment[0], PIX, axis=0, tiled=True)

    top, low = rims(x, HALO_IN, band)
    g_top, g_low = rims(gout, HALO_OUT, band)

    def as_rows(v):
        return v.reshape(rows, SUB, SUB, hidden)

    def as_bands(v):
        return v.reshape(nlo, area, hidden)

    def as_sides(v, n):
        return v.reshape(2, n, SUB, SUB, hidden)

    hid, hid_halo, sums_one = expand(x, top, low, w_expand_all)
    hid_halo = as_sides(hid_halo, HALO_IN)
    sums_one = shares(sums_one, 1, group)
    spatial, spatial_halo, sums_two = spread(count, side, as_rows(hid), hid_halo, gains, biases, taps, sums_one)
    sums_two = shares(sums_two, 1, group)
    m, s, se_part = gather(count, as_bands(spatial), gout, gains, biases, w_project_t, sums_two)
    ses = shares(se_part, nlo, nhi)
    q, q_halo, back_two, values = proj_back(
        count,
        side,
        as_bands(spatial),
        spatial_halo.reshape(2, -1, hidden),
        gout,
        g_top,
        g_low,
        gains,
        biases,
        w_project_t,
        se_weights,
        ses,
        sums_two,
    )
    backs_two = shares(back_two, 1, group)
    out, g_project = project(count, as_bands(spatial), x, gains, biases, w_project_all, values, m, s, sums_two)
    output = restore(deal(out.reshape(frames, chans, area)))
    q1, back_one, g_dw = spread_back(
        count,
        side,
        as_rows(hid),
        hid_halo,
        spatial,
        spatial_halo,
        as_rows(q),
        as_sides(q_halo, HALO_OUT),
        gains,
        biases,
        taps,
        sums_one,
        sums_two,
        backs_two,
    )
    backs_one = shares(back_one, 1, group)
    g_expand, grad_x = expand_back(count, as_bands(q1), hid, x, gout, gains, w_expand_t, sums_one, backs_one)
    grad_frames = uncrop(deal(grad_x.reshape(frames, chans, area)), col_offsets, flip_flags)

    lead = (hi == 0).astype(F32)
    excite_row, logit, pooled = values[0:1], values[2:3], values[3:4]
    squeezed, grad_sq = values[4, :reduced], values[5, :reduced]
    logit, grad_sq = logit * lead, grad_sq * lead
    g_sq_t = grad_sq[:, None] * pooled
    g_ex = squeezed[:, None] * logit
    spare = jnp.zeros((reduced, nz, chans), F32)
    spare = spare.at[0].set(logit.reshape(nz, chans))
    spare = spare.at[1, :, :reduced].set(jnp.broadcast_to(grad_sq, (nz, reduced)))
    se_grads = jnp.concatenate(
        [
            g_sq_t.reshape(reduced, nz, chans),
            g_ex.reshape(reduced, nz, chans),
            spare,
            jnp.zeros((reduced, nz, hidden_dev - 3 * chans), F32),
        ],
        axis=2,
    ).reshape(reduced, hidden)
    small = jnp.concatenate(
        [
            g_dw,
            back_one[1:2],
            back_two[1:2],
            back_one[0:1],
            back_two[0:1],
            jnp.zeros((3, hidden), F32),
            se_grads,
            jnp.zeros((16, hidden), F32),
        ],
        axis=0,
    )
    n_pix = nhi * nlo

    def everywhere(v):
        return lax.all_gather(v, PIX, axis=0, tiled=True)

    g_project = everywhere(sum_to_group(g_project))
    small = everywhere(sum_to_group(small))
    g_expand = everywhere(sum_to_group(g_expand))
    se_block = small[32 : 32 + reduced]
    block_len = first_moment.shape[2]
    grads = in_blocks(
        [
            g_expand,
            small[: TAPS + 4],
            g_project.T,
            se_block[:, :chans].T,
            se_block[1, 2 * chans : 2 * chans + reduced],
            se_block[:, chans : 2 * chans],
            se_block[0, 2 * chans : 3 * chans],
        ],
        block_len,
    )
    weights = in_blocks(
        [
            w_expand,
            w_dw,
            norm_gains,
            norm_biases,
            w_project,
            squeeze_matrix,
            se_down_bias,
            excite_matrix,
            excite_bias_row,
        ],
        block_len,
    )
    seg_sizes, seg_rates = segments(chan_in, hidden_dev, chans, reduced, TAPS, hidden)
    bounds = [sum(seg_sizes[: i + 1]) for i in range(len(seg_sizes))]
    me = (hi * nlo + lax.axis_index("lo")).astype(jnp.int32).reshape(1)
    first_next, second_next, new = adam(
        me, owners, grads, weights, first_all, second_all, first_moment, second_moment, bounds, seg_rates
    )
    new_params = new.reshape(-1)[: bounds[-1]][None, :]
    return (output, grad_frames, first_next, second_next, new_params)


def solution(mesh):
    nz, n_pix = mesh.shape["chan"], mesh.shape["pix"]
    placed = (
        P(None, "chan", PIX),
        P(None, "chan", PIX),
        P(),
        P(),
        P(),
        P(None, "chan"),
        P(None, "chan"),
        P(None, "chan"),
        P(None, "chan"),
        P("chan", None),
        P("chan", None),
        P(),
        P(None, "chan"),
        P("chan"),
        P("chan", PIX, None),
        P("chan", PIX, None),
    )

    def run(*arrays):
        nlo = arrays[0].shape[0] // nz
        return jax.shard_map(
            local,
            mesh=Mesh(mesh.devices.reshape(nz, n_pix // nlo, nlo), ALL),
            in_specs=placed,
            out_specs=(
                P(None, "chan", PIX),
                P(None, "chan", PIX),
                P("chan", PIX, None),
                P("chan", PIX, None),
                P("chan", None),
            ),
            check_vma=False,
        )(*arrays)

    return run
```

time: 3010 us -> 612 us (0.20)
  waiting for transfers between devices: 935 us -> 72.2 us
  blocking collectives: 1060 us -> 208 us
  local copies, waits for them, and re-layouts: 443 us -> 94.6 us
  other arithmetic: 320 us -> 8.34 us
  Pallas kernels: 0 us -> 133 us
  matrix products: 131 us -> 0 us
  loops' own time: 40.7 us -> 0 us
    psum x24 -> x0, blocking collectives: 1030 us -> none  [the longest x16 710 us: pixel_totals(): total_one, total_two = lax.psum((wide_one, wide_two), ('chan', 'pix'))]
    while x24 -> x0, waiting for transfers between devices: 589 us -> none
    all_gather x8 -> x2, waiting for transfers between devices: 340 us -> 0.02 us  [the longest x1 0.02 us: local(): w_expand_all = lax.all_gather(w_expand, 'chan', axis=1, tiled=True)]
    scatter x83 -> x2, local copies, waits for them, and re-layouts: 180 us -> 0.08 us  [the longest x1 0.07 us: local(): spare.at[1, :, :reduced].set(jnp.broadcast_to(grad_sq, (nz, reduced)))]
    pallas_call x0 -> x12, Pallas kernels: none -> 133 us  [the longest x1 47.1 us: spread_back(): pl.pallas_call(partial(spread_back_kernel, len(backs), count), grid=(hidd...]
    dot_general x48 -> x0, matrix products: 131 us -> none  [the longest x4 27.4 us: run_group(): jnp.einsum('gfpe,gfcp->ec', second_flat, grad_full, precision=precise_set...]
    reduce_sum x25 -> x6, other arithmetic: 131 us -> 6.76 us  [the longest x3 3.82 us: sum_to_group(): return jnp.sum(lax.all_to_all(mine, 'chan', 0, 0, tiled=True), axis=0)]
    all_gather x1 -> x7, blocking collectives: 16.4 us -> 133 us  [the longest x1 60.4 us: local(): hidden_rows = lax.all_gather(hidden_rows, 'chan', axis=1, tiled=True)]
  transfers between devices with their start and end apart: 34 -> 30, of which waited for: 24 -> 10; matrix products, arithmetic and copies ran while one was open for 15% -> 9% of each run, Pallas kernels for 0% -> 11%
where the time goes in v1:
time: 612 us; the launch traced here: 603 us
  blocking collectives  208 us (34%)
  Pallas kernels  133 us (22%)
  local copies, waits for them, and re-layouts  94.6 us (15%)
  waiting for transfers between devices  72.2 us (12%)
  starting transfers between devices  71.5 us (12%)
  between operations  14.7 us (2%)
  other arithmetic  8.34 us (1%)
    all_gather x1, blocking collectives, local(): hidden_rows = lax.all_gather(hidden_rows, 'chan', axis=1, tiled=True)  60.4 us
    all_to_all x1, blocking collectives, deal(): return lax.all_to_all(x, SPREAD, 0, 0, tiled=True)  55.2 us
    unnamed x142, local copies, waits for them, and re-layouts  51.8 us
    pallas_call x1, Pallas kernels, spread_back(): pl.pallas_call(partial(spread_back_kernel, len(backs), count), grid=(hidd...  47.1 us
    all_to_all x3, waiting for transfers between devices, deal(): return lax.all_to_all(x, SPREAD, 0, 0, tiled=True)  42.3 us
    all_gather x3, blocking collectives, everywhere(): return lax.all_gather(v, PIX, axis=0, tiled=True)  28.1 us
    pallas_call x1, Pallas kernels, spread(): pl.pallas_call(partial(spread_kernel, len(sums), count), grid=(hidden //...  25.1 us
    ppermute x17, starting transfers between devices, exchange(): return lax.ppermute(x, ALL, [(i, i ^ stride) for i in range(n)])  20.1 us
  transfers between devices with their start and end apart: 30, of which 10 were waited for; matrix products, arithmetic and copies ran while one was open for 9% of the time, Pallas kernels for 11%

profile of v1, /device:TPU:15, one launch (start us, length us, event | category | flops | bytes accessed | tf_op | source)
XLA Modules:
  0.0 602.8 jit_solution(11405217268847305723)
XLA Ops:
  7.2 1.7 copy-done.35
  10.2 3.2 crop.1
  14.8 6.6 %all-to-all-start = ((f32[16,64,512]{2,1,0:T(8,128)}), f32[16,64,512]{2,1,0:T(8,128)S(1)}, u32[]{:S(2)}, u32[]{:S(2)}) async-start(f32[16,64,512]{2,1,0:T(8,128)} %copy-done.12), calls=%async_computation | async-start | bytes 4194304 | tf_op jit(solution)/shard_map/all_to_all | solution.py:107
  21.3 1.6 copy-done.9
  22.9 2.1 order.1
  26.4 42.3 %all-to-all-done = f32[16,64,512]{2,1,0:T(8,128)S(1)} async-done(((f32[16,64,512]{2,1,0:T(8,128)}), f32[16,64,512]{2,1,0:T(8,128)S(1)}, u32[]{:S(2)}, u32[]{:S(2)}) %all-to-all-start) | async-done | bytes 2097184 | tf_op jit(solution)/shard_map/all_to_all | solution.py:107
  68.7 4.9 all-to-all-start.1
  78.1 4.7 collective-permute-start.1
  82.8 60.4 %all_gather.31 = f32[29,1024]{1,0:T(8,128)S(1)} all-gather(f32[29,256]{1,0:T(8,128)S(1)} %pad_maximum_fusion), channel_id=1, replica_groups=mesh['chan'=4,'hi'=2,'lo'=4] {'chan'}, dimensions={1}, use_global_device_ids=true | all-gather | bytes 148480 | tf_op jit(solution)/shard_map/all_gather | solution.py:996
  143.2 1.6 copy.88.w_ref
  146.5 6.6 %expand.1 = (f32[4,512,1024]{2,1,0:T(8,128)S(1)}, f32[2,256,1024]{2,1,0:T(8,128)S(1)}, f32[2,1024]{1,0:T(2,128)S(1)}) custom-call(f32[4,4,64,512]{3,2,1,0:T(8,128)S(1)} %bitcast.75, f32[4,1,64,256]{3,2,1,0:T(8,128)S(1)} %copy-done.37, f32[4,1,64,256]{3,2,1,0:T(8,128)} %collective-permute-done.1.low_ref, f32[256,1024]{1,0:T(8,128)S(1)} %copy.88.w_ref), custom_call_target="tpu_custom_call" | custom-call | flops 4026531840 | bytes 8388608 | tf_op jit(solution)/shard_map/expand/pallas_call | solution.py:284
  153.0 3.3 copy-done
  156.4 2.4 collective-permute-start.2
  160.4 1.9 collective-permute-start.5
  162.2 10.4 %all-gather.3 = f32[4,33,64]{2,1,0:T(8,128)S(1)} all-gather(f32[1,33,64]{2,1,0:T(8,128)S(1)} %copy-done.52), channel_id=2, replica_groups=mesh['chan'=4,'hi'=2,'lo'=4] {'chan'}, dimensions={0}, use_global_device_ids=true | all-gather | bytes 42240 | tf_op jit(solution)/shard_map/all_gather | solution.py:1001
  172.8 25.1 %spread.1 = (f32[32,8,8,1024]{3,2,1,0:T(8,128)S(1)}, f32[2,2,8,8,1024]{4,3,2,1,0:T(8,128)S(1)}, f32[2,1024]{1,0:T(2,128)S(1)}) custom-call(s32[2]{0:T(128)S(1)} %add_convert_fusion.side_ref, f32[32,8,8,1024]{3,2,1,0:T(8,128)} %bitcast.69, f32[2,4,8,8,1024]{4,3,2,1,0:T(8,128)S(1)} %bitcast.78, f32[2,1024]{1,0:T(2,128)S(1)} %get-tuple-element.107.gain_ref, ...), custom_call_target="tpu_custom_call" | custom-call | flops 1677721600 | bytes 16777216 | tf_op jit(solution)/shard_map/spread/pallas_call | solution.py:406
  197.9 3.3 copy-done.1
  202.1 4.0 collective-permute-start.8
  206.2 2.6 copy.92.wt_ref
  211.5 1.7 fusion.1
  214.5 4.6 collective-permute-start.7
  219.1 3.4 copy-done.2
  223.7 7.2 %gather.1 = (f32[256,1024]{1,0:T(8,128)S(1)}, f32[1,1024]{1,0:T(1,128)S(1)}, f32[2,256]{1,0:T(2,128)S(1)}) custom-call(f32[4,512,1024]{2,1,0:T(8,128)S(1)} %bitcast.73, f32[4,4,64,512]{3,2,1,0:T(8,128)} %bitcast.7.gout_ref, f32[2,1024]{1,0:T(2,128)S(1)} %get-tuple-element.107.gain_ref, f32[2,1024]{1,0:T(2,128)S(1)} %get-tuple-element.106.bias_ref, ...), custom_call_target="tpu_custom_call" | custom-call | flops 3221225472 | bytes 8388608 | tf_op jit(solution)/shard_map/gather/pallas_call | solution.py:467
  232.5 1.9 collective-permute-done.12.rest_1_
  236.8 12.7 %proj_back.1 = (f32[4,512,1024]{2,1,0:T(8,128)}, f32[2,128,1024]{2,1,0:T(8,128)S(1)}, f32[2,1024]{1,0:T(2,128)S(1)}, f32[8,256]{1,0:T(8,128)S(1)}) custom-call(s32[2]{0:T(128)S(1)} %add_convert_fusion.side_ref, f32[4,512,1024]{2,1,0:T(8,128)} %bitcast.71, f32[2,128,1024]{2,1,0:T(8,128)S(1)} %bitcast.88, f32[4,4,64,512]{3,2,1,0:T(8,128)} %bitcast.7.gout_ref, ...), custom_call_target="tpu_custom_call" | custom-call | flops 3623878656 | bytes 16777216 | tf_op jit(solution)/shard_map/proj_back/pallas_call | solution.py:587
  251.9 2.6 collective-permute-start.13
  255.6 2.4 collective-permute-start.16
  259.1 1.6 copy-done.5
  263.1 47.1 %spread_back.1 = (f32[32,8,8,1024]{3,2,1,0:T(8,128)}, f32[2,1024]{1,0:T(2,128)S(1)}, f32[25,1024]{1,0:T(8,128)S(1)}) custom-call(s32[2]{0:T(128)S(1)} %add_convert_fusion.side_ref, f32[32,8,8,1024]{3,2,1,0:T(8,128)} %bitcast.70, f32[2,4,8,8,1024]{4,3,2,1,0:T(8,128)S(1)} %bitcast.79, f32[32,8,8,1024]{3,2,1,0:T(8,128)} %copy-done.1, ...), custom_call_target="tpu_custom_call" | custom-call | flops 3355443200 | bytes 33554432 | tf_op jit(solution)/shard_map/spread_back/pallas_call | solution.py:763
  310.2 3.3 concatenate.25
  313.6 12.5 %all_to_all.50 = f32[8,8,1024]{2,1,0:T(8,128)} all-to-all(f32[8,8,1024]{2,1,0:T(8,128)} %bitcast.103), channel_id=1, replica_groups=mesh['chan'=4,'hi'=2,'lo'=4] {'hi','lo'}, dimensions={0} | all-to-all | bytes 524288 | tf_op jit(solution)/shard_map/all_to_all | solution.py:953
  326.1 1.6 reduce_sum.56
  327.7 4.6 all-to-all-start.7
  333.5 8.2 %project.1 = (f32[4,4,64,512]{3,2,1,0:T(8,128)S(1)}, f32[256,1024]{1,0:T(8,128)S(1)}) custom-call(f32[4,512,1024]{2,1,0:T(8,128)} %bitcast.72, f32[4,4,64,512]{3,2,1,0:T(8,128)S(1)} %bitcast.76, f32[2,1024]{1,0:T(2,128)S(1)} %get-tuple-element.107.gain_ref, f32[2,1024]{1,0:T(2,128)S(1)} %get-tuple-element.106.bias_ref, f32[1024,256]{1,0:T(8,128)S(1)} %copy-done.6, ...), custom_call_target="tpu_custom_call" | custom-call | flops 3221225472 | bytes 8388608 | tf_op jit(solution)/shard_map/project/pallas_call | solution.py:646
  344.0 7.6 %all-to-all-start.8 = ((f32[8,32,1024]{2,1,0:T(8,128)}), f32[8,32,1024]{2,1,0:T(8,128)}, u32[]{:S(2)}, u32[]{:S(2)}) async-start(f32[8,32,1024]{2,1,0:T(8,128)} %bitcast.86), calls=%async_computation.8 | async-start | bytes 2097152 | tf_op jit(solution)/shard_map/all_to_all | solution.py:953
  353.1 2.3 collective-permute-start.20
  355.5 9.0 %collective-permute-done.18.rest_5_ = f32[2,1024]{1,0:T(2,128)S(1)} collective-permute-done((f32[2,1024]{1,0:T(2,128)S(1)}, f32[2,1024]{1,0:T(2,128)S(1)}, u32[]{:S(2)}, u32[]{:S(2)}) %collective-permute-start.18) | collective-permute-done | bytes 8224 | tf_op jit(solution)/shard_map/ppermute | solution.py:90
  364.6 10.8 %expand_back.1 = (f32[256,1024]{1,0:T(8,128)S(1)}, f32[4,4,64,512]{3,2,1,0:T(8,128)S(1)}) custom-call(f32[4,512,1024]{2,1,0:T(8,128)} %bitcast.121, f32[4,512,1024]{2,1,0:T(8,128)} %copy-done, f32[4,4,64,512]{3,2,1,0:T(8,128)S(1)} %bitcast.77, f32[4,4,64,512]{3,2,1,0:T(8,128)} %bitcast.7.gout_ref, f32[2,1024]{1,0:T(2,128)S(1)} %get-tuple-element.107.gain_ref, ...), custom_call_target="tpu_custom_call" | custom-call | flops 6442450944 | bytes 16777216 | tf_op jit(solution)/shard_map/expand_back/pallas_call | solution.py:812
  377.7 6.2 %all-to-all-start.4 = ((f32[8,32,1024]{2,1,0:T(8,128)}), f32[8,32,1024]{2,1,0:T(8,128)S(1)}, u32[]{:S(2)}, u32[]{:S(2)}) async-start(f32[8,32,1024]{2,1,0:T(8,128)} %bitcast.87), calls=%async_computation.4 | async-start | bytes 2097152 | tf_op jit(solution)/shard_map/all_to_all | solution.py:953
  386.0 10.6 %all-to-all-done.4 = f32[8,32,1024]{2,1,0:T(8,128)S(1)} async-done(((f32[8,32,1024]{2,1,0:T(8,128)}), f32[8,32,1024]{2,1,0:T(8,128)S(1)}, u32[]{:S(2)}, u32[]{:S(2)}) %all-to-all-start.4) | async-done | bytes 1048608 | tf_op jit(solution)/shard_map/all_to_all | solution.py:953
  396.6 4.5 all-to-all-start.9
  401.3 4.2 all-to-all-done.9
  405.5 7.9 %all_to_all.51 = f32[4,32,256]{2,1,0:T(8,128)} all-to-all(f32[4,32,256]{2,1,0:T(8,128)S(1)} %copy.95), channel_id=1, replica_groups=mesh['chan'=4,'hi'=2,'lo'=4] {'chan'}, dimensions={0} | all-to-all | bytes 262144 | tf_op jit(solution)/shard_map/all_to_all | solution.py:955
  413.5 55.2 %all_to_all.52.x_ref = f32[16,64,512]{2,1,0:T(8,128)S(1)} all-to-all(f32[16,64,512]{2,1,0:T(8,128)} %bitcast.84), channel_id=1, replica_groups=mesh['chan'=4,'hi'=2,'lo'=4] {'chan','lo'}, dimensions={0} | all-to-all | bytes 4194304 | tf_op jit(solution)/shard_map/all_to_all | solution.py:107
  468.7 5.1 all-to-all-start.3
  474.4 1.8 concatenate.27
  477.0 15.1 %all-gather.2 = f32[1,208,1024]{2,0,1:T(1,128)S(1)} all-gather(f32[1,26,1024]{2,0,1:T(1,128)S(1)} %copy-done.46), channel_id=4, replica_groups=mesh['chan'=4,'hi'=2,'lo'=4] {'hi','lo'}, dimensions={1}, use_global_device_ids=true | all-gather | bytes 958464 | tf_op jit(solution)/shard_map/all_gather | solution.py:1009
  493.0 18.5 %all-gather.1 = f32[1,208,1024]{2,0,1:T(1,128)S(1)} all-gather(f32[1,26,1024]{2,0,1:T(1,128)S(1)} %copy-done.47), channel_id=3, replica_groups=mesh['chan'=4,'hi'=2,'lo'=4] {'hi','lo'}, dimensions={1}, use_global_device_ids=true | all-gather | bytes 958464 | tf_op jit(solution)/shard_map/all_gather | solution.py:1008
  514.1 8.7 %all_gather.36 = f32[64,256]{1,0:T(8,128)S(1)} all-gather(f32[8,256]{1,0:T(8,128)S(1)} %reduce_sum.57), channel_id=1, replica_groups=mesh['chan'=4,'hi'=2,'lo'=4] {'hi','lo'}, dimensions={0}, use_global_device_ids=true | all-gather | bytes 73728 | tf_op jit(solution)/shard_map/all_gather | solution.py:1102
  524.1 1.4 reshape.242
  525.5 1.4 fusion.5
  531.1 1.5 reduce_sum.59
  532.7 10.2 %all_gather.37 = f32[256,256]{1,0:T(8,128)} all-gather(f32[32,256]{1,0:T(8,128)} %reduce_sum.59), channel_id=1, replica_groups=mesh['chan'=4,'hi'=2,'lo'=4] {'hi','lo'}, dimensions={0}, use_global_device_ids=true | all-gather | bytes 294912 | tf_op jit(solution)/shard_map/all_gather | solution.py:1102
  542.9 1.8 copy.97
  544.7 1.8 copy.109
  546.4 1.5 reduce_sum.55
  548.0 9.1 %all_gather.35 = f32[256,256]{1,0:T(8,128)S(1)} all-gather(f32[32,256]{1,0:T(8,128)} %reduce_sum.55), channel_id=1, replica_groups=mesh['chan'=4,'hi'=2,'lo'=4] {'hi','lo'}, dimensions={0}, use_global_device_ids=true | all-gather | bytes 294912 | tf_op jit(solution)/shard_map/all_gather | solution.py:1102
  557.9 10.6 %concatenate.26 = f32[140624]{0:T(1024)} concatenate(f32[65536]{0:T(1024)} %bitcast.100, f32[7424]{0:T(1024)} %reshape.242, f32[65536]{0:T(1024)} %bitcast.97, f32[1024]{0:T(1024)S(1)} %reshape.246, f32[16]{0:T(128)} %slice_bitcast_fusion.2, f32[1024]{0:T(1024)S(1)} %reshape.247, f32[64]{0:T(128)S(1)} %slice_bitcast_fusion.1), dimensions={0} | concatenate | bytes 1124992 | tf_op jit(solution)/shard_map/concatenate | solution.py:861
  568.6 1.9 pad.14
  570.5 2.0 reshape.248.grad_ref
  577.4 1.7 adam.1
  582.3 3.4 broadcast_in_dim.28
  587.2 3.3 restore.1
  590.5 5.5 uncrop.1
  (231 shorter events, 59.4 us)
Async XLA Ops:
  7.2 1.7 copy-start.35
  14.8 54.0 %all-to-all-start = ((f32[16,64,512]{2,1,0:T(8,128)}), f32[16,64,512]{2,1,0:T(8,128)S(1)}, u32[]{:S(2)}, u32[]{:S(2)}) async-start(f32[16,64,512]{2,1,0:T(8,128)} %copy-done.12), calls=%async_computation | async-start | bytes 4194304 | tf_op jit(solution)/shard_map/all_to_all | solution.py:107
  26.3 47.3 %copy-start.42 = (f32[256,256]{1,0:T(8,128)S(1)}, f32[256,256]{1,0:T(8,128)}, u32[]{:S(2)}) copy-start(f32[256,256]{1,0:T(8,128)} %param.25) | copy-start | bytes 786436
  26.3 49.0 %copy-start.53 = (f32[64,16]{0,1:T(8,128)S(1)}, f32[64,16]{0,1:T(8,128)}, u32[]{:S(2)}) copy-start(f32[64,16]{0,1:T(8,128)} %param.30) | copy-start | bytes 12292
  26.4 49.0 %copy-start.55 = (f32[16,64]{1,0:T(8,128)S(1)}, f32[16,64]{1,0:T(8,128)}, u32[]{:S(2)}) copy-start(f32[16,64]{1,0:T(8,128)} %param.32) | copy-start | bytes 12292
  26.4 49.0 %copy-start.61 = (f32[64]{0:T(128)S(1)}, f32[64]{0:T(128)}, u32[]{:S(2)}) copy-start(f32[64]{0:T(128)} %param.33) | copy-start | bytes 772
  26.4 49.6 %copy-start.49 = (f32[25,256]{1,0:T(8,128)S(1)}, f32[25,256]{1,0:T(8,128)}, u32[]{:S(2)}) copy-start(f32[25,256]{1,0:T(8,128)} %param.26) | copy-start | bytes 76804
  26.4 49.6 %copy-start.57 = (f32[2,256]{1,0:T(2,128)S(1)}, f32[2,256]{1,0:T(2,128)}, u32[]{:S(2)}) copy-start(f32[2,256]{1,0:T(2,128)} %param.27) | copy-start | bytes 6148
  26.4 49.6 %copy-start.59 = (f32[2,256]{1,0:T(2,128)S(1)}, f32[2,256]{1,0:T(2,128)}, u32[]{:S(2)}) copy-start(f32[2,256]{1,0:T(2,128)} %param.28) | copy-start | bytes 6148
  68.7 142.8 %all-to-all-start.1 = ((f32[16,64,512]{2,1,0:T(8,128)}), f32[16,64,512]{2,1,0:T(8,128)}, u32[]{:S(2)}, u32[]{:S(2)}) async-start(f32[16,64,512]{2,1,0:T(8,128)} %copy-done.3), calls=%async_computation.1 | async-start | bytes 4194304 | tf_op jit(solution)/shard_map/all_to_all | solution.py:107
  73.6 69.6 %all-gather.7.cloned.1.call-start = ((), (), s32[]{:S(2)}) async-start(), calls=%async_computation.10 | async-start | bytes 1310720 | tf_op jit(solution)/shard_map/all_gather | solution.py:993
  74.6 131.6 %all-gather.9.cloned.1.call-start = ((), (), s32[]{:S(2)}) async-start(), calls=%async_computation.11 | async-start | bytes 1310720 | tf_op jit(solution)/shard_map/all_gather | solution.py:994
  76.8 68.0 %collective-permute-start = (f32[4,1,64,256]{3,2,1,0:T(8,128)}, f32[4,1,64,256]{3,2,1,0:T(8,128)S(1)}, u32[]{:S(2)}, u32[]{:S(2)}) collective-permute-start(f32[4,1,64,256]{3,2,1,0:T(8,128)} %get-tuple-element.105), channel_id=1, source_target_pairs={{0,4},{1,5},{2,6},{3,7},{8,12},{9,13},{10,14},{11,15},{16,20},{17,... | collective-permute-start | bytes 786440 | tf_op jit(solution)/shard_map/ppermute | solution.py:122
  78.1 67.4 %collective-permute-start.1 = (f32[4,1,64,256]{3,2,1,0:T(8,128)}, f32[4,1,64,256]{3,2,1,0:T(8,128)}, u32[]{:S(2)}, u32[]{:S(2)}) collective-permute-start(f32[4,1,64,256]{3,2,1,0:T(8,128)} %get-tuple-element.104), channel_id=1, source_target_pairs={{4,0},{5,1},{6,2},{7,3},{12,8},{13,9},{14,10},{15,11},{20,16},{21,... | collective-permute-start | bytes 786440 | tf_op jit(solution)/shard_map/ppermute | solution.py:123
  146.5 15.8 %copy-start.52 = (f32[1,33,64]{2,1,0:T(8,128)S(1)}, f32[1,33,64]{2,1,0:T(8,128)}, u32[]{:S(2)}) copy-start(f32[1,33,64]{2,1,0:T(8,128)} %maximum_bitcast_fusion) | copy-start | bytes 25348
  153.0 3.3 copy-start
  156.4 41.5 %copy-start.4 = (f32[2,256,1024]{2,1,0:T(8,128)}, f32[2,256,1024]{2,1,0:T(8,128)S(1)}, u32[]{:S(2)}) copy-start(f32[2,256,1024]{2,1,0:T(8,128)S(1)} %get-tuple-element.53) | copy-start | bytes 6291460
  156.4 3.2 collective-permute-start.2
  159.6 13.1 %collective-permute-start.3 = (f32[2,1024]{1,0:T(2,128)S(1)}, f32[2,1024]{1,0:T(2,128)S(1)}, u32[]{:S(2)}, u32[]{:S(2)}) collective-permute-start(f32[2,1024]{1,0:T(2,128)S(1)} %add.25.rest_0_), channel_id=1, source_target_pairs={{0,2},{1,3},{2,0},{3,1},{4,6},{5,7},{6,4},{7,5},{8,10},{9,11},{10,... | collective-permute-start | bytes 24584 | tf_op jit(solution)/shard_map/ppermute | solution.py:90
  160.1 12.5 %collective-permute-start.4 = (f32[2,1024]{1,0:T(2,128)S(1)}, f32[2,1024]{1,0:T(2,128)S(1)}, u32[]{:S(2)}, u32[]{:S(2)}) collective-permute-start(f32[2,1024]{1,0:T(2,128)S(1)} %add.25.rest_0_), channel_id=1, source_target_pairs={{0,4},{1,5},{2,6},{3,7},{4,0},{5,1},{6,2},{7,3},{8,12},{9,13},{10,... | collective-permute-start | bytes 24584 | tf_op jit(solution)/shard_map/ppermute | solution.py:90
  160.4 12.3 %collective-permute-start.5 = (f32[2,1024]{1,0:T(2,128)S(1)}, f32[2,1024]{1,0:T(2,128)S(1)}, u32[]{:S(2)}, u32[]{:S(2)}) collective-permute-start(f32[2,1024]{1,0:T(2,128)S(1)} %add.25.rest_0_), channel_id=1, source_target_pairs={{0,6},{1,7},{2,4},{3,5},{4,2},{5,3},{6,0},{7,1},{8,14},{9,15},{10,... | collective-permute-start | bytes 24584 | tf_op jit(solution)/shard_map/ppermute | solution.py:90
  197.9 3.3 copy-start.1
  202.1 6.6 %collective-permute-start.8 = (f32[2,1024]{1,0:T(2,128)S(1)}, f32[2,1024]{1,0:T(2,128)S(1)}, u32[]{:S(2)}, u32[]{:S(2)}) collective-permute-start(f32[2,1024]{1,0:T(2,128)S(1)} %get-tuple-element.57), channel_id=1, source_target_pairs={{0,1},{1,0},{2,3},{3,2},{4,5},{5,4},{6,7},{7,6},{8,9},{9,8},{10,11... | collective-permute-start | bytes 24584 | tf_op jit(solution)/shard_map/ppermute | solution.py:90
  208.8 10.3 %collective-permute-start.10 = (f32[2,1024]{1,0:T(2,128)S(1)}, f32[2,1024]{1,0:T(2,128)S(1)}, u32[]{:S(2)}, u32[]{:S(2)}) collective-permute-start(f32[2,1024]{1,0:T(2,128)S(1)} %add.26.rest_0_.rest_2_.rest_4_), channel_id=1, source_target_pairs={{0,4},{1,5},{2,6},{3,7},{4,0},{5,1},{6,2},{7,3},{8,12},{9,13},{10,... | collective-permute-start | bytes 24584 | tf_op jit(solution)/shard_map/ppermute | solution.py:90
  209.0 10.1 %collective-permute-start.11 = (f32[2,1024]{1,0:T(2,128)S(1)}, f32[2,1024]{1,0:T(2,128)S(1)}, u32[]{:S(2)}, u32[]{:S(2)}) collective-permute-start(f32[2,1024]{1,0:T(2,128)S(1)} %add.26.rest_0_.rest_2_.rest_4_), channel_id=1, source_target_pairs={{0,6},{1,7},{2,4},{3,5},{4,2},{5,3},{6,0},{7,1},{8,14},{9,15},{10,... | collective-permute-start | bytes 24584 | tf_op jit(solution)/shard_map/ppermute | solution.py:90
  210.2 8.9 %collective-permute-start.9 = (f32[2,1024]{1,0:T(2,128)S(1)}, f32[2,1024]{1,0:T(2,128)S(1)}, u32[]{:S(2)}, u32[]{:S(2)}) collective-permute-start(f32[2,1024]{1,0:T(2,128)S(1)} %add.26.rest_0_.rest_2_.rest_4_), channel_id=1, source_target_pairs={{0,2},{1,3},{2,0},{3,1},{4,6},{5,7},{6,4},{7,5},{8,10},{9,11},{10,... | collective-permute-start | bytes 24584 | tf_op jit(solution)/shard_map/ppermute | solution.py:90
  213.2 19.3 %collective-permute-start.6 = (f32[4,1,64,128]{3,2,1,0:T(8,128)}, f32[4,1,64,128]{3,2,1,0:T(8,128)S(1)}, u32[]{:S(2)}, u32[]{:S(2)}) collective-permute-start(f32[4,1,64,128]{3,2,1,0:T(8,128)} %get-tuple-element.103), channel_id=1, source_target_pairs={{0,4},{1,5},{2,6},{3,7},{8,12},{9,13},{10,14},{11,15},{16,20},{17,... | collective-permute-start | bytes 393224 | tf_op jit(solution)/shard_map/ppermute | solution.py:122
  214.5 18.0 %collective-permute-start.7 = (f32[4,1,64,128]{3,2,1,0:T(8,128)}, f32[4,1,64,128]{3,2,1,0:T(8,128)}, u32[]{:S(2)}, u32[]{:S(2)}) collective-permute-start(f32[4,1,64,128]{3,2,1,0:T(8,128)} %get-tuple-element.102), channel_id=1, source_target_pairs={{4,0},{5,1},{6,2},{7,3},{12,8},{13,9},{14,10},{15,11},{20,16},{21,... | collective-permute-start | bytes 393224 | tf_op jit(solution)/shard_map/ppermute | solution.py:123
  219.1 3.4 copy-start.2
  223.7 10.7 %copy-start.34 = (f32[16]{0:T(128)S(1)}, f32[16]{0:T(128)}, u32[]{:S(2)}) copy-start(f32[16]{0:T(128)} %param.31) | copy-start | bytes 196
  231.9 2.4 collective-permute-start.12
  251.9 3.4 collective-permute-start.13
  255.4 2.7 collective-permute-start.14
  255.6 2.5 collective-permute-start.15
  255.6 3.5 collective-permute-start.16
  259.1 1.6 copy-start.5
  310.2 22.1 %copy-start.6 = (f32[1024,256]{1,0:T(8,128)S(1)}, f32[1024,256]{1,0:T(8,128)}, u32[]{:S(2)}) copy-start(f32[1024,256]{1,0:T(8,128)} %all-gather.9.cloned.1.call-done.w_ref) | copy-start | bytes 3145732
  327.7 16.3 %all-to-all-start.7 = ((f32[4,8,256]{2,1,0:T(8,128)}), f32[4,8,256]{2,1,0:T(8,128)S(1)}, u32[]{:S(2)}, u32[]{:S(2)}) async-start(f32[4,8,256]{2,1,0:T(8,128)} %bitcast.31), calls=%async_computation.7 | async-start | bytes 65536 | tf_op jit(solution)/shard_map/all_to_all | solution.py:955
  344.0 20.6 %copy-start.15 = (f32[256,1024]{0,1:T(8,128)S(1)}, f32[256,1024]{0,1:T(8,128)}, u32[]{:S(2)}) copy-start(f32[256,1024]{0,1:T(8,128)} %all-gather.7.cloned.1.call-done) | copy-start | bytes 3145732
  344.0 31.4 %copy-start.51 = (f32[4,8,256]{2,1,0:T(8,128)}, f32[4,8,256]{2,1,0:T(8,128)S(1)}, u32[]{:S(2)}) copy-start(f32[4,8,256]{2,1,0:T(8,128)S(1)} %all-to-all-done.7) | copy-start | bytes 98308
  344.0 33.7 %all-to-all-start.8 = ((f32[8,32,1024]{2,1,0:T(8,128)}), f32[8,32,1024]{2,1,0:T(8,128)}, u32[]{:S(2)}, u32[]{:S(2)}) async-start(f32[8,32,1024]{2,1,0:T(8,128)} %bitcast.86), calls=%async_computation.8 | async-start | bytes 2097152 | tf_op jit(solution)/shard_map/all_to_all | solution.py:953
  351.6 1.2 collective-permute-start.17
  352.8 11.6 %collective-permute-start.18 = (f32[2,1024]{1,0:T(2,128)S(1)}, f32[2,1024]{1,0:T(2,128)S(1)}, u32[]{:S(2)}, u32[]{:S(2)}) collective-permute-start(f32[2,1024]{1,0:T(2,128)S(1)} %add.28.rest_4_), channel_id=1, source_target_pairs={{0,2},{1,3},{2,0},{3,1},{4,6},{5,7},{6,4},{7,5},{8,10},{9,11},{10,... | collective-permute-start | bytes 24584 | tf_op jit(solution)/shard_map/ppermute | solution.py:90
  353.1 11.6 %collective-permute-start.19 = (f32[2,1024]{1,0:T(2,128)S(1)}, f32[2,1024]{1,0:T(2,128)S(1)}, u32[]{:S(2)}, u32[]{:S(2)}) collective-permute-start(f32[2,1024]{1,0:T(2,128)S(1)} %add.28.rest_4_), channel_id=1, source_target_pairs={{0,4},{1,5},{2,6},{3,7},{4,0},{5,1},{6,2},{7,3},{8,12},{9,13},{10,... | collective-permute-start | bytes 24584 | tf_op jit(solution)/shard_map/ppermute | solution.py:90
  353.1 11.5 %collective-permute-start.20 = (f32[2,1024]{1,0:T(2,128)S(1)}, f32[2,1024]{1,0:T(2,128)S(1)}, u32[]{:S(2)}, u32[]{:S(2)}) collective-permute-start(f32[2,1024]{1,0:T(2,128)S(1)} %add.28.rest_4_), channel_id=1, source_target_pairs={{0,6},{1,7},{2,4},{3,5},{4,2},{5,3},{6,0},{7,1},{8,14},{9,15},{10,... | collective-permute-start | bytes 24584 | tf_op jit(solution)/shard_map/ppermute | solution.py:90
  377.7 18.9 %all-to-all-start.4 = ((f32[8,32,1024]{2,1,0:T(8,128)}), f32[8,32,1024]{2,1,0:T(8,128)S(1)}, u32[]{:S(2)}, u32[]{:S(2)}) async-start(f32[8,32,1024]{2,1,0:T(8,128)} %bitcast.87), calls=%async_computation.4 | async-start | bytes 2097152 | tf_op jit(solution)/shard_map/all_to_all | solution.py:953
  396.6 8.9 %all-to-all-start.9 = ((f32[4,32,256]{2,1,0:T(8,128)}), f32[4,32,256]{2,1,0:T(8,128)S(1)}, u32[]{:S(2)}, u32[]{:S(2)}) async-start(f32[4,32,256]{2,1,0:T(8,128)} %copy.96), calls=%async_computation.9 | async-start | bytes 262144 | tf_op jit(solution)/shard_map/all_to_all | solution.py:955
  405.5 7.9 %copy-start.45 = (f32[4,32,256]{2,1,0:T(8,128)}, f32[4,32,256]{2,1,0:T(8,128)S(1)}, u32[]{:S(2)}) copy-start(f32[4,32,256]{2,1,0:T(8,128)S(1)} %all-to-all-done.9) | copy-start | bytes 393220
  468.7 5.2 copy-start.54
  468.7 5.3 copy-start.50
  468.7 5.3 copy-start.56
  468.7 5.3 copy-start.43
  468.7 5.5 copy-start.44
  468.7 5.7 copy-start.58
  468.7 5.7 copy-start.60
  468.7 5.7 copy-start.62
  468.7 121.8 %all-to-all-start.3 = ((f32[16,64,512]{2,1,0:T(8,128)}), f32[16,64,512]{2,1,0:T(8,128)}, u32[]{:S(2)}, u32[]{:S(2)}) async-start(f32[16,64,512]{2,1,0:T(8,128)} %bitcast.83), calls=%async_computation.3 | async-start | bytes 4194304 | tf_op jit(solution)/shard_map/all_to_all | solution.py:107
  474.2 2.2 copy-start.46
  476.3 16.0 %copy-start.47 = (f32[1,26,1024]{2,0,1:T(1,128)S(1)}, f32[1,26,1024]{2,0,1:T(1,128)}, u32[]{:S(2)}) copy-start(f32[1,26,1024]{2,0,1:T(1,128)} %param.34) | copy-start | bytes 319492
  492.2 20.5 %copy-start.33 = (s32[138,1]{0,1:T(1,128)S(1)}, s32[138,1]{0,1:T(1,128)}, u32[]{:S(2)}) copy-start(s32[138,1]{0,1:T(1,128)} %param.24) | copy-start | bytes 1660
  581.1 4.6 copy-start.32
  581.1 5.3 copy-start.30
  587.2 3.3 copy-start.39
  587.2 3.3 copy-start.41
  (29 other events, 29.7 us)
Sparse Core Ops, SparseCore 0:
  76.0 48.8 all-gather.6
  126.5 32.2 all-gather.8

commit v2 on v1

v2 whole, which is shorter than its diff:
```python
from functools import partial
import math

import jax
import jax.numpy as jnp
from jax import lax
from jax.experimental import pallas as pl
from jax.experimental.pallas import tpu as pltpu
from jax.sharding import Mesh, PartitionSpec as P

K = 5
FRAME_ROWS = 64
FRAME_COLUMNS = 64
CLIP_LEN = 4
MB = 4
STEP = 5
WIN = 80
SUB = 8
TAPS = K * K
HALO_IN = 4
SMALL = 64
HALO_OUT = 2

norm_eps = 1e-05
beta_first = 0.5
beta_second = 0.6
adam_eps = 1e-08
weight_decay = 0.1

F32 = jnp.float32
BF16 = jnp.bfloat16
ALL = ("chan", "hi", "lo")
PIX = ("hi", "lo")
SPREAD = ("chan", "lo")
VMEM_BYTES = 60 * 2**20


def params(dims=1):
    return pltpu.CompilerParams(vmem_limit_bytes=VMEM_BYTES, dimension_semantics=("arbitrary",) * dims)


def cost(us):
    return pl.CostEstimate(flops=int(us * 1.1e9), bytes_accessed=int(us * 3.5e6), transcendentals=0)


def sigmoid(v):
    return 0.5 * jnp.tanh(0.5 * v) + 0.5


def split(v):
    high = v.astype(BF16)
    return high, (v - high.astype(F32)).astype(BF16)


def dot(a, b):
    return jnp.dot(a, b, preferred_element_type=F32)


def dot3(a, b):
    return dot(a[0], b[0]) + (dot(a[0], b[1]) + dot(a[1], b[0]))


def exact_dot(a, b):
    return jnp.dot(a, b, preferred_element_type=F32, precision=lax.Precision.HIGHEST)


def total(refs):
    value = refs[0][...]
    for ref in refs[1:]:
        value = value + ref[...]
    return value


def norm_terms(sums, count, gain, bias):
    mean = sums[0:1] / count
    inverse = lax.rsqrt(sums[1:2] / count - mean * mean + norm_eps)
    scale = gain * inverse
    return mean, inverse, scale, bias - mean * scale


def back_terms(sums, back, count, gain):
    mean = sums[0:1] / count
    inverse = lax.rsqrt(sums[1:2] / count - mean * mean + norm_eps)
    a = gain * inverse
    b = -a * inverse * (back[1:2] / count)
    return a, b, -a * (back[0:1] / count) - b * mean


def exchange(x, stride):
    n = lax.axis_size(ALL)
    return lax.ppermute(x, ALL, [(i, i ^ stride) for i in range(n)])


def shares(x, base, size):
    bits = size.bit_length() - 1
    parts = [x]
    if bits % 2:
        parts = [x, exchange(x, base)]
        base, bits = base * 2, bits - 1
    while bits:
        x = sum(parts[1:], parts[0])
        parts = [x] + [exchange(x, base * k) for k in (1, 2, 3)]
        base, bits = base * 4, bits - 2
    return parts


def deal(x):
    return lax.all_to_all(x, SPREAD, 0, 0, tiled=True)


def edge(x, rows, band, first):
    if rows >= band:
        n = rows // band
        return x[:, :n] if first else x[:, x.shape[1] - n :]
    width = rows * FRAME_COLUMNS
    return x[:, :1, :, :width] if first else x[:, -1:, :, x.shape[3] - width :]


def rims(x, rows, band):
    n = lax.axis_size("hi")
    if n == 2:
        mine = jnp.where(lax.axis_index("hi") == 0, edge(x, rows, band, False), edge(x, rows, band, True))
        other = lax.ppermute(mine, "hi", [(0, 1), (1, 0)])
        return other, other
    down = [(i, i + 1) for i in range(n - 1)]
    up = [(i + 1, i) for i in range(n - 1)]
    top = lax.ppermute(edge(x, rows, band, False), "hi", down)
    low = lax.ppermute(edge(x, rows, band, True), "hi", up)
    return top, low


def near(n_pix):
    return n_pix == 8


def gather_pix(x):
    n_pix = lax.axis_size(PIX)
    if not near(n_pix):
        return [lax.all_gather(x, PIX, axis=0)], [list(range(n_pix))]
    b = x[None]
    b = jnp.concatenate([b, exchange(b, 2)])
    b = jnp.concatenate([b, exchange(b, 4)])
    return [b, exchange(b, 1)], [[0, 2, 4, 6], [1, 3, 5, 7]]


def gather_chan(x):
    nz, n_pix = lax.axis_size("chan"), lax.axis_size(PIX)
    if not near(n_pix):
        return list(lax.all_gather(x, "chan", axis=0))
    return [x] + [exchange(x, k * n_pix) for k in range(1, nz)]


def source_column(p, left, flip):
    row, c, s = p // FRAME_COLUMNS, (p // SUB) % SUB, p % SUB
    j = s * SUB + c
    return row * WIN + left + jnp.where(flip == 1, FRAME_COLUMNS - 1 - j, j)


def plain_place(p):
    row, c, s = p // FRAME_COLUMNS, (p // SUB) % SUB, p % SUB
    return row * FRAME_COLUMNS + s * SUB + c


def pick(x, chosen):
    rows = x.shape[0] * x.shape[1]
    high, low = split(x.reshape(rows, x.shape[2]))
    return (dot(high, chosen) + dot(low, chosen)).reshape(x.shape[0], x.shape[1], chosen.shape[1])


def crop_kernel(left_ref, flip_ref, raw_ref, out_ref):
    k = pl.program_id(0)
    width, area = raw_ref.shape[2], out_ref.shape[2]
    p = lax.broadcasted_iota(jnp.int32, (1, area), 1)
    place = source_column(p, left_ref[k], flip_ref[k])
    q = lax.broadcasted_iota(jnp.int32, (width, area), 0)
    out_ref[...] = pick(raw_ref[...], (q == place).astype(F32).astype(BF16))


def crop(raw, left, flip):
    frames, chans, width = raw.shape
    area = width // WIN * FRAME_COLUMNS
    return pl.pallas_call(
        crop_kernel,
        grid=(frames // CLIP_LEN,),
        in_specs=[
            pl.BlockSpec(memory_space=pltpu.SMEM),
            pl.BlockSpec(memory_space=pltpu.SMEM),
            pl.BlockSpec((CLIP_LEN, chans, width), lambda k: (k, 0, 0)),
        ],
        out_specs=pl.BlockSpec((CLIP_LEN, chans, area), lambda k: (k, 0, 0)),
        out_shape=jax.ShapeDtypeStruct((frames, chans, area), F32),
        compiler_params=params(),
        cost_estimate=cost(5),
        name="crop",
    )(left, flip, raw)


def order_kernel(x_ref, out_ref):
    area = x_ref.shape[2]
    p = lax.broadcasted_iota(jnp.int32, (1, area), 1)
    q = lax.broadcasted_iota(jnp.int32, (area, area), 0)
    out_ref[...] = pick(x_ref[...], (q == plain_place(p)).astype(F32).astype(BF16))


def order(x):
    frames, chans, area = x.shape
    return pl.pallas_call(
        order_kernel,
        grid=(frames // CLIP_LEN,),
        in_specs=[pl.BlockSpec((CLIP_LEN, chans, area), lambda k: (k, 0, 0))],
        out_specs=pl.BlockSpec((CLIP_LEN, chans, area), lambda k: (k, 0, 0)),
        out_shape=jax.ShapeDtypeStruct((frames, chans, area), F32),
        compiler_params=params(),
        cost_estimate=cost(1),
        name="order",
    )(x)


def restore_kernel(x_ref, out_ref):
    area = x_ref.shape[2]
    p = lax.broadcasted_iota(jnp.int32, (area, 1), 0)
    q = lax.broadcasted_iota(jnp.int32, (area, area), 1)
    out_ref[...] = pick(x_ref[...], (q == plain_place(p)).astype(F32).astype(BF16))


def restore(x):
    frames, chans, area = x.shape
    return pl.pallas_call(
        restore_kernel,
        grid=(frames // CLIP_LEN,),
        in_specs=[pl.BlockSpec((CLIP_LEN, chans, area), lambda k: (k, 0, 0))],
        out_specs=pl.BlockSpec((CLIP_LEN, chans, area), lambda k: (k, 0, 0)),
        out_shape=jax.ShapeDtypeStruct((frames, chans, area), F32),
        compiler_params=params(),
        cost_estimate=cost(5),
        name="restore",
    )(x)


def uncrop_kernel(left_ref, flip_ref, x_ref, y_ref, out_ref):
    k = pl.program_id(0)
    area, width = x_ref.shape[2], out_ref.shape[2]
    q = lax.broadcasted_iota(jnp.int32, (area, width), 1)
    out = None
    for half, ref in enumerate((x_ref, y_ref)):
        p = lax.broadcasted_iota(jnp.int32, (area, 1), 0) + half * area
        place = source_column(p, left_ref[k], flip_ref[k])
        term = pick(ref[...], (q == place).astype(F32).astype(BF16))
        out = term if out is None else out + term
    out_ref[...] = out


def uncrop(x, y, left, flip):
    frames, chans, area = x.shape
    width = 2 * area // FRAME_COLUMNS * WIN
    return pl.pallas_call(
        uncrop_kernel,
        grid=(frames // CLIP_LEN,),
        in_specs=[
            pl.BlockSpec(memory_space=pltpu.SMEM),
            pl.BlockSpec(memory_space=pltpu.SMEM),
            pl.BlockSpec((CLIP_LEN, chans, area), lambda k: (k, 0, 0)),
            pl.BlockSpec((CLIP_LEN, chans, area), lambda k: (k, 0, 0)),
        ],
        out_specs=pl.BlockSpec((CLIP_LEN, chans, width), lambda k: (k, 0, 0)),
        out_shape=jax.ShapeDtypeStruct((frames, chans, width), F32),
        compiler_params=params(),
        cost_estimate=cost(5),
        name="uncrop",
    )(left, flip, x, y)


def chunks(width):
    step = 256 if width % 256 == 0 else width
    return [slice(i, i + step) for i in range(0, width, step)]


def expand_kernel(x_ref, high_ref, low_ref, own_ref, sum_ref, gram_ref):
    @pl.when(pl.program_id(0) == 0)
    def _():
        sum_ref[...] = jnp.zeros_like(sum_ref)
        gram_ref[...] = jnp.zeros_like(gram_ref)

    chan_all, hidden = high_ref.shape
    plain = x_ref[:, 0].reshape(chan_all, x_ref.shape[3])
    turned = plain.T
    x = split(turned)
    for cut in chunks(hidden):
        y = dot3(x, (high_ref[:, cut], low_ref[:, cut]))
        own_ref[0, :, cut] = y
        sum_ref[0:1, cut] += jnp.sum(y, axis=0, keepdims=True)
        sum_ref[1:2, cut] += jnp.sum(y * y, axis=0, keepdims=True)
    gram_ref[:, 0:chan_all] += dot3(split(plain), x)
    gram_ref[:, chan_all:] += jnp.broadcast_to(jnp.sum(plain, axis=1, keepdims=True), (chan_all, 128))


def whole(shape):
    return pl.BlockSpec(shape, lambda *_: (0,) * len(shape))


def expand(x, high, low):
    nz, bands, chans, area = x.shape
    hidden = high.shape[1]
    return pl.pallas_call(
        expand_kernel,
        grid=(bands,),
        in_specs=[
            pl.BlockSpec((nz, 1, chans, area), lambda t: (0, t, 0, 0)),
            whole(high.shape),
            whole(low.shape),
        ],
        out_specs=[
            pl.BlockSpec((1, area, hidden), lambda t: (t, 0, 0)),
            whole((2, hidden)),
            whole((nz * chans, nz * chans + 128)),
        ],
        out_shape=[
            jax.ShapeDtypeStruct((bands, area, hidden), F32),
            jax.ShapeDtypeStruct((2, hidden), F32),
            jax.ShapeDtypeStruct((nz * chans, nz * chans + 128), F32),
        ],
        compiler_params=params(),
        cost_estimate=cost(8),
        name="expand",
    )(x, high, low)


def fill_sides(pad, row):
    s = lax.broadcasted_iota(jnp.int32, (SUB, 128), 0)
    for k in range(2):
        left = pltpu.roll(pad[row, SUB + k], 1, 0)
        pad[row, k] = jnp.where(s == 0, 0.0, left)
        right = pltpu.roll(pad[row, 2 + k], SUB - 1, 0)
        pad[row, SUB + 2 + k] = jnp.where(s == SUB - 1, 0.0, right)


def clear_rows(pad, start, count):
    for row in range(start, start + count):
        pad[row] = jnp.zeros(pad.shape[1:], F32)


def tap_rows(pad, w_ref, start, count, c, flipped=False):
    acc = [None] * count
    for b in range(K):
        for row in range(count + K - 1):
            value = pad[start + row, c + b]
            for a in range(K):
                o = row - a
                if 0 <= o < count:
                    tap = a * K + b
                    term = value * w_ref[TAPS - 1 - tap if flipped else tap]
                    acc[o] = term if acc[o] is None else acc[o] + term
    return acc


def turn_rims(refs, side_ref, high, low):
    for side, ref in enumerate(refs):
        chan_all, width = ref.shape[0] * ref.shape[2], ref.shape[3]

        @pl.when(side_ref[side] == 1)
        def _(side=side, ref=ref, chan_all=chan_all, width=width):
            for k in range(ref.shape[1]):
                here = slice(k * width, (k + 1) * width)
                high[side, here], low[side, here] = split(ref[:, k].reshape(chan_all, width).T)


def spread_kernel(
    parts, count, side_ref, top_ref, low_ref, own_ref, high_ref, lower_ref, gain_ref, bias_ref, w_ref, *rest
):
    sums = rest[:parts]
    out_ref, edge_ref, hid_ref, sum_ref, pad, terms, rim_high, rim_low = rest[parts:]
    rows = own_ref.shape[0]
    _, _, scale, shift = norm_terms(total(sums), count, gain_ref[0:1], bias_ref[0:1])
    terms[0] = jnp.broadcast_to(scale, (SUB, 128))
    terms[1] = jnp.broadcast_to(shift, (SUB, 128))

    @pl.when(pl.program_id(0) == 0)
    def _():
        turn_rims((top_ref, low_ref), side_ref, rim_high, rim_low)

    def act(value):
        v = value * terms[0] + terms[1]
        return v * sigmoid(v)

    def own_row(r, _):
        for c in range(SUB):
            pad[r + HALO_IN, c + 2] = act(own_ref[r, c])
        fill_sides(pad, r + HALO_IN)
        return 0

    lax.fori_loop(0, rows, own_row, 0)
    for side, start, first in ((0, 0, HALO_IN - HALO_OUT), (1, rows + HALO_IN, 0)):

        @pl.when(side_ref[side] == 1)
        def _(side=side, start=start, first=first):
            halo = dot3((rim_high[side], rim_low[side]), (high_ref[...], lower_ref[...]))
            halo = halo.reshape(HALO_IN, SUB, SUB, 128)
            hid_ref[side] = halo[first : first + HALO_OUT]
            pad[start : start + HALO_IN, 2 : SUB + 2] = act(halo)
            for r in range(HALO_IN):
                fill_sides(pad, start + r)

        @pl.when(side_ref[side] == 0)
        def _(side=side, start=start):
            clear_rows(pad, start, HALO_IN)
            hid_ref[side] = jnp.zeros(hid_ref.shape[1:], F32)

    def group(i, carry):
        one, two = carry
        r = i * SUB
        for c in range(SUB):
            acc = tap_rows(pad, w_ref, r + 2, SUB, c)
            for o in range(SUB):
                out_ref[r + o, c] = acc[o]
                one = one + acc[o]
                two = two + acc[o] * acc[o]
        return one, two

    zero = jnp.zeros((SUB, 128), F32)
    one, two = lax.fori_loop(0, rows // SUB, group, (zero, zero))
    sum_ref[0:1] = jnp.sum(one, axis=0, keepdims=True)
    sum_ref[1:2] = jnp.sum(two, axis=0, keepdims=True)
    for side, start in ((0, 0), (1, rows + 2)):

        @pl.when(side_ref[side] == 1)
        def _(side=side, start=start):
            for c in range(SUB):
                acc = tap_rows(pad, w_ref, start, HALO_OUT, c)
                for o in range(HALO_OUT):
                    edge_ref[side, o, c] = acc[o]

        @pl.when(side_ref[side] == 0)
        def _(side=side):
            edge_ref[side] = jnp.zeros(edge_ref.shape[1:], F32)


def lanes(shape):
    lead = len(shape) - 1
    return pl.BlockSpec(tuple(shape[:-1]) + (128,), lambda e: (0,) * lead + (e,))


def spread(count, side, top, low, own, w_high, w_low, gains, biases, taps, sums):
    rows, hidden = own.shape[0], own.shape[-1]
    chan_all = w_high.shape[0]
    arrays = [own, w_high, w_low, gains, biases, taps, *sums]
    edge_shape = (2, HALO_OUT, SUB, SUB, hidden)
    rim_shape = (2, HALO_IN * FRAME_COLUMNS, chan_all)
    return pl.pallas_call(
        partial(spread_kernel, len(sums), count),
        grid=(hidden // 128,),
        in_specs=[pl.BlockSpec(memory_space=pltpu.SMEM), whole(top.shape), whole(low.shape)]
        + [lanes(a.shape) for a in arrays],
        out_specs=[
            lanes((rows, SUB, SUB, hidden)),
            lanes(edge_shape),
            lanes(edge_shape),
            lanes((2, hidden)),
        ],
        out_shape=[
            jax.ShapeDtypeStruct((rows, SUB, SUB, hidden), F32),
            jax.ShapeDtypeStruct(edge_shape, F32),
            jax.ShapeDtypeStruct(edge_shape, F32),
            jax.ShapeDtypeStruct((2, hidden), F32),
        ],
        scratch_shapes=[
            pltpu.VMEM((rows + 2 * HALO_IN, SUB + 4, SUB, 128), F32),
            pltpu.VMEM((2, SUB, 128), F32),
            pltpu.VMEM(rim_shape, BF16),
            pltpu.VMEM(rim_shape, BF16),
        ],
        compiler_params=params(),
        cost_estimate=cost(25),
        name="spread",
    )(side, top, low, *arrays)


def as_row(columns):
    width = columns.shape[1]
    folded = columns[:, 0:128]
    for i in range(128, width, 128):
        folded = folded + columns[:, i : i + 128]
    return jnp.sum(folded.T, axis=0, keepdims=True)


def gather_kernel(parts, count, own_ref, gout_ref, gain_ref, bias_ref, wt_ref, high_ref, low_ref, *rest):
    sums, (m_ref, s_ref, se_ref, proj_ref) = rest[:parts], rest[parts:]
    t = pl.program_id(0)
    chan_all, hidden = wt_ref.shape

    @pl.when(t == 0)
    def _():
        m_ref[...] = jnp.zeros_like(m_ref)
        s_ref[...] = jnp.zeros_like(s_ref)

    _, _, scale, shift = norm_terms(total(sums), count, gain_ref[1:2], bias_ref[1:2])
    gout = split(gout_ref[:, 0].reshape(chan_all, gout_ref.shape[3]))
    proj = None
    for cut in chunks(hidden):
        v = own_ref[0, :, cut] * scale[:, cut] + shift[:, cut]
        act = v * sigmoid(v)
        s_ref[0:1, cut] += jnp.sum(act, axis=0, keepdims=True)
        act = split(act)
        m_ref[:, cut] += dot3(gout, act)
        term = dot3(act, (high_ref[cut], low_ref[cut]))
        proj = term if proj is None else proj + term
    proj_ref[0] = proj

    @pl.when(t == pl.num_programs(0) - 1)
    def _():
        wt = wt_ref[...]
        se_ref[0:1] = as_row(s_ref[...] * wt)
        se_ref[1:2] = as_row(m_ref[...] * wt)


def gather(count, own, gout, gains, biases, wt, w_high, w_low, sums):
    nz, bands, chans, area = gout.shape
    hidden = wt.shape[1]
    chan_all = nz * chans
    return pl.pallas_call(
        partial(gather_kernel, len(sums), count),
        grid=(bands,),
        in_specs=[
            pl.BlockSpec((1, area, hidden), lambda t: (t, 0, 0)),
            pl.BlockSpec((nz, 1, chans, area), lambda t: (0, t, 0, 0)),
            whole(gains.shape),
            whole(biases.shape),
            whole(wt.shape),
            whole(w_high.shape),
            whole(w_low.shape),
        ]
        + [whole(s.shape) for s in sums],
        out_specs=[
            whole((chan_all, hidden)),
            whole((1, hidden)),
            whole((2, chan_all)),
            pl.BlockSpec((1, area, chan_all), lambda t: (t, 0, 0)),
        ],
        out_shape=[
            jax.ShapeDtypeStruct((chan_all, hidden), F32),
            jax.ShapeDtypeStruct((1, hidden), F32),
            jax.ShapeDtypeStruct((2, chan_all), F32),
            jax.ShapeDtypeStruct((bands, area, chan_all), F32),
        ],
        compiler_params=params(),
        cost_estimate=cost(13),
        name="gather",
    )(own, gout, gains, biases, wt, w_high, w_low, *sums)


def column(row):
    return jnp.broadcast_to(row, (SUB, row.shape[1])).T[:, 0:1]


def padded_dot(row, matrix):
    return exact_dot(jnp.broadcast_to(row, (SUB, row.shape[1])), matrix)[0:1]


def slope_terms(sums, count, gain_ref, bias_ref):
    mean, inverse, _, _ = norm_terms(sums, count, gain_ref[1:2], bias_ref[1:2])
    return mean, inverse, gain_ref[1:2], bias_ref[1:2]


def second_grad(gout, weights, k_row, value, terms, cut):
    mean, inverse, gain, bias = terms
    grad = dot3(gout, (weights[0][:, cut], weights[1][:, cut])) + k_row[:, cut]
    centered = (value - mean[:, cut]) * inverse[:, cut]
    v = centered * gain[:, cut] + bias[:, cut]
    s = sigmoid(v)
    return grad * (s + v * s * (1.0 - s)), centered


def proj_back_kernel(
    pairs,
    parts,
    count,
    own_ref,
    gout_ref,
    gain_ref,
    bias_ref,
    wt_ref,
    sq_ref,
    sqt_ref,
    down_ref,
    ex_ref,
    ext_ref,
    exb_ref,
    *rest,
):
    ses, sums = rest[:pairs], rest[pairs : pairs + parts]
    q_ref, sum_ref, val_ref, w_high, w_low, k_row = rest[pairs + parts :]
    chan_all, hidden = wt_ref.shape
    reduced = ex_ref.shape[0]

    @pl.when(pl.program_id(0) == 0)
    def _():
        se = total(ses)
        pooled = se[0:1] / (FRAME_ROWS * FRAME_COLUMNS)
        pre = padded_dot(pooled, sq_ref[...]) + down_ref[...]
        gate = sigmoid(pre)
        squeezed = pre * gate
        excite = sigmoid(padded_dot(squeezed, ex_ref[...]) + exb_ref[...])
        logit = se[1:2] * excite * (1.0 - excite)
        slope = gate * (1.0 + pre * (1.0 - gate))
        grad_sq = padded_dot(logit, ext_ref[...]) * slope
        pool_grad = padded_dot(grad_sq, sqt_ref[...]) / (FRAME_ROWS * FRAME_COLUMNS)
        val_ref[...] = jnp.zeros_like(val_ref)
        val_ref[0:1] = excite
        val_ref[1:2] = pool_grad
        val_ref[2:3] = logit
        val_ref[3:4] = pooled
        val_ref[4:5, 0:reduced] = squeezed
        val_ref[5:6, 0:reduced] = grad_sq
        wt = wt_ref[...]
        w_high[...], w_low[...] = split(wt * column(excite))
        k_row[...] = jnp.sum(wt * column(pool_grad), axis=0, keepdims=True)
        sum_ref[...] = jnp.zeros_like(sum_ref)

    terms = slope_terms(total(sums), count, gain_ref, bias_ref)
    gout = split(gout_ref[:, 0].reshape(chan_all, gout_ref.shape[3]).T)
    for cut in chunks(hidden):
        q, centered = second_grad(gout, (w_high, w_low), k_row, own_ref[0, :, cut], terms, cut)
        q_ref[0, :, cut] = q
        sum_ref[0:1, cut] += jnp.sum(q, axis=0, keepdims=True)
        sum_ref[1:2, cut] += jnp.sum(q * centered, axis=0, keepdims=True)


def proj_back(count, own, gout, gains, biases, wt, se_weights, ses, sums):
    nz, bands, chans, area = gout.shape
    hidden = wt.shape[1]
    chan_all = nz * chans
    fixed = [gains, biases, wt, *se_weights, *ses, *sums]
    return pl.pallas_call(
        partial(proj_back_kernel, len(ses), len(sums), count),
        grid=(bands,),
        in_specs=[
            pl.BlockSpec((1, area, hidden), lambda t: (t, 0, 0)),
            pl.BlockSpec((nz, 1, chans, area), lambda t: (0, t, 0, 0)),
        ]
        + [whole(a.shape) for a in fixed],
        out_specs=[
            pl.BlockSpec((1, area, hidden), lambda t: (t, 0, 0)),
            whole((2, hidden)),
            whole((SUB, chan_all)),
            whole(wt.shape),
            whole(wt.shape),
            whole((1, hidden)),
        ],
        out_shape=[
            jax.ShapeDtypeStruct((bands, area, hidden), F32),
            jax.ShapeDtypeStruct((2, hidden), F32),
            jax.ShapeDtypeStruct((SUB, chan_all), F32),
            jax.ShapeDtypeStruct(wt.shape, BF16),
            jax.ShapeDtypeStruct(wt.shape, BF16),
            jax.ShapeDtypeStruct((1, hidden), F32),
        ],
        compiler_params=params(),
        cost_estimate=cost(12),
        name="proj_back",
    )(own, gout, *fixed)


def project_kernel(proj_ref, x_ref, val_ref, m_ref, s_ref, out_ref, grad_ref):
    nz, _, chans, area = x_ref.shape

    @pl.when(pl.program_id(0) == 0)
    def _():
        grad_ref[...] = column(val_ref[0:1]) * m_ref[...] + column(val_ref[1:2]) * s_ref[...]

    out = (proj_ref[0] * val_ref[0:1]).T
    out_ref[:, 0] = x_ref[:, 0] + out.reshape(nz, chans, area)


def project(proj, x, values, m, s):
    nz, bands, chans, area = x.shape
    fixed = [values, m, s]
    return pl.pallas_call(
        project_kernel,
        grid=(bands,),
        in_specs=[
            pl.BlockSpec((1, area, nz * chans), lambda t: (t, 0, 0)),
            pl.BlockSpec((nz, 1, chans, area), lambda t: (0, t, 0, 0)),
        ]
        + [whole(a.shape) for a in fixed],
        out_specs=[pl.BlockSpec((nz, 1, chans, area), lambda t: (0, t, 0, 0)), whole(m.shape)],
        out_shape=[
            jax.ShapeDtypeStruct((nz, bands, chans, area), F32),
            jax.ShapeDtypeStruct(m.shape, F32),
        ],
        compiler_params=params(),
        cost_estimate=cost(4),
        name="project",
    )(proj, x, *fixed)


def spread_back_kernel(
    parts,
    count,
    side_ref,
    top_ref,
    low_ref,
    hid_ref,
    hid_halo_ref,
    own_ref,
    halo_ref,
    q_ref,
    high_ref,
    lower_ref,
    k_ref,
    gain_ref,
    bias_ref,
    w_ref,
    *rest,
):
    sums_one, sums_two, backs = (rest[i * parts : (i + 1) * parts] for i in range(3))
    out_ref, sum_ref, tap_ref, pad, grad, terms, rim_high, rim_low = rest[3 * parts :]
    rows = own_ref.shape[0]

    @pl.when(pl.program_id(0) == 0)
    def _():
        turn_rims((top_ref, low_ref), side_ref, rim_high, rim_low)

    mean, inverse, scale, shift = norm_terms(total(sums_one), count, gain_ref[0:1], bias_ref[0:1])
    a, b, c0 = back_terms(total(sums_two), total(backs), count, gain_ref[1:2])
    for i, row in enumerate((scale, shift, a, b, c0, mean, inverse)):
        terms[i] = jnp.broadcast_to(row, (SUB, 128))

    def act(value):
        v = value * terms[0] + terms[1]
        return v * sigmoid(v)

    def grad_in(q, value):
        return q * terms[2] + (value * terms[3] + terms[4])

    def own_row(r, _):
        for c in range(SUB):
            pad[r + HALO_OUT, c + 2] = act(hid_ref[r, c])
            grad[r + HALO_OUT, c + 2] = grad_in(q_ref[r, c], own_ref[r, c])
        fill_sides(pad, r + HALO_OUT)
        fill_sides(grad, r + HALO_OUT)
        return 0

    lax.fori_loop(0, rows, own_row, 0)
    slope = slope_terms(total(sums_two), count, gain_ref, bias_ref)
    for side, start in ((0, 0), (1, rows + HALO_OUT)):

        @pl.when(side_ref[side] == 1)
        def _(side=side, start=start):
            value = halo_ref[side].reshape(HALO_OUT * FRAME_COLUMNS, 128)
            weights = (high_ref, lower_ref)
            gout = (rim_high[side], rim_low[side])
            q, _ = second_grad(gout, weights, k_ref, value, slope, slice(0, 128))
            edge = grad_in(q.reshape(HALO_OUT, SUB, SUB, 128), halo_ref[side])
            grad[start : start + HALO_OUT, 2 : SUB + 2] = edge
            pad[start : start + HALO_OUT, 2 : SUB + 2] = act(hid_halo_ref[side])
            for r in range(HALO_OUT):
                fill_sides(pad, start + r)
                fill_sides(grad, start + r)

        @pl.when(side_ref[side] == 0)
        def _(start=start):
            clear_rows(pad, start, HALO_OUT)
            clear_rows(grad, start, HALO_OUT)

    def weight_group(i, acc):
        acc = list(acc)
        r = i // SUB * SUB
        c = i % SUB
        mine = [grad[r + HALO_OUT + o, c + 2] for o in range(SUB)]
        for bb in range(K):
            for row in range(SUB + K - 1):
                value = pad[r + row, c + bb]
                for aa in range(K):
                    o = row - aa
                    if 0 <= o < SUB:
                        acc[aa * K + bb] = acc[aa * K + bb] + value * mine[o]
        return tuple(acc)

    zero = jnp.zeros((SUB, 128), F32)
    acc = lax.fori_loop(0, rows, weight_group, (zero,) * TAPS)
    for tap in range(TAPS):
        tap_ref[tap : tap + 1] = jnp.sum(acc[tap], axis=0, keepdims=True)

    def group(i, carry):
        one, two = carry
        r = i * SUB
        for c in range(SUB):
            acc = tap_rows(grad, w_ref, r, SUB, c, flipped=True)
            for o in range(SUB):
                hidden = hid_ref[r + o, c]
                v = hidden * terms[0] + terms[1]
                s = sigmoid(v)
                value = acc[o] * (s + v * s * (1.0 - s))
                out_ref[r + o, c] = value
                one = one + value
                two = two + value * ((hidden - terms[5]) * terms[6])
        return one, two

    one, two = lax.fori_loop(0, rows // SUB, group, (zero, zero))
    sum_ref[0:1] = jnp.sum(one, axis=0, keepdims=True)
    sum_ref[1:2] = jnp.sum(two, axis=0, keepdims=True)


def spread_back(
    count, side, top, low, hid, hid_halo, own, halo, q, weights, gains, biases, taps, sums_one, sums_two, backs
):
    rows, hidden = own.shape[0], own.shape[-1]
    arrays = [hid, hid_halo, own, halo, q, *weights, gains, biases, taps, *sums_one, *sums_two, *backs]
    rim_shape = (2, HALO_OUT * FRAME_COLUMNS, weights[0].shape[0])
    return pl.pallas_call(
        partial(spread_back_kernel, len(backs), count),
        grid=(hidden // 128,),
        in_specs=[pl.BlockSpec(memory_space=pltpu.SMEM), whole(top.shape), whole(low.shape)]
        + [lanes(a.shape) for a in arrays],
        out_specs=[lanes((rows, SUB, SUB, hidden)), lanes((2, hidden)), lanes((TAPS, hidden))],
        out_shape=[
            jax.ShapeDtypeStruct((rows, SUB, SUB, hidden), F32),
            jax.ShapeDtypeStruct((2, hidden), F32),
            jax.ShapeDtypeStruct((TAPS, hidden), F32),
        ],
        scratch_shapes=[
            pltpu.VMEM((rows + 2 * HALO_OUT, SUB + 4, SUB, 128), F32),
            pltpu.VMEM((rows + 2 * HALO_OUT, SUB + 4, SUB, 128), F32),
            pltpu.VMEM((7, SUB, 128), F32),
            pltpu.VMEM(rim_shape, BF16),
            pltpu.VMEM(rim_shape, BF16),
        ],
        compiler_params=params(),
        cost_estimate=cost(47),
        name="spread_back",
    )(side, top, low, *arrays)


def expand_grad(q_ref, hid_ref, terms, cut):
    a, b, c = terms
    return split(q_ref[0, :, cut] * a[:, cut] + (hid_ref[0, :, cut] * b[:, cut] + c[:, cut]))


def input_kernel(parts, count, half, q_ref, hid_ref, gout_ref, gain_ref, w_high, w_low, *rest):
    sums, backs, out_ref = rest[:parts], rest[parts : 2 * parts], rest[2 * parts]
    nz, _, chans, area = out_ref.shape
    terms = back_terms(total(sums), total(backs), count, gain_ref[0:1])
    out = None
    for cut in chunks(w_high.shape[0]):
        term = dot3(expand_grad(q_ref, hid_ref, terms, cut), (w_high[cut], w_low[cut]))
        out = term if out is None else out + term
    own = gout_ref[:, 0]
    if own.shape[2] > area:
        own = own[:, :, half * area : (half + 1) * area]
    out_ref[:, 0] = own + out.T.reshape(nz, chans, area)


def input_grad(count, half, q, hid, gout, gains, w_high, w_low, sums, backs):
    nz, bands, chans, area = gout.shape
    hidden = w_high.shape[0]
    area //= 2
    fixed = [gains, w_high, w_low, *sums, *backs]
    return pl.pallas_call(
        partial(input_kernel, len(sums), count, half),
        grid=(bands,),
        in_specs=[
            pl.BlockSpec((1, area, hidden), lambda t: (t, half, 0)),
            pl.BlockSpec((1, area, hidden), lambda t: (t, half, 0)),
            whole_half(nz, chans, area, half),
        ]
        + [whole(v.shape) for v in fixed],
        out_specs=pl.BlockSpec((nz, 1, chans, area), lambda t: (0, t, 0, 0)),
        out_shape=jax.ShapeDtypeStruct((nz, bands, chans, area), F32),
        compiler_params=params(),
        cost_estimate=cost(5),
        name="input_grad",
    )(q, hid, gout, *fixed)


def whole_half(nz, chans, area, half):
    if area % 128 == 0:
        return pl.BlockSpec((nz, 1, chans, area), lambda t: (0, t, 0, half))
    return pl.BlockSpec((nz, 1, chans, 2 * area), lambda t: (0, t, 0, 0))


def weight_kernel(chans, reduced, ids_ref, q_ref, x_ref, tap_ref, one_ref, two_ref, val_ref, *rest):
    outs, acc, small = rest[:-2], rest[-2], rest[-1]
    nz, _, _, area = x_ref.shape
    chan_all, hidden = acc.shape
    width = hidden // nz
    t = pl.program_id(0)

    @pl.when(t == 0)
    def _():
        acc[...] = jnp.zeros_like(acc)
        small[...] = jnp.zeros_like(small)
        small[0:TAPS] = tap_ref[...]
        small[TAPS : TAPS + 1] = one_ref[1:2]
        small[TAPS + 1 : TAPS + 2] = two_ref[1:2]
        small[TAPS + 2 : TAPS + 3] = one_ref[0:1]
        small[TAPS + 3 : TAPS + 4] = two_ref[0:1]
        lead = (ids_ref[1] == 0).astype(F32)
        logit, pooled = val_ref[2:3] * lead, val_ref[3:4]
        squeezed, grad_sq = val_ref[4:5, 0:reduced], val_ref[5:6, 0:reduced] * lead
        g_sq = column(grad_sq) * pooled
        g_ex = column(squeezed) * logit
        for z in range(nz):
            own, at = slice(z * chans, (z + 1) * chans), z * width
            small[32 : 32 + reduced, at : at + chans] = g_sq[:, own]
            small[32 : 32 + reduced, at + chans : at + 2 * chans] = g_ex[:, own]
            small[32:33, at + 2 * chans : at + 3 * chans] = logit[:, own]
            small[33:34, at + 2 * chans : at + 2 * chans + reduced] = grad_sq

    x = split(x_ref[:, 0].reshape(chan_all, area))
    for cut in chunks(hidden):
        acc[:, cut] += dot3(x, split(q_ref[0, :, cut]))

    @pl.when(t == pl.num_programs(0) - 1)
    def _():
        n = len(outs)
        r, m = chan_all // n, SMALL // n
        for i, out in enumerate(outs):
            p = ids_ref[0] ^ i
            out[0:r] = acc[pl.ds(pl.multiple_of(p * r, r), r), :]
            out[r : r + m] = small[pl.ds(pl.multiple_of(p * m, m), m), :]


def weight_grad(ids, pieces, q, x, taps, one, two, values, reduced):
    nz, bands, chans, area = x.shape
    hidden = q.shape[2]
    chan_all = nz * chans
    fixed = [taps, one, two, values]
    shape = ((chan_all + SMALL) // pieces, hidden)
    return pl.pallas_call(
        partial(weight_kernel, chans, reduced),
        grid=(bands,),
        in_specs=[
            pl.BlockSpec(memory_space=pltpu.SMEM),
            pl.BlockSpec((1, area, hidden), lambda t: (t, 0, 0)),
            pl.BlockSpec((nz, 1, chans, area), lambda t: (0, t, 0, 0)),
        ]
        + [whole(v.shape) for v in fixed],
        out_specs=[whole(shape)] * pieces,
        out_shape=[jax.ShapeDtypeStruct(shape, F32)] * pieces,
        scratch_shapes=[pltpu.VMEM((chan_all, hidden), F32), pltpu.VMEM((SMALL, hidden), F32)],
        compiler_params=params(),
        cost_estimate=cost(7),
        name="weight_grad",
    )(ids, q, x, *fixed)


def collect_kernel(n, nz, parts, count, ids_ref, early_ref, gram_ref, high_ref, low_ref, gain_ref, *rest):
    pieces, sums, backs = rest[:n], rest[n : n + parts], rest[n + parts : n + 2 * parts]
    outs, acc = rest[n + 2 * parts : -1], rest[-1]
    value = total(pieces)
    rows, width = value.shape[0], acc.shape[2]
    r, chan_all = early_ref.shape[0], high_ref.shape[0]
    a, b, c = back_terms(total(sums), total(backs), count, gain_ref[0:1])
    gram = gram_ref[...]
    hid = dot3(split(gram[:, 0:chan_all]), (high_ref[...], low_ref[...]))
    grad = a * value[0:r] + (b * hid + c * gram[:, chan_all : chan_all + 1])
    for z in range(nz):
        here = slice(z * width, (z + 1) * width)
        acc[z, 0:r] = grad[:, here]
        acc[z, r:rows] = value[r:, here]
        acc[z, rows:] = early_ref[:, here]
    for k, out in enumerate(outs):
        out[...] = acc[ids_ref[2] ^ k]


def collect(count, ids, nz, pieces, early, gram, w_high, w_low, gains, sums, backs):
    width = early.shape[1] // nz
    rows = pieces[0].shape[0] + early.shape[0]
    arrays = [early, gram, w_high, w_low, gains, *pieces, *sums, *backs]
    return pl.pallas_call(
        partial(collect_kernel, len(pieces), nz, len(sums), count),
        grid=(1,),
        in_specs=[pl.BlockSpec(memory_space=pltpu.SMEM)] + [whole(a.shape) for a in arrays],
        out_specs=[whole((rows, width))] * nz,
        out_shape=[jax.ShapeDtypeStruct((rows, width), F32)] * nz,
        scratch_shapes=[pltpu.VMEM((nz, rows, width), F32)],
        compiler_params=params(),
        cost_estimate=cost(3),
        name="collect",
    )(ids, *arrays)


def segments(chan_in, hidden_dev, chan_dev, reduced, tap_count, hidden_all):
    seg_sizes = [
        chan_in * hidden_dev,
        tap_count * hidden_dev,
        2 * hidden_dev,
        2 * hidden_dev,
        hidden_dev * chan_in,
        chan_dev * reduced,
        reduced,
        reduced * chan_dev,
        chan_dev,
    ]
    seg_rates = [
        0.5 / math.sqrt(chan_in),
        0.5 / math.sqrt(tap_count),
        0.3,
        0.3,
        0.5 * math.sqrt(8.0 / hidden_all),
        2.0 / math.sqrt(chan_in),
        0.3,
        1.0 / math.sqrt(reduced),
        0.3,
    ]
    return (seg_sizes, seg_rates)


def pack_kernel(at_ref, we_ref, wp_ref, dw_ref, gain_ref, bias_ref, sq_ref, ex_ref, exb_ref, out_ref, small):
    p = at_ref[0]
    chan_in, width = we_ref.shape
    chans, reduced = sq_ref.shape
    m = small.shape[0] * out_ref.shape[0] // (2 * chan_in + small.shape[0])
    r = (out_ref.shape[0] - m) // 2
    small[...] = jnp.zeros_like(small)
    small[0:TAPS] = dw_ref[...]
    small[TAPS : TAPS + 2] = gain_ref[...]
    small[TAPS + 2 : TAPS + 4] = bias_ref[...]
    small[32 : 32 + reduced, 0:chans] = sq_ref[...].T
    small[32 : 32 + reduced, chans : 2 * chans] = ex_ref[...]
    small[32:33, 2 * chans : 3 * chans] = exb_ref[...]
    out_ref[0:r] = we_ref[pl.ds(pl.multiple_of(p * r, r), r), :]
    if chan_in == width:
        out_ref[r : 2 * r] = wp_ref[pl.ds(pl.multiple_of(p * r, r), r), :]
    else:
        row, part = p * r % width, p * r // width
        out_ref[r : 2 * r] = wp_ref[
            pl.ds(pl.multiple_of(row, r), r), pl.ds(pl.multiple_of(part * width, 128), width)
        ]
    out_ref[2 * r : 2 * r + m] = small[pl.ds(pl.multiple_of(p * m, m), m), :]


def pack_weights(at, w_expand, w_dw, norm_gains, norm_biases, w_project, squeeze_matrix, excite_matrix, excite_bias_row):
    n_pix = lax.axis_size(PIX)
    chan_in, width = w_expand.shape
    arrays = [
        w_expand,
        w_project,
        w_dw,
        norm_gains,
        norm_biases,
        squeeze_matrix,
        excite_matrix,
        excite_bias_row[None],
    ]
    shape = ((2 * chan_in + SMALL) // n_pix, width)
    return pl.pallas_call(
        pack_kernel,
        grid=(1,),
        in_specs=[pl.BlockSpec(memory_space=pltpu.SMEM)] + [whole(a.shape) for a in arrays],
        out_specs=whole(shape),
        out_shape=jax.ShapeDtypeStruct(shape, F32),
        scratch_shapes=[pltpu.VMEM((SMALL, width), F32)],
        compiler_params=params(),
        cost_estimate=cost(2),
        name="pack_weights",
    )(at, *arrays)


def weights_kernel(
    chan_in,
    chans,
    orders,
    base_ref,
    *refs,
):
    slabs = refs[: len(orders)]
    (
        we_high,
        we_low,
        wet_high,
        wet_low,
        wp_high,
        wp_low,
        wpt_ref,
        tap_ref,
        gain_ref,
        bias_ref,
        sq_ref,
        sqt_ref,
        ex_ref,
        ext_ref,
        exb_ref,
        first,
        second,
        small,
    ) = refs[len(orders) :]
    nz, width = first.shape[0], first.shape[2]
    n_pix = sum(len(order) for order in orders)
    r, m = chan_in // n_pix, SMALL // n_pix
    reduced = ex_ref.shape[0]
    for ref, order in zip(slabs, orders):
        for i, p in enumerate(order):
            at = base_ref[0] ^ p
            wide = pl.ds(pl.multiple_of(at * r, r), r)
            for z in range(nz):
                here = slice(z * width, (z + 1) * width)
                group = base_ref[1] ^ z
                first[group, wide, :] = ref[i, 0:r, here]
                second[group, wide, :] = ref[i, r : 2 * r, here]
                small[group, pl.ds(pl.multiple_of(at * m, m), m), :] = ref[i, 2 * r : 2 * r + m, here]
    parts = chan_in // width
    for z in range(nz):
        here = slice(z * width, (z + 1) * width)
        own = slice(z * chans, (z + 1) * chans)
        we = first[z]
        we_high[:, here], we_low[:, here] = split(we)
        wet_high[here], wet_low[here] = split(we.T)
        for h in range(parts):
            wp = second[z, h * width : (h + 1) * width]
            cols = slice(h * width, (h + 1) * width)
            wp_high[here, cols], wp_low[here, cols] = split(wp)
            wpt_ref[cols, here] = wp.T
        for tap in range(TAPS):
            tap_ref[tap, :, here] = jnp.broadcast_to(small[z, tap : tap + 1], (SUB, width))
        gain_ref[:, here] = small[z, TAPS : TAPS + 2]
        bias_ref[:, here] = small[z, TAPS + 2 : TAPS + 4]
        sqt_ref[:, own] = small[z, 32 : 32 + reduced, 0:chans]
        ex_ref[:, own] = small[z, 32 : 32 + reduced, chans : 2 * chans]
        exb_ref[:, own] = small[z, 32:33, 2 * chans : 3 * chans]
    sq_ref[...] = sqt_ref[...].T
    ext_ref[...] = ex_ref[...].T


def order_weights(base, slabs, orders, nz, chan_in, chans, reduced):
    hidden = slabs[0].shape[2]
    width = hidden // nz
    shapes = (
        [((chan_in, hidden), BF16)] * 2
        + [((hidden, chan_in), BF16)] * 4
        + [
            ((chan_in, hidden), F32),
            ((TAPS, SUB, hidden), F32),
            ((2, hidden), F32),
            ((2, hidden), F32),
            ((chan_in, reduced), F32),
            ((reduced, chan_in), F32),
            ((reduced, chan_in), F32),
            ((chan_in, reduced), F32),
            ((1, chan_in), F32),
        ]
    )
    return pl.pallas_call(
        partial(weights_kernel, chan_in, chans, orders),
        grid=(1,),
        in_specs=[pl.BlockSpec(memory_space=pltpu.SMEM)] + [whole(a.shape) for a in slabs],
        out_specs=[whole(shape) for shape, _ in shapes],
        out_shape=[jax.ShapeDtypeStruct(shape, kind) for shape, kind in shapes],
        scratch_shapes=[
            pltpu.VMEM((nz, chan_in, width), F32),
            pltpu.VMEM((nz, chan_in, width), F32),
            pltpu.VMEM((nz, SMALL, width), F32),
        ],
        compiler_params=params(),
        cost_estimate=cost(1),
        name="order_weights",
    )(base, *slabs)


def thirds(v):
    high = v.astype(BF16)
    rest = v - high.astype(F32)
    mid = rest.astype(BF16)
    return high, mid, (rest - mid.astype(F32)).astype(BF16)


def choose(chosen, v):
    high, mid, low = thirds(v)
    return (dot(chosen, high) + dot(chosen, mid)) + dot(chosen, low)


def choose_lanes(v, chosen):
    high, mid, low = thirds(v)
    return (dot(high, chosen) + dot(mid, chosen)) + dot(low, chosen)


def ones(condition):
    return condition.astype(F32).astype(BF16)


def lay_flat(v, start, width):
    n, m = v.shape
    place = lax.broadcasted_iota(jnp.int32, (m, width), 1) - start
    column_of = lax.broadcasted_iota(jnp.int32, (m, width), 0)
    wide = choose_lanes(v, ones((place + 64 * m) % m == column_of))
    place = lax.broadcasted_iota(jnp.int32, (n, width), 1) - start
    low = lax.broadcasted_iota(jnp.int32, (n, width), 0) * m
    return jnp.sum(jnp.where((place >= low) & (place < low + m), wide, 0.0), axis=0, keepdims=True)


def fill_blocks(out, first, middle, flip, last, squeeze, down, excite, bias):
    blocks, length = out.shape
    tiles, n, _ = first.shape
    width = tiles * 128
    per = length // width
    for i in range(per):
        for u in range(tiles):
            at = i * width + u * 128
            out[0 : n // per, at : at + 128] = first[u, pl.ds(i, n // per, stride=per), :]
    for k in range(TAPS + 4):
        row = n + k
        out[row // per : row // per + 1, row % per * width : (row % per + 1) * width] = middle[k : k + 1, :]
    base = n + TAPS + 4
    parts = last // width
    step = per // parts
    for h in range(parts):
        for e in range(step):
            row = base + parts * e + h
            block, slot = row // per, row % per
            count = width // step
            for u in range(tiles):
                at = slot * width + u * 128
                out[block : block + count, at : at + 128] = flip[
                    h * tiles + u, pl.ds(e, count, stride=step), :
                ]
    start = (base + width * parts) * width
    block = start // length
    start -= block * length
    tail_width = (blocks - block) * length
    tail = lay_flat(squeeze, start, tail_width)
    start += squeeze.shape[0] * squeeze.shape[1]
    tail = tail + lay_flat(down, start, tail_width)
    start += down.shape[1]
    tail = tail + lay_flat(excite, start, tail_width)
    start += excite.shape[0] * excite.shape[1]
    tail = tail + lay_flat(bias, start, tail_width)
    inside = lax.broadcasted_iota(jnp.int32, (1, length), 1)
    kept = jnp.where(inside < (base + width * parts) * width - block * length, out[block : block + 1, :], 0.0)
    out[block : block + 1, :] = kept + tail[:, 0:length]
    for k in range(1, blocks - block):
        out[block + k : block + k + 1, :] = tail[:, k * length : (k + 1) * length]


def prepare_kernel(
    orders,
    base_ref,
    col_ref,
    we_ref,
    dw_ref,
    gain_ref,
    bias_ref,
    wp_ref,
    sq_ref,
    down_ref,
    ex_ref,
    exb_ref,
    *rest,
):
    slabs = rest[: len(orders)]
    weight, first_ref, second_ref, head, flip, middle, moments, ranked = rest[len(orders) :]
    blocks, length = weight.shape
    chan_in, width = we_ref.shape
    devices, room = moments.shape[1:3]
    middle[0:TAPS] = dw_ref[...]
    middle[TAPS : TAPS + 2] = gain_ref[...]
    middle[TAPS + 2 : TAPS + 4] = bias_ref[...]
    for u in range(width // 128):
        head[u] = we_ref[:, u * 128 : (u + 1) * 128]
    for u in range(chan_in // 128):
        flip[u] = wp_ref[:, u * 128 : (u + 1) * 128]
    fill_blocks(
        weight, head, middle, flip, chan_in, sq_ref[...], down_ref[...], ex_ref[...], exb_ref[...]
    )
    at = 0
    home = jnp.zeros(col_ref.shape, jnp.int32)
    own_col = col_ref[...]
    for ref, order in zip(slabs, orders):
        for k, p in enumerate(order):
            for m in range(2):
                moments[m, at] = ref[k, m * room : (m + 1) * room]
            home = jnp.where(own_col == base_ref[0] ^ p, at, home)
            at += 1
    ranked[...] = jnp.broadcast_to(own_col.astype(F32), ranked.shape)
    own_row = ranked[...].T[0:1].astype(jnp.int32)
    i = lax.broadcasted_iota(jnp.int32, (blocks, blocks), 0)
    j = lax.broadcasted_iota(jnp.int32, (blocks, blocks), 1)
    earlier = (own_row == own_col) & (j < i)
    rank = jnp.sum(jnp.where(earlier, 1.0, 0.0), axis=1, keepdims=True).astype(jnp.int32)
    slot = home * room + rank
    chosen = ones(lax.broadcasted_iota(jnp.int32, (blocks, devices * room), 1) == slot)
    first_ref[...] = choose(chosen, moments[0].reshape(devices * room, length))
    second_ref[...] = choose(chosen, moments[1].reshape(devices * room, length))


def prepare(base, owners, weights, slabs, orders, length):
    blocks = owners.shape[0]
    chan_in, width = weights[0].shape
    devices = sum(len(o) for o in orders)
    arrays = [owners, *weights, *slabs]
    return pl.pallas_call(
        partial(prepare_kernel, orders),
        grid=(1,),
        in_specs=[pl.BlockSpec(memory_space=pltpu.SMEM)] + [whole(a.shape) for a in arrays],
        out_specs=[whole((blocks, length))] * 3,
        out_shape=[jax.ShapeDtypeStruct((blocks, length), F32)] * 3,
        scratch_shapes=[
            pltpu.VMEM((width // 128, chan_in, 128), F32),
            pltpu.VMEM((chan_in // 128, width, 128), F32),
            pltpu.VMEM((32, width), F32),
            pltpu.VMEM((2, devices, slabs[0].shape[1] // 2, length), F32),
            pltpu.VMEM((blocks, 128), F32),
        ],
        compiler_params=params(),
        cost_estimate=cost(5),
        name="prepare",
    )(base, *arrays)


def adam_kernel(
    bounds,
    rates,
    orders,
    chans,
    reduced,
    me_ref,
    col_ref,
    weight_ref,
    old_one_ref,
    old_two_ref,
    first_ref,
    second_ref,
    *rest,
):
    grad_slabs = rest[: len(orders)]
    first_out, second_out, new_ref, grad, head, flip, tall, small, ranked = rest[len(orders) :]
    blocks, length = grad.shape
    capacity = first_ref.shape[0]
    chan_in, width = tall.shape
    devices = sum(len(order) for order in orders)
    r, m = chan_in // devices, SMALL // devices
    for ref, order in zip(grad_slabs, orders):
        for k, i in enumerate(order):
            p = me_ref[1] ^ i
            for u in range(width // 128):
                head[u, pl.ds(pl.multiple_of(p * r, r), r), :] = ref[k, 0:r, u * 128 : (u + 1) * 128]
            small[pl.ds(pl.multiple_of(p * m, m), m), :] = ref[k, r : r + m]
            tall[pl.ds(pl.multiple_of(p * r, r), r), :] = ref[k, r + m : 2 * r + m]
    for u in range(chan_in // 128):
        flip[u] = tall[u * 128 : (u + 1) * 128].T
    fill_blocks(
        grad,
        head,
        small,
        flip,
        chan_in,
        small[32 : 32 + reduced, 0:chans].T,
        small[33:34, 2 * chans : 2 * chans + reduced],
        small[32 : 32 + reduced, chans : 2 * chans],
        small[32:33, 2 * chans : 3 * chans],
    )

    own_col = col_ref[...]
    ranked[...] = jnp.broadcast_to(own_col.astype(F32), ranked.shape)
    own_row = ranked[...].T[0:1].astype(jnp.int32)
    i = lax.broadcasted_iota(jnp.int32, (blocks, blocks), 0)
    j = lax.broadcasted_iota(jnp.int32, (blocks, blocks), 1)
    earlier = (own_row == own_col) & (i < j)
    rank = jnp.sum(jnp.where(earlier, 1.0, 0.0), axis=0, keepdims=True).astype(jnp.int32)
    g = grad[...]
    mine = lax.broadcasted_iota(jnp.int32, (capacity, blocks), 0)
    owned = choose(ones((mine == rank) & (own_row == me_ref[0])), g)
    first_out[:, 0] = beta_first * first_ref[:, 0] + (1.0 - beta_first) * owned
    second_out[:, 0] = beta_second * second_ref[:, 0] + (1.0 - beta_second) * owned * owned

    first = beta_first * old_one_ref[...] + (1.0 - beta_first) * g
    second = beta_second * old_two_ref[...] + (1.0 - beta_second) * g * g
    first_hat = first / (1.0 - beta_first**STEP)
    second_hat = second / (1.0 - beta_second**STEP)
    place = lax.broadcasted_iota(jnp.int32, (blocks, length), 0) * length + lax.broadcasted_iota(
        jnp.int32, (blocks, length), 1
    )
    rate = jnp.zeros((blocks, length), F32)
    for bound, value in zip(reversed(bounds), reversed(rates)):
        rate = jnp.where(place < bound, jnp.float32(value), rate)
    grad[...] = weight_ref[...] * (1.0 - rate * weight_decay) - rate * first_hat / (
        jnp.sqrt(second_hat) + adam_eps
    )
    for k in range(blocks):
        end = min((k + 1) * length, new_ref.shape[1])
        new_ref[:, k * length : end] = grad[k : k + 1, 0 : end - k * length]


def adam(ids, owners, prepared, first, second, grads, orders, chan_in, chans, reduced, bounds, rates):
    blocks, length = prepared[0].shape
    width = grads[0].shape[2]
    arrays = [owners, *prepared, first, second, *grads]
    new_shape = (1, bounds[-1])
    return pl.pallas_call(
        partial(adam_kernel, bounds, rates, orders, chans, reduced),
        grid=(1,),
        in_specs=[pl.BlockSpec(memory_space=pltpu.SMEM)] + [whole(a.shape) for a in arrays],
        out_specs=[whole(first.shape), whole(second.shape), whole(new_shape)],
        out_shape=[
            jax.ShapeDtypeStruct(first.shape, F32),
            jax.ShapeDtypeStruct(second.shape, F32),
            jax.ShapeDtypeStruct(new_shape, F32),
        ],
        scratch_shapes=[
            pltpu.VMEM((blocks, length), F32),
            pltpu.VMEM((width // 128, chan_in, 128), F32),
            pltpu.VMEM((chan_in // 128, width, 128), F32),
            pltpu.VMEM((chan_in, width), F32),
            pltpu.VMEM((SMALL, width), F32),
            pltpu.VMEM((blocks, 128), F32),
        ],
        compiler_params=params(),
        cost_estimate=cost(4),
        name="adam",
    )(ids, *arrays)


def deal_rows(rows):
    n_pix = lax.axis_size(PIX)
    n, hidden = rows.shape
    dealt = lax.all_to_all(rows.reshape(n_pix, n // n_pix, hidden), PIX, 0, 0, tiled=True)
    return jnp.sum(dealt, axis=0)


def together(*values):
    return lax.optimization_barrier(values)


def local(
    frames_raw,
    grad_out,
    col_offsets,
    flip_flags,
    owners,
    w_expand,
    w_dw,
    norm_gains,
    norm_biases,
    w_project,
    squeeze_matrix,
    se_down_bias,
    excite_matrix,
    excite_bias_row,
    first_moment,
    second_moment,
):
    nz, nhi, nlo = (lax.axis_size(axis) for axis in ALL)
    frames, chans, stored = frames_raw.shape
    band = stored // WIN
    area = band * FRAME_COLUMNS
    rows = nlo * band
    chan_in, hidden_dev = w_expand.shape
    hidden = hidden_dev * nz
    reduced = squeeze_matrix.shape[1]
    group = nz // MB * nhi * nlo
    count = float(frames // MB * FRAME_ROWS * FRAME_COLUMNS)
    hi = lax.axis_index("hi")
    side = jnp.stack([(hi > 0).astype(jnp.int32), (hi < nhi - 1).astype(jnp.int32)])

    n_pix = nhi * nlo
    me = hi * nlo + lax.axis_index("lo")
    relative = me if near(n_pix) else 0 * me
    z_relative = lax.axis_index("chan") if near(n_pix) else 0 * me

    slab = pack_weights(
        me.astype(jnp.int32).reshape(1),
        w_expand,
        w_dw,
        norm_gains,
        norm_biases,
        w_project,
        squeeze_matrix,
        excite_matrix,
        excite_bias_row,
    )
    crops = crop(frames_raw, col_offsets, flip_flags)
    crops, *slab = together(crops, *gather_chan(slab))
    x = deal(crops).reshape(nz, nlo, chans, area)
    slabs, orders = gather_pix(jnp.concatenate(slab, axis=1))
    (
        we_high,
        we_low,
        wet_high,
        wet_low,
        wp_high,
        wp_low,
        w_project_t,
        taps,
        gains,
        biases,
        sq_all,
        sq_t,
        ex_all,
        ex_t,
        ex_bias,
    ) = order_weights(
        jnp.stack([relative, z_relative]), slabs, orders, nz, chan_in, chans, reduced
    )
    se_weights = [sq_all, sq_t, se_down_bias[None], ex_all, ex_t, ex_bias]
    ordered = order(grad_out)
    x, ordered, we_high, we_low = together(x, ordered, we_high, we_low)

    top, low = rims(x, HALO_IN, band)

    def as_rows(v):
        return v.reshape(rows, SUB, SUB, hidden)

    def as_bands(v):
        return v.reshape(nlo, area, hidden)

    def as_sides(v, n):
        return v.reshape(2, n, SUB, SUB, hidden)

    hid, sums_one, gram = expand(x, we_high, we_low)
    hid, ordered = together(hid, ordered)
    gout = deal(ordered).reshape(nz, nlo, chans, area)
    g_top, g_low = rims(gout, HALO_OUT, band)
    sums_one = shares(sums_one, 1, group)
    spatial, spatial_halo, hid_halo, sums_two = spread(
        count, side, top, low, as_rows(hid), we_high, we_low, gains, biases, taps, sums_one
    )
    first_turned, second_turned, spatial = together(
        first_moment.transpose(1, 0, 2), second_moment.transpose(1, 0, 2), spatial
    )
    capacity = first_moment.shape[1]
    room = ((0, -capacity % SUB), (0, 0))
    moments = jnp.concatenate([jnp.pad(v[:, 0], room) for v in (first_turned, second_turned)])
    moments = lax.all_gather(moments, PIX, axis=0)
    sums_two = shares(sums_two, 1, group)
    m, s, se_part, proj = gather(
        count, as_bands(spatial), gout, gains, biases, w_project_t, wp_high, wp_low, sums_two
    )
    ses = shares(se_part, nlo, nhi)
    ses, g_top, g_low = together(ses, g_top, g_low)
    q, back_two, values, *w4 = proj_back(
        count, as_bands(spatial), gout, gains, biases, w_project_t, se_weights, ses, sums_two
    )
    backs_two = shares(back_two, 1, group)
    out, g_project = project(proj, x, values, m, s)
    backs_two, out, g_project = together(backs_two, out, g_project)
    out = deal(out.reshape(frames, chans, area))
    q1, back_one, g_dw = spread_back(
        count,
        side,
        g_top,
        g_low,
        as_rows(hid),
        hid_halo,
        spatial,
        spatial_halo,
        as_rows(q),
        w4,
        gains,
        biases,
        taps,
        sums_one,
        sums_two,
        backs_two,
    )
    backs_one = shares(back_one, 1, group)

    ids = jnp.stack([relative, hi, z_relative]).astype(jnp.int32)
    pieces = weight_grad(
        ids, n_pix if near(n_pix) else 1, as_bands(q1), x, g_dw, back_one, back_two, values, reduced
    )
    if near(n_pix):
        early = lax.psum_scatter(g_project, PIX, scatter_dimension=0, tiled=True)
        gram = lax.psum_scatter(gram, PIX, scatter_dimension=0, tiled=True)
    else:
        early, gram = deal_rows(g_project), deal_rows(gram)
    q1, out, early, gram, *pieces = together(q1, out, early, gram, *pieces)

    def input_half(half, q1):
        grad = input_grad(count, half, as_bands(q1), hid, gout, gains, wet_high, wet_low, sums_one, backs_one)
        return grad.reshape(frames, chans, area // 2)

    grad_one = input_half(0, q1)
    grad_one, q1, *pieces = together(grad_one, q1, *pieces)
    if near(n_pix):
        pieces = [pieces[0]] + [exchange(pieces[i], i) for i in range(1, n_pix)]
        moments, out, pieces[1] = together(moments, out, pieces[1])
    else:
        pieces = [jnp.concatenate([deal_rows(pieces[0][:chan_in]), deal_rows(pieces[0][chan_in:])])]
    grad_two = input_half(1, q1)
    output = restore(out)
    weights = [
        w_expand,
        w_dw,
        norm_gains,
        norm_biases,
        w_project,
        squeeze_matrix,
        se_down_bias[None],
        excite_matrix,
        excite_bias_row[None],
    ]
    block_len = first_moment.shape[2]
    natural = [list(range(n_pix))]
    base = jnp.zeros((1,), jnp.int32)
    prepared = prepare(base, owners, weights, [moments], natural, block_len)
    grad_two, output, prepared, *pieces = together(grad_two, output, prepared, *pieces)
    groups = collect(count, ids, nz, pieces, early, gram, we_high, we_low, gains, sums_one, backs_one)
    if near(n_pix):
        others = [groups[0]] + [exchange(groups[k], k * n_pix) for k in range(1, nz)]
    else:
        others = list(lax.all_to_all(jnp.stack(groups), "chan", 0, 0, tiled=True))
    grad_one = deal(grad_one)
    grad_one, grad_two, *others = together(grad_one, grad_two, *others)
    summed = sum(others[1:], others[0])
    grad_two = deal(grad_two)
    grads, _ = gather_pix(summed)
    seg_sizes, seg_rates = segments(chan_in, hidden_dev, chans, reduced, TAPS, hidden)
    bounds = [sum(seg_sizes[: i + 1]) for i in range(len(seg_sizes))]
    first_next, second_next, new_params = adam(
        jnp.stack([me, relative]).astype(jnp.int32),
        owners,
        prepared,
        first_turned,
        second_turned,
        grads,
        orders,
        chan_in,
        chans,
        reduced,
        bounds,
        seg_rates,
    )
    first_next, second_next = first_next.transpose(1, 0, 2), second_next.transpose(1, 0, 2)
    grad_frames = uncrop(grad_one, grad_two, col_offsets, flip_flags)
    return (output, grad_frames, first_next, second_next, new_params)


def solution(mesh):
    nz, n_pix = mesh.shape["chan"], mesh.shape["pix"]
    placed = (
        P(None, "chan", PIX),
        P(None, "chan", PIX),
        P(),
        P(),
        P(),
        P(None, "chan"),
        P(None, "chan"),
        P(None, "chan"),
        P(None, "chan"),
        P("chan", None),
        P("chan", None),
        P(),
        P(None, "chan"),
        P("chan"),
        P("chan", PIX, None),
        P("chan", PIX, None),
    )

    def run(*arrays):
        nlo = arrays[0].shape[0] // nz
        return jax.shard_map(
            local,
            mesh=Mesh(mesh.devices.reshape(nz, n_pix // nlo, nlo), ALL),
            in_specs=placed,
            out_specs=(
                P(None, "chan", PIX),
                P(None, "chan", PIX),
                P("chan", PIX, None),
                P("chan", PIX, None),
                P("chan", None),
            ),
            check_vma=False,
        )(*arrays)

    return run
```

time: 612 us -> 356 us (0.58); the launches traced: 603 us -> 353 us
  blocking collectives: 208 us -> 0 us
  local copies, waits for them, and re-layouts: 94.6 us -> 9.07 us
  Pallas kernels: 133 us -> 176 us
    all_gather x7 -> x0, blocking collectives: 133 us -> none  [the longest x1 60.4 us: local(): hidden_rows = lax.all_gather(hidden_rows, 'chan', axis=1, tiled=True)]
    all_to_all x3 -> x0, blocking collectives: 75.7 us -> none  [the longest x1 55.2 us: deal(): return lax.all_to_all(x, SPREAD, 0, 0, tiled=True)]
    ppermute x17 -> x36, waiting for transfers between devices: 14.2 us -> 61.7 us  [exchange(): return lax.ppermute(x, ALL, [(i, i ^ stride) for i in range(n)])]
    unnamed x142 -> x97, local copies, waits for them, and re-layouts: 51.8 us -> 9.07 us
    all_to_all x3 -> x5, waiting for transfers between devices: 42.3 us -> 11.7 us  [deal(): return lax.all_to_all(x, SPREAD, 0, 0, tiled=True)]
    pallas_call x4 -> x10, Pallas kernels: 27.2 us -> 54.6 us  [the longest x2 13.9 us: input_grad(): pl.pallas_call(partial(input_kernel, len(sums), count, half), grid=(bands...]
    all_to_all x3 -> x5, starting transfers between devices: 16.6 us -> 40.1 us  [deal(): return lax.all_to_all(x, SPREAD, 0, 0, tiled=True)]
    all_to_all x4 -> x0, starting transfers between devices: 22.9 us -> none  [the longest x2 13.8 us: sum_to_group(): lax.all_to_all(rows.reshape(n_pix, n // n_pix, hidden), PIX, 0, 0, tiled=...]
  transfers between devices with their start and end apart: 30 -> 46, of which waited for: 10 -> 20; matrix products, arithmetic and copies ran while one was open for 9% -> 2% of each run, Pallas kernels for 11% -> 45%
where the time goes in v2:
time: 356 us; the launch traced here: 353 us
  Pallas kernels  176 us (49%)
  starting transfers between devices  73.7 us (21%)
  waiting for transfers between devices  73.5 us (21%)
  between operations  14.3 us (4%)
  local copies, waits for them, and re-layouts  9.07 us (3%)
  other arithmetic  6.54 us (2%)
    ppermute x36, waiting for transfers between devices, exchange(): return lax.ppermute(x, ALL, [(i, i ^ stride) for i in range(n)])  61.7 us
    pallas_call x1, Pallas kernels, spread_back(): pl.pallas_call(partial(spread_back_kernel, len(backs), count), grid=(hidd...  49.6 us
    all_to_all x5, starting transfers between devices, deal(): return lax.all_to_all(x, SPREAD, 0, 0, tiled=True)  40.1 us
    ppermute x36, starting transfers between devices, exchange(): return lax.ppermute(x, ALL, [(i, i ^ stride) for i in range(n)])  32.9 us
    pallas_call x1, Pallas kernels, spread(): pl.pallas_call(partial(spread_kernel, len(sums), count), grid=(hidden //...  27.2 us
    pallas_call x2, Pallas kernels, input_grad(): pl.pallas_call(partial(input_kernel, len(sums), count, half), grid=(bands...  13.9 us
    pallas_call x1, Pallas kernels, proj_back(): pl.pallas_call(partial(proj_back_kernel, len(ses), len(sums), count), gri...  12.6 us
    pallas_call x1, Pallas kernels, gather(): pl.pallas_call(partial(gather_kernel, len(sums), count), grid=(bands,), i...  11.8 us
  transfers between devices with their start and end apart: 46, of which 20 were waited for; matrix products, arithmetic and copies ran while one was open for 2% of the time, Pallas kernels for 45%

profile of v2, /device:TPU:15, one launch (start us, length us, event | category | flops | bytes accessed | tf_op | source)
XLA Modules:
  0.0 353.1 jit_solution(139432937181172820)
XLA Ops:
  7.2 1.4 copy.26.sq_ref
  8.6 1.8 pack_weights.1
  10.5 2.3 collective-permute-start.1
  13.0 5.2 %crop.1 = f32[16,64,512]{2,1,0:T(8,128)} custom-call(s32[4]{0:T(128)} %left_ref.3, s32[4]{0:T(128)} %flip_ref.3, f32[16,64,640]{2,1,0:T(8,128)} %raw_ref.1), custom_call_target="tpu_custom_call" | custom-call | flops 5500000256 | bytes 17500000 | tf_op jit(solution)/shard_map/crop/pallas_call | solution.py:182
  18.8 7.8 %all-to-all-start = ((f32[16,64,512]{2,1,0:T(8,128)}), f32[16,64,512]{2,1,0:T(8,128)S(1)}, u32[]{:S(2)}, u32[]{:S(2)}) async-start(f32[16,64,512]{2,1,0:T(8,128)} %crop.1), calls=%async_computation | async-start | bytes 4194304 | tf_op jit(solution)/shard_map/all_to_all | solution.py:108
  27.0 18.4 %collective-permute-done.3 = f32[1,72,1024]{2,1,0:T(8,128)S(1)} collective-permute-done((f32[1,72,1024]{2,1,0:T(8,128)S(1)}, f32[1,72,1024]{2,1,0:T(8,128)S(1)}, u32[]{:S(2)}, u32[]{:S(2)}) %collective-permute-start.3) | collective-permute-done | bytes 294944 | tf_op jit(solution)/shard_map/ppermute | solution.py:91
  45.8 13.7 %collective-permute-done.4 = f32[2,72,1024]{2,1,0:T(8,128)S(1)} collective-permute-done((f32[2,72,1024]{2,1,0:T(8,128)S(1)}, f32[2,72,1024]{2,1,0:T(8,128)S(1)}, u32[]{:S(2)}, u32[]{:S(2)}) %collective-permute-start.4) | collective-permute-done | bytes 589856 | tf_op jit(solution)/shard_map/ppermute | solution.py:91
  59.6 1.9 collective-permute-start.5
  61.5 4.7 %order.1 = f32[16,64,512]{2,1,0:T(8,128)} custom-call(f32[16,64,512]{2,1,0:T(8,128)} %x_ref.1), custom_call_target="tpu_custom_call" | custom-call | flops 1100000000 | bytes 3500000 | tf_op jit(solution)/shard_map/order/pallas_call | solution.py:207
  66.9 4.6 %order_weights.1 = (bf16[256,1024]{1,0:T(8,128)(2,1)}, bf16[256,1024]{1,0:T(8,128)(2,1)}, bf16[1024,256]{1,0:T(8,128)(2,1)}, bf16[1024,256]{1,0:T(8,128)(2,1)}, ...) custom-call(s32[2]{0:T(128)} %pad_add_fusion.base_ref, ...), custom_call_target="tpu_custom_call" | custom-call | flops 1100000000 | bytes 3500000 | tf_op jit(solution)/shard_map/order_weights/pallas_call | solution.py:1142
  71.5 2.6 all-to-all-done
  74.1 1.3 copy-done.1
  75.4 8.2 %expand.1 = (f32[4,512,1024]{2,1,0:T(8,128)}, f32[2,1024]{1,0:T(2,128)}, f32[256,384]{1,0:T(8,128)}) custom-call(f32[4,4,64,512]{3,2,1,0:T(8,128)} %bitcast.42, bf16[256,1024]{1,0:T(8,128)(2,1)} %get-tuple-element.136.high_ref, bf16[256,1024]{1,0:T(8,128)(2,1)} %get-tuple-element.137.low_ref.lower_ref), custom_call_target="tpu_custom_call" | custom-call | flops 8800000000 | bytes 28000000 | tf_op jit(solution)/shard_map/expand/pallas_call | solution.py:304
  83.6 9.1 %all-to-all-start.1 = ((f32[16,64,512]{2,1,0:T(8,128)}), f32[16,64,512]{2,1,0:T(8,128)S(1)}, u32[]{:S(2)}, u32[]{:S(2)}) async-start(f32[16,64,512]{2,1,0:T(8,128)} %order.1), calls=%async_computation.1 | async-start | bytes 4194304 | tf_op jit(solution)/shard_map/all_to_all | solution.py:108
  92.8 1.1 slice_select_fusion
  94.8 0.8 collective-permute-done.7
  96.0 1.3 collective-permute-start.9
  97.3 1.1 collective-permute-start.10
  99.0 3.7 %collective-permute-done.8.rest_1_.rest_9_ = f32[2,1024]{1,0:T(2,128)S(1)} collective-permute-done((f32[2,1024]{1,0:T(2,128)S(1)}, f32[2,1024]{1,0:T(2,128)S(1)}, u32[]{:S(2)}, u32[]{:S(2)}) %collective-permute-start.8) | collective-permute-done | bytes 8224 | tf_op jit(solution)/shard_map/ppermute | solution.py:91
  103.4 27.2 %spread.1 = (f32[32,8,8,1024]{3,2,1,0:T(8,128)}, f32[2,2,8,8,1024]{4,3,2,1,0:T(8,128)}, f32[2,2,8,8,1024]{4,3,2,1,0:T(8,128)}, f32[2,1024]{1,0:T(2,128)}) custom-call(s32[2]{0:T(128)} %add_convert_fusion.side_ref, f32[4,1,64,256]{3,2,1,0:T(8,128)} %copy-done.24, f32[4,1,64,256]{3,2,1,0:T(8,128)} %copy-done.24, f32[32,8,8,1024]{3,2,1,0:T(8,128)} %bitcast.31, ...), custom_call_target="tpu_custom_call" | custom-call | flops 27499999232 | bytes 87500000 | tf_op jit(solution)/shard_map/spread/pallas_call | solution.py:448
  130.6 0.9 collective-permute-start.11
  131.6 1.0 collective-permute-done.11
  133.3 1.2 collective-permute-start.12
  134.5 1.2 collective-permute-start.13
  136.0 4.5 %all-to-all-done.1 = f32[16,64,512]{2,1,0:T(8,128)S(1)} async-done(((f32[16,64,512]{2,1,0:T(8,128)}), f32[16,64,512]{2,1,0:T(8,128)S(1)}, u32[]{:S(2)}, u32[]{:S(2)}) %all-to-all-start.1) | async-done | bytes 2097184 | tf_op jit(solution)/shard_map/all_to_all | solution.py:108
  140.7 1.1 copy-done
  141.8 11.8 %gather.1 = (f32[256,1024]{1,0:T(8,128)}, f32[1,1024]{1,0:T(1,128)}, f32[2,256]{1,0:T(2,128)}, f32[4,512,256]{2,1,0:T(8,128)}) custom-call(f32[4,512,1024]{2,1,0:T(8,128)} %bitcast.56, f32[4,4,64,512]{3,2,1,0:T(8,128)} %bitcast.37, f32[2,1024]{1,0:T(2,128)} %get-tuple-element.141.gain_ref, f32[2,1024]{1,0:T(2,128)} %get-tuple-element.142.bias_ref, ...), custom_call_target="tpu_custom_call" | custom-call | flops 14300000256 | bytes 45500000 | tf_op jit(solution)/shard_map/gather/pallas_call | solution.py:519
  153.6 0.9 collective-permute-start.15
  154.7 1.6 collective-permute-done.15.rest_1_
  156.9 12.6 %proj_back.1 = (f32[4,512,1024]{2,1,0:T(8,128)}, f32[2,1024]{1,0:T(2,128)}, f32[8,256]{1,0:T(8,128)}, bf16[256,1024]{1,0:T(8,128)(2,1)}, bf16[256,1024]{1,0:T(8,128)(2,1)}, /*index=5*/f32[1,1024]{1,0:T(1,128)}) custom-call(f32[4,512,1024]{2,1,0:T(8,128)} %bitcast.57, f32[4,4,64,512]{3,2,1,0:T(8,128)} %bitcast.38, f32[2,1024]{1,0:T(2,128)} %get-tuple-element.141.gain_ref, ...), custom_call_target="tpu_custom_call" | custom-call | flops 13200000000 | bytes 42000000 | tf_op jit(solution)/shard_map/proj_back/pallas_call | solution.py:632
  169.5 1.2 collective-permute-start.17
  170.6 1.0 collective-permute-done.17
  172.6 1.0 collective-permute-start.19
  173.6 1.5 collective-permute-start.20
  175.0 5.6 %project.1 = (f32[4,4,64,512]{3,2,1,0:T(8,128)}, f32[256,1024]{1,0:T(8,128)}) custom-call(f32[4,512,256]{2,1,0:T(8,128)} %get-tuple-element.169.proj_ref, f32[4,4,64,512]{3,2,1,0:T(8,128)} %bitcast.44, f32[8,256]{1,0:T(8,128)} %get-tuple-element.170.val_ref, f32[256,1024]{1,0:T(8,128)} %get-tuple-element.171.m_ref, f32[1,1024]{1,0:T(1,128)} %get-tuple-element.172.s_ref), custom_call_target="tpu_custom_call" | custom-call | flops 4400000000 | bytes 14000000 | tf_op jit(solution)/shard_map/project/pallas_call | solution.py:676
  181.7 10.1 %all-to-all-start.2 = ((f32[16,64,512]{2,1,0:T(8,128)}), f32[16,64,512]{2,1,0:T(8,128)S(1)}, u32[]{:S(2)}, u32[]{:S(2)}) async-start(f32[16,64,512]{2,1,0:T(8,128)} %bitcast.46), calls=%async_computation.2 | async-start | bytes 4194304 | tf_op jit(solution)/shard_map/all_to_all | solution.py:108
  191.8 49.6 %spread_back.1 = (f32[32,8,8,1024]{3,2,1,0:T(8,128)}, f32[2,1024]{1,0:T(2,128)}, f32[25,1024]{1,0:T(8,128)}) custom-call(s32[2]{0:T(128)} %add_convert_fusion.side_ref, f32[4,1,64,128]{3,2,1,0:T(8,128)} %copy-done.39, f32[4,1,64,128]{3,2,1,0:T(8,128)} %copy-done.39, f32[32,8,8,1024]{3,2,1,0:T(8,128)} %bitcast.32, ...), custom_call_target="tpu_custom_call" | custom-call | flops 51699998720 | bytes 164500000 | tf_op jit(solution)/shard_map/spread_back/pallas_call | solution.py:809
  244.1 2.1 collective-permute-start.24
  246.2 8.1 %weight_grad.1 = (f32[40,1024]{1,0:T(8,128)}, f32[40,1024]{1,0:T(8,128)}, f32[40,1024]{1,0:T(8,128)}, f32[40,1024]{1,0:T(8,128)}, f32[40,1024]{1,0:T(8,128)}, /*...) custom-call(s32[3]{0:T(128)} %pad_add_fusion.1.ids_ref, f32[4,512,1024]{2,1,0:T(8,128)} %bitcast.33, ...), custom_call_target="tpu_custom_call" | custom-call | flops 7699999744 | bytes 24500000 | tf_op jit(solution)/shard_map/weight_grad/pallas_call | solution.py:928
  255.2 7.1 %input_grad.2 = f32[4,4,64,256]{3,2,1,0:T(8,128)} custom-call(f32[4,512,1024]{2,1,0:T(8,128)} %bitcast.34, f32[4,512,1024]{2,1,0:T(8,128)} %get-tuple-element.140.hid_ref, f32[4,4,64,512]{3,2,1,0:T(8,128)} %bitcast.39, f32[2,1024]{1,0:T(2,128)} %get-tuple-element.141.gain_ref, bf16[1024,256]{1,0:T(8,128)(2,1)} %get-tuple-element.194.w_high, ...), custom_call_target="tpu_custom_call" | custom-call | flops 5500000256 | bytes 17500000 | tf_op jit(solution)/shard_map/input_grad/pallas_call | solution.py:857
  262.3 7.1 %all-to-all-start.3 = ((f32[16,64,256]{2,1,0:T(8,128)}), f32[16,64,256]{2,1,0:T(8,128)S(1)}, u32[]{:S(2)}, u32[]{:S(2)}) async-start(f32[16,64,256]{2,1,0:T(8,128)} %bitcast.41), calls=%async_computation.5 | async-start | bytes 2097152 | tf_op jit(solution)/shard_map/all_to_all | solution.py:108
  269.4 0.7 copy.27.col_ref
  270.8 1.5 collective-permute-start.27
  272.6 1.5 collective-permute-start.29
  274.1 6.8 %input_grad.3 = f32[4,4,64,256]{3,2,1,0:T(8,128)} custom-call(f32[4,512,1024]{2,1,0:T(8,128)} %bitcast.35, f32[4,512,1024]{2,1,0:T(8,128)} %get-tuple-element.140.hid_ref, f32[4,4,64,512]{3,2,1,0:T(8,128)} %bitcast.40, f32[2,1024]{1,0:T(2,128)} %get-tuple-element.141.gain_ref, bf16[1024,256]{1,0:T(8,128)(2,1)} %get-tuple-element.194.w_high, ...), custom_call_target="tpu_custom_call" | custom-call | flops 5500000256 | bytes 17500000 | tf_op jit(solution)/shard_map/input_grad/pallas_call | solution.py:857
  281.2 4.9 %restore.1 = f32[16,64,512]{2,1,0:T(8,128)} custom-call(f32[16,64,512]{2,1,0:T(8,128)} %copy-done.2), custom_call_target="tpu_custom_call" | custom-call | flops 5500000256 | bytes 17500000 | tf_op jit(solution)/shard_map/restore/pallas_call | solution.py:228
  286.1 2.6 collective-permute-start.31
  288.6 4.6 %prepare.1 = (f32[138,1024]{1,0:T(8,128)}, f32[138,1024]{1,0:T(8,128)}, f32[138,1024]{1,0:T(8,128)}) custom-call(s32[1]{0:T(128)} %constant.21.clone.1.base_ref, s32[138,1]{1,0:T(8,128)} %copy.27.col_ref, f32[256,256]{1,0:T(8,128)} %we_ref.3, f32[25,256]{1,0:T(8,128)} %dw_ref.3, f32[2,256]{1,0:T(2,128)} %gain_ref.3, f32[2,256]{1,0:T(2,128)} %bias_ref.3, ...), custom_call_target="tpu_custom_call" | custom-call | flops 5500000256 | bytes 17500000 | tf_op jit(solution)/shard_map/prepare/pallas_call | solution.py:1289
  293.3 2.8 collective-permute-done.31.rest_7_
  296.7 2.8 collect.1
  299.8 2.2 collective-permute-start.33
  302.3 1.2 collective-permute-done.32
  303.5 2.5 collective-permute-done.33
  306.0 3.4 collective-permute-done.34
  309.4 5.9 %all-to-all-start.4 = ((f32[16,64,256]{2,1,0:T(8,128)}), f32[16,64,256]{2,1,0:T(8,128)S(1)}, u32[]{:S(2)}, u32[]{:S(2)}) async-start(f32[16,64,256]{2,1,0:T(8,128)} %bitcast.20), calls=%async_computation.6 | async-start | bytes 2097152 | tf_op jit(solution)/shard_map/all_to_all | solution.py:108
  315.7 6.7 %collective-permute-done.35 = f32[1,72,256]{2,1,0:T(8,128)S(1)} collective-permute-done((f32[1,72,256]{2,1,0:T(8,128)S(1)}, f32[1,72,256]{2,1,0:T(8,128)S(1)}, u32[]{:S(2)}, u32[]{:S(2)}) %collective-permute-start.35) | collective-permute-done | bytes 73760 | tf_op jit(solution)/shard_map/ppermute | solution.py:91
  322.4 1.3 collective-permute-start.36
  323.7 3.1 collective-permute-done.36
  326.9 2.0 collective-permute-start.37
  330.0 0.7 copy-done.23
  330.8 4.9 %adam.1 = (f32[26,1,1024]{2,1,0:T(1,128)}, f32[26,1,1024]{2,1,0:T(1,128)}, f32[1,140624]{1,0:T(1,128)}) custom-call(s32[2]{0:T(128)} %pad_add_fusion.2.me_ref, s32[138,1]{1,0:T(8,128)} %copy.27.col_ref, f32[138,1024]{1,0:T(8,128)} %get-tuple-element.241.weight_ref, f32[138,1024]{1,0:T(8,128)} %get-tuple-element.242.old_one_ref, ...), custom_call_target="tpu_custom_call" | custom-call | flops 4400000000 | bytes 14000000 | tf_op jit(solution)/shard_map/adam/pallas_call | solution.py:1387
  335.7 4.5 %all-to-all-done.4.y_ref = f32[16,64,256]{2,1,0:T(8,128)S(1)} async-done(((f32[16,64,256]{2,1,0:T(8,128)}), f32[16,64,256]{2,1,0:T(8,128)S(1)}, u32[]{:S(2)}, u32[]{:S(2)}) %all-to-all-start.4) | async-done | bytes 1048608 | tf_op jit(solution)/shard_map/all_to_all | solution.py:108
  340.2 1.0 copy-done.5
  341.2 5.4 %uncrop.1 = f32[16,64,640]{2,1,0:T(8,128)} custom-call(s32[4]{0:T(128)} %left_ref.3, s32[4]{0:T(128)} %flip_ref.3, f32[16,64,256]{2,1,0:T(8,128)} %copy-done.4, f32[16,64,256]{2,1,0:T(8,128)} %copy-done.5), custom_call_target="tpu_custom_call" | custom-call | flops 5500000256 | bytes 17500000 | tf_op jit(solution)/shard_map/uncrop/pallas_call | solution.py:256
  (163 shorter events, 16.1 us)
Async XLA Ops:
  10.3 7.9 %collective-permute-start = (f32[72,256]{1,0:T(8,128)}, f32[72,256]{1,0:T(8,128)S(1)}, u32[]{:S(2)}, u32[]{:S(2)}) collective-permute-start(f32[72,256]{1,0:T(8,128)} %pack_weights.1), channel_id=1, source_target_pairs={{0,8},{1,9},{2,10},{3,11},{4,12},{5,13},{6,14},{7,15},{8,0},{9,1},... | collective-permute-start | bytes 221192 | tf_op jit(solution)/shard_map/ppermute | solution.py:91
  10.5 7.7 %collective-permute-start.1 = (f32[72,256]{1,0:T(8,128)}, f32[72,256]{1,0:T(8,128)S(1)}, u32[]{:S(2)}, u32[]{:S(2)}) collective-permute-start(f32[72,256]{1,0:T(8,128)} %pack_weights.1), channel_id=1, source_target_pairs={{0,16},{1,17},{2,18},{3,19},{4,20},{5,21},{6,22},{7,23},{8,24},{9,... | collective-permute-start | bytes 221192 | tf_op jit(solution)/shard_map/ppermute | solution.py:91
  12.8 6.0 %collective-permute-start.2 = (f32[72,256]{1,0:T(8,128)}, f32[72,256]{1,0:T(8,128)S(1)}, u32[]{:S(2)}, u32[]{:S(2)}) collective-permute-start(f32[72,256]{1,0:T(8,128)} %pack_weights.1), channel_id=1, source_target_pairs={{0,24},{1,25},{2,26},{3,27},{4,28},{5,29},{6,30},{7,31},{8,16},{9,... | collective-permute-start | bytes 221192 | tf_op jit(solution)/shard_map/ppermute | solution.py:91
  18.2 8.5 %copy-start.11 = (f32[72,256]{1,0:T(8,128)S(1)}, f32[72,256]{1,0:T(8,128)}, u32[]{:S(2)}) copy-start(f32[72,256]{1,0:T(8,128)} %pack_weights.1) | copy-start | bytes 221188
  18.8 55.3 %all-to-all-start = ((f32[16,64,512]{2,1,0:T(8,128)}), f32[16,64,512]{2,1,0:T(8,128)S(1)}, u32[]{:S(2)}, u32[]{:S(2)}) async-start(f32[16,64,512]{2,1,0:T(8,128)} %crop.1), calls=%async_computation | async-start | bytes 4194304 | tf_op jit(solution)/shard_map/all_to_all | solution.py:108
  26.7 18.8 %collective-permute-start.3 = (f32[1,72,1024]{2,1,0:T(8,128)S(1)}, f32[1,72,1024]{2,1,0:T(8,128)S(1)}, u32[]{:S(2)}, u32[]{:S(2)}) collective-permute-start(f32[1,72,1024]{2,1,0:T(8,128)S(1)} %maximum_bitcast_fusion), channel_id=1, source_target_pairs={{0,2},{1,3},{2,0},{3,1},{4,6},{5,7},{6,4},{7,5},{8,10},{9,11},{10,... | collective-permute-start | bytes 884744 | tf_op jit(solution)/shard_map/ppermute | solution.py:91
  45.5 13.9 %collective-permute-start.4 = (f32[2,72,1024]{2,1,0:T(8,128)S(1)}, f32[2,72,1024]{2,1,0:T(8,128)S(1)}, u32[]{:S(2)}, u32[]{:S(2)}) collective-permute-start(f32[2,72,1024]{2,1,0:T(8,128)S(1)} %pad_maximum_fusion.1), channel_id=1, source_target_pairs={{0,4},{1,5},{2,6},{3,7},{4,0},{5,1},{6,2},{7,3},{8,12},{9,13},{10,... | collective-permute-start | bytes 1769480 | tf_op jit(solution)/shard_map/ppermute | solution.py:91
  59.6 7.3 %collective-permute-start.5 = (f32[4,72,1024]{2,1,0:T(8,128)S(1)}, f32[4,72,1024]{2,1,0:T(8,128)}, u32[]{:S(2)}, u32[]{:S(2)}) collective-permute-start(f32[4,72,1024]{2,1,0:T(8,128)S(1)} %pad_maximum_fusion.refs_0_), channel_id=1, source_target_pairs={{0,1},{1,0},{2,3},{3,2},{4,5},{5,4},{6,7},{7,6},{8,9},{9,8},{10,11... | collective-permute-start | bytes 3538952 | tf_op jit(solution)/shard_map/ppermute | solution.py:91
  83.6 10.6 %copy-start.21 = (f32[2,1024]{1,0:T(2,128)S(1)}, f32[2,1024]{1,0:T(2,128)}, u32[]{:S(2)}) copy-start(f32[2,1024]{1,0:T(2,128)} %get-tuple-element.144) | copy-start | bytes 24580
  83.6 56.9 %all-to-all-start.1 = ((f32[16,64,512]{2,1,0:T(8,128)}), f32[16,64,512]{2,1,0:T(8,128)S(1)}, u32[]{:S(2)}, u32[]{:S(2)}) async-start(f32[16,64,512]{2,1,0:T(8,128)} %order.1), calls=%async_computation.1 | async-start | bytes 4194304 | tf_op jit(solution)/shard_map/all_to_all | solution.py:108
  92.8 161.6 %reduce-scatter.5.cloned.1.call-start = ((), (), s32[]{:S(2)}) async-start(), calls=%async_computation.8 | async-start | bytes 442368 | tf_op jit(solution)/shard_map/reduce_scatter | solution.py:1561
  93.9 8.8 %collective-permute-start.6 = (f32[4,1,64,256]{3,2,1,0:T(8,128)S(1)}, f32[4,1,64,256]{3,2,1,0:T(8,128)S(1)}, u32[]{:S(2)}, u32[]{:S(2)}) collective-permute-start(f32[4,1,64,256]{3,2,1,0:T(8,128)S(1)} %slice_select_fusion), channel_id=1, source_target_pairs={{0,4},{4,0},{1,5},{5,1},{2,6},{6,2},{3,7},{7,3},{8,12},{12,8},{9,1... | collective-permute-start | bytes 786440 | tf_op jit(solution)/shard_map/ppermute | solution.py:123
  94.2 1.5 collective-permute-start.7
  95.7 7.1 %copy-start.9 = (f32[2,1024]{1,0:T(2,128)}, f32[2,1024]{1,0:T(2,128)S(1)}, u32[]{:S(2)}) copy-start(f32[2,1024]{1,0:T(2,128)S(1)} %add.33.rest_0_.rest_8_) | copy-start | bytes 24580
  95.7 7.0 %collective-permute-start.8 = (f32[2,1024]{1,0:T(2,128)S(1)}, f32[2,1024]{1,0:T(2,128)S(1)}, u32[]{:S(2)}, u32[]{:S(2)}) collective-permute-start(f32[2,1024]{1,0:T(2,128)S(1)} %add.33.rest_0_.rest_8_), channel_id=1, source_target_pairs={{0,2},{1,3},{2,0},{3,1},{4,6},{5,7},{6,4},{7,5},{8,10},{9,11},{10,... | collective-permute-start | bytes 24584 | tf_op jit(solution)/shard_map/ppermute | solution.py:91
  96.0 6.6 %collective-permute-start.9 = (f32[2,1024]{1,0:T(2,128)S(1)}, f32[2,1024]{1,0:T(2,128)S(1)}, u32[]{:S(2)}, u32[]{:S(2)}) collective-permute-start(f32[2,1024]{1,0:T(2,128)S(1)} %add.33.rest_0_.rest_8_), channel_id=1, source_target_pairs={{0,4},{1,5},{2,6},{3,7},{4,0},{5,1},{6,2},{7,3},{8,12},{9,13},{10,... | collective-permute-start | bytes 24584 | tf_op jit(solution)/shard_map/ppermute | solution.py:91
  97.3 5.5 %collective-permute-start.10 = (f32[2,1024]{1,0:T(2,128)S(1)}, f32[2,1024]{1,0:T(2,128)S(1)}, u32[]{:S(2)}, u32[]{:S(2)}) collective-permute-start(f32[2,1024]{1,0:T(2,128)S(1)} %add.33.rest_0_.rest_8_), channel_id=1, source_target_pairs={{0,6},{1,7},{2,4},{3,5},{4,2},{5,3},{6,0},{7,1},{8,14},{9,15},{10,... | collective-permute-start | bytes 24584 | tf_op jit(solution)/shard_map/ppermute | solution.py:91
  130.6 2.0 collective-permute-start.11
  133.3 7.4 %copy-start.19 = (f32[2,1024]{1,0:T(2,128)}, f32[2,1024]{1,0:T(2,128)S(1)}, u32[]{:S(2)}) copy-start(f32[2,1024]{1,0:T(2,128)S(1)} %add.34.rest_0_.rest_2_.rest_4_) | copy-start | bytes 24580
  133.3 7.3 %collective-permute-start.12 = (f32[2,1024]{1,0:T(2,128)S(1)}, f32[2,1024]{1,0:T(2,128)S(1)}, u32[]{:S(2)}, u32[]{:S(2)}) collective-permute-start(f32[2,1024]{1,0:T(2,128)S(1)} %add.34.rest_0_.rest_2_.rest_4_), channel_id=1, source_target_pairs={{0,2},{1,3},{2,0},{3,1},{4,6},{5,7},{6,4},{7,5},{8,10},{9,11},{10,... | collective-permute-start | bytes 24584 | tf_op jit(solution)/shard_map/ppermute | solution.py:91
  134.5 6.1 %collective-permute-start.13 = (f32[2,1024]{1,0:T(2,128)S(1)}, f32[2,1024]{1,0:T(2,128)S(1)}, u32[]{:S(2)}, u32[]{:S(2)}) collective-permute-start(f32[2,1024]{1,0:T(2,128)S(1)} %add.34.rest_0_.rest_2_.rest_4_), channel_id=1, source_target_pairs={{0,4},{1,5},{2,6},{3,7},{4,0},{5,1},{6,2},{7,3},{8,12},{9,13},{10,... | collective-permute-start | bytes 24584 | tf_op jit(solution)/shard_map/ppermute | solution.py:91
  135.7 5.0 %collective-permute-start.14 = (f32[2,1024]{1,0:T(2,128)S(1)}, f32[2,1024]{1,0:T(2,128)S(1)}, u32[]{:S(2)}, u32[]{:S(2)}) collective-permute-start(f32[2,1024]{1,0:T(2,128)S(1)} %add.34.rest_0_.rest_2_.rest_4_), channel_id=1, source_target_pairs={{0,6},{1,7},{2,4},{3,5},{4,2},{5,3},{6,0},{7,1},{8,14},{9,15},{10,... | collective-permute-start | bytes 24584 | tf_op jit(solution)/shard_map/ppermute | solution.py:91
  140.5 15.8 %collective-permute-start.16 = (f32[4,1,64,128]{3,2,1,0:T(8,128)S(1)}, f32[4,1,64,128]{3,2,1,0:T(8,128)S(1)}, u32[]{:S(2)}, u32[]{:S(2)}) collective-permute-start(f32[4,1,64,128]{3,2,1,0:T(8,128)S(1)} %slice_select_fusion.1), channel_id=1, source_target_pairs={{0,4},{4,0},{1,5},{5,1},{2,6},{6,2},{3,7},{7,3},{8,12},{12,8},{9,1... | collective-permute-start | bytes 393224 | tf_op jit(solution)/shard_map/ppermute | solution.py:123
  153.6 2.7 collective-permute-start.15
  154.5 99.9 %reduce-scatter.3.cloned.1.call-start = ((), (), s32[]{:S(2)}) async-start(), calls=%async_computation.7 | async-start | bytes 1179648 | tf_op jit(solution)/shard_map/reduce_scatter | solution.py:1560
  156.3 13.2 %copy-start.39 = (f32[4,1,64,128]{3,2,1,0:T(8,128)}, f32[4,1,64,128]{3,2,1,0:T(8,128)S(1)}, u32[]{:S(2)}) copy-start(f32[4,1,64,128]{3,2,1,0:T(8,128)S(1)} %collective-permute-done.16.top_ref.low_ref) | copy-start | bytes 393220
  169.5 2.2 collective-permute-start.17
  172.4 8.3 %copy-start.20 = (f32[2,1024]{1,0:T(2,128)}, f32[2,1024]{1,0:T(2,128)S(1)}, u32[]{:S(2)}) copy-start(f32[2,1024]{1,0:T(2,128)S(1)} %add.35.rest_8_) | copy-start | bytes 24580
  172.4 8.3 %collective-permute-start.18 = (f32[2,1024]{1,0:T(2,128)S(1)}, f32[2,1024]{1,0:T(2,128)S(1)}, u32[]{:S(2)}, u32[]{:S(2)}) collective-permute-start(f32[2,1024]{1,0:T(2,128)S(1)} %add.35.rest_8_), channel_id=1, source_target_pairs={{0,2},{1,3},{2,0},{3,1},{4,6},{5,7},{6,4},{7,5},{8,10},{9,11},{10,... | collective-permute-start | bytes 24584 | tf_op jit(solution)/shard_map/ppermute | solution.py:91
  172.6 8.1 %collective-permute-start.19 = (f32[2,1024]{1,0:T(2,128)S(1)}, f32[2,1024]{1,0:T(2,128)S(1)}, u32[]{:S(2)}, u32[]{:S(2)}) collective-permute-start(f32[2,1024]{1,0:T(2,128)S(1)} %add.35.rest_8_), channel_id=1, source_target_pairs={{0,4},{1,5},{2,6},{3,7},{4,0},{5,1},{6,2},{7,3},{8,12},{9,13},{10,... | collective-permute-start | bytes 24584 | tf_op jit(solution)/shard_map/ppermute | solution.py:91
  173.6 7.1 %collective-permute-start.20 = (f32[2,1024]{1,0:T(2,128)S(1)}, f32[2,1024]{1,0:T(2,128)S(1)}, u32[]{:S(2)}, u32[]{:S(2)}) collective-permute-start(f32[2,1024]{1,0:T(2,128)S(1)} %add.35.rest_8_), channel_id=1, source_target_pairs={{0,6},{1,7},{2,4},{3,5},{4,2},{5,3},{6,0},{7,1},{8,14},{9,15},{10,... | collective-permute-start | bytes 24584 | tf_op jit(solution)/shard_map/ppermute | solution.py:91
  180.8 100.4 %all-gather.3.cloned.1.call-start = ((), (), s32[]{:S(2)}) async-start(), calls=%async_computation.9 | async-start | bytes 2359296 | tf_op jit(solution)/shard_map/all_gather | solution.py:1521
  181.7 72.8 %all-to-all-start.2 = ((f32[16,64,512]{2,1,0:T(8,128)}), f32[16,64,512]{2,1,0:T(8,128)S(1)}, u32[]{:S(2)}, u32[]{:S(2)}) async-start(f32[16,64,512]{2,1,0:T(8,128)} %bitcast.46), calls=%async_computation.2 | async-start | bytes 4194304 | tf_op jit(solution)/shard_map/all_to_all | solution.py:108
  241.4 1.5 collective-permute-start.21
  243.6 10.8 %copy-start.10 = (f32[2,1024]{1,0:T(2,128)}, f32[2,1024]{1,0:T(2,128)S(1)}, u32[]{:S(2)}) copy-start(f32[2,1024]{1,0:T(2,128)S(1)} %add.36.rest_4_.rest_12_) | copy-start | bytes 24580
  243.6 10.9 %collective-permute-start.22 = (f32[2,1024]{1,0:T(2,128)S(1)}, f32[2,1024]{1,0:T(2,128)S(1)}, u32[]{:S(2)}, u32[]{:S(2)}) collective-permute-start(f32[2,1024]{1,0:T(2,128)S(1)} %add.36.rest_4_.rest_12_), channel_id=1, source_target_pairs={{0,2},{1,3},{2,0},{3,1},{4,6},{5,7},{6,4},{7,5},{8,10},{9,11},{10,... | collective-permute-start | bytes 24584 | tf_op jit(solution)/shard_map/ppermute | solution.py:91
  243.9 10.6 %collective-permute-start.23 = (f32[2,1024]{1,0:T(2,128)S(1)}, f32[2,1024]{1,0:T(2,128)S(1)}, u32[]{:S(2)}, u32[]{:S(2)}) collective-permute-start(f32[2,1024]{1,0:T(2,128)S(1)} %add.36.rest_4_.rest_12_), channel_id=1, source_target_pairs={{0,4},{1,5},{2,6},{3,7},{4,0},{5,1},{6,2},{7,3},{8,12},{9,13},{10,... | collective-permute-start | bytes 24584 | tf_op jit(solution)/shard_map/ppermute | solution.py:91
  244.1 10.4 %collective-permute-start.24 = (f32[2,1024]{1,0:T(2,128)S(1)}, f32[2,1024]{1,0:T(2,128)S(1)}, u32[]{:S(2)}, u32[]{:S(2)}) collective-permute-start(f32[2,1024]{1,0:T(2,128)S(1)} %add.36.rest_4_.rest_12_), channel_id=1, source_target_pairs={{0,6},{1,7},{2,4},{3,5},{4,2},{5,3},{6,0},{7,1},{8,14},{9,15},{10,... | collective-permute-start | bytes 24584 | tf_op jit(solution)/shard_map/ppermute | solution.py:91
  254.4 7.9 %copy-start.2 = (f32[16,64,512]{2,1,0:T(8,128)}, f32[16,64,512]{2,1,0:T(8,128)S(1)}, u32[]{:S(2)}) copy-start(f32[16,64,512]{2,1,0:T(8,128)S(1)} %all-to-all-done.2.x_ref) | copy-start | bytes 6291460
  262.3 7.2 %copy-start.22 = (s32[138,1]{0,1:T(1,128)S(1)}, s32[138,1]{0,1:T(1,128)}, u32[]{:S(2)}) copy-start(s32[138,1]{0,1:T(1,128)} %param.20) | copy-start | bytes 1660
  262.3 7.9 %copy-start.36 = (f32[40,1024]{1,0:T(8,128)S(1)}, f32[40,1024]{1,0:T(8,128)}, u32[]{:S(2)}) copy-start(f32[40,1024]{1,0:T(8,128)} %get-tuple-element.208) | copy-start | bytes 491524
  262.3 8.2 %copy-start.34 = (f32[40,1024]{1,0:T(8,128)S(1)}, f32[40,1024]{1,0:T(8,128)}, u32[]{:S(2)}) copy-start(f32[40,1024]{1,0:T(8,128)} %get-tuple-element.216) | copy-start | bytes 491524
  262.3 8.5 %copy-start.29 = (f32[40,1024]{1,0:T(8,128)S(1)}, f32[40,1024]{1,0:T(8,128)}, u32[]{:S(2)}) copy-start(f32[40,1024]{1,0:T(8,128)} %get-tuple-element.217) | copy-start | bytes 491524
  262.3 10.0 %copy-start.28 = (f32[40,1024]{1,0:T(8,128)S(1)}, f32[40,1024]{1,0:T(8,128)}, u32[]{:S(2)}) copy-start(f32[40,1024]{1,0:T(8,128)} %get-tuple-element.218) | copy-start | bytes 491524
  262.3 10.2 %copy-start.27 = (f32[40,1024]{1,0:T(8,128)S(1)}, f32[40,1024]{1,0:T(8,128)}, u32[]{:S(2)}) copy-start(f32[40,1024]{1,0:T(8,128)} %get-tuple-element.219) | copy-start | bytes 491524
  262.3 47.0 %all-to-all-start.3 = ((f32[16,64,256]{2,1,0:T(8,128)}), f32[16,64,256]{2,1,0:T(8,128)S(1)}, u32[]{:S(2)}, u32[]{:S(2)}) async-start(f32[16,64,256]{2,1,0:T(8,128)} %bitcast.41), calls=%async_computation.5 | async-start | bytes 2097152 | tf_op jit(solution)/shard_map/all_to_all | solution.py:108
  270.2 10.7 %collective-permute-start.25 = (f32[40,1024]{1,0:T(8,128)S(1)}, f32[40,1024]{1,0:T(8,128)S(1)}, u32[]{:S(2)}, u32[]{:S(2)}) collective-permute-start(f32[40,1024]{1,0:T(8,128)S(1)} %copy-done.36), channel_id=1, source_target_pairs={{0,1},{1,0},{2,3},{3,2},{4,5},{5,4},{6,7},{7,6},{8,9},{9,8},{10,11... | collective-permute-start | bytes 491528 | tf_op jit(solution)/shard_map/ppermute | solution.py:91
  270.6 15.5 %collective-permute-start.26 = (f32[40,1024]{1,0:T(8,128)S(1)}, f32[40,1024]{1,0:T(8,128)S(1)}, u32[]{:S(2)}, u32[]{:S(2)}) collective-permute-start(f32[40,1024]{1,0:T(8,128)S(1)} %copy-done.34), channel_id=1, source_target_pairs={{0,2},{1,3},{2,0},{3,1},{4,6},{5,7},{6,4},{7,5},{8,10},{9,11},{10,... | collective-permute-start | bytes 491528 | tf_op jit(solution)/shard_map/ppermute | solution.py:91
  270.8 22.4 %collective-permute-start.27 = (f32[40,1024]{1,0:T(8,128)S(1)}, f32[40,1024]{1,0:T(8,128)S(1)}, u32[]{:S(2)}, u32[]{:S(2)}) collective-permute-start(f32[40,1024]{1,0:T(8,128)S(1)} %copy-done.29), channel_id=1, source_target_pairs={{0,3},{1,2},{2,1},{3,0},{4,7},{5,6},{6,5},{7,4},{8,11},{9,10},{10,... | collective-permute-start | bytes 491528 | tf_op jit(solution)/shard_map/ppermute | solution.py:91
  272.4 20.9 %collective-permute-start.28 = (f32[40,1024]{1,0:T(8,128)S(1)}, f32[40,1024]{1,0:T(8,128)S(1)}, u32[]{:S(2)}, u32[]{:S(2)}) collective-permute-start(f32[40,1024]{1,0:T(8,128)S(1)} %copy-done.28), channel_id=1, source_target_pairs={{0,4},{1,5},{2,6},{3,7},{4,0},{5,1},{6,2},{7,3},{8,12},{9,13},{10,... | collective-permute-start | bytes 491528 | tf_op jit(solution)/shard_map/ppermute | solution.py:91
  272.6 20.7 %collective-permute-start.29 = (f32[40,1024]{1,0:T(8,128)S(1)}, f32[40,1024]{1,0:T(8,128)S(1)}, u32[]{:S(2)}, u32[]{:S(2)}) collective-permute-start(f32[40,1024]{1,0:T(8,128)S(1)} %copy-done.27), channel_id=1, source_target_pairs={{0,5},{1,4},{2,7},{3,6},{4,1},{5,0},{6,3},{7,2},{8,13},{9,12},{10,... | collective-permute-start | bytes 491528 | tf_op jit(solution)/shard_map/ppermute | solution.py:91
  274.1 6.8 %copy-start.26 = (f32[40,1024]{1,0:T(8,128)S(1)}, f32[40,1024]{1,0:T(8,128)}, u32[]{:S(2)}) copy-start(f32[40,1024]{1,0:T(8,128)} %get-tuple-element.220) | copy-start | bytes 491524
  280.9 12.4 %collective-permute-start.30 = (f32[40,1024]{1,0:T(8,128)S(1)}, f32[40,1024]{1,0:T(8,128)S(1)}, u32[]{:S(2)}, u32[]{:S(2)}) collective-permute-start(f32[40,1024]{1,0:T(8,128)S(1)} %copy-done.26), channel_id=1, source_target_pairs={{0,6},{1,7},{2,4},{3,5},{4,2},{5,3},{6,0},{7,1},{8,14},{9,15},{10,... | collective-permute-start | bytes 491528 | tf_op jit(solution)/shard_map/ppermute | solution.py:91
  286.0 7.2 %copy-start.31 = (f32[40,1024]{1,0:T(8,128)}, f32[40,1024]{1,0:T(8,128)S(1)}, u32[]{:S(2)}) copy-start(f32[40,1024]{1,0:T(8,128)S(1)} %collective-permute-done.26.rest_2_) | copy-start | bytes 491524
  286.1 10.0 %collective-permute-start.31 = (f32[40,1024]{1,0:T(8,128)S(1)}, f32[40,1024]{1,0:T(8,128)S(1)}, u32[]{:S(2)}, u32[]{:S(2)}) collective-permute-start(f32[40,1024]{1,0:T(8,128)S(1)} %copy-done.25), channel_id=1, source_target_pairs={{0,7},{1,6},{2,5},{3,4},{4,3},{5,2},{6,1},{7,0},{8,15},{9,14},{10,... | collective-permute-start | bytes 491528 | tf_op jit(solution)/shard_map/ppermute | solution.py:91
  299.5 15.8 %copy-start.12 = (f32[72,256]{1,0:T(8,128)S(1)}, f32[72,256]{1,0:T(8,128)}, u32[]{:S(2)}) copy-start(f32[72,256]{1,0:T(8,128)} %get-tuple-element.244) | copy-start | bytes 221188
  299.5 3.9 %collective-permute-start.32 = (f32[72,256]{1,0:T(8,128)}, f32[72,256]{1,0:T(8,128)S(1)}, u32[]{:S(2)}, u32[]{:S(2)}) collective-permute-start(f32[72,256]{1,0:T(8,128)} %get-tuple-element.236), channel_id=1, source_target_pairs={{0,8},{1,9},{2,10},{3,11},{4,12},{5,13},{6,14},{7,15},{8,0},{9,1},... | collective-permute-start | bytes 221192 | tf_op jit(solution)/shard_map/ppermute | solution.py:91
  299.8 6.2 %collective-permute-start.33 = (f32[72,256]{1,0:T(8,128)}, f32[72,256]{1,0:T(8,128)S(1)}, u32[]{:S(2)}, u32[]{:S(2)}) collective-permute-start(f32[72,256]{1,0:T(8,128)} %get-tuple-element.237), channel_id=1, source_target_pairs={{0,16},{1,17},{2,18},{3,19},{4,20},{5,21},{6,22},{7,23},{8,24},{9,... | collective-permute-start | bytes 221192 | tf_op jit(solution)/shard_map/ppermute | solution.py:91
  302.0 7.4 %collective-permute-start.34 = (f32[72,256]{1,0:T(8,128)}, f32[72,256]{1,0:T(8,128)S(1)}, u32[]{:S(2)}, u32[]{:S(2)}) collective-permute-start(f32[72,256]{1,0:T(8,128)} %get-tuple-element.238), channel_id=1, source_target_pairs={{0,24},{1,25},{2,26},{3,27},{4,28},{5,29},{6,30},{7,31},{8,16},{9,... | collective-permute-start | bytes 221192 | tf_op jit(solution)/shard_map/ppermute | solution.py:91
  309.4 26.3 %copy-start.4 = (f32[16,64,256]{2,1,0:T(8,128)}, f32[16,64,256]{2,1,0:T(8,128)S(1)}, u32[]{:S(2)}) copy-start(f32[16,64,256]{2,1,0:T(8,128)S(1)} %all-to-all-done.3.x_ref) | copy-start | bytes 3145732
  309.4 30.8 %all-to-all-start.4 = ((f32[16,64,256]{2,1,0:T(8,128)}), f32[16,64,256]{2,1,0:T(8,128)S(1)}, u32[]{:S(2)}, u32[]{:S(2)}) async-start(f32[16,64,256]{2,1,0:T(8,128)} %bitcast.20), calls=%async_computation.6 | async-start | bytes 2097152 | tf_op jit(solution)/shard_map/all_to_all | solution.py:108
  315.4 7.0 %collective-permute-start.35 = (f32[1,72,256]{2,1,0:T(8,128)S(1)}, f32[1,72,256]{2,1,0:T(8,128)S(1)}, u32[]{:S(2)}, u32[]{:S(2)}) collective-permute-start(f32[1,72,256]{2,1,0:T(8,128)S(1)} %add_bitcast_fusion), channel_id=1, source_target_pairs={{0,2},{1,3},{2,0},{3,1},{4,6},{5,7},{6,4},{7,5},{8,10},{9,11},{10,... | collective-permute-start | bytes 221192 | tf_op jit(solution)/shard_map/ppermute | solution.py:91
  322.4 4.4 %collective-permute-start.36 = (f32[2,72,256]{2,1,0:T(8,128)S(1)}, f32[2,72,256]{2,1,0:T(8,128)S(1)}, u32[]{:S(2)}, u32[]{:S(2)}) collective-permute-start(f32[2,72,256]{2,1,0:T(8,128)S(1)} %pad_maximum_fusion.3), channel_id=1, source_target_pairs={{0,4},{1,5},{2,6},{3,7},{4,0},{5,1},{6,2},{7,3},{8,12},{9,13},{10,... | collective-permute-start | bytes 442376 | tf_op jit(solution)/shard_map/ppermute | solution.py:91
  326.9 3.2 collective-permute-start.37
  (29 other events, 59.1 us)
Sparse Core Ops, SparseCore 0:
  154.6 35.7 reduce-scatter.4
  193.6 38.6 reduce-scatter.2
  234.2 31.0 all-gather.2

commit v3 on v2

--- a/solution.py
+++ b/solution.py
@@ -32,7 +32,7 @@
 ALL = ("chan", "hi", "lo")
 PIX = ("hi", "lo")
 SPREAD = ("chan", "lo")
-VMEM_BYTES = 60 * 2**20
+VMEM_BYTES = 62 * 2**20
 
 
 def params(dims=1):
@@ -45,6 +45,15 @@
 
 def sigmoid(v):
     return 0.5 * jnp.tanh(0.5 * v) + 0.5
+
+
+def swish_half(h):
+    return h + h * jnp.tanh(h)
+
+
+def slope_half(h):
+    t = jnp.tanh(h)
+    return 1.0 + (t + h * (1.0 - t * t))
 
 
 def split(v):
@@ -58,10 +67,6 @@
 
 def dot3(a, b):
     return dot(a[0], b[0]) + (dot(a[0], b[1]) + dot(a[1], b[0]))
-
-
-def exact_dot(a, b):
-    return jnp.dot(a, b, preferred_element_type=F32, precision=lax.Precision.HIGHEST)
 
 
 def total(refs):
@@ -91,7 +96,7 @@
     return lax.ppermute(x, ALL, [(i, i ^ stride) for i in range(n)])
 
 
-def shares(x, base, size):
+def shares(x, base, size, after=()):
     bits = size.bit_length() - 1
     parts = [x]
     if bits % 2:
@@ -99,6 +104,10 @@
         base, bits = base * 2, bits - 1
     while bits:
         x = sum(parts[1:], parts[0])
+        if after:
+            x, *kept = together(x, *after)
+            after[:] = kept
+            after = ()
         parts = [x] + [exchange(x, base * k) for k in (1, 2, 3)]
         base, bits = base * 4, bits - 2
     return parts
@@ -133,14 +142,16 @@
     return n_pix == 8
 
 
-def gather_pix(x):
+def gather_pix(x, beside=None):
     n_pix = lax.axis_size(PIX)
     if not near(n_pix):
-        return [lax.all_gather(x, PIX, axis=0)], [list(range(n_pix))]
+        return [lax.all_gather(x, PIX, axis=0)], [list(range(n_pix))], beside
     b = x[None]
     b = jnp.concatenate([b, exchange(b, 2)])
+    if beside is not None:
+        b, beside = together(b, beside)
     b = jnp.concatenate([b, exchange(b, 4)])
-    return [b, exchange(b, 1)], [[0, 2, 4, 6], [1, 3, 5, 7]]
+    return [b, exchange(b, 1)], [[0, 2, 4, 6], [1, 3, 5, 7]], beside
 
 
 def gather_chan(x):
@@ -211,7 +222,7 @@
         out_specs=pl.BlockSpec((CLIP_LEN, chans, area), lambda k: (k, 0, 0)),
         out_shape=jax.ShapeDtypeStruct((frames, chans, area), F32),
         compiler_params=params(),
-        cost_estimate=cost(1),
+        cost_estimate=cost(25),
         name="order",
     )(x)
 
@@ -232,18 +243,19 @@
         out_specs=pl.BlockSpec((CLIP_LEN, chans, area), lambda k: (k, 0, 0)),
         out_shape=jax.ShapeDtypeStruct((frames, chans, area), F32),
         compiler_params=params(),
-        cost_estimate=cost(5),
+        cost_estimate=cost(1),
         name="restore",
     )(x)
 
 
 def uncrop_kernel(left_ref, flip_ref, x_ref, y_ref, out_ref):
     k = pl.program_id(0)
-    area, width = x_ref.shape[2], out_ref.shape[2]
-    q = lax.broadcasted_iota(jnp.int32, (area, width), 1)
+    width = out_ref.shape[2]
     out = None
-    for half, ref in enumerate((x_ref, y_ref)):
-        p = lax.broadcasted_iota(jnp.int32, (area, 1), 0) + half * area
+    for start, ref in ((0, x_ref), (x_ref.shape[2], y_ref)):
+        area = ref.shape[2]
+        q = lax.broadcasted_iota(jnp.int32, (area, width), 1)
+        p = lax.broadcasted_iota(jnp.int32, (area, 1), 0) + start
         place = source_column(p, left_ref[k], flip_ref[k])
         term = pick(ref[...], (q == place).astype(F32).astype(BF16))
         out = term if out is None else out + term
@@ -252,7 +264,7 @@
 
 def uncrop(x, y, left, flip):
     frames, chans, area = x.shape
-    width = 2 * area // FRAME_COLUMNS * WIN
+    width = (area + y.shape[2]) // FRAME_COLUMNS * WIN
     return pl.pallas_call(
         uncrop_kernel,
         grid=(frames // CLIP_LEN,),
@@ -260,12 +272,12 @@
             pl.BlockSpec(memory_space=pltpu.SMEM),
             pl.BlockSpec(memory_space=pltpu.SMEM),
             pl.BlockSpec((CLIP_LEN, chans, area), lambda k: (k, 0, 0)),
-            pl.BlockSpec((CLIP_LEN, chans, area), lambda k: (k, 0, 0)),
+            pl.BlockSpec((CLIP_LEN, chans, y.shape[2]), lambda k: (k, 0, 0)),
         ],
         out_specs=pl.BlockSpec((CLIP_LEN, chans, width), lambda k: (k, 0, 0)),
         out_shape=jax.ShapeDtypeStruct((frames, chans, width), F32),
         compiler_params=params(),
-        cost_estimate=cost(5),
+        cost_estimate=cost(1),
         name="uncrop",
     )(left, flip, x, y)
 
@@ -298,19 +310,34 @@
     return pl.BlockSpec(shape, lambda *_: (0,) * len(shape))
 
 
+def by_steps(nz, bands, chans, area):
+    run = area
+    n = area // run
+
+    def tall(hidden):
+        return pl.BlockSpec((1, run, hidden), lambda t: (t // n, t % n, 0))
+
+    def out(hidden):
+        return pl.BlockSpec((1, run, hidden), lambda t: (t // n, t % n, 0))
+
+    wide = pl.BlockSpec((nz, 1, chans, run), lambda t: (0, t // n, 0, t % n))
+    return (bands * n,), tall, out, wide
+
+
 def expand(x, high, low):
     nz, bands, chans, area = x.shape
+    grid, _, tall, wide = by_steps(nz, bands, chans, area)
     hidden = high.shape[1]
     return pl.pallas_call(
         expand_kernel,
-        grid=(bands,),
+        grid=grid,
         in_specs=[
-            pl.BlockSpec((nz, 1, chans, area), lambda t: (0, t, 0, 0)),
+            wide,
             whole(high.shape),
             whole(low.shape),
         ],
         out_specs=[
-            pl.BlockSpec((1, area, hidden), lambda t: (t, 0, 0)),
+            tall(hidden),
             whole((2, hidden)),
             whole((nz * chans, nz * chans + 128)),
         ],
@@ -364,31 +391,117 @@
                 high[side, here], low[side, here] = split(ref[:, k].reshape(chan_all, width).T)
 
 
+def raise_rows(d):
+    e1, o1 = d[2] + d[6] - 4.25 * d[4], d[1] + d[5] - 4.25 * d[3]
+    e2, o2 = 0.25 * d[2] - 1.25 * d[4] + d[6], 0.5 * d[1] - 2.5 * d[3] + 2.0 * d[5]
+    e3, o3 = 4.0 * d[2] - 5.0 * d[4] + d[6], 2.0 * d[1] - 2.5 * d[3] + 0.5 * d[5]
+    return [
+        d[0] - d[6] + 5.25 * (d[4] - d[2]),
+        e1 + o1,
+        e1 - o1,
+        e2 + o2,
+        e2 - o2,
+        e3 + o3,
+        e3 - o3,
+        d[7] - d[1] + 5.25 * (d[3] - d[5]),
+    ]
+
+
+POINT_SCALES = (1.0, -2.0 / 9.0, -2.0 / 9.0, 1.0 / 90.0, 1.0 / 90.0, 32.0 / 45.0, 32.0 / 45.0)
+POINT_PLACES = (0.0, 1.0, -1.0, 2.0, -2.0, 0.5, -0.5)
+POINTS = 8
+GROUP = 4
+
+
+def tap_factors():
+    rows = [[scale * place**a for a in range(K)] for scale, place in zip(POINT_SCALES, POINT_PLACES)]
+    return rows + [[0.0] * (K - 1) + [1.0]]
+
+
+def mix(factors, values):
+    out = None
+    for factor, value in zip(factors, values):
+        if factor != 0.0:
+            term = value if factor == 1.0 else value * factor
+            out = term if out is None else out + term
+    return out
+
+
+def lower(m):
+    s1, d1, s2, d2, s3, d3 = m[1] + m[2], m[1] - m[2], m[3] + m[4], m[3] - m[4], m[5] + m[6], m[5] - m[6]
+    return [
+        m[0] + s1 + (s2 + s3),
+        d1 + (2.0 * d2 + 0.5 * d3),
+        s1 + (4.0 * s2 + 0.25 * s3),
+        d1 + m[7] + (8.0 * d2 + 0.125 * d3),
+    ]
+
+
+def spread_points(g):
+    e1, o1 = g[0] + g[2], g[1] + g[3]
+    e2, o2 = g[0] + 4.0 * g[2], 2.0 * g[1] + 8.0 * g[3]
+    e3, o3 = g[0] + 0.25 * g[2], 0.5 * g[1] + 0.125 * g[3]
+    return [g[0], e1 + o1, e1 - o1, e2 + o2, e2 - o2, e3 + o3, e3 - o3, g[3]]
+
+
+def raise_all(pad, first, raised):
+    def one(g, _):
+        for c in range(SUB):
+            d = [pad[first + GROUP * g + k, c + 2] for k in range(2 * GROUP)]
+            for p, value in enumerate(raise_rows(d)):
+                raised[g, p, c + 2] = value
+        for p in range(POINTS):
+            fill_sides(raised.at[g], p)
+        return 0
+
+    lax.fori_loop(0, raised.shape[0], one, 0)
+
+
+def raise_taps(w_ref, taps, flipped=False, scale=1.0):
+    for b in range(K):
+        column_taps = []
+        for a in range(K):
+            tap = a * K + b
+            column_taps.append(w_ref[TAPS - 1 - tap if flipped else tap])
+        for p, factors in enumerate(tap_factors()):
+            taps[p * K + b] = mix([scale * factor for factor in factors], column_taps)
+
+
+def four_rows(raised, taps, g, columns):
+    m = []
+    for p in range(POINTS):
+        values = {c: raised[g, p, c] for c in range(columns[0], columns[-1] + K)}
+        row = []
+        for c in columns:
+            row.append(mix([1.0] * K, [values[c + b] * taps[p * K + b] for b in range(K)]))
+        m.append(row)
+    return [lower([m[p][i] for p in range(POINTS)]) for i in range(len(columns))]
+
+
 def spread_kernel(
     parts, count, side_ref, top_ref, low_ref, own_ref, high_ref, lower_ref, gain_ref, bias_ref, w_ref, *rest
 ):
     sums = rest[:parts]
-    out_ref, edge_ref, hid_ref, sum_ref, pad, terms, rim_high, rim_low = rest[parts:]
+    out_ref, edge_ref, hid_ref, sum_ref, pad, terms, rim_high, rim_low, raised, taps = rest[parts:]
     rows = own_ref.shape[0]
     _, _, scale, shift = norm_terms(total(sums), count, gain_ref[0:1], bias_ref[0:1])
-    terms[0] = jnp.broadcast_to(scale, (SUB, 128))
-    terms[1] = jnp.broadcast_to(shift, (SUB, 128))
+    terms[0] = jnp.broadcast_to(0.5 * scale, (SUB, 128))
+    terms[1] = jnp.broadcast_to(0.5 * shift, (SUB, 128))
 
     @pl.when(pl.program_id(0) == 0)
     def _():
         turn_rims((top_ref, low_ref), side_ref, rim_high, rim_low)
 
     def act(value):
-        v = value * terms[0] + terms[1]
-        return v * sigmoid(v)
-
-    def own_row(r, _):
-        for c in range(SUB):
-            pad[r + HALO_IN, c + 2] = act(own_ref[r, c])
-        fill_sides(pad, r + HALO_IN)
+        return swish_half(value * terms[0] + terms[1])
+
+    def own_rows(i, _):
+        for k in range(GROUP):
+            for c in range(SUB):
+                pad[GROUP * i + k + HALO_IN, c + 2] = act(own_ref[GROUP * i + k, c])
         return 0
 
-    lax.fori_loop(0, rows, own_row, 0)
+    lax.fori_loop(0, rows // GROUP, own_rows, 0)
     for side, start, first in ((0, 0, HALO_IN - HALO_OUT), (1, rows + HALO_IN, 0)):
 
         @pl.when(side_ref[side] == 1)
@@ -397,27 +510,30 @@
             halo = halo.reshape(HALO_IN, SUB, SUB, 128)
             hid_ref[side] = halo[first : first + HALO_OUT]
             pad[start : start + HALO_IN, 2 : SUB + 2] = act(halo)
-            for r in range(HALO_IN):
-                fill_sides(pad, start + r)
+            edge_row = min(start, rows + 2)
+            for r in range(HALO_OUT + K - 1):
+                fill_sides(pad, edge_row + r)
 
         @pl.when(side_ref[side] == 0)
         def _(side=side, start=start):
             clear_rows(pad, start, HALO_IN)
             hid_ref[side] = jnp.zeros(hid_ref.shape[1:], F32)
 
-    def group(i, carry):
+    raise_taps(w_ref, taps)
+    raise_all(pad, 2, raised)
+
+    def group(g, carry):
         one, two = carry
-        r = i * SUB
-        for c in range(SUB):
-            acc = tap_rows(pad, w_ref, r + 2, SUB, c)
-            for o in range(SUB):
-                out_ref[r + o, c] = acc[o]
-                one = one + acc[o]
-                two = two + acc[o] * acc[o]
+        for columns in (range(0, SUB // 2), range(SUB // 2, SUB)):
+            for c, values in zip(columns, four_rows(raised, taps, g, columns)):
+                for o, value in enumerate(values):
+                    out_ref[GROUP * g + o, c] = value
+                    one = one + value
+                    two = two + value * value
         return one, two
 
     zero = jnp.zeros((SUB, 128), F32)
-    one, two = lax.fori_loop(0, rows // SUB, group, (zero, zero))
+    one, two = lax.fori_loop(0, rows // GROUP, group, (zero, zero))
     sum_ref[0:1] = jnp.sum(one, axis=0, keepdims=True)
     sum_ref[1:2] = jnp.sum(two, axis=0, keepdims=True)
     for side, start in ((0, 0), (1, rows + 2)):
@@ -467,9 +583,11 @@
             pltpu.VMEM((2, SUB, 128), F32),
             pltpu.VMEM(rim_shape, BF16),
             pltpu.VMEM(rim_shape, BF16),
+            pltpu.VMEM((rows // GROUP, POINTS, SUB + 4, SUB, 128), F32),
+            pltpu.VMEM((POINTS * K, SUB, 128), F32),
         ],
         compiler_params=params(),
-        cost_estimate=cost(25),
+        cost_estimate=cost(10),
         name="spread",
     )(side, top, low, *arrays)
 
@@ -493,11 +611,11 @@
         s_ref[...] = jnp.zeros_like(s_ref)
 
     _, _, scale, shift = norm_terms(total(sums), count, gain_ref[1:2], bias_ref[1:2])
+    scale, shift = 0.5 * scale, 0.5 * shift
     gout = split(gout_ref[:, 0].reshape(chan_all, gout_ref.shape[3]))
     proj = None
     for cut in chunks(hidden):
-        v = own_ref[0, :, cut] * scale[:, cut] + shift[:, cut]
-        act = v * sigmoid(v)
+        act = swish_half(own_ref[0, :, cut] * scale[:, cut] + shift[:, cut])
         s_ref[0:1, cut] += jnp.sum(act, axis=0, keepdims=True)
         act = split(act)
         m_ref[:, cut] += dot3(gout, act)
@@ -516,12 +634,13 @@
     nz, bands, chans, area = gout.shape
     hidden = wt.shape[1]
     chan_all = nz * chans
+    grid, tall, put, wide = by_steps(nz, bands, chans, area)
     return pl.pallas_call(
         partial(gather_kernel, len(sums), count),
-        grid=(bands,),
+        grid=grid,
         in_specs=[
-            pl.BlockSpec((1, area, hidden), lambda t: (t, 0, 0)),
-            pl.BlockSpec((nz, 1, chans, area), lambda t: (0, t, 0, 0)),
+            tall(hidden),
+            wide,
             whole(gains.shape),
             whole(biases.shape),
             whole(wt.shape),
@@ -533,7 +652,7 @@
             whole((chan_all, hidden)),
             whole((1, hidden)),
             whole((2, chan_all)),
-            pl.BlockSpec((1, area, chan_all), lambda t: (t, 0, 0)),
+            put(chan_all),
         ],
         out_shape=[
             jax.ShapeDtypeStruct((chan_all, hidden), F32),
@@ -551,22 +670,14 @@
     return jnp.broadcast_to(row, (SUB, row.shape[1])).T[:, 0:1]
 
 
-def padded_dot(row, matrix):
-    return exact_dot(jnp.broadcast_to(row, (SUB, row.shape[1])), matrix)[0:1]
-
-
 def slope_terms(sums, count, gain_ref, bias_ref):
-    mean, inverse, _, _ = norm_terms(sums, count, gain_ref[1:2], bias_ref[1:2])
-    return mean, inverse, gain_ref[1:2], bias_ref[1:2]
+    _, _, scale, shift = norm_terms(sums, count, gain_ref[1:2], bias_ref[1:2])
+    return 0.5 * scale, 0.5 * shift
 
 
 def second_grad(gout, weights, k_row, value, terms, cut):
-    mean, inverse, gain, bias = terms
-    grad = dot3(gout, (weights[0][:, cut], weights[1][:, cut])) + k_row[:, cut]
-    centered = (value - mean[:, cut]) * inverse[:, cut]
-    v = centered * gain[:, cut] + bias[:, cut]
-    s = sigmoid(v)
-    return grad * (s + v * s * (1.0 - s)), centered
+    h = value * terms[0][:, cut] + terms[1][:, cut]
+    return (dot3(gout, (weights[0][:, cut], weights[1][:, cut])) + k_row[:, cut]) * slope_half(h), h
 
 
 def proj_back_kernel(
@@ -578,39 +689,37 @@
     gain_ref,
     bias_ref,
     wt_ref,
-    sq_ref,
     sqt_ref,
     down_ref,
     ex_ref,
-    ext_ref,
     exb_ref,
     *rest,
 ):
     ses, sums = rest[:pairs], rest[pairs : pairs + parts]
-    q_ref, sum_ref, val_ref, w_high, w_low, k_row = rest[pairs + parts :]
+    q_ref, sum_ref, val_ref, col_ref, w_high, w_low, k_row = rest[pairs + parts :]
     chan_all, hidden = wt_ref.shape
-    reduced = ex_ref.shape[0]
 
     @pl.when(pl.program_id(0) == 0)
     def _():
         se = total(ses)
         pooled = se[0:1] / (FRAME_ROWS * FRAME_COLUMNS)
-        pre = padded_dot(pooled, sq_ref[...]) + down_ref[...]
+        sqt, ex = sqt_ref[...], ex_ref[...]
+        pre = jnp.sum(sqt * pooled, axis=1, keepdims=True) + down_ref[...]
         gate = sigmoid(pre)
         squeezed = pre * gate
-        excite = sigmoid(padded_dot(squeezed, ex_ref[...]) + exb_ref[...])
+        excite = sigmoid(jnp.sum(ex * squeezed, axis=0, keepdims=True) + exb_ref[...])
         logit = se[1:2] * excite * (1.0 - excite)
         slope = gate * (1.0 + pre * (1.0 - gate))
-        grad_sq = padded_dot(logit, ext_ref[...]) * slope
-        pool_grad = padded_dot(grad_sq, sqt_ref[...]) / (FRAME_ROWS * FRAME_COLUMNS)
+        grad_sq = jnp.sum(ex * logit, axis=1, keepdims=True) * slope
+        pool_grad = jnp.sum(sqt * grad_sq, axis=0, keepdims=True) / (FRAME_ROWS * FRAME_COLUMNS)
         val_ref[...] = jnp.zeros_like(val_ref)
         val_ref[0:1] = excite
         val_ref[1:2] = pool_grad
         val_ref[2:3] = logit
         val_ref[3:4] = pooled
-        val_ref[4:5, 0:reduced] = squeezed
-        val_ref[5:6, 0:reduced] = grad_sq
-        wt = wt_ref[...]
+        lane = lax.broadcasted_iota(jnp.int32, col_ref.shape, 1)
+        col_ref[...] = jnp.where(lane == 0, squeezed, jnp.where(lane == 1, grad_sq, 0.0))
+        wt = 0.5 * wt_ref[...]
         w_high[...], w_low[...] = split(wt * column(excite))
         k_row[...] = jnp.sum(wt * column(pool_grad), axis=0, keepdims=True)
         sum_ref[...] = jnp.zeros_like(sum_ref)
@@ -618,29 +727,36 @@
     terms = slope_terms(total(sums), count, gain_ref, bias_ref)
     gout = split(gout_ref[:, 0].reshape(chan_all, gout_ref.shape[3]).T)
     for cut in chunks(hidden):
-        q, centered = second_grad(gout, (w_high, w_low), k_row, own_ref[0, :, cut], terms, cut)
+        q, h = second_grad(gout, (w_high, w_low), k_row, own_ref[0, :, cut], terms, cut)
         q_ref[0, :, cut] = q
         sum_ref[0:1, cut] += jnp.sum(q, axis=0, keepdims=True)
-        sum_ref[1:2, cut] += jnp.sum(q * centered, axis=0, keepdims=True)
+        sum_ref[1:2, cut] += jnp.sum(q * h, axis=0, keepdims=True)
+
+    @pl.when(pl.program_id(0) == pl.num_programs(0) - 1)
+    def _():
+        sum_ref[1:2] = (2.0 * sum_ref[1:2] - bias_ref[1:2] * sum_ref[0:1]) / gain_ref[1:2]
 
 
 def proj_back(count, own, gout, gains, biases, wt, se_weights, ses, sums):
     nz, bands, chans, area = gout.shape
     hidden = wt.shape[1]
     chan_all = nz * chans
+    reduced = se_weights[0].shape[0]
     fixed = [gains, biases, wt, *se_weights, *ses, *sums]
+    grid, tall, put, wide = by_steps(nz, bands, chans, area)
     return pl.pallas_call(
         partial(proj_back_kernel, len(ses), len(sums), count),
-        grid=(bands,),
+        grid=grid,
         in_specs=[
-            pl.BlockSpec((1, area, hidden), lambda t: (t, 0, 0)),
-            pl.BlockSpec((nz, 1, chans, area), lambda t: (0, t, 0, 0)),
+            tall(hidden),
+            wide,
         ]
         + [whole(a.shape) for a in fixed],
         out_specs=[
-            pl.BlockSpec((1, area, hidden), lambda t: (t, 0, 0)),
+            put(hidden),
             whole((2, hidden)),
             whole((SUB, chan_all)),
+            whole((reduced, 128)),
             whole(wt.shape),
             whole(wt.shape),
             whole((1, hidden)),
@@ -649,6 +765,7 @@
             jax.ShapeDtypeStruct((bands, area, hidden), F32),
             jax.ShapeDtypeStruct((2, hidden), F32),
             jax.ShapeDtypeStruct((SUB, chan_all), F32),
+            jax.ShapeDtypeStruct((reduced, 128), F32),
             jax.ShapeDtypeStruct(wt.shape, BF16),
             jax.ShapeDtypeStruct(wt.shape, BF16),
             jax.ShapeDtypeStruct((1, hidden), F32),
@@ -673,15 +790,16 @@
 def project(proj, x, values, m, s):
     nz, bands, chans, area = x.shape
     fixed = [values, m, s]
+    grid, tall, put, wide = by_steps(nz, bands, chans, area)
     return pl.pallas_call(
         project_kernel,
-        grid=(bands,),
+        grid=grid,
         in_specs=[
-            pl.BlockSpec((1, area, nz * chans), lambda t: (t, 0, 0)),
-            pl.BlockSpec((nz, 1, chans, area), lambda t: (0, t, 0, 0)),
+            tall(nz * chans),
+            wide,
         ]
         + [whole(a.shape) for a in fixed],
-        out_specs=[pl.BlockSpec((nz, 1, chans, area), lambda t: (0, t, 0, 0)), whole(m.shape)],
+        out_specs=[wide, whole(m.shape)],
         out_shape=[
             jax.ShapeDtypeStruct((nz, bands, chans, area), F32),
             jax.ShapeDtypeStruct(m.shape, F32),
@@ -712,34 +830,33 @@
     *rest,
 ):
     sums_one, sums_two, backs = (rest[i * parts : (i + 1) * parts] for i in range(3))
-    out_ref, sum_ref, tap_ref, pad, grad, terms, rim_high, rim_low = rest[3 * parts :]
+    out_ref, sum_ref, tap_ref, pad, grad, terms, rim_high, rim_low, raised, points, taps = rest[3 * parts :]
     rows = own_ref.shape[0]
 
     @pl.when(pl.program_id(0) == 0)
     def _():
         turn_rims((top_ref, low_ref), side_ref, rim_high, rim_low)
 
-    mean, inverse, scale, shift = norm_terms(total(sums_one), count, gain_ref[0:1], bias_ref[0:1])
+    _, _, scale, shift = norm_terms(total(sums_one), count, gain_ref[0:1], bias_ref[0:1])
     a, b, c0 = back_terms(total(sums_two), total(backs), count, gain_ref[1:2])
-    for i, row in enumerate((scale, shift, a, b, c0, mean, inverse)):
+    for i, row in enumerate((0.5 * scale, 0.5 * shift, a, b, c0)):
         terms[i] = jnp.broadcast_to(row, (SUB, 128))
 
     def act(value):
-        v = value * terms[0] + terms[1]
-        return v * sigmoid(v)
+        return swish_half(value * terms[0] + terms[1])
 
     def grad_in(q, value):
         return q * terms[2] + (value * terms[3] + terms[4])
 
-    def own_row(r, _):
-        for c in range(SUB):
-            pad[r + HALO_OUT, c + 2] = act(hid_ref[r, c])
-            grad[r + HALO_OUT, c + 2] = grad_in(q_ref[r, c], own_ref[r, c])
-        fill_sides(pad, r + HALO_OUT)
-        fill_sides(grad, r + HALO_OUT)
+    def own_rows(i, _):
+        for k in range(GROUP):
+            r = GROUP * i + k
+            for c in range(SUB):
+                pad[r + HALO_OUT, c + 2] = act(hid_ref[r, c])
+                grad[r + HALO_OUT, c + 2] = grad_in(q_ref[r, c], own_ref[r, c])
         return 0
 
-    lax.fori_loop(0, rows, own_row, 0)
+    lax.fori_loop(0, rows // GROUP, own_rows, 0)
     slope = slope_terms(total(sums_two), count, gain_ref, bias_ref)
     for side, start in ((0, 0), (1, rows + HALO_OUT)):
 
@@ -752,52 +869,69 @@
             edge = grad_in(q.reshape(HALO_OUT, SUB, SUB, 128), halo_ref[side])
             grad[start : start + HALO_OUT, 2 : SUB + 2] = edge
             pad[start : start + HALO_OUT, 2 : SUB + 2] = act(hid_halo_ref[side])
-            for r in range(HALO_OUT):
-                fill_sides(pad, start + r)
-                fill_sides(grad, start + r)
 
         @pl.when(side_ref[side] == 0)
         def _(start=start):
             clear_rows(pad, start, HALO_OUT)
             clear_rows(grad, start, HALO_OUT)
 
-    def weight_group(i, acc):
-        acc = list(acc)
-        r = i // SUB * SUB
-        c = i % SUB
-        mine = [grad[r + HALO_OUT + o, c + 2] for o in range(SUB)]
-        for bb in range(K):
-            for row in range(SUB + K - 1):
-                value = pad[r + row, c + bb]
-                for aa in range(K):
-                    o = row - aa
-                    if 0 <= o < SUB:
-                        acc[aa * K + bb] = acc[aa * K + bb] + value * mine[o]
-        return tuple(acc)
-
+    raise_all(pad, 0, raised)
+
+    def point_group(g, _):
+        for c in range(SUB):
+            mine = [grad[GROUP * g + HALO_OUT + k, c + 2] for k in range(GROUP)]
+            for p, value in enumerate(spread_points(mine)):
+                points[g, p, c] = value
+        return 0
+
+    lax.fori_loop(0, rows // GROUP, point_group, 0)
     zero = jnp.zeros((SUB, 128), F32)
-    acc = lax.fori_loop(0, rows, weight_group, (zero,) * TAPS)
+    factors = tap_factors()
+    tap_sums = [None] * TAPS
+    for p in range(0, POINTS, 2):
+
+        def weight_group(g, acc, p=p):
+            acc = list(acc)
+            for k in range(2):
+                values = [raised[g, p + k, c] for c in range(SUB + K - 1)]
+                for c in range(SUB):
+                    mine = points[g, p + k, c]
+                    for b in range(K):
+                        at = (k * 2 + c % 2) * K + b
+                        acc[at] = acc[at] + values[c + b] * mine
+            return tuple(acc)
+
+        acc = lax.fori_loop(0, rows // GROUP, weight_group, (zero,) * (4 * K))
+        for k in range(2):
+            for b in range(K):
+                value = jnp.sum(acc[2 * k * K + b] + acc[(2 * k + 1) * K + b], axis=0, keepdims=True)
+                for a in range(K):
+                    if factors[p + k][a] != 0.0:
+                        term = value * factors[p + k][a]
+                        old = tap_sums[a * K + b]
+                        tap_sums[a * K + b] = term if old is None else old + term
     for tap in range(TAPS):
-        tap_ref[tap : tap + 1] = jnp.sum(acc[tap], axis=0, keepdims=True)
-
-    def group(i, carry):
+        tap_ref[tap : tap + 1] = tap_sums[tap]
+
+    raise_taps(w_ref, taps, flipped=True, scale=0.5)
+    raise_all(grad, 0, raised)
+
+    def group(g, carry):
         one, two = carry
-        r = i * SUB
-        for c in range(SUB):
-            acc = tap_rows(grad, w_ref, r, SUB, c, flipped=True)
-            for o in range(SUB):
-                hidden = hid_ref[r + o, c]
-                v = hidden * terms[0] + terms[1]
-                s = sigmoid(v)
-                value = acc[o] * (s + v * s * (1.0 - s))
-                out_ref[r + o, c] = value
-                one = one + value
-                two = two + value * ((hidden - terms[5]) * terms[6])
+        for columns in (range(0, SUB // 2), range(SUB // 2, SUB)):
+            for c, values in zip(columns, four_rows(raised, taps, g, columns)):
+                for o, value in enumerate(values):
+                    h = hid_ref[GROUP * g + o, c] * terms[0] + terms[1]
+                    value = value * slope_half(h)
+                    out_ref[GROUP * g + o, c] = value
+                    one = one + value
+                    two = two + value * h
         return one, two
 
-    one, two = lax.fori_loop(0, rows // SUB, group, (zero, zero))
-    sum_ref[0:1] = jnp.sum(one, axis=0, keepdims=True)
-    sum_ref[1:2] = jnp.sum(two, axis=0, keepdims=True)
+    one, two = lax.fori_loop(0, rows // GROUP, group, (zero, zero))
+    one, two = jnp.sum(one, axis=0, keepdims=True), jnp.sum(two, axis=0, keepdims=True)
+    sum_ref[0:1] = one
+    sum_ref[1:2] = (2.0 * two - bias_ref[0:1] * one) / gain_ref[0:1]
 
 
 def spread_back(
@@ -820,12 +954,15 @@
         scratch_shapes=[
             pltpu.VMEM((rows + 2 * HALO_OUT, SUB + 4, SUB, 128), F32),
             pltpu.VMEM((rows + 2 * HALO_OUT, SUB + 4, SUB, 128), F32),
-            pltpu.VMEM((7, SUB, 128), F32),
+            pltpu.VMEM((5, SUB, 128), F32),
             pltpu.VMEM(rim_shape, BF16),
             pltpu.VMEM(rim_shape, BF16),
+            pltpu.VMEM((rows // GROUP, POINTS, SUB + 4, SUB, 128), F32),
+            pltpu.VMEM((rows // GROUP, POINTS, SUB, SUB, 128), F32),
+            pltpu.VMEM((POINTS * K, SUB, 128), F32),
         ],
         compiler_params=params(),
-        cost_estimate=cost(47),
+        cost_estimate=cost(150),
         name="spread_back",
     )(side, top, low, *arrays)
 
@@ -835,7 +972,7 @@
     return split(q_ref[0, :, cut] * a[:, cut] + (hid_ref[0, :, cut] * b[:, cut] + c[:, cut]))
 
 
-def input_kernel(parts, count, half, q_ref, hid_ref, gout_ref, gain_ref, w_high, w_low, *rest):
+def input_kernel(parts, count, start, q_ref, hid_ref, gout_ref, gain_ref, w_high, w_low, *rest):
     sums, backs, out_ref = rest[:parts], rest[parts : 2 * parts], rest[2 * parts]
     nz, _, chans, area = out_ref.shape
     terms = back_terms(total(sums), total(backs), count, gain_ref[0:1])
@@ -845,39 +982,37 @@
         out = term if out is None else out + term
     own = gout_ref[:, 0]
     if own.shape[2] > area:
-        own = own[:, :, half * area : (half + 1) * area]
+        own = own[:, :, start : start + area]
     out_ref[:, 0] = own + out.T.reshape(nz, chans, area)
 
 
-def input_grad(count, half, q, hid, gout, gains, w_high, w_low, sums, backs):
+def input_grad(count, start, width, q, hid, gout, gains, w_high, w_low, sums, backs):
     nz, bands, chans, area = gout.shape
     hidden = w_high.shape[0]
-    area //= 2
+    at = start // width
     fixed = [gains, w_high, w_low, *sums, *backs]
+    if width % 128 == 0:
+        gout_spec = pl.BlockSpec((nz, 1, chans, width), lambda t: (0, t, 0, at))
+    else:
+        gout_spec = pl.BlockSpec((nz, 1, chans, area), lambda t: (0, t, 0, 0))
     return pl.pallas_call(
-        partial(input_kernel, len(sums), count, half),
+        partial(input_kernel, len(sums), count, start),
         grid=(bands,),
         in_specs=[
-            pl.BlockSpec((1, area, hidden), lambda t: (t, half, 0)),
-            pl.BlockSpec((1, area, hidden), lambda t: (t, half, 0)),
-            whole_half(nz, chans, area, half),
+            pl.BlockSpec((1, width, hidden), lambda t: (t, at, 0)),
+            pl.BlockSpec((1, width, hidden), lambda t: (t, at, 0)),
+            gout_spec,
         ]
         + [whole(v.shape) for v in fixed],
-        out_specs=pl.BlockSpec((nz, 1, chans, area), lambda t: (0, t, 0, 0)),
-        out_shape=jax.ShapeDtypeStruct((nz, bands, chans, area), F32),
+        out_specs=pl.BlockSpec((nz, 1, chans, width), lambda t: (0, t, 0, 0)),
+        out_shape=jax.ShapeDtypeStruct((nz, bands, chans, width), F32),
         compiler_params=params(),
-        cost_estimate=cost(5),
+        cost_estimate=cost(12),
         name="input_grad",
     )(q, hid, gout, *fixed)
 
 
-def whole_half(nz, chans, area, half):
-    if area % 128 == 0:
-        return pl.BlockSpec((nz, 1, chans, area), lambda t: (0, t, 0, half))
-    return pl.BlockSpec((nz, 1, chans, 2 * area), lambda t: (0, t, 0, 0))
-
-
-def weight_kernel(chans, reduced, ids_ref, q_ref, x_ref, tap_ref, one_ref, two_ref, val_ref, *rest):
+def weight_kernel(chans, ids_ref, q_ref, x_ref, tap_ref, one_ref, two_ref, val_ref, col_ref, *rest):
     outs, acc, small = rest[:-2], rest[-2], rest[-1]
     nz, _, _, area = x_ref.shape
     chan_all, hidden = acc.shape
@@ -895,15 +1030,17 @@
         small[TAPS + 3 : TAPS + 4] = two_ref[0:1]
         lead = (ids_ref[1] == 0).astype(F32)
         logit, pooled = val_ref[2:3] * lead, val_ref[3:4]
-        squeezed, grad_sq = val_ref[4:5, 0:reduced], val_ref[5:6, 0:reduced] * lead
-        g_sq = column(grad_sq) * pooled
-        g_ex = column(squeezed) * logit
+        reduced = col_ref.shape[0]
+        grad_sq = col_ref[:, 1:2] * lead
+        g_sq = grad_sq * pooled
+        g_ex = col_ref[:, 0:1] * logit
+        grad_row = jnp.broadcast_to(grad_sq, (reduced, 128)).T[0:1]
         for z in range(nz):
             own, at = slice(z * chans, (z + 1) * chans), z * width
             small[32 : 32 + reduced, at : at + chans] = g_sq[:, own]
             small[32 : 32 + reduced, at + chans : at + 2 * chans] = g_ex[:, own]
             small[32:33, at + 2 * chans : at + 3 * chans] = logit[:, own]
-            small[33:34, at + 2 * chans : at + 2 * chans + reduced] = grad_sq
+            small[33:34, at + 2 * chans : at + 2 * chans + reduced] = grad_row
 
     x = split(x_ref[:, 0].reshape(chan_all, area))
     for cut in chunks(hidden):
@@ -911,27 +1048,30 @@
 
     @pl.when(t == pl.num_programs(0) - 1)
     def _():
-        n = len(outs)
+        n = sum(out.shape[0] for out in outs)
         r, m = chan_all // n, SMALL // n
-        for i, out in enumerate(outs):
-            p = ids_ref[0] ^ i
-            out[0:r] = acc[pl.ds(pl.multiple_of(p * r, r), r), :]
-            out[r : r + m] = small[pl.ds(pl.multiple_of(p * m, m), m), :]
-
-
-def weight_grad(ids, pieces, q, x, taps, one, two, values, reduced):
+        for core, out in enumerate(outs):
+            for i in range(out.shape[0]):
+                p = ids_ref[0] ^ (i * len(outs) + core)
+                out[i, 0:r] = acc[pl.ds(pl.multiple_of(p * r, r), r), :]
+                out[i, r : r + m] = small[pl.ds(pl.multiple_of(p * m, m), m), :]
+
+
+def weight_grad(ids, shape, q, x, taps, one, two, values, columns):
     nz, bands, chans, area = x.shape
     hidden = q.shape[2]
     chan_all = nz * chans
-    fixed = [taps, one, two, values]
-    shape = ((chan_all + SMALL) // pieces, hidden)
+    fixed = [taps, one, two, values, columns]
+    pieces, chips = shape
+    shape = (chips, (chan_all + SMALL) // (pieces * chips), hidden)
+    grid, tall, put, wide = by_steps(nz, bands, chans, area)
     return pl.pallas_call(
-        partial(weight_kernel, chans, reduced),
-        grid=(bands,),
+        partial(weight_kernel, chans),
+        grid=grid,
         in_specs=[
             pl.BlockSpec(memory_space=pltpu.SMEM),
-            pl.BlockSpec((1, area, hidden), lambda t: (t, 0, 0)),
-            pl.BlockSpec((nz, 1, chans, area), lambda t: (0, t, 0, 0)),
+            tall(hidden),
+            wide,
         ]
         + [whole(v.shape) for v in fixed],
         out_specs=[whole(shape)] * pieces,
@@ -941,6 +1081,25 @@
         cost_estimate=cost(7),
         name="weight_grad",
     )(ids, q, x, *fixed)
+
+
+def merge_kernel(one_ref, two_ref, *outs):
+    for i, out in enumerate(outs):
+        out[...] = one_ref[i] + two_ref[i]
+
+
+def merge(one, two):
+    n = one.shape[0]
+    return pl.pallas_call(
+        merge_kernel,
+        grid=(1,),
+        in_specs=[whole(one.shape), whole(two.shape)],
+        out_specs=[whole(one.shape[1:])] * n,
+        out_shape=[jax.ShapeDtypeStruct(one.shape[1:], F32)] * n,
+        compiler_params=params(),
+        cost_estimate=cost(2),
+        name="merge",
+    )(one, two)
 
 
 def collect_kernel(n, nz, parts, count, ids_ref, early_ref, gram_ref, high_ref, low_ref, gain_ref, *rest):
@@ -1008,14 +1167,14 @@
 def pack_kernel(at_ref, we_ref, wp_ref, dw_ref, gain_ref, bias_ref, sq_ref, ex_ref, exb_ref, out_ref, small):
     p = at_ref[0]
     chan_in, width = we_ref.shape
-    chans, reduced = sq_ref.shape
+    reduced, chans = sq_ref.shape
     m = small.shape[0] * out_ref.shape[0] // (2 * chan_in + small.shape[0])
     r = (out_ref.shape[0] - m) // 2
     small[...] = jnp.zeros_like(small)
     small[0:TAPS] = dw_ref[...]
     small[TAPS : TAPS + 2] = gain_ref[...]
     small[TAPS + 2 : TAPS + 4] = bias_ref[...]
-    small[32 : 32 + reduced, 0:chans] = sq_ref[...].T
+    small[32 : 32 + reduced, 0:chans] = sq_ref[...]
     small[32 : 32 + reduced, chans : 2 * chans] = ex_ref[...]
     small[32:33, 2 * chans : 3 * chans] = exb_ref[...]
     out_ref[0:r] = we_ref[pl.ds(pl.multiple_of(p * r, r), r), :]
@@ -1038,7 +1197,7 @@
         w_dw,
         norm_gains,
         norm_biases,
-        squeeze_matrix,
+        squeeze_matrix.T,
         excite_matrix,
         excite_bias_row[None],
     ]
@@ -1075,10 +1234,8 @@
         tap_ref,
         gain_ref,
         bias_ref,
-        sq_ref,
         sqt_ref,
         ex_ref,
-        ext_ref,
         exb_ref,
         first,
         second,
@@ -1117,8 +1274,6 @@
         sqt_ref[:, own] = small[z, 32 : 32 + reduced, 0:chans]
         ex_ref[:, own] = small[z, 32 : 32 + reduced, chans : 2 * chans]
         exb_ref[:, own] = small[z, 32:33, 2 * chans : 3 * chans]
-    sq_ref[...] = sqt_ref[...].T
-    ext_ref[...] = ex_ref[...].T
 
 
 def order_weights(base, slabs, orders, nz, chan_in, chans, reduced):
@@ -1132,10 +1287,8 @@
             ((TAPS, SUB, hidden), F32),
             ((2, hidden), F32),
             ((2, hidden), F32),
-            ((chan_in, reduced), F32),
             ((reduced, chan_in), F32),
             ((reduced, chan_in), F32),
-            ((chan_in, reduced), F32),
             ((1, chan_in), F32),
         ]
     )
@@ -1151,7 +1304,7 @@
             pltpu.VMEM((nz, SMALL, width), F32),
         ],
         compiler_params=params(),
-        cost_estimate=cost(1),
+        cost_estimate=cost(3),
         name="order_weights",
     )(base, *slabs)
 
@@ -1258,7 +1411,7 @@
     for u in range(chan_in // 128):
         flip[u] = wp_ref[:, u * 128 : (u + 1) * 128]
     fill_blocks(
-        weight, head, middle, flip, chan_in, sq_ref[...], down_ref[...], ex_ref[...], exb_ref[...]
+        weight, head, middle, flip, chan_in, sq_ref[...].T, down_ref[...], ex_ref[...], exb_ref[...]
     )
     at = 0
     home = jnp.zeros(col_ref.shape, jnp.int32)
@@ -1300,7 +1453,7 @@
             pltpu.VMEM((blocks, 128), F32),
         ],
         compiler_params=params(),
-        cost_estimate=cost(5),
+        cost_estimate=cost(1),
         name="prepare",
     )(base, *arrays)
 
@@ -1403,7 +1556,7 @@
             pltpu.VMEM((blocks, 128), F32),
         ],
         compiler_params=params(),
-        cost_estimate=cost(4),
+        cost_estimate=cost(10),
         name="adam",
     )(ids, *arrays)
 
@@ -1469,7 +1622,8 @@
     crops = crop(frames_raw, col_offsets, flip_flags)
     crops, *slab = together(crops, *gather_chan(slab))
     x = deal(crops).reshape(nz, nlo, chans, area)
-    slabs, orders = gather_pix(jnp.concatenate(slab, axis=1))
+    ordered = order(grad_out)
+    slabs, orders, ordered = gather_pix(jnp.concatenate(slab, axis=1), ordered)
     (
         we_high,
         we_low,
@@ -1481,19 +1635,14 @@
         taps,
         gains,
         biases,
-        sq_all,
         sq_t,
         ex_all,
-        ex_t,
         ex_bias,
     ) = order_weights(
         jnp.stack([relative, z_relative]), slabs, orders, nz, chan_in, chans, reduced
     )
-    se_weights = [sq_all, sq_t, se_down_bias[None], ex_all, ex_t, ex_bias]
-    ordered = order(grad_out)
+    se_weights = [sq_t, se_down_bias[:, None], ex_all, ex_bias]
     x, ordered, we_high, we_low = together(x, ordered, we_high, we_low)
-
-    top, low = rims(x, HALO_IN, band)
 
     def as_rows(v):
         return v.reshape(rows, SUB, SUB, hidden)
@@ -1505,10 +1654,12 @@
         return v.reshape(2, n, SUB, SUB, hidden)
 
     hid, sums_one, gram = expand(x, we_high, we_low)
-    hid, ordered = together(hid, ordered)
+    later = [x]
+    sums_one = shares(sums_one, 1, group, later)
+    [x] = later
+    top, low = rims(x, HALO_IN, band)
     gout = deal(ordered).reshape(nz, nlo, chans, area)
     g_top, g_low = rims(gout, HALO_OUT, band)
-    sums_one = shares(sums_one, 1, group)
     spatial, spatial_halo, hid_halo, sums_two = spread(
         count, side, top, low, as_rows(hid), we_high, we_low, gains, biases, taps, sums_one
     )
@@ -1525,12 +1676,11 @@
     )
     ses = shares(se_part, nlo, nhi)
     ses, g_top, g_low = together(ses, g_top, g_low)
-    q, back_two, values, *w4 = proj_back(
+    q, back_two, values, columns, *w4 = proj_back(
         count, as_bands(spatial), gout, gains, biases, w_project_t, se_weights, ses, sums_two
     )
     backs_two = shares(back_two, 1, group)
     out, g_project = project(proj, x, values, m, s)
-    backs_two, out, g_project = together(backs_two, out, g_project)
     out = deal(out.reshape(frames, chans, area))
     q1, back_one, g_dw = spread_back(
         count,
@@ -1550,31 +1700,40 @@
         sums_two,
         backs_two,
     )
-    backs_one = shares(back_one, 1, group)
+    later = [q1]
+    backs_one = shares(back_one, 1, group, later)
+    [q1] = later
 
     ids = jnp.stack([relative, hi, z_relative]).astype(jnp.int32)
     pieces = weight_grad(
-        ids, n_pix if near(n_pix) else 1, as_bands(q1), x, g_dw, back_one, back_two, values, reduced
+        ids, (2, n_pix // 2) if near(n_pix) else (1, 1), as_bands(q1), x, g_dw, back_one, back_two, values, columns
     )
     if near(n_pix):
         early = lax.psum_scatter(g_project, PIX, scatter_dimension=0, tiled=True)
         gram = lax.psum_scatter(gram, PIX, scatter_dimension=0, tiled=True)
     else:
         early, gram = deal_rows(g_project), deal_rows(gram)
-    q1, out, early, gram, *pieces = together(q1, out, early, gram, *pieces)
-
-    def input_half(half, q1):
-        grad = input_grad(count, half, as_bands(q1), hid, gout, gains, wet_high, wet_low, sums_one, backs_one)
-        return grad.reshape(frames, chans, area // 2)
-
-    grad_one = input_half(0, q1)
+    q1, out, early, gram, moments, *pieces = together(q1, out, early, gram, moments, *pieces)
+
+    def input_part(start, width, q1):
+        grad = input_grad(
+            count, start, width, as_bands(q1), hid, gout, gains, wet_high, wet_low, sums_one, backs_one
+        )
+        return grad.reshape(frames, chans, width)
+
+    most = area // 2
+    grad_one = input_part(0, most, q1)
+    if near(n_pix):
+        pieces = [pieces[0], exchange(pieces[1], 1)]
     grad_one, q1, *pieces = together(grad_one, q1, *pieces)
     if near(n_pix):
-        pieces = [pieces[0]] + [exchange(pieces[i], i) for i in range(1, n_pix)]
-        moments, out, pieces[1] = together(moments, out, pieces[1])
+        pieces = list(merge(*pieces))
+        pieces[0], out = together(pieces[0], out)
+        pieces = [pieces[0]] + [exchange(pieces[i], 2 * i) for i in range(1, n_pix // 2)]
     else:
-        pieces = [jnp.concatenate([deal_rows(pieces[0][:chan_in]), deal_rows(pieces[0][chan_in:])])]
-    grad_two = input_half(1, q1)
+        whole_rows = pieces[0][0]
+        pieces = [jnp.concatenate([deal_rows(whole_rows[:chan_in]), deal_rows(whole_rows[chan_in:])])]
+    grad_two = input_part(most, area - most, q1)
     output = restore(out)
     weights = [
         w_expand,
@@ -1582,7 +1741,7 @@
         norm_gains,
         norm_biases,
         w_project,
-        squeeze_matrix,
+        squeeze_matrix.T,
         se_down_bias[None],
         excite_matrix,
         excite_bias_row[None],
@@ -1591,17 +1750,17 @@
     natural = [list(range(n_pix))]
     base = jnp.zeros((1,), jnp.int32)
     prepared = prepare(base, owners, weights, [moments], natural, block_len)
-    grad_two, output, prepared, *pieces = together(grad_two, output, prepared, *pieces)
+    grad_two, output, *pieces = together(grad_two, output, *pieces)
     groups = collect(count, ids, nz, pieces, early, gram, we_high, we_low, gains, sums_one, backs_one)
     if near(n_pix):
         others = [groups[0]] + [exchange(groups[k], k * n_pix) for k in range(1, nz)]
     else:
         others = list(lax.all_to_all(jnp.stack(groups), "chan", 0, 0, tiled=True))
     grad_one = deal(grad_one)
-    grad_one, grad_two, *others = together(grad_one, grad_two, *others)
+    grad_one, grad_two, *groups = together(grad_one, grad_two, *groups)
     summed = sum(others[1:], others[0])
     grad_two = deal(grad_two)
-    grads, _ = gather_pix(summed)
+    grads, _, prepared = gather_pix(summed, prepared)
     seg_sizes, seg_rates = segments(chan_in, hidden_dev, chans, reduced, TAPS, hidden)
     bounds = [sum(seg_sizes[: i + 1]) for i in range(len(seg_sizes))]
     first_next, second_next, new_params = adam(

time: 356 us -> 316 us (0.89)
  waiting for transfers between devices: 73.5 us -> 57.7 us
  Pallas kernels: 176 us -> 161 us
  starting transfers between devices: 73.7 us -> 67.6 us
    ppermute x36 -> x33, waiting for transfers between devices: 61.7 us -> 32.8 us  [exchange(): return lax.ppermute(x, ALL, [(i, i ^ stride) for i in range(n)])]
    all_to_all x5, waiting for transfers between devices: 11.7 us -> 24.2 us  [deal(): return lax.all_to_all(x, SPREAD, 0, 0, tiled=True)]
    pallas_call x1, Pallas kernels: 49.6 us -> 38.8 us  [spread_back(): pl.pallas_call(partial(spread_back_kernel, len(backs), count), grid=(hidd...]
    all_to_all x5, starting transfers between devices: 40.1 us -> 34.9 us  [deal(): return lax.all_to_all(x, SPREAD, 0, 0, tiled=True)]
    pallas_call x1, Pallas kernels: 27.2 us -> 22.2 us  [spread(): pl.pallas_call(partial(spread_kernel, len(sums), count), grid=(hidden //...]
    unnamed x97 -> x70, local copies, waits for them, and re-layouts: 9.07 us -> 5.44 us
    pallas_call x6 -> x7, Pallas kernels: 47.7 us -> 49.1 us  [the longest x2 13.6 us: input_grad(): pl.pallas_call(partial(input_kernel, len(sums), count, start), grid=(band...]
    ppermute x36 -> x33, starting transfers between devices: 32.9 us -> 32 us  [exchange(): return lax.ppermute(x, ALL, [(i, i ^ stride) for i in range(n)])]
  transfers between devices with their start and end apart: 46 -> 43, of which waited for: 20 -> 16; matrix products, arithmetic and copies ran while one was open for 2% -> 3% of each run, Pallas kernels for 45% -> 49%
where the time goes in v3:
time: 316 us; the launch traced here: 315 us
  Pallas kernels  161 us (51%)
  starting transfers between devices  67.6 us (21%)
  waiting for transfers between devices  57.7 us (18%)
  between operations  14.1 us (4%)
  other arithmetic  8.24 us (3%)
  local copies, waits for them, and re-layouts  6.17 us (2%)
    pallas_call x1, Pallas kernels, spread_back(): pl.pallas_call(partial(spread_back_kernel, len(backs), count), grid=(hidd...  38.8 us
    all_to_all x5, starting transfers between devices, deal(): return lax.all_to_all(x, SPREAD, 0, 0, tiled=True)  34.9 us
    ppermute x33, waiting for transfers between devices, exchange(): return lax.ppermute(x, ALL, [(i, i ^ stride) for i in range(n)])  32.8 us
    ppermute x33, starting transfers between devices, exchange(): return lax.ppermute(x, ALL, [(i, i ^ stride) for i in range(n)])  32 us
    all_to_all x5, waiting for transfers between devices, deal(): return lax.all_to_all(x, SPREAD, 0, 0, tiled=True)  24.2 us
    pallas_call x1, Pallas kernels, spread(): pl.pallas_call(partial(spread_kernel, len(sums), count), grid=(hidden //...  22.2 us
    pallas_call x2, Pallas kernels, input_grad(): pl.pallas_call(partial(input_kernel, len(sums), count, start), grid=(band...  13.6 us
    pallas_call x1, Pallas kernels, proj_back(): pl.pallas_call(partial(proj_back_kernel, len(ses), len(sums), count), gri...  12 us
  transfers between devices with their start and end apart: 43, of which 16 were waited for; matrix products, arithmetic and copies ran while one was open for 3% of the time, Pallas kernels for 49%

profile of v3, /device:TPU:15, one launch (start us, length us, event | category | flops | bytes accessed | tf_op | source)
XLA Modules:
  0.0 314.7 jit_solution(5668569111281231884)
XLA Ops:
  7.2 1.8 pack_weights.1
  9.1 2.3 collective-permute-start.1
  11.6 5.2 %crop.1 = f32[16,64,512]{2,1,0:T(8,128)} custom-call(s32[4]{0:T(128)} %left_ref.3, s32[4]{0:T(128)} %flip_ref.3, f32[16,64,640]{2,1,0:T(8,128)} %raw_ref.1), custom_call_target="tpu_custom_call" | custom-call | flops 5500000256 | bytes 17500000 | tf_op jit(solution)/shard_map/crop/pallas_call | solution.py:193
  17.8 8.3 %all-to-all-start = ((f32[16,64,512]{2,1,0:T(8,128)}), f32[16,64,512]{2,1,0:T(8,128)}, u32[]{:S(2)}, u32[]{:S(2)}) async-start(f32[16,64,512]{2,1,0:T(8,128)} %crop.1), calls=%async_computation | async-start | bytes 4194304 | tf_op jit(solution)/shard_map/all_to_all | solution.py:117
  26.1 4.7 %order.1 = f32[16,64,512]{2,1,0:T(8,128)} custom-call(f32[16,64,512]{2,1,0:T(8,128)} %x_ref.1), custom_call_target="tpu_custom_call" | custom-call | flops 27499999232 | bytes 87500000 | tf_op jit(solution)/shard_map/order/pallas_call | solution.py:218
  31.2 14.4 %collective-permute-done.4 = f32[2,72,1024]{2,1,0:T(8,128)S(1)} collective-permute-done((f32[2,72,1024]{2,1,0:T(8,128)S(1)}, f32[2,72,1024]{2,1,0:T(8,128)S(1)}, u32[]{:S(2)}, u32[]{:S(2)}) %collective-permute-start.4) | collective-permute-done | bytes 589856 | tf_op jit(solution)/shard_map/ppermute | solution.py:96
  45.7 1.2 collective-permute-start.5
  47.5 2.0 collective-permute-done.5.refs_1_
  49.4 4.6 %order_weights.1 = (bf16[256,1024]{1,0:T(8,128)(2,1)}, bf16[256,1024]{1,0:T(8,128)(2,1)}, bf16[1024,256]{1,0:T(8,128)(2,1)}, bf16[1024,256]{1,0:T(8,128)(2,1)}, ...) custom-call(s32[2]{0:T(128)} %pad_add_fusion.base_ref, ...), custom_call_target="tpu_custom_call" | custom-call | flops 3300000000 | bytes 10500000 | tf_op jit(solution)/shard_map/order_weights/pallas_call | solution.py:1295
  54.0 19.6 %all-to-all-done = f32[16,64,512]{2,1,0:T(8,128)} async-done(((f32[16,64,512]{2,1,0:T(8,128)}), f32[16,64,512]{2,1,0:T(8,128)}, u32[]{:S(2)}, u32[]{:S(2)}) %all-to-all-start) | async-done | bytes 2097184 | tf_op jit(solution)/shard_map/all_to_all | solution.py:117
  73.6 4.9 %all-to-all-start.1 = ((f32[16,64,512]{2,1,0:T(8,128)}), f32[16,64,512]{2,1,0:T(8,128)}, u32[]{:S(2)}, u32[]{:S(2)}) async-start(f32[16,64,512]{2,1,0:T(8,128)} %order.1), calls=%async_computation.1 | async-start | bytes 4194304 | tf_op jit(solution)/shard_map/all_to_all | solution.py:117
  78.6 8.2 %expand.1 = (f32[4,512,1024]{2,1,0:T(8,128)}, f32[2,1024]{1,0:T(2,128)}, f32[256,384]{1,0:T(8,128)}) custom-call(f32[4,4,64,512]{3,2,1,0:T(8,128)} %bitcast.7.x_ref, bf16[256,1024]{1,0:T(8,128)(2,1)} %get-tuple-element.114.high_ref, bf16[256,1024]{1,0:T(8,128)(2,1)} %get-tuple-element.115.low_ref.lower_ref), custom_call_target="tpu_custom_call" | custom-call | flops 8800000000 | bytes 28000000 | tf_op jit(solution)/shard_map/expand/pallas_call | solution.py:331
  87.2 1.0 collective-permute-done.6
  88.2 0.7 add.33.rest_0_.rest_4_
  88.9 1.1 slice_select_fusion
  90.3 1.2 collective-permute-start.10
  91.5 1.2 collective-permute-start.8
  94.3 3.7 %collective-permute-done.9.rest_2_.rest_6_ = f32[2,1024]{1,0:T(2,128)S(1)} collective-permute-done((f32[2,1024]{1,0:T(2,128)S(1)}, f32[2,1024]{1,0:T(2,128)S(1)}, u32[]{:S(2)}, u32[]{:S(2)}) %collective-permute-start.9) | collective-permute-done | bytes 8224 | tf_op jit(solution)/shard_map/ppermute | solution.py:96
  98.8 22.2 %spread.1 = (f32[32,8,8,1024]{3,2,1,0:T(8,128)}, f32[2,2,8,8,1024]{4,3,2,1,0:T(8,128)}, f32[2,2,8,8,1024]{4,3,2,1,0:T(8,128)}, f32[2,1024]{1,0:T(2,128)}) custom-call(s32[2]{0:T(128)} %add_convert_fusion.side_ref, f32[4,1,64,256]{3,2,1,0:T(8,128)} %copy-done.15, f32[4,1,64,256]{3,2,1,0:T(8,128)} %copy-done.15, f32[32,8,8,1024]{3,2,1,0:T(8,128)} %bitcast.47, ...), custom_call_target="tpu_custom_call" | custom-call | flops 11000000512 | bytes 35000000 | tf_op jit(solution)/shard_map/spread/pallas_call | solution.py:564
  121.0 0.7 select_maximum_fusion
  121.8 1.1 collective-permute-start.11
  122.9 1.0 collective-permute-done.11
  123.9 0.7 add.34.rest_0_.rest_2_.rest_4_
  125.1 2.2 collective-permute-start.14
  127.3 1.0 slice_select_fusion.1
  129.3 11.6 %gather.1 = (f32[256,1024]{1,0:T(8,128)}, f32[1,1024]{1,0:T(1,128)}, f32[2,256]{1,0:T(2,128)}, f32[4,512,256]{2,1,0:T(8,128)}) custom-call(f32[4,512,1024]{2,1,0:T(8,128)} %bitcast.49, f32[4,4,64,512]{3,2,1,0:T(8,128)} %bitcast.12.gout_ref, f32[2,1024]{1,0:T(2,128)} %get-tuple-element.119.gain_ref, f32[2,1024]{1,0:T(2,128)} %get-tuple-element.120.bias_ref, ...), custom_call_target="tpu_custom_call" | custom-call | flops 14300000256 | bytes 45500000 | tf_op jit(solution)/shard_map/gather/pallas_call | solution.py:638
  140.9 1.3 collective-permute-start.15
  142.2 0.7 copy.25.down_ref
  142.8 1.0 collective-permute-done.15.rest_1_
  144.4 12.0 %proj_back.1 = (f32[4,512,1024]{2,1,0:T(8,128)}, f32[2,1024]{1,0:T(2,128)}, f32[8,256]{1,0:T(8,128)}, f32[16,128]{1,0:T(8,128)}, bf16[256,1024]{1,0:T(8,128)(2,1...) custom-call(f32[4,512,1024]{2,1,0:T(8,128)} %bitcast.50, f32[4,4,64,512]{3,2,1,0:T(8,128)} %bitcast.12.gout_ref, ...), custom_call_target="tpu_custom_call" | custom-call | flops 13200000000 | bytes 42000000 | tf_op jit(solution)/shard_map/proj_back/pallas_call | solution.py:747
  156.4 3.1 collective-permute-start.17
  159.5 1.0 collective-permute-done.17
  160.5 0.7 add.35.rest_8_
  161.2 1.0 collective-permute-start.18
  162.2 1.4 collective-permute-start.19
  163.9 5.5 %project.1 = (f32[4,4,64,512]{3,2,1,0:T(8,128)}, f32[256,1024]{1,0:T(8,128)}) custom-call(f32[4,512,256]{2,1,0:T(8,128)} %get-tuple-element.148.proj_ref, f32[4,4,64,512]{3,2,1,0:T(8,128)} %bitcast.7.x_ref, f32[8,256]{1,0:T(8,128)} %get-tuple-element.149.val_ref, f32[256,1024]{1,0:T(8,128)} %get-tuple-element.150.m_ref, f32[1,1024]{1,0:T(1,128)} %get-tuple-element.151.s_ref), custom_call_target="tpu_custom_call" | custom-call | flops 4400000000 | bytes 14000000 | tf_op jit(solution)/shard_map/project/pallas_call | solution.py:794
  169.4 6.9 %all-to-all-start.2 = ((f32[16,64,512]{2,1,0:T(8,128)}), f32[16,64,512]{2,1,0:T(8,128)}, u32[]{:S(2)}, u32[]{:S(2)}) async-start(f32[16,64,512]{2,1,0:T(8,128)} %bitcast.33), calls=%async_computation.2 | async-start | bytes 4194304 | tf_op jit(solution)/shard_map/all_to_all | solution.py:117
  176.3 0.7 reduce-scatter.3.cloned.1.call-update
  177.7 38.8 %spread_back.1 = (f32[32,8,8,1024]{3,2,1,0:T(8,128)}, f32[2,1024]{1,0:T(2,128)}, f32[25,1024]{1,0:T(8,128)}) custom-call(s32[2]{0:T(128)} %add_convert_fusion.side_ref, f32[4,1,64,128]{3,2,1,0:T(8,128)} %copy-done.19, f32[4,1,64,128]{3,2,1,0:T(8,128)} %copy-done.19, f32[32,8,8,1024]{3,2,1,0:T(8,128)} %bitcast.48, ...), custom_call_target="tpu_custom_call" | custom-call | flops 165000003584 | bytes 525000000 | tf_op jit(solution)/shard_map/spread_back/pallas_call | solution.py:943
  217.9 0.7 add.36.rest_4_.rest_8_
  218.9 1.1 collective-permute-start.23
  220.0 1.3 collective-permute-start.24
  221.3 8.0 %weight_grad.1 = (f32[4,40,1024]{2,1,0:T(8,128)}, f32[4,40,1024]{2,1,0:T(8,128)}) custom-call(s32[3]{0:T(128)} %pad_add_fusion.1.ids_ref, f32[4,512,1024]{2,1,0:T(8,128)} %bitcast.51, f32[4,4,64,512]{3,2,1,0:T(8,128)} %bitcast.7.x_ref, f32[25,1024]{1,0:T(8,128)} %get-tuple-element.157.tap_ref, f32[2,1024]{1,0:T(2,128)} %get-tuple-element.145.one_ref, ...), custom_call_target="tpu_custom_call" | custom-call | flops 7699999744 | bytes 24500000 | tf_op jit(solution)/shard_map/weight_grad/pallas_call | solution.py:1068
  229.4 1.2 collective-permute-start.25
  231.3 6.8 %input_grad.2 = f32[4,4,64,256]{3,2,1,0:T(8,128)} custom-call(f32[4,512,1024]{2,1,0:T(8,128)} %bitcast.52, f32[4,512,1024]{2,1,0:T(8,128)} %get-tuple-element.118.hid_ref, f32[4,4,64,512]{3,2,1,0:T(8,128)} %bitcast.12.gout_ref, f32[2,1024]{1,0:T(2,128)} %get-tuple-element.119.gain_ref, bf16[1024,256]{1,0:T(8,128)(2,1)} %get-tuple-element.162.w_high, ...), custom_call_target="tpu_custom_call" | custom-call | flops 13200000000 | bytes 42000000 | tf_op jit(solution)/shard_map/input_grad/pallas_call | solution.py:998
  238.1 5.8 %all-to-all-start.3 = ((f32[16,64,256]{2,1,0:T(8,128)}), f32[16,64,256]{2,1,0:T(8,128)S(1)}, u32[]{:S(2)}, u32[]{:S(2)}) async-start(f32[16,64,256]{2,1,0:T(8,128)} %bitcast.35), calls=%async_computation.5 | async-start | bytes 2097152 | tf_op jit(solution)/shard_map/all_to_all | solution.py:117
  243.9 2.2 merge.1
  246.3 1.1 collective-permute-start.27
  247.4 1.3 collective-permute-start.28
  248.7 6.8 %input_grad.3 = f32[4,4,64,256]{3,2,1,0:T(8,128)} custom-call(f32[4,512,1024]{2,1,0:T(8,128)} %bitcast.53, f32[4,512,1024]{2,1,0:T(8,128)} %get-tuple-element.118.hid_ref, f32[4,4,64,512]{3,2,1,0:T(8,128)} %bitcast.12.gout_ref, f32[2,1024]{1,0:T(2,128)} %get-tuple-element.119.gain_ref, bf16[1024,256]{1,0:T(8,128)(2,1)} %get-tuple-element.162.w_high, ...), custom_call_target="tpu_custom_call" | custom-call | flops 13200000000 | bytes 42000000 | tf_op jit(solution)/shard_map/input_grad/pallas_call | solution.py:998
  255.5 4.8 %restore.1 = f32[16,64,512]{2,1,0:T(8,128)} custom-call(f32[16,64,512]{2,1,0:T(8,128)} %all-to-all-done.2.x_ref), custom_call_target="tpu_custom_call" | custom-call | flops 1100000000 | bytes 3500000 | tf_op jit(solution)/shard_map/restore/pallas_call | solution.py:239
  261.1 2.6 collect.1
  263.7 3.0 collective-permute-start.29
  267.1 0.9 collective-permute-start.31
  268.0 0.8 copy.27.col_ref
  268.8 9.0 %all-to-all-start.4 = ((f32[16,64,256]{2,1,0:T(8,128)}), f32[16,64,256]{2,1,0:T(8,128)}, u32[]{:S(2)}, u32[]{:S(2)}) async-start(f32[16,64,256]{2,1,0:T(8,128)} %bitcast.34), calls=%async_computation.6 | async-start | bytes 2097152 | tf_op jit(solution)/shard_map/all_to_all | solution.py:117
  278.2 4.7 %prepare.1 = (f32[138,1024]{1,0:T(8,128)}, f32[138,1024]{1,0:T(8,128)}, f32[138,1024]{1,0:T(8,128)}) custom-call(s32[1]{0:T(128)} %constant.21.clone.1.base_ref, s32[138,1]{1,0:T(8,128)} %copy.27.col_ref, f32[256,256]{1,0:T(8,128)} %we_ref.3, f32[25,256]{1,0:T(8,128)} %dw_ref.3, f32[2,256]{1,0:T(2,128)} %gain_ref.3, f32[2,256]{1,0:T(2,128)} %bias_ref.3, ...), custom_call_target="tpu_custom_call" | custom-call | flops 1100000000 | bytes 3500000 | tf_op jit(solution)/shard_map/prepare/pallas_call | solution.py:1442
  282.9 2.1 collective-permute-done.32
  285.4 4.2 %collective-permute-done.33 = f32[2,72,256]{2,1,0:T(8,128)S(1)} collective-permute-done((f32[2,72,256]{2,1,0:T(8,128)S(1)}, f32[2,72,256]{2,1,0:T(8,128)S(1)}, u32[]{:S(2)}, u32[]{:S(2)}) %collective-permute-start.33) | collective-permute-done | bytes 147488 | tf_op jit(solution)/shard_map/ppermute | solution.py:96
  289.6 1.7 collective-permute-start.34
  292.6 0.7 copy-done.14
  293.3 4.9 %adam.1 = (f32[26,1,1024]{2,1,0:T(1,128)}, f32[26,1,1024]{2,1,0:T(1,128)}, f32[1,140624]{1,0:T(1,128)}) custom-call(s32[2]{0:T(128)} %pad_add_fusion.2.me_ref, s32[138,1]{1,0:T(8,128)} %copy.27.col_ref, f32[138,1024]{1,0:T(8,128)} %get-tuple-element.196.weight_ref, f32[138,1024]{1,0:T(8,128)} %get-tuple-element.197.old_one_ref, ...), custom_call_target="tpu_custom_call" | custom-call | flops 11000000512 | bytes 35000000 | tf_op jit(solution)/shard_map/adam/pallas_call | solution.py:1540
  298.2 4.5 %all-to-all-done.4.y_ref = f32[16,64,256]{2,1,0:T(8,128)} async-done(((f32[16,64,256]{2,1,0:T(8,128)}), f32[16,64,256]{2,1,0:T(8,128)}, u32[]{:S(2)}, u32[]{:S(2)}) %all-to-all-start.4) | async-done | bytes 1048608 | tf_op jit(solution)/shard_map/all_to_all | solution.py:117
  302.8 5.4 %uncrop.1 = f32[16,64,640]{2,1,0:T(8,128)} custom-call(s32[4]{0:T(128)} %left_ref.3, s32[4]{0:T(128)} %flip_ref.3, f32[16,64,256]{2,1,0:T(8,128)} %copy-done, f32[16,64,256]{2,1,0:T(8,128)} %all-to-all-done.4.y_ref), custom_call_target="tpu_custom_call" | custom-call | flops 1100000000 | bytes 3500000 | tf_op jit(solution)/shard_map/uncrop/pallas_call | solution.py:268
  (132 shorter events, 14.2 us)
Async XLA Ops:
  9.0 8.5 %copy-start.4 = (f32[72,256]{1,0:T(8,128)S(1)}, f32[72,256]{1,0:T(8,128)}, u32[]{:S(2)}) copy-start(f32[72,256]{1,0:T(8,128)} %pack_weights.1) | copy-start | bytes 221188
  9.0 7.9 %collective-permute-start = (f32[72,256]{1,0:T(8,128)}, f32[72,256]{1,0:T(8,128)S(1)}, u32[]{:S(2)}, u32[]{:S(2)}) collective-permute-start(f32[72,256]{1,0:T(8,128)} %pack_weights.1), channel_id=1, source_target_pairs={{0,8},{1,9},{2,10},{3,11},{4,12},{5,13},{6,14},{7,15},{8,0},{9,1},... | collective-permute-start | bytes 221192 | tf_op jit(solution)/shard_map/ppermute | solution.py:96
  9.1 7.7 %collective-permute-start.1 = (f32[72,256]{1,0:T(8,128)}, f32[72,256]{1,0:T(8,128)S(1)}, u32[]{:S(2)}, u32[]{:S(2)}) collective-permute-start(f32[72,256]{1,0:T(8,128)} %pack_weights.1), channel_id=1, source_target_pairs={{0,16},{1,17},{2,18},{3,19},{4,20},{5,21},{6,22},{7,23},{8,24},{9,... | collective-permute-start | bytes 221192 | tf_op jit(solution)/shard_map/ppermute | solution.py:96
  11.4 6.0 %collective-permute-start.2 = (f32[72,256]{1,0:T(8,128)}, f32[72,256]{1,0:T(8,128)S(1)}, u32[]{:S(2)}, u32[]{:S(2)}) collective-permute-start(f32[72,256]{1,0:T(8,128)} %pack_weights.1), channel_id=1, source_target_pairs={{0,24},{1,25},{2,26},{3,27},{4,28},{5,29},{6,30},{7,31},{8,16},{9,... | collective-permute-start | bytes 221192 | tf_op jit(solution)/shard_map/ppermute | solution.py:96
  17.5 13.4 %collective-permute-start.3 = (f32[1,72,1024]{2,1,0:T(8,128)S(1)}, f32[1,72,1024]{2,1,0:T(8,128)S(1)}, u32[]{:S(2)}, u32[]{:S(2)}) collective-permute-start(f32[1,72,1024]{2,1,0:T(8,128)S(1)} %maximum_bitcast_fusion), channel_id=1, source_target_pairs={{0,2},{1,3},{2,0},{3,1},{4,6},{5,7},{6,4},{7,5},{8,10},{9,11},{10,... | collective-permute-start | bytes 884744 | tf_op jit(solution)/shard_map/ppermute | solution.py:96
  17.8 55.9 %all-to-all-start = ((f32[16,64,512]{2,1,0:T(8,128)}), f32[16,64,512]{2,1,0:T(8,128)}, u32[]{:S(2)}, u32[]{:S(2)}) async-start(f32[16,64,512]{2,1,0:T(8,128)} %crop.1), calls=%async_computation | async-start | bytes 4194304 | tf_op jit(solution)/shard_map/all_to_all | solution.py:117
  30.9 14.7 %collective-permute-start.4 = (f32[2,72,1024]{2,1,0:T(8,128)S(1)}, f32[2,72,1024]{2,1,0:T(8,128)S(1)}, u32[]{:S(2)}, u32[]{:S(2)}) collective-permute-start(f32[2,72,1024]{2,1,0:T(8,128)S(1)} %pad_maximum_fusion), channel_id=1, source_target_pairs={{0,4},{1,5},{2,6},{3,7},{4,0},{5,1},{6,2},{7,3},{8,12},{9,13},{10,... | collective-permute-start | bytes 1769480 | tf_op jit(solution)/shard_map/ppermute | solution.py:96
  45.7 3.8 %copy-start.1 = (f32[4,72,1024]{2,1,0:T(8,128)}, f32[4,72,1024]{2,1,0:T(8,128)S(1)}, u32[]{:S(2)}) copy-start(f32[4,72,1024]{2,1,0:T(8,128)S(1)} %constant_dynamic-update-slice_fusion.refs_0_) | copy-start | bytes 3538948
  45.7 3.8 %collective-permute-start.5 = (f32[4,72,1024]{2,1,0:T(8,128)S(1)}, f32[4,72,1024]{2,1,0:T(8,128)}, u32[]{:S(2)}, u32[]{:S(2)}) collective-permute-start(f32[4,72,1024]{2,1,0:T(8,128)S(1)} %constant_dynamic-update-slice_fusion.refs_0_), channel_id=1, source_target_pairs={{0,1},{1,0},{2,3},{3,2},{4,5},{5,4},{6,7},{7,6},{8,9},{9,8},{10,11... | collective-permute-start | bytes 3538952 | tf_op jit(solution)/shard_map/ppermute | solution.py:96
  73.6 53.7 %all-to-all-start.1 = ((f32[16,64,512]{2,1,0:T(8,128)}), f32[16,64,512]{2,1,0:T(8,128)}, u32[]{:S(2)}, u32[]{:S(2)}) async-start(f32[16,64,512]{2,1,0:T(8,128)} %order.1), calls=%async_computation.1 | async-start | bytes 4194304 | tf_op jit(solution)/shard_map/all_to_all | solution.py:117
  78.5 150.8 %reduce-scatter.5.cloned.1.call-start = ((), (), s32[]{:S(2)}) async-start(), calls=%async_computation.8 | async-start | bytes 442368 | tf_op jit(solution)/shard_map/reduce_scatter | solution.py:1713
  86.8 1.4 collective-permute-start.6
  88.9 9.2 %copy-start.7 = (f32[2,1024]{1,0:T(2,128)}, f32[2,1024]{1,0:T(2,128)S(1)}, u32[]{:S(2)}) copy-start(f32[2,1024]{1,0:T(2,128)S(1)} %add.33.rest_0_.rest_4_) | copy-start | bytes 24580
  90.0 8.1 %collective-permute-start.7 = (f32[4,1,64,256]{3,2,1,0:T(8,128)S(1)}, f32[4,1,64,256]{3,2,1,0:T(8,128)S(1)}, u32[]{:S(2)}, u32[]{:S(2)}) collective-permute-start(f32[4,1,64,256]{3,2,1,0:T(8,128)S(1)} %slice_select_fusion), channel_id=1, source_target_pairs={{0,4},{4,0},{1,5},{5,1},{2,6},{6,2},{3,7},{7,3},{8,12},{12,8},{9,1... | collective-permute-start | bytes 786440 | tf_op jit(solution)/shard_map/ppermute | solution.py:132
  90.3 3.7 %collective-permute-start.10 = (f32[2,1024]{1,0:T(2,128)S(1)}, f32[2,1024]{1,0:T(2,128)S(1)}, u32[]{:S(2)}, u32[]{:S(2)}) collective-permute-start(f32[2,1024]{1,0:T(2,128)S(1)} %add.33.rest_0_.rest_4_), channel_id=1, source_target_pairs={{0,6},{1,7},{2,4},{3,5},{4,2},{5,3},{6,0},{7,1},{8,14},{9,15},{10,... | collective-permute-start | bytes 24584 | tf_op jit(solution)/shard_map/ppermute | solution.py:96
  91.5 2.8 collective-permute-start.8
  92.7 5.4 %collective-permute-start.9 = (f32[2,1024]{1,0:T(2,128)S(1)}, f32[2,1024]{1,0:T(2,128)S(1)}, u32[]{:S(2)}, u32[]{:S(2)}) collective-permute-start(f32[2,1024]{1,0:T(2,128)S(1)} %add.33.rest_0_.rest_4_), channel_id=1, source_target_pairs={{0,4},{1,5},{2,6},{3,7},{4,0},{5,1},{6,2},{7,3},{8,12},{9,13},{10,... | collective-permute-start | bytes 24584 | tf_op jit(solution)/shard_map/ppermute | solution.py:96
  93.6 135.8 %all-gather.3.cloned.1.call-start = ((), (), s32[]{:S(2)}) async-start(), calls=%async_computation.9 | async-start | bytes 2359296 | tf_op jit(solution)/shard_map/all_gather | solution.py:1672
  94.0 4.1 %copy-start.20 = (f32[2,1024]{1,0:T(2,128)}, f32[2,1024]{1,0:T(2,128)S(1)}, u32[]{:S(2)}) copy-start(f32[2,1024]{1,0:T(2,128)S(1)} %collective-permute-done.10.rest_3_.rest_7_) | copy-start | bytes 24580
  94.3 3.8 %copy-start.21 = (f32[2,1024]{1,0:T(2,128)}, f32[2,1024]{1,0:T(2,128)S(1)}, u32[]{:S(2)}) copy-start(f32[2,1024]{1,0:T(2,128)S(1)} %collective-permute-done.8.rest_1_.rest_5_) | copy-start | bytes 24580
  98.0 0.7 copy-start.15
  98.8 22.2 %copy-start.2 = (f32[1,26,1024]{2,0,1:T(1,128)S(1)}, f32[1,26,1024]{2,0,1:T(1,128)}, u32[]{:S(2)}) copy-start(f32[1,26,1024]{2,0,1:T(1,128)} %param.31) | copy-start | bytes 319492
  98.8 22.2 %copy-start.3 = (f32[1,26,1024]{2,0,1:T(1,128)S(1)}, f32[1,26,1024]{2,0,1:T(1,128)}, u32[]{:S(2)}) copy-start(f32[1,26,1024]{2,0,1:T(1,128)} %param.30) | copy-start | bytes 319492
  121.8 2.2 collective-permute-start.11
  124.6 4.0 %copy-start.8 = (f32[2,1024]{1,0:T(2,128)}, f32[2,1024]{1,0:T(2,128)S(1)}, u32[]{:S(2)}) copy-start(f32[2,1024]{1,0:T(2,128)S(1)} %add.34.rest_0_.rest_2_.rest_4_) | copy-start | bytes 24580
  124.6 3.9 %collective-permute-start.12 = (f32[2,1024]{1,0:T(2,128)S(1)}, f32[2,1024]{1,0:T(2,128)S(1)}, u32[]{:S(2)}, u32[]{:S(2)}) collective-permute-start(f32[2,1024]{1,0:T(2,128)S(1)} %add.34.rest_0_.rest_2_.rest_4_), channel_id=1, source_target_pairs={{0,2},{1,3},{2,0},{3,1},{4,6},{5,7},{6,4},{7,5},{8,10},{9,11},{10,... | collective-permute-start | bytes 24584 | tf_op jit(solution)/shard_map/ppermute | solution.py:96
  124.9 3.7 %collective-permute-start.13 = (f32[2,1024]{1,0:T(2,128)S(1)}, f32[2,1024]{1,0:T(2,128)S(1)}, u32[]{:S(2)}, u32[]{:S(2)}) collective-permute-start(f32[2,1024]{1,0:T(2,128)S(1)} %add.34.rest_0_.rest_2_.rest_4_), channel_id=1, source_target_pairs={{0,4},{1,5},{2,6},{3,7},{4,0},{5,1},{6,2},{7,3},{8,12},{9,13},{10,... | collective-permute-start | bytes 24584 | tf_op jit(solution)/shard_map/ppermute | solution.py:96
  125.1 3.5 %collective-permute-start.14 = (f32[2,1024]{1,0:T(2,128)S(1)}, f32[2,1024]{1,0:T(2,128)S(1)}, u32[]{:S(2)}, u32[]{:S(2)}) collective-permute-start(f32[2,1024]{1,0:T(2,128)S(1)} %add.34.rest_0_.rest_2_.rest_4_), channel_id=1, source_target_pairs={{0,6},{1,7},{2,4},{3,5},{4,2},{5,3},{6,0},{7,1},{8,14},{9,15},{10,... | collective-permute-start | bytes 24584 | tf_op jit(solution)/shard_map/ppermute | solution.py:96
  128.3 15.5 %collective-permute-start.16 = (f32[4,1,64,128]{3,2,1,0:T(8,128)S(1)}, f32[4,1,64,128]{3,2,1,0:T(8,128)S(1)}, u32[]{:S(2)}, u32[]{:S(2)}) collective-permute-start(f32[4,1,64,128]{3,2,1,0:T(8,128)S(1)} %slice_select_fusion.1), channel_id=1, source_target_pairs={{0,4},{4,0},{1,5},{5,1},{2,6},{6,2},{3,7},{7,3},{8,12},{12,8},{9,1... | collective-permute-start | bytes 393224 | tf_op jit(solution)/shard_map/ppermute | solution.py:132
  129.2 12.9 %copy-start.12 = (f32[16]{0:T(128)S(1)}, f32[16]{0:T(128)}, u32[]{:S(2)}) copy-start(f32[16]{0:T(128)} %param.27) | copy-start | bytes 196
  140.9 2.9 collective-permute-start.15
  143.8 12.6 %copy-start.19 = (f32[4,1,64,128]{3,2,1,0:T(8,128)}, f32[4,1,64,128]{3,2,1,0:T(8,128)S(1)}, u32[]{:S(2)}) copy-start(f32[4,1,64,128]{3,2,1,0:T(8,128)S(1)} %collective-permute-done.16.top_ref.low_ref) | copy-start | bytes 393220
  156.4 4.1 %collective-permute-start.17 = (f32[2,1024]{1,0:T(2,128)}, f32[2,1024]{1,0:T(2,128)S(1)}, u32[]{:S(2)}, u32[]{:S(2)}) collective-permute-start(f32[2,1024]{1,0:T(2,128)} %get-tuple-element.144.two_ref), channel_id=1, source_target_pairs={{0,1},{1,0},{2,3},{3,2},{4,5},{5,4},{6,7},{7,6},{8,9},{9,8},{10,11... | collective-permute-start | bytes 24584 | tf_op jit(solution)/shard_map/ppermute | solution.py:96
  161.2 8.1 %copy-start.10 = (f32[2,1024]{1,0:T(2,128)}, f32[2,1024]{1,0:T(2,128)S(1)}, u32[]{:S(2)}) copy-start(f32[2,1024]{1,0:T(2,128)S(1)} %add.35.rest_8_) | copy-start | bytes 24580
  161.2 15.8 %collective-permute-start.18 = (f32[2,1024]{1,0:T(2,128)S(1)}, f32[2,1024]{1,0:T(2,128)S(1)}, u32[]{:S(2)}, u32[]{:S(2)}) collective-permute-start(f32[2,1024]{1,0:T(2,128)S(1)} %add.35.rest_8_), channel_id=1, source_target_pairs={{0,2},{1,3},{2,0},{3,1},{4,6},{5,7},{6,4},{7,5},{8,10},{9,11},{10,... | collective-permute-start | bytes 24584 | tf_op jit(solution)/shard_map/ppermute | solution.py:96
  162.2 14.8 %collective-permute-start.19 = (f32[2,1024]{1,0:T(2,128)S(1)}, f32[2,1024]{1,0:T(2,128)S(1)}, u32[]{:S(2)}, u32[]{:S(2)}) collective-permute-start(f32[2,1024]{1,0:T(2,128)S(1)} %add.35.rest_8_), channel_id=1, source_target_pairs={{0,4},{1,5},{2,6},{3,7},{4,0},{5,1},{6,2},{7,3},{8,12},{9,13},{10,... | collective-permute-start | bytes 24584 | tf_op jit(solution)/shard_map/ppermute | solution.py:96
  163.6 13.5 %collective-permute-start.20 = (f32[2,1024]{1,0:T(2,128)S(1)}, f32[2,1024]{1,0:T(2,128)S(1)}, u32[]{:S(2)}, u32[]{:S(2)}) collective-permute-start(f32[2,1024]{1,0:T(2,128)S(1)} %add.35.rest_8_), channel_id=1, source_target_pairs={{0,6},{1,7},{2,4},{3,5},{4,2},{5,3},{6,0},{7,1},{8,14},{9,15},{10,... | collective-permute-start | bytes 24584 | tf_op jit(solution)/shard_map/ppermute | solution.py:96
  169.4 60.0 %all-to-all-start.2 = ((f32[16,64,512]{2,1,0:T(8,128)}), f32[16,64,512]{2,1,0:T(8,128)}, u32[]{:S(2)}, u32[]{:S(2)}) async-start(f32[16,64,512]{2,1,0:T(8,128)} %bitcast.33), calls=%async_computation.2 | async-start | bytes 4194304 | tf_op jit(solution)/shard_map/all_to_all | solution.py:117
  176.3 53.1 %reduce-scatter.3.cloned.1.call-start = ((), (), s32[]{:S(2)}) async-start(), calls=%async_computation.7 | async-start | bytes 1179648 | tf_op jit(solution)/shard_map/reduce_scatter | solution.py:1712
  216.5 1.5 collective-permute-start.21
  218.6 10.7 %copy-start.9 = (f32[2,1024]{1,0:T(2,128)}, f32[2,1024]{1,0:T(2,128)S(1)}, u32[]{:S(2)}) copy-start(f32[2,1024]{1,0:T(2,128)S(1)} %add.36.rest_4_.rest_8_) | copy-start | bytes 24580
  218.6 12.0 %collective-permute-start.22 = (f32[2,1024]{1,0:T(2,128)S(1)}, f32[2,1024]{1,0:T(2,128)S(1)}, u32[]{:S(2)}, u32[]{:S(2)}) collective-permute-start(f32[2,1024]{1,0:T(2,128)S(1)} %add.36.rest_4_.rest_8_), channel_id=1, source_target_pairs={{0,2},{1,3},{2,0},{3,1},{4,6},{5,7},{6,4},{7,5},{8,10},{9,11},{10,... | collective-permute-start | bytes 24584 | tf_op jit(solution)/shard_map/ppermute | solution.py:96
  218.9 11.7 %collective-permute-start.23 = (f32[2,1024]{1,0:T(2,128)S(1)}, f32[2,1024]{1,0:T(2,128)S(1)}, u32[]{:S(2)}, u32[]{:S(2)}) collective-permute-start(f32[2,1024]{1,0:T(2,128)S(1)} %add.36.rest_4_.rest_8_), channel_id=1, source_target_pairs={{0,4},{1,5},{2,6},{3,7},{4,0},{5,1},{6,2},{7,3},{8,12},{9,13},{10,... | collective-permute-start | bytes 24584 | tf_op jit(solution)/shard_map/ppermute | solution.py:96
  220.0 10.7 %collective-permute-start.24 = (f32[2,1024]{1,0:T(2,128)S(1)}, f32[2,1024]{1,0:T(2,128)S(1)}, u32[]{:S(2)}, u32[]{:S(2)}) collective-permute-start(f32[2,1024]{1,0:T(2,128)S(1)} %add.36.rest_4_.rest_8_), channel_id=1, source_target_pairs={{0,6},{1,7},{2,4},{3,5},{4,2},{5,3},{6,0},{7,1},{8,14},{9,15},{10,... | collective-permute-start | bytes 24584 | tf_op jit(solution)/shard_map/ppermute | solution.py:96
  229.4 8.7 %collective-permute-start.25 = (f32[4,40,1024]{2,1,0:T(8,128)}, f32[4,40,1024]{2,1,0:T(8,128)S(1)}, u32[]{:S(2)}, u32[]{:S(2)}) collective-permute-start(f32[4,40,1024]{2,1,0:T(8,128)} %get-tuple-element.166), channel_id=1, source_target_pairs={{0,1},{1,0},{2,3},{3,2},{4,5},{5,4},{6,7},{7,6},{8,9},{9,8},{10,11... | collective-permute-start | bytes 1966088 | tf_op jit(solution)/shard_map/ppermute | solution.py:96
  238.1 5.8 %copy-start.13 = (f32[4,40,1024]{2,1,0:T(8,128)}, f32[4,40,1024]{2,1,0:T(8,128)S(1)}, u32[]{:S(2)}) copy-start(f32[4,40,1024]{2,1,0:T(8,128)S(1)} %collective-permute-done.25.two_ref) | copy-start | bytes 1966084
  238.1 30.7 %all-to-all-start.3 = ((f32[16,64,256]{2,1,0:T(8,128)}), f32[16,64,256]{2,1,0:T(8,128)S(1)}, u32[]{:S(2)}, u32[]{:S(2)}) async-start(f32[16,64,256]{2,1,0:T(8,128)} %bitcast.35), calls=%async_computation.5 | async-start | bytes 2097152 | tf_op jit(solution)/shard_map/all_to_all | solution.py:117
  246.0 14.3 %collective-permute-start.26 = (f32[40,1024]{1,0:T(8,128)}, f32[40,1024]{1,0:T(8,128)S(1)}, u32[]{:S(2)}, u32[]{:S(2)}) collective-permute-start(f32[40,1024]{1,0:T(8,128)} %get-tuple-element.174), channel_id=1, source_target_pairs={{0,2},{1,3},{2,0},{3,1},{4,6},{5,7},{6,4},{7,5},{8,10},{9,11},{10,... | collective-permute-start | bytes 491528 | tf_op jit(solution)/shard_map/ppermute | solution.py:96
  246.3 14.0 %collective-permute-start.27 = (f32[40,1024]{1,0:T(8,128)}, f32[40,1024]{1,0:T(8,128)S(1)}, u32[]{:S(2)}, u32[]{:S(2)}) collective-permute-start(f32[40,1024]{1,0:T(8,128)} %get-tuple-element.175), channel_id=1, source_target_pairs={{0,4},{1,5},{2,6},{3,7},{4,0},{5,1},{6,2},{7,3},{8,12},{9,13},{10,... | collective-permute-start | bytes 491528 | tf_op jit(solution)/shard_map/ppermute | solution.py:96
  247.4 12.9 %collective-permute-start.28 = (f32[40,1024]{1,0:T(8,128)}, f32[40,1024]{1,0:T(8,128)S(1)}, u32[]{:S(2)}, u32[]{:S(2)}) collective-permute-start(f32[40,1024]{1,0:T(8,128)} %get-tuple-element.176), channel_id=1, source_target_pairs={{0,6},{1,7},{2,4},{3,5},{4,2},{5,3},{6,0},{7,1},{8,14},{9,15},{10,... | collective-permute-start | bytes 491528 | tf_op jit(solution)/shard_map/ppermute | solution.py:96
  260.3 0.7 copy-start.17
  260.3 0.8 copy-start.18
  261.1 6.9 %copy-start.11 = (s32[138,1]{0,1:T(1,128)S(1)}, s32[138,1]{0,1:T(1,128)}, u32[]{:S(2)}) copy-start(s32[138,1]{0,1:T(1,128)} %param.20) | copy-start | bytes 1660
  263.7 14.1 %copy-start.6 = (f32[72,256]{1,0:T(8,128)S(1)}, f32[72,256]{1,0:T(8,128)}, u32[]{:S(2)}) copy-start(f32[72,256]{1,0:T(8,128)} %get-tuple-element.186) | copy-start | bytes 221188
  263.7 14.0 %collective-permute-start.29 = (f32[72,256]{1,0:T(8,128)}, f32[72,256]{1,0:T(8,128)S(1)}, u32[]{:S(2)}, u32[]{:S(2)}) collective-permute-start(f32[72,256]{1,0:T(8,128)} %get-tuple-element.187), channel_id=1, source_target_pairs={{0,8},{1,9},{2,10},{3,11},{4,12},{5,13},{6,14},{7,15},{8,0},{9,1},... | collective-permute-start | bytes 221192 | tf_op jit(solution)/shard_map/ppermute | solution.py:96
  266.7 11.1 %collective-permute-start.30 = (f32[72,256]{1,0:T(8,128)}, f32[72,256]{1,0:T(8,128)S(1)}, u32[]{:S(2)}, u32[]{:S(2)}) collective-permute-start(f32[72,256]{1,0:T(8,128)} %get-tuple-element.188), channel_id=1, source_target_pairs={{0,16},{1,17},{2,18},{3,19},{4,20},{5,21},{6,22},{7,23},{8,24},{9,... | collective-permute-start | bytes 221192 | tf_op jit(solution)/shard_map/ppermute | solution.py:96
  267.1 10.7 %collective-permute-start.31 = (f32[72,256]{1,0:T(8,128)}, f32[72,256]{1,0:T(8,128)S(1)}, u32[]{:S(2)}, u32[]{:S(2)}) collective-permute-start(f32[72,256]{1,0:T(8,128)} %get-tuple-element.189), channel_id=1, source_target_pairs={{0,24},{1,25},{2,26},{3,27},{4,28},{5,29},{6,30},{7,31},{8,16},{9,... | collective-permute-start | bytes 221192 | tf_op jit(solution)/shard_map/ppermute | solution.py:96
  268.7 14.1 %copy-start = (f32[16,64,256]{2,1,0:T(8,128)}, f32[16,64,256]{2,1,0:T(8,128)S(1)}, u32[]{:S(2)}) copy-start(f32[16,64,256]{2,1,0:T(8,128)S(1)} %all-to-all-done.3.x_ref) | copy-start | bytes 3145732
  268.8 34.0 %all-to-all-start.4 = ((f32[16,64,256]{2,1,0:T(8,128)}), f32[16,64,256]{2,1,0:T(8,128)}, u32[]{:S(2)}, u32[]{:S(2)}) async-start(f32[16,64,256]{2,1,0:T(8,128)} %bitcast.34), calls=%async_computation.6 | async-start | bytes 2097152 | tf_op jit(solution)/shard_map/all_to_all | solution.py:117
  277.8 7.1 %collective-permute-start.32 = (f32[1,72,256]{2,1,0:T(8,128)S(1)}, f32[1,72,256]{2,1,0:T(8,128)S(1)}, u32[]{:S(2)}, u32[]{:S(2)}) collective-permute-start(f32[1,72,256]{2,1,0:T(8,128)S(1)} %add_bitcast_fusion), channel_id=1, source_target_pairs={{0,2},{1,3},{2,0},{3,1},{4,6},{5,7},{6,4},{7,5},{8,10},{9,11},{10,... | collective-permute-start | bytes 221192 | tf_op jit(solution)/shard_map/ppermute | solution.py:96
  284.9 4.7 %collective-permute-start.33 = (f32[2,72,256]{2,1,0:T(8,128)S(1)}, f32[2,72,256]{2,1,0:T(8,128)S(1)}, u32[]{:S(2)}, u32[]{:S(2)}) collective-permute-start(f32[2,72,256]{2,1,0:T(8,128)S(1)} %pad_maximum_fusion.1), channel_id=1, source_target_pairs={{0,4},{1,5},{2,6},{3,7},{4,0},{5,1},{6,2},{7,3},{8,12},{9,13},{10,... | collective-permute-start | bytes 442376 | tf_op jit(solution)/shard_map/ppermute | solution.py:96
  289.6 2.9 copy-start.5
  289.6 2.9 collective-permute-start.34
  292.6 0.7 copy-start.14
  (12 other events, 7.2 us)
Sparse Core Ops, SparseCore 0:
  93.7 36.6 reduce-scatter.4
  132.3 28.5 all-gather.2
  180.3 38.3 reduce-scatter.2

commit v4 on v3

--- a/solution.py
+++ b/solution.py
@@ -445,16 +445,18 @@
 
 
 def raise_all(pad, first, raised):
-    def one(g, _):
-        for c in range(SUB):
-            d = [pad[first + GROUP * g + k, c + 2] for k in range(2 * GROUP)]
-            for p, value in enumerate(raise_rows(d)):
-                raised[g, p, c + 2] = value
-        for p in range(POINTS):
-            fill_sides(raised.at[g], p)
+    def two(i, _):
+        for k in range(2):
+            g = 2 * i + k
+            for c in range(SUB):
+                d = [pad[first + GROUP * g + n, c + 2] for n in range(2 * GROUP)]
+                for p, value in enumerate(raise_rows(d)):
+                    raised[g, p, c + 2] = value
+            for p in range(POINTS):
+                fill_sides(raised.at[g], p)
         return 0
 
-    lax.fori_loop(0, raised.shape[0], one, 0)
+    lax.fori_loop(0, raised.shape[0] // 2, two, 0)
 
 
 def raise_taps(w_ref, taps, flipped=False, scale=1.0):
@@ -686,9 +688,13 @@
     count,
     own_ref,
     gout_ref,
+    proj_ref,
+    x_ref,
     gain_ref,
     bias_ref,
     wt_ref,
+    m_ref,
+    s_ref,
     sqt_ref,
     down_ref,
     ex_ref,
@@ -696,7 +702,7 @@
     *rest,
 ):
     ses, sums = rest[:pairs], rest[pairs : pairs + parts]
-    q_ref, sum_ref, val_ref, col_ref, w_high, w_low, k_row = rest[pairs + parts :]
+    q_ref, sum_ref, val_ref, col_ref, w_high, w_low, k_row, out_ref, grad_ref = rest[pairs + parts :]
     chan_all, hidden = wt_ref.shape
 
     @pl.when(pl.program_id(0) == 0)
@@ -720,8 +726,10 @@
         lane = lax.broadcasted_iota(jnp.int32, col_ref.shape, 1)
         col_ref[...] = jnp.where(lane == 0, squeezed, jnp.where(lane == 1, grad_sq, 0.0))
         wt = 0.5 * wt_ref[...]
-        w_high[...], w_low[...] = split(wt * column(excite))
-        k_row[...] = jnp.sum(wt * column(pool_grad), axis=0, keepdims=True)
+        tall_excite, tall_pool = column(excite), column(pool_grad)
+        w_high[...], w_low[...] = split(wt * tall_excite)
+        k_row[...] = jnp.sum(wt * tall_pool, axis=0, keepdims=True)
+        grad_ref[...] = tall_excite * m_ref[...] + tall_pool * s_ref[...]
         sum_ref[...] = jnp.zeros_like(sum_ref)
 
     terms = slope_terms(total(sums), count, gain_ref, bias_ref)
@@ -732,23 +740,28 @@
         sum_ref[0:1, cut] += jnp.sum(q, axis=0, keepdims=True)
         sum_ref[1:2, cut] += jnp.sum(q * h, axis=0, keepdims=True)
 
+    nz, _, chans, area = x_ref.shape
+    out_ref[:, 0] = x_ref[:, 0] + (proj_ref[0] * val_ref[0:1]).T.reshape(nz, chans, area)
+
     @pl.when(pl.program_id(0) == pl.num_programs(0) - 1)
     def _():
         sum_ref[1:2] = (2.0 * sum_ref[1:2] - bias_ref[1:2] * sum_ref[0:1]) / gain_ref[1:2]
 
 
-def proj_back(count, own, gout, gains, biases, wt, se_weights, ses, sums):
+def proj_back(count, own, gout, proj, x, gains, biases, wt, m, s, se_weights, ses, sums):
     nz, bands, chans, area = gout.shape
     hidden = wt.shape[1]
     chan_all = nz * chans
     reduced = se_weights[0].shape[0]
-    fixed = [gains, biases, wt, *se_weights, *ses, *sums]
+    fixed = [gains, biases, wt, m, s, *se_weights, *ses, *sums]
     grid, tall, put, wide = by_steps(nz, bands, chans, area)
     return pl.pallas_call(
         partial(proj_back_kernel, len(ses), len(sums), count),
         grid=grid,
         in_specs=[
             tall(hidden),
+            wide,
+            tall(chan_all),
             wide,
         ]
         + [whole(a.shape) for a in fixed],
@@ -760,6 +773,8 @@
             whole(wt.shape),
             whole(wt.shape),
             whole((1, hidden)),
+            wide,
+            whole(m.shape),
         ],
         out_shape=[
             jax.ShapeDtypeStruct((bands, area, hidden), F32),
@@ -769,45 +784,13 @@
             jax.ShapeDtypeStruct(wt.shape, BF16),
             jax.ShapeDtypeStruct(wt.shape, BF16),
             jax.ShapeDtypeStruct((1, hidden), F32),
+            jax.ShapeDtypeStruct(x.shape, F32),
+            jax.ShapeDtypeStruct(m.shape, F32),
         ],
         compiler_params=params(),
         cost_estimate=cost(12),
         name="proj_back",
-    )(own, gout, *fixed)
-
-
-def project_kernel(proj_ref, x_ref, val_ref, m_ref, s_ref, out_ref, grad_ref):
-    nz, _, chans, area = x_ref.shape
-
-    @pl.when(pl.program_id(0) == 0)
-    def _():
-        grad_ref[...] = column(val_ref[0:1]) * m_ref[...] + column(val_ref[1:2]) * s_ref[...]
-
-    out = (proj_ref[0] * val_ref[0:1]).T
-    out_ref[:, 0] = x_ref[:, 0] + out.reshape(nz, chans, area)
-
-
-def project(proj, x, values, m, s):
-    nz, bands, chans, area = x.shape
-    fixed = [values, m, s]
-    grid, tall, put, wide = by_steps(nz, bands, chans, area)
-    return pl.pallas_call(
-        project_kernel,
-        grid=grid,
-        in_specs=[
-            tall(nz * chans),
-            wide,
-        ]
-        + [whole(a.shape) for a in fixed],
-        out_specs=[wide, whole(m.shape)],
-        out_shape=[
-            jax.ShapeDtypeStruct((nz, bands, chans, area), F32),
-            jax.ShapeDtypeStruct(m.shape, F32),
-        ],
-        compiler_params=params(),
-        cost_estimate=cost(4),
-        name="project",
-    )(proj, x, *fixed)
+    )(own, gout, proj, x, *fixed)
 
 
 def spread_back_kernel(
@@ -877,31 +860,33 @@
 
     raise_all(pad, 0, raised)
 
-    def point_group(g, _):
-        for c in range(SUB):
-            mine = [grad[GROUP * g + HALO_OUT + k, c + 2] for k in range(GROUP)]
-            for p, value in enumerate(spread_points(mine)):
-                points[g, p, c] = value
+    def point_groups(i, _):
+        for g in (2 * i, 2 * i + 1):
+            for c in range(SUB):
+                mine = [grad[GROUP * g + HALO_OUT + k, c + 2] for k in range(GROUP)]
+                for p, value in enumerate(spread_points(mine)):
+                    points[g, p, c] = value
         return 0
 
-    lax.fori_loop(0, rows // GROUP, point_group, 0)
+    lax.fori_loop(0, rows // GROUP // 2, point_groups, 0)
     zero = jnp.zeros((SUB, 128), F32)
     factors = tap_factors()
     tap_sums = [None] * TAPS
     for p in range(0, POINTS, 2):
 
-        def weight_group(g, acc, p=p):
+        def weight_groups(i, acc, p=p):
             acc = list(acc)
-            for k in range(2):
-                values = [raised[g, p + k, c] for c in range(SUB + K - 1)]
-                for c in range(SUB):
-                    mine = points[g, p + k, c]
-                    for b in range(K):
-                        at = (k * 2 + c % 2) * K + b
-                        acc[at] = acc[at] + values[c + b] * mine
+            for g in (2 * i, 2 * i + 1):
+                for k in range(2):
+                    values = [raised[g, p + k, c] for c in range(SUB + K - 1)]
+                    for c in range(SUB):
+                        mine = points[g, p + k, c]
+                        for b in range(K):
+                            at = (k * 2 + c % 2) * K + b
+                            acc[at] = acc[at] + values[c + b] * mine
             return tuple(acc)
 
-        acc = lax.fori_loop(0, rows // GROUP, weight_group, (zero,) * (4 * K))
+        acc = lax.fori_loop(0, rows // GROUP // 2, weight_groups, (zero,) * (4 * K))
         for k in range(2):
             for b in range(K):
                 value = jnp.sum(acc[2 * k * K + b] + acc[(2 * k + 1) * K + b], axis=0, keepdims=True)
@@ -1624,6 +1609,10 @@
     x = deal(crops).reshape(nz, nlo, chans, area)
     ordered = order(grad_out)
     slabs, orders, ordered = gather_pix(jnp.concatenate(slab, axis=1), ordered)
+    first_turned, second_turned = first_moment.transpose(1, 0, 2), second_moment.transpose(1, 0, 2)
+    first_turned, second_turned, *slabs = together(first_turned, second_turned, *slabs)
+    room = ((0, -first_moment.shape[1] % SUB), (0, 0))
+    moments = jnp.concatenate([jnp.pad(v[:, 0], room) for v in (first_turned, second_turned)])
     (
         we_high,
         we_low,
@@ -1642,7 +1631,8 @@
         jnp.stack([relative, z_relative]), slabs, orders, nz, chan_in, chans, reduced
     )
     se_weights = [sq_t, se_down_bias[:, None], ex_all, ex_bias]
-    x, ordered, we_high, we_low = together(x, ordered, we_high, we_low)
+    x, ordered, we_high, we_low, moments = together(x, ordered, we_high, we_low, moments)
+    moments = lax.all_gather(moments, PIX, axis=0)
 
     def as_rows(v):
         return v.reshape(rows, SUB, SUB, hidden)
@@ -1663,24 +1653,16 @@
     spatial, spatial_halo, hid_halo, sums_two = spread(
         count, side, top, low, as_rows(hid), we_high, we_low, gains, biases, taps, sums_one
     )
-    first_turned, second_turned, spatial = together(
-        first_moment.transpose(1, 0, 2), second_moment.transpose(1, 0, 2), spatial
-    )
-    capacity = first_moment.shape[1]
-    room = ((0, -capacity % SUB), (0, 0))
-    moments = jnp.concatenate([jnp.pad(v[:, 0], room) for v in (first_turned, second_turned)])
-    moments = lax.all_gather(moments, PIX, axis=0)
     sums_two = shares(sums_two, 1, group)
     m, s, se_part, proj = gather(
         count, as_bands(spatial), gout, gains, biases, w_project_t, wp_high, wp_low, sums_two
     )
     ses = shares(se_part, nlo, nhi)
     ses, g_top, g_low = together(ses, g_top, g_low)
-    q, back_two, values, columns, *w4 = proj_back(
-        count, as_bands(spatial), gout, gains, biases, w_project_t, se_weights, ses, sums_two
+    q, back_two, values, columns, *w4, out, g_project = proj_back(
+        count, as_bands(spatial), gout, proj, x, gains, biases, w_project_t, m, s, se_weights, ses, sums_two
     )
     backs_two = shares(back_two, 1, group)
-    out, g_project = project(proj, x, values, m, s)
     out = deal(out.reshape(frames, chans, area))
     q1, back_one, g_dw = spread_back(
         count,

time: 316 us -> 311 us (0.984)
  Pallas kernels: 161 us -> 157 us
    pallas_call x1 -> x0, Pallas kernels: 5.49 us -> none  [project(): pl.pallas_call(project_kernel, grid=grid, in_specs=[tall(nz * chans), wid...]
  transfers between devices with their start and end apart: 43 -> 43, of which waited for: 16 -> 16; matrix products, arithmetic and copies ran while one was open for 3% -> 3% of each run, Pallas kernels for 49% -> 48%
where the time goes in v4:
time: 311 us; the launch traced here: 310 us
  Pallas kernels  157 us (50%)
  starting transfers between devices  68.3 us (22%)
  waiting for transfers between devices  56.2 us (18%)
  between operations  14.1 us (5%)
  other arithmetic  8.24 us (3%)
  local copies, waits for them, and re-layouts  6.28 us (2%)
    pallas_call x1, Pallas kernels, spread_back(): pl.pallas_call(partial(spread_back_kernel, len(backs), count), grid=(hidd...  37.4 us
    all_to_all x5, starting transfers between devices, deal(): return lax.all_to_all(x, SPREAD, 0, 0, tiled=True)  34.9 us
    ppermute x33, starting transfers between devices, exchange(): return lax.ppermute(x, ALL, [(i, i ^ stride) for i in range(n)])  32.7 us
    ppermute x33, waiting for transfers between devices, exchange(): return lax.ppermute(x, ALL, [(i, i ^ stride) for i in range(n)])  32.4 us
    all_to_all x5, waiting for transfers between devices, deal(): return lax.all_to_all(x, SPREAD, 0, 0, tiled=True)  23.2 us
    pallas_call x1, Pallas kernels, spread(): pl.pallas_call(partial(spread_kernel, len(sums), count), grid=(hidden //...  22.1 us
    pallas_call x1, Pallas kernels, proj_back(): pl.pallas_call(partial(proj_back_kernel, len(ses), len(sums), count), gri...  14.7 us
    pallas_call x2, Pallas kernels, input_grad(): pl.pallas_call(partial(input_kernel, len(sums), count, start), grid=(band...  13.6 us
  transfers between devices with their start and end apart: 43, of which 16 were waited for; matrix products, arithmetic and copies ran while one was open for 3% of the time, Pallas kernels for 48%

profile of v4, /device:TPU:15, one launch (start us, length us, event | category | flops | bytes accessed | tf_op | source)
XLA Modules:
  0.0 309.7 jit_solution(2952184376120849394)
XLA Ops:
  7.2 1.8 pack_weights.1
  9.1 2.3 collective-permute-start.1
  11.6 5.2 %crop.1 = f32[16,64,512]{2,1,0:T(8,128)} custom-call(s32[4]{0:T(128)} %left_ref.3, s32[4]{0:T(128)} %flip_ref.3, f32[16,64,640]{2,1,0:T(8,128)} %raw_ref.1), custom_call_target="tpu_custom_call" | custom-call | flops 5500000256 | bytes 17500000 | tf_op jit(solution)/shard_map/crop/pallas_call | solution.py:193
  17.8 8.3 %all-to-all-start = ((f32[16,64,512]{2,1,0:T(8,128)}), f32[16,64,512]{2,1,0:T(8,128)}, u32[]{:S(2)}, u32[]{:S(2)}) async-start(f32[16,64,512]{2,1,0:T(8,128)} %crop.1), calls=%async_computation | async-start | bytes 4194304 | tf_op jit(solution)/shard_map/all_to_all | solution.py:117
  26.1 4.7 %order.1 = f32[16,64,512]{2,1,0:T(8,128)} custom-call(f32[16,64,512]{2,1,0:T(8,128)} %x_ref.1), custom_call_target="tpu_custom_call" | custom-call | flops 27499999232 | bytes 87500000 | tf_op jit(solution)/shard_map/order/pallas_call | solution.py:218
  31.3 14.4 %collective-permute-done.4 = f32[2,72,1024]{2,1,0:T(8,128)S(1)} collective-permute-done((f32[2,72,1024]{2,1,0:T(8,128)S(1)}, f32[2,72,1024]{2,1,0:T(8,128)S(1)}, u32[]{:S(2)}, u32[]{:S(2)}) %collective-permute-start.4) | collective-permute-done | bytes 589856 | tf_op jit(solution)/shard_map/ppermute | solution.py:96
  45.7 1.2 collective-permute-start.5
  47.5 1.9 collective-permute-done.5.refs_1_
  49.4 0.8 select_maximum_fusion
  50.4 4.6 %order_weights.1 = (bf16[256,1024]{1,0:T(8,128)(2,1)}, bf16[256,1024]{1,0:T(8,128)(2,1)}, bf16[1024,256]{1,0:T(8,128)(2,1)}, bf16[1024,256]{1,0:T(8,128)(2,1)}, ...) custom-call(s32[2]{0:T(128)} %pad_add_fusion.base_ref, ...), custom_call_target="tpu_custom_call" | custom-call | flops 3300000000 | bytes 10500000 | tf_op jit(solution)/shard_map/order_weights/pallas_call | solution.py:1280
  55.0 18.6 %all-to-all-done = f32[16,64,512]{2,1,0:T(8,128)} async-done(((f32[16,64,512]{2,1,0:T(8,128)}), f32[16,64,512]{2,1,0:T(8,128)}, u32[]{:S(2)}, u32[]{:S(2)}) %all-to-all-start) | async-done | bytes 2097184 | tf_op jit(solution)/shard_map/all_to_all | solution.py:117
  73.6 4.9 %all-to-all-start.1 = ((f32[16,64,512]{2,1,0:T(8,128)}), f32[16,64,512]{2,1,0:T(8,128)}, u32[]{:S(2)}, u32[]{:S(2)}) async-start(f32[16,64,512]{2,1,0:T(8,128)} %order.1), calls=%async_computation.1 | async-start | bytes 4194304 | tf_op jit(solution)/shard_map/all_to_all | solution.py:117
  78.6 8.2 %expand.1 = (f32[4,512,1024]{2,1,0:T(8,128)}, f32[2,1024]{1,0:T(2,128)}, f32[256,384]{1,0:T(8,128)}) custom-call(f32[4,4,64,512]{3,2,1,0:T(8,128)} %bitcast.5.x_ref, bf16[256,1024]{1,0:T(8,128)(2,1)} %get-tuple-element.120.high_ref, bf16[256,1024]{1,0:T(8,128)(2,1)} %get-tuple-element.121.low_ref.lower_ref), custom_call_target="tpu_custom_call" | custom-call | flops 8800000000 | bytes 28000000 | tf_op jit(solution)/shard_map/expand/pallas_call | solution.py:331
  87.3 1.0 collective-permute-done.6
  88.3 0.7 add.33.rest_0_.rest_4_
  89.0 1.1 slice_select_fusion
  90.4 1.2 collective-permute-start.10
  91.6 1.2 collective-permute-start.8
  93.1 0.7 add_convert_fusion.side_ref
  94.4 3.7 %collective-permute-done.9.rest_2_.rest_6_ = f32[2,1024]{1,0:T(2,128)S(1)} collective-permute-done((f32[2,1024]{1,0:T(2,128)S(1)}, f32[2,1024]{1,0:T(2,128)S(1)}, u32[]{:S(2)}, u32[]{:S(2)}) %collective-permute-start.9) | collective-permute-done | bytes 8224 | tf_op jit(solution)/shard_map/ppermute | solution.py:96
  98.9 22.1 %spread.1 = (f32[32,8,8,1024]{3,2,1,0:T(8,128)}, f32[2,2,8,8,1024]{4,3,2,1,0:T(8,128)}, f32[2,2,8,8,1024]{4,3,2,1,0:T(8,128)}, f32[2,1024]{1,0:T(2,128)}) custom-call(s32[2]{0:T(128)} %add_convert_fusion.side_ref, f32[4,1,64,256]{3,2,1,0:T(8,128)} %copy-done.16, f32[4,1,64,256]{3,2,1,0:T(8,128)} %copy-done.16, f32[32,8,8,1024]{3,2,1,0:T(8,128)} %bitcast.47, ...), custom_call_target="tpu_custom_call" | custom-call | flops 11000000512 | bytes 35000000 | tf_op jit(solution)/shard_map/spread/pallas_call | solution.py:566
  121.0 1.1 collective-permute-start.11
  122.1 1.0 collective-permute-done.11
  123.1 0.7 add.34.rest_0_.rest_2_.rest_4_
  124.3 2.2 collective-permute-start.14
  126.5 1.0 slice_select_fusion.1
  128.3 11.6 %gather.1 = (f32[256,1024]{1,0:T(8,128)}, f32[1,1024]{1,0:T(1,128)}, f32[2,256]{1,0:T(2,128)}, f32[4,512,256]{2,1,0:T(8,128)}) custom-call(f32[4,512,1024]{2,1,0:T(8,128)} %bitcast.49, f32[4,4,64,512]{3,2,1,0:T(8,128)} %bitcast.12.gout_ref, f32[2,1024]{1,0:T(2,128)} %get-tuple-element.125.gain_ref, f32[2,1024]{1,0:T(2,128)} %get-tuple-element.126.bias_ref, ...), custom_call_target="tpu_custom_call" | custom-call | flops 14300000256 | bytes 45500000 | tf_op jit(solution)/shard_map/gather/pallas_call | solution.py:640
  139.9 1.5 collective-permute-start.15
  141.4 0.7 copy.25.down_ref
  143.0 14.7 %proj_back.1 = (f32[4,512,1024]{2,1,0:T(8,128)}, f32[2,1024]{1,0:T(2,128)}, f32[8,256]{1,0:T(8,128)}, f32[16,128]{1,0:T(8,128)}, bf16[256,1024]{1,0:T(8,128)(2,1...) custom-call(f32[4,512,1024]{2,1,0:T(8,128)} %bitcast.50, ...), custom_call_target="tpu_custom_call" | custom-call | flops 13200000000 | bytes 42000000 | tf_op jit(solution)/shard_map/proj_back/pallas_call | solution.py:758
  157.6 3.5 %collective-permute-start.17 = (f32[2,1024]{1,0:T(2,128)}, f32[2,1024]{1,0:T(2,128)S(1)}, u32[]{:S(2)}, u32[]{:S(2)}) collective-permute-start(f32[2,1024]{1,0:T(2,128)} %get-tuple-element.152.two_ref), channel_id=1, source_target_pairs={{0,1},{1,0},{2,3},{3,2},{4,5},{5,4},{6,7},{7,6},{8,9},{9,8},{10,11... | collective-permute-start | bytes 24584 | tf_op jit(solution)/shard_map/ppermute | solution.py:96
  161.1 1.0 collective-permute-done.17
  162.2 0.7 add.35.rest_8_
  162.9 1.2 collective-permute-start.18
  164.1 1.3 collective-permute-start.19
  165.5 6.8 %all-to-all-start.2 = ((f32[16,64,512]{2,1,0:T(8,128)}), f32[16,64,512]{2,1,0:T(8,128)}, u32[]{:S(2)}, u32[]{:S(2)}) async-start(f32[16,64,512]{2,1,0:T(8,128)} %bitcast.33), calls=%async_computation.2 | async-start | bytes 4194304 | tf_op jit(solution)/shard_map/all_to_all | solution.py:117
  173.8 37.4 %spread_back.1 = (f32[32,8,8,1024]{3,2,1,0:T(8,128)}, f32[2,1024]{1,0:T(2,128)}, f32[25,1024]{1,0:T(8,128)}) custom-call(s32[2]{0:T(128)} %add_convert_fusion.side_ref, f32[4,1,64,128]{3,2,1,0:T(8,128)} %copy-done.20, f32[4,1,64,128]{3,2,1,0:T(8,128)} %copy-done.20, f32[32,8,8,1024]{3,2,1,0:T(8,128)} %bitcast.48, ...), custom_call_target="tpu_custom_call" | custom-call | flops 165000003584 | bytes 525000000 | tf_op jit(solution)/shard_map/spread_back/pallas_call | solution.py:928
  212.6 0.7 add.36.rest_4_.rest_8_
  213.6 1.3 collective-permute-start.23
  214.9 1.1 collective-permute-start.24
  216.0 8.0 %weight_grad.1 = (f32[4,40,1024]{2,1,0:T(8,128)}, f32[4,40,1024]{2,1,0:T(8,128)}) custom-call(s32[3]{0:T(128)} %pad_add_fusion.1.ids_ref, f32[4,512,1024]{2,1,0:T(8,128)} %bitcast.51, f32[4,4,64,512]{3,2,1,0:T(8,128)} %bitcast.5.x_ref, f32[25,1024]{1,0:T(8,128)} %get-tuple-element.160.tap_ref, f32[2,1024]{1,0:T(2,128)} %get-tuple-element.153.one_ref, ...), custom_call_target="tpu_custom_call" | custom-call | flops 7699999744 | bytes 24500000 | tf_op jit(solution)/shard_map/weight_grad/pallas_call | solution.py:1053
  224.1 1.2 collective-permute-start.25
  226.0 6.8 %input_grad.2 = f32[4,4,64,256]{3,2,1,0:T(8,128)} custom-call(f32[4,512,1024]{2,1,0:T(8,128)} %bitcast.52, f32[4,512,1024]{2,1,0:T(8,128)} %get-tuple-element.124.hid_ref, f32[4,4,64,512]{3,2,1,0:T(8,128)} %bitcast.12.gout_ref, f32[2,1024]{1,0:T(2,128)} %get-tuple-element.125.gain_ref, bf16[1024,256]{1,0:T(8,128)(2,1)} %get-tuple-element.166.w_high, ...), custom_call_target="tpu_custom_call" | custom-call | flops 13200000000 | bytes 42000000 | tf_op jit(solution)/shard_map/input_grad/pallas_call | solution.py:983
  232.7 5.8 %all-to-all-start.3 = ((f32[16,64,256]{2,1,0:T(8,128)}), f32[16,64,256]{2,1,0:T(8,128)S(1)}, u32[]{:S(2)}, u32[]{:S(2)}) async-start(f32[16,64,256]{2,1,0:T(8,128)} %bitcast.35), calls=%async_computation.5 | async-start | bytes 2097152 | tf_op jit(solution)/shard_map/all_to_all | solution.py:117
  238.5 2.2 merge.1
  241.0 1.3 collective-permute-start.27
  242.3 1.1 collective-permute-start.28
  243.4 6.8 %input_grad.3 = f32[4,4,64,256]{3,2,1,0:T(8,128)} custom-call(f32[4,512,1024]{2,1,0:T(8,128)} %bitcast.53, f32[4,512,1024]{2,1,0:T(8,128)} %get-tuple-element.124.hid_ref, f32[4,4,64,512]{3,2,1,0:T(8,128)} %bitcast.12.gout_ref, f32[2,1024]{1,0:T(2,128)} %get-tuple-element.125.gain_ref, bf16[1024,256]{1,0:T(8,128)(2,1)} %get-tuple-element.166.w_high, ...), custom_call_target="tpu_custom_call" | custom-call | flops 13200000000 | bytes 42000000 | tf_op jit(solution)/shard_map/input_grad/pallas_call | solution.py:983
  250.2 4.8 %restore.1 = f32[16,64,512]{2,1,0:T(8,128)} custom-call(f32[16,64,512]{2,1,0:T(8,128)} %all-to-all-done.2.x_ref), custom_call_target="tpu_custom_call" | custom-call | flops 1100000000 | bytes 3500000 | tf_op jit(solution)/shard_map/restore/pallas_call | solution.py:239
  255.0 0.6 copy-done.17
  255.8 2.6 collect.1
  258.4 3.2 %collective-permute-start.29 = (f32[72,256]{1,0:T(8,128)}, f32[72,256]{1,0:T(8,128)S(1)}, u32[]{:S(2)}, u32[]{:S(2)}) collective-permute-start(f32[72,256]{1,0:T(8,128)} %get-tuple-element.191), channel_id=1, source_target_pairs={{0,8},{1,9},{2,10},{3,11},{4,12},{5,13},{6,14},{7,15},{8,0},{9,1},... | collective-permute-start | bytes 221192 | tf_op jit(solution)/shard_map/ppermute | solution.py:96
  262.0 0.9 collective-permute-start.31
  262.9 0.8 copy.27.col_ref
  263.7 9.0 %all-to-all-start.4 = ((f32[16,64,256]{2,1,0:T(8,128)}), f32[16,64,256]{2,1,0:T(8,128)}, u32[]{:S(2)}, u32[]{:S(2)}) async-start(f32[16,64,256]{2,1,0:T(8,128)} %bitcast.34), calls=%async_computation.6 | async-start | bytes 2097152 | tf_op jit(solution)/shard_map/all_to_all | solution.py:117
  273.1 4.7 %prepare.1 = (f32[138,1024]{1,0:T(8,128)}, f32[138,1024]{1,0:T(8,128)}, f32[138,1024]{1,0:T(8,128)}) custom-call(s32[1]{0:T(128)} %constant.21.clone.1.base_ref, s32[138,1]{1,0:T(8,128)} %copy.27.col_ref, f32[256,256]{1,0:T(8,128)} %we_ref.3, f32[25,256]{1,0:T(8,128)} %dw_ref.3, f32[2,256]{1,0:T(2,128)} %gain_ref.3, f32[2,256]{1,0:T(2,128)} %bias_ref.3, ...), custom_call_target="tpu_custom_call" | custom-call | flops 1100000000 | bytes 3500000 | tf_op jit(solution)/shard_map/prepare/pallas_call | solution.py:1427
  277.8 2.1 collective-permute-done.32
  280.1 4.4 %collective-permute-done.33 = f32[2,72,256]{2,1,0:T(8,128)S(1)} collective-permute-done((f32[2,72,256]{2,1,0:T(8,128)S(1)}, f32[2,72,256]{2,1,0:T(8,128)S(1)}, u32[]{:S(2)}, u32[]{:S(2)}) %collective-permute-start.33) | collective-permute-done | bytes 147488 | tf_op jit(solution)/shard_map/ppermute | solution.py:96
  284.5 1.7 collective-permute-start.34
  286.8 0.6 collective-permute-done.34.rest_1_
  287.5 0.7 copy-done.15
  288.2 4.9 %adam.1 = (f32[26,1,1024]{2,1,0:T(1,128)}, f32[26,1,1024]{2,1,0:T(1,128)}, f32[1,140624]{1,0:T(1,128)}) custom-call(s32[2]{0:T(128)} %pad_add_fusion.2.me_ref, s32[138,1]{1,0:T(8,128)} %copy.27.col_ref, f32[138,1024]{1,0:T(8,128)} %get-tuple-element.200.weight_ref, f32[138,1024]{1,0:T(8,128)} %get-tuple-element.201.old_one_ref, ...), custom_call_target="tpu_custom_call" | custom-call | flops 11000000512 | bytes 35000000 | tf_op jit(solution)/shard_map/adam/pallas_call | solution.py:1525
  293.1 4.5 %all-to-all-done.4.y_ref = f32[16,64,256]{2,1,0:T(8,128)} async-done(((f32[16,64,256]{2,1,0:T(8,128)}), f32[16,64,256]{2,1,0:T(8,128)}, u32[]{:S(2)}, u32[]{:S(2)}) %all-to-all-start.4) | async-done | bytes 1048608 | tf_op jit(solution)/shard_map/all_to_all | solution.py:117
  297.7 5.5 %uncrop.1 = f32[16,64,640]{2,1,0:T(8,128)} custom-call(s32[4]{0:T(128)} %left_ref.3, s32[4]{0:T(128)} %flip_ref.3, f32[16,64,256]{2,1,0:T(8,128)} %copy-done, f32[16,64,256]{2,1,0:T(8,128)} %all-to-all-done.4.y_ref), custom_call_target="tpu_custom_call" | custom-call | flops 1100000000 | bytes 3500000 | tf_op jit(solution)/shard_map/uncrop/pallas_call | solution.py:268
  (133 shorter events, 13.1 us)
Async XLA Ops:
  9.0 8.5 %copy-start.4 = (f32[72,256]{1,0:T(8,128)S(1)}, f32[72,256]{1,0:T(8,128)}, u32[]{:S(2)}) copy-start(f32[72,256]{1,0:T(8,128)} %pack_weights.1) | copy-start | bytes 221188
  9.0 7.9 %collective-permute-start = (f32[72,256]{1,0:T(8,128)}, f32[72,256]{1,0:T(8,128)S(1)}, u32[]{:S(2)}, u32[]{:S(2)}) collective-permute-start(f32[72,256]{1,0:T(8,128)} %pack_weights.1), channel_id=1, source_target_pairs={{0,8},{1,9},{2,10},{3,11},{4,12},{5,13},{6,14},{7,15},{8,0},{9,1},... | collective-permute-start | bytes 221192 | tf_op jit(solution)/shard_map/ppermute | solution.py:96
  9.1 7.7 %collective-permute-start.1 = (f32[72,256]{1,0:T(8,128)}, f32[72,256]{1,0:T(8,128)S(1)}, u32[]{:S(2)}, u32[]{:S(2)}) collective-permute-start(f32[72,256]{1,0:T(8,128)} %pack_weights.1), channel_id=1, source_target_pairs={{0,16},{1,17},{2,18},{3,19},{4,20},{5,21},{6,22},{7,23},{8,24},{9,... | collective-permute-start | bytes 221192 | tf_op jit(solution)/shard_map/ppermute | solution.py:96
  11.4 6.0 %collective-permute-start.2 = (f32[72,256]{1,0:T(8,128)}, f32[72,256]{1,0:T(8,128)S(1)}, u32[]{:S(2)}, u32[]{:S(2)}) collective-permute-start(f32[72,256]{1,0:T(8,128)} %pack_weights.1), channel_id=1, source_target_pairs={{0,24},{1,25},{2,26},{3,27},{4,28},{5,29},{6,30},{7,31},{8,16},{9,... | collective-permute-start | bytes 221192 | tf_op jit(solution)/shard_map/ppermute | solution.py:96
  17.5 13.4 %collective-permute-start.3 = (f32[1,72,1024]{2,1,0:T(8,128)S(1)}, f32[1,72,1024]{2,1,0:T(8,128)S(1)}, u32[]{:S(2)}, u32[]{:S(2)}) collective-permute-start(f32[1,72,1024]{2,1,0:T(8,128)S(1)} %maximum_bitcast_fusion), channel_id=1, source_target_pairs={{0,2},{1,3},{2,0},{3,1},{4,6},{5,7},{6,4},{7,5},{8,10},{9,11},{10,... | collective-permute-start | bytes 884744 | tf_op jit(solution)/shard_map/ppermute | solution.py:96
  17.8 55.9 %all-to-all-start = ((f32[16,64,512]{2,1,0:T(8,128)}), f32[16,64,512]{2,1,0:T(8,128)}, u32[]{:S(2)}, u32[]{:S(2)}) async-start(f32[16,64,512]{2,1,0:T(8,128)} %crop.1), calls=%async_computation | async-start | bytes 4194304 | tf_op jit(solution)/shard_map/all_to_all | solution.py:117
  30.9 18.5 %copy-start.2 = (f32[1,26,1024]{2,0,1:T(1,128)S(1)}, f32[1,26,1024]{2,0,1:T(1,128)}, u32[]{:S(2)}) copy-start(f32[1,26,1024]{2,0,1:T(1,128)} %param.31) | copy-start | bytes 319492
  30.9 18.5 %copy-start.3 = (f32[1,26,1024]{2,0,1:T(1,128)S(1)}, f32[1,26,1024]{2,0,1:T(1,128)}, u32[]{:S(2)}) copy-start(f32[1,26,1024]{2,0,1:T(1,128)} %param.30) | copy-start | bytes 319492
  30.9 14.7 %collective-permute-start.4 = (f32[2,72,1024]{2,1,0:T(8,128)S(1)}, f32[2,72,1024]{2,1,0:T(8,128)S(1)}, u32[]{:S(2)}, u32[]{:S(2)}) collective-permute-start(f32[2,72,1024]{2,1,0:T(8,128)S(1)} %pad_maximum_fusion), channel_id=1, source_target_pairs={{0,4},{1,5},{2,6},{3,7},{4,0},{5,1},{6,2},{7,3},{8,12},{9,13},{10,... | collective-permute-start | bytes 1769480 | tf_op jit(solution)/shard_map/ppermute | solution.py:96
  45.7 4.7 %copy-start.1 = (f32[4,72,1024]{2,1,0:T(8,128)}, f32[4,72,1024]{2,1,0:T(8,128)S(1)}, u32[]{:S(2)}) copy-start(f32[4,72,1024]{2,1,0:T(8,128)S(1)} %constant_dynamic-update-slice_fusion.refs_0_) | copy-start | bytes 3538948
  45.7 3.6 %collective-permute-start.5 = (f32[4,72,1024]{2,1,0:T(8,128)S(1)}, f32[4,72,1024]{2,1,0:T(8,128)S(1)}, u32[]{:S(2)}, u32[]{:S(2)}) collective-permute-start(f32[4,72,1024]{2,1,0:T(8,128)S(1)} %constant_dynamic-update-slice_fusion.refs_0_), channel_id=1, source_target_pairs={{0,1},{1,0},{2,3},{3,2},{4,5},{5,4},{6,7},{7,6},{8,9},{9,8},{10,11... | collective-permute-start | bytes 3538952 | tf_op jit(solution)/shard_map/ppermute | solution.py:96
  49.3 1.1 copy-start.13
  73.6 52.8 %all-to-all-start.1 = ((f32[16,64,512]{2,1,0:T(8,128)}), f32[16,64,512]{2,1,0:T(8,128)}, u32[]{:S(2)}, u32[]{:S(2)}) async-start(f32[16,64,512]{2,1,0:T(8,128)} %order.1), calls=%async_computation.1 | async-start | bytes 4194304 | tf_op jit(solution)/shard_map/all_to_all | solution.py:117
  78.5 145.5 %reduce-scatter.5.cloned.1.call-start = ((), (), s32[]{:S(2)}) async-start(), calls=%async_computation.8 | async-start | bytes 442368 | tf_op jit(solution)/shard_map/reduce_scatter | solution.py:1695
  86.8 137.2 %all-gather.3.cloned.1.call-start = ((), (), s32[]{:S(2)}) async-start(), calls=%async_computation.9 | async-start | bytes 2359296 | tf_op jit(solution)/shard_map/all_gather | solution.py:1635
  86.9 1.5 collective-permute-start.6
  89.0 9.2 %copy-start.7 = (f32[2,1024]{1,0:T(2,128)}, f32[2,1024]{1,0:T(2,128)S(1)}, u32[]{:S(2)}) copy-start(f32[2,1024]{1,0:T(2,128)S(1)} %add.33.rest_0_.rest_4_) | copy-start | bytes 24580
  90.1 8.1 %collective-permute-start.7 = (f32[4,1,64,256]{3,2,1,0:T(8,128)S(1)}, f32[4,1,64,256]{3,2,1,0:T(8,128)S(1)}, u32[]{:S(2)}, u32[]{:S(2)}) collective-permute-start(f32[4,1,64,256]{3,2,1,0:T(8,128)S(1)} %slice_select_fusion), channel_id=1, source_target_pairs={{0,4},{4,0},{1,5},{5,1},{2,6},{6,2},{3,7},{7,3},{8,12},{12,8},{9,1... | collective-permute-start | bytes 786440 | tf_op jit(solution)/shard_map/ppermute | solution.py:132
  90.4 3.6 %collective-permute-start.10 = (f32[2,1024]{1,0:T(2,128)S(1)}, f32[2,1024]{1,0:T(2,128)S(1)}, u32[]{:S(2)}, u32[]{:S(2)}) collective-permute-start(f32[2,1024]{1,0:T(2,128)S(1)} %add.33.rest_0_.rest_4_), channel_id=1, source_target_pairs={{0,6},{1,7},{2,4},{3,5},{4,2},{5,3},{6,0},{7,1},{8,14},{9,15},{10,... | collective-permute-start | bytes 24584 | tf_op jit(solution)/shard_map/ppermute | solution.py:96
  91.6 2.8 collective-permute-start.8
  92.8 5.4 %collective-permute-start.9 = (f32[2,1024]{1,0:T(2,128)S(1)}, f32[2,1024]{1,0:T(2,128)S(1)}, u32[]{:S(2)}, u32[]{:S(2)}) collective-permute-start(f32[2,1024]{1,0:T(2,128)S(1)} %add.33.rest_0_.rest_4_), channel_id=1, source_target_pairs={{0,4},{1,5},{2,6},{3,7},{4,0},{5,1},{6,2},{7,3},{8,12},{9,13},{10,... | collective-permute-start | bytes 24584 | tf_op jit(solution)/shard_map/ppermute | solution.py:96
  94.0 4.2 %copy-start.21 = (f32[2,1024]{1,0:T(2,128)}, f32[2,1024]{1,0:T(2,128)S(1)}, u32[]{:S(2)}) copy-start(f32[2,1024]{1,0:T(2,128)S(1)} %collective-permute-done.10.rest_3_.rest_7_) | copy-start | bytes 24580
  94.4 3.8 %copy-start.22 = (f32[2,1024]{1,0:T(2,128)}, f32[2,1024]{1,0:T(2,128)S(1)}, u32[]{:S(2)}) copy-start(f32[2,1024]{1,0:T(2,128)S(1)} %collective-permute-done.8.rest_1_.rest_5_) | copy-start | bytes 24580
  121.0 2.2 collective-permute-start.11
  123.8 3.9 %copy-start.8 = (f32[2,1024]{1,0:T(2,128)}, f32[2,1024]{1,0:T(2,128)S(1)}, u32[]{:S(2)}) copy-start(f32[2,1024]{1,0:T(2,128)S(1)} %add.34.rest_0_.rest_2_.rest_4_) | copy-start | bytes 24580
  123.8 3.9 %collective-permute-start.12 = (f32[2,1024]{1,0:T(2,128)S(1)}, f32[2,1024]{1,0:T(2,128)S(1)}, u32[]{:S(2)}, u32[]{:S(2)}) collective-permute-start(f32[2,1024]{1,0:T(2,128)S(1)} %add.34.rest_0_.rest_2_.rest_4_), channel_id=1, source_target_pairs={{0,2},{1,3},{2,0},{3,1},{4,6},{5,7},{6,4},{7,5},{8,10},{9,11},{10,... | collective-permute-start | bytes 24584 | tf_op jit(solution)/shard_map/ppermute | solution.py:96
  124.1 3.6 %collective-permute-start.13 = (f32[2,1024]{1,0:T(2,128)S(1)}, f32[2,1024]{1,0:T(2,128)S(1)}, u32[]{:S(2)}, u32[]{:S(2)}) collective-permute-start(f32[2,1024]{1,0:T(2,128)S(1)} %add.34.rest_0_.rest_2_.rest_4_), channel_id=1, source_target_pairs={{0,4},{1,5},{2,6},{3,7},{4,0},{5,1},{6,2},{7,3},{8,12},{9,13},{10,... | collective-permute-start | bytes 24584 | tf_op jit(solution)/shard_map/ppermute | solution.py:96
  124.3 3.5 %collective-permute-start.14 = (f32[2,1024]{1,0:T(2,128)S(1)}, f32[2,1024]{1,0:T(2,128)S(1)}, u32[]{:S(2)}, u32[]{:S(2)}) collective-permute-start(f32[2,1024]{1,0:T(2,128)S(1)} %add.34.rest_0_.rest_2_.rest_4_), channel_id=1, source_target_pairs={{0,6},{1,7},{2,4},{3,5},{4,2},{5,3},{6,0},{7,1},{8,14},{9,15},{10,... | collective-permute-start | bytes 24584 | tf_op jit(solution)/shard_map/ppermute | solution.py:96
  127.5 15.0 %collective-permute-start.16 = (f32[4,1,64,128]{3,2,1,0:T(8,128)S(1)}, f32[4,1,64,128]{3,2,1,0:T(8,128)S(1)}, u32[]{:S(2)}, u32[]{:S(2)}) collective-permute-start(f32[4,1,64,128]{3,2,1,0:T(8,128)S(1)} %slice_select_fusion.1), channel_id=1, source_target_pairs={{0,4},{4,0},{1,5},{5,1},{2,6},{6,2},{3,7},{7,3},{8,12},{12,8},{9,1... | collective-permute-start | bytes 393224 | tf_op jit(solution)/shard_map/ppermute | solution.py:132
  128.3 13.1 %copy-start.12 = (f32[16]{0:T(128)S(1)}, f32[16]{0:T(128)}, u32[]{:S(2)}) copy-start(f32[16]{0:T(128)} %param.27) | copy-start | bytes 196
  139.9 2.5 collective-permute-start.15
  142.4 15.2 %copy-start.20 = (f32[4,1,64,128]{3,2,1,0:T(8,128)}, f32[4,1,64,128]{3,2,1,0:T(8,128)S(1)}, u32[]{:S(2)}) copy-start(f32[4,1,64,128]{3,2,1,0:T(8,128)S(1)} %collective-permute-done.16.top_ref.low_ref) | copy-start | bytes 393220
  157.6 4.5 %collective-permute-start.17 = (f32[2,1024]{1,0:T(2,128)}, f32[2,1024]{1,0:T(2,128)S(1)}, u32[]{:S(2)}, u32[]{:S(2)}) collective-permute-start(f32[2,1024]{1,0:T(2,128)} %get-tuple-element.152.two_ref), channel_id=1, source_target_pairs={{0,1},{1,0},{2,3},{3,2},{4,5},{5,4},{6,7},{7,6},{8,9},{9,8},{10,11... | collective-permute-start | bytes 24584 | tf_op jit(solution)/shard_map/ppermute | solution.py:96
  162.9 2.7 copy-start.10
  162.9 10.2 %collective-permute-start.18 = (f32[2,1024]{1,0:T(2,128)S(1)}, f32[2,1024]{1,0:T(2,128)S(1)}, u32[]{:S(2)}, u32[]{:S(2)}) collective-permute-start(f32[2,1024]{1,0:T(2,128)S(1)} %add.35.rest_8_), channel_id=1, source_target_pairs={{0,2},{1,3},{2,0},{3,1},{4,6},{5,7},{6,4},{7,5},{8,10},{9,11},{10,... | collective-permute-start | bytes 24584 | tf_op jit(solution)/shard_map/ppermute | solution.py:96
  164.1 9.1 %collective-permute-start.19 = (f32[2,1024]{1,0:T(2,128)S(1)}, f32[2,1024]{1,0:T(2,128)S(1)}, u32[]{:S(2)}, u32[]{:S(2)}) collective-permute-start(f32[2,1024]{1,0:T(2,128)S(1)} %add.35.rest_8_), channel_id=1, source_target_pairs={{0,4},{1,5},{2,6},{3,7},{4,0},{5,1},{6,2},{7,3},{8,12},{9,13},{10,... | collective-permute-start | bytes 24584 | tf_op jit(solution)/shard_map/ppermute | solution.py:96
  165.4 7.8 %collective-permute-start.20 = (f32[2,1024]{1,0:T(2,128)S(1)}, f32[2,1024]{1,0:T(2,128)S(1)}, u32[]{:S(2)}, u32[]{:S(2)}) collective-permute-start(f32[2,1024]{1,0:T(2,128)S(1)} %add.35.rest_8_), channel_id=1, source_target_pairs={{0,6},{1,7},{2,4},{3,5},{4,2},{5,3},{6,0},{7,1},{8,14},{9,15},{10,... | collective-permute-start | bytes 24584 | tf_op jit(solution)/shard_map/ppermute | solution.py:96
  165.5 58.5 %all-to-all-start.2 = ((f32[16,64,512]{2,1,0:T(8,128)}), f32[16,64,512]{2,1,0:T(8,128)}, u32[]{:S(2)}, u32[]{:S(2)}) async-start(f32[16,64,512]{2,1,0:T(8,128)} %bitcast.33), calls=%async_computation.2 | async-start | bytes 4194304 | tf_op jit(solution)/shard_map/all_to_all | solution.py:117
  172.4 51.7 %reduce-scatter.3.cloned.1.call-start = ((), (), s32[]{:S(2)}) async-start(), calls=%async_computation.7 | async-start | bytes 1179648 | tf_op jit(solution)/shard_map/reduce_scatter | solution.py:1694
  211.1 1.5 collective-permute-start.21
  213.3 10.7 %copy-start.9 = (f32[2,1024]{1,0:T(2,128)}, f32[2,1024]{1,0:T(2,128)S(1)}, u32[]{:S(2)}) copy-start(f32[2,1024]{1,0:T(2,128)S(1)} %add.36.rest_4_.rest_8_) | copy-start | bytes 24580
  213.3 12.0 %collective-permute-start.22 = (f32[2,1024]{1,0:T(2,128)S(1)}, f32[2,1024]{1,0:T(2,128)S(1)}, u32[]{:S(2)}, u32[]{:S(2)}) collective-permute-start(f32[2,1024]{1,0:T(2,128)S(1)} %add.36.rest_4_.rest_8_), channel_id=1, source_target_pairs={{0,2},{1,3},{2,0},{3,1},{4,6},{5,7},{6,4},{7,5},{8,10},{9,11},{10,... | collective-permute-start | bytes 24584 | tf_op jit(solution)/shard_map/ppermute | solution.py:96
  213.6 11.7 %collective-permute-start.23 = (f32[2,1024]{1,0:T(2,128)S(1)}, f32[2,1024]{1,0:T(2,128)S(1)}, u32[]{:S(2)}, u32[]{:S(2)}) collective-permute-start(f32[2,1024]{1,0:T(2,128)S(1)} %add.36.rest_4_.rest_8_), channel_id=1, source_target_pairs={{0,4},{1,5},{2,6},{3,7},{4,0},{5,1},{6,2},{7,3},{8,12},{9,13},{10,... | collective-permute-start | bytes 24584 | tf_op jit(solution)/shard_map/ppermute | solution.py:96
  214.9 10.5 %collective-permute-start.24 = (f32[2,1024]{1,0:T(2,128)S(1)}, f32[2,1024]{1,0:T(2,128)S(1)}, u32[]{:S(2)}, u32[]{:S(2)}) collective-permute-start(f32[2,1024]{1,0:T(2,128)S(1)} %add.36.rest_4_.rest_8_), channel_id=1, source_target_pairs={{0,6},{1,7},{2,4},{3,5},{4,2},{5,3},{6,0},{7,1},{8,14},{9,15},{10,... | collective-permute-start | bytes 24584 | tf_op jit(solution)/shard_map/ppermute | solution.py:96
  224.1 8.7 %collective-permute-start.25 = (f32[4,40,1024]{2,1,0:T(8,128)}, f32[4,40,1024]{2,1,0:T(8,128)S(1)}, u32[]{:S(2)}, u32[]{:S(2)}) collective-permute-start(f32[4,40,1024]{2,1,0:T(8,128)} %get-tuple-element.170), channel_id=1, source_target_pairs={{0,1},{1,0},{2,3},{3,2},{4,5},{5,4},{6,7},{7,6},{8,9},{9,8},{10,11... | collective-permute-start | bytes 1966088 | tf_op jit(solution)/shard_map/ppermute | solution.py:96
  232.7 5.8 %copy-start.14 = (f32[4,40,1024]{2,1,0:T(8,128)}, f32[4,40,1024]{2,1,0:T(8,128)S(1)}, u32[]{:S(2)}) copy-start(f32[4,40,1024]{2,1,0:T(8,128)S(1)} %collective-permute-done.25.two_ref) | copy-start | bytes 1966084
  232.7 30.9 %all-to-all-start.3 = ((f32[16,64,256]{2,1,0:T(8,128)}), f32[16,64,256]{2,1,0:T(8,128)S(1)}, u32[]{:S(2)}, u32[]{:S(2)}) async-start(f32[16,64,256]{2,1,0:T(8,128)} %bitcast.35), calls=%async_computation.5 | async-start | bytes 2097152 | tf_op jit(solution)/shard_map/all_to_all | solution.py:117
  240.7 14.3 %collective-permute-start.26 = (f32[40,1024]{1,0:T(8,128)}, f32[40,1024]{1,0:T(8,128)S(1)}, u32[]{:S(2)}, u32[]{:S(2)}) collective-permute-start(f32[40,1024]{1,0:T(8,128)} %get-tuple-element.178), channel_id=1, source_target_pairs={{0,2},{1,3},{2,0},{3,1},{4,6},{5,7},{6,4},{7,5},{8,10},{9,11},{10,... | collective-permute-start | bytes 491528 | tf_op jit(solution)/shard_map/ppermute | solution.py:96
  241.0 14.0 %collective-permute-start.27 = (f32[40,1024]{1,0:T(8,128)}, f32[40,1024]{1,0:T(8,128)S(1)}, u32[]{:S(2)}, u32[]{:S(2)}) collective-permute-start(f32[40,1024]{1,0:T(8,128)} %get-tuple-element.179), channel_id=1, source_target_pairs={{0,4},{1,5},{2,6},{3,7},{4,0},{5,1},{6,2},{7,3},{8,12},{9,13},{10,... | collective-permute-start | bytes 491528 | tf_op jit(solution)/shard_map/ppermute | solution.py:96
  242.3 12.7 %collective-permute-start.28 = (f32[40,1024]{1,0:T(8,128)}, f32[40,1024]{1,0:T(8,128)S(1)}, u32[]{:S(2)}, u32[]{:S(2)}) collective-permute-start(f32[40,1024]{1,0:T(8,128)} %get-tuple-element.180), channel_id=1, source_target_pairs={{0,6},{1,7},{2,4},{3,5},{4,2},{5,3},{6,0},{7,1},{8,14},{9,15},{10,... | collective-permute-start | bytes 491528 | tf_op jit(solution)/shard_map/ppermute | solution.py:96
  255.0 0.7 copy-start.18
  255.0 0.8 copy-start.19
  255.8 7.1 %copy-start.11 = (s32[138,1]{0,1:T(1,128)S(1)}, s32[138,1]{0,1:T(1,128)}, u32[]{:S(2)}) copy-start(s32[138,1]{0,1:T(1,128)} %param.20) | copy-start | bytes 1660
  258.4 14.3 %copy-start.6 = (f32[72,256]{1,0:T(8,128)S(1)}, f32[72,256]{1,0:T(8,128)}, u32[]{:S(2)}) copy-start(f32[72,256]{1,0:T(8,128)} %get-tuple-element.190) | copy-start | bytes 221188
  258.4 14.3 %collective-permute-start.29 = (f32[72,256]{1,0:T(8,128)}, f32[72,256]{1,0:T(8,128)S(1)}, u32[]{:S(2)}, u32[]{:S(2)}) collective-permute-start(f32[72,256]{1,0:T(8,128)} %get-tuple-element.191), channel_id=1, source_target_pairs={{0,8},{1,9},{2,10},{3,11},{4,12},{5,13},{6,14},{7,15},{8,0},{9,1},... | collective-permute-start | bytes 221192 | tf_op jit(solution)/shard_map/ppermute | solution.py:96
  261.6 11.1 %collective-permute-start.30 = (f32[72,256]{1,0:T(8,128)}, f32[72,256]{1,0:T(8,128)S(1)}, u32[]{:S(2)}, u32[]{:S(2)}) collective-permute-start(f32[72,256]{1,0:T(8,128)} %get-tuple-element.192), channel_id=1, source_target_pairs={{0,16},{1,17},{2,18},{3,19},{4,20},{5,21},{6,22},{7,23},{8,24},{9,... | collective-permute-start | bytes 221192 | tf_op jit(solution)/shard_map/ppermute | solution.py:96
  262.0 10.7 %collective-permute-start.31 = (f32[72,256]{1,0:T(8,128)}, f32[72,256]{1,0:T(8,128)S(1)}, u32[]{:S(2)}, u32[]{:S(2)}) collective-permute-start(f32[72,256]{1,0:T(8,128)} %get-tuple-element.193), channel_id=1, source_target_pairs={{0,24},{1,25},{2,26},{3,27},{4,28},{5,29},{6,30},{7,31},{8,16},{9,... | collective-permute-start | bytes 221192 | tf_op jit(solution)/shard_map/ppermute | solution.py:96
  263.7 14.1 %copy-start = (f32[16,64,256]{2,1,0:T(8,128)}, f32[16,64,256]{2,1,0:T(8,128)S(1)}, u32[]{:S(2)}) copy-start(f32[16,64,256]{2,1,0:T(8,128)S(1)} %all-to-all-done.3.x_ref) | copy-start | bytes 3145732
  263.7 34.0 %all-to-all-start.4 = ((f32[16,64,256]{2,1,0:T(8,128)}), f32[16,64,256]{2,1,0:T(8,128)}, u32[]{:S(2)}, u32[]{:S(2)}) async-start(f32[16,64,256]{2,1,0:T(8,128)} %bitcast.34), calls=%async_computation.6 | async-start | bytes 2097152 | tf_op jit(solution)/shard_map/all_to_all | solution.py:117
  272.7 7.1 %collective-permute-start.32 = (f32[1,72,256]{2,1,0:T(8,128)S(1)}, f32[1,72,256]{2,1,0:T(8,128)S(1)}, u32[]{:S(2)}, u32[]{:S(2)}) collective-permute-start(f32[1,72,256]{2,1,0:T(8,128)S(1)} %add_bitcast_fusion), channel_id=1, source_target_pairs={{0,2},{1,3},{2,0},{3,1},{4,6},{5,7},{6,4},{7,5},{8,10},{9,11},{10,... | collective-permute-start | bytes 221192 | tf_op jit(solution)/shard_map/ppermute | solution.py:96
  279.9 4.7 %collective-permute-start.33 = (f32[2,72,256]{2,1,0:T(8,128)S(1)}, f32[2,72,256]{2,1,0:T(8,128)S(1)}, u32[]{:S(2)}, u32[]{:S(2)}) collective-permute-start(f32[2,72,256]{2,1,0:T(8,128)S(1)} %pad_maximum_fusion.1), channel_id=1, source_target_pairs={{0,4},{1,5},{2,6},{3,7},{4,0},{5,1},{6,2},{7,3},{8,12},{9,13},{10,... | collective-permute-start | bytes 442376 | tf_op jit(solution)/shard_map/ppermute | solution.py:96
  284.5 2.9 copy-start.5
  284.5 2.9 collective-permute-start.34
  287.5 0.7 copy-start.15
  (13 other events, 7.8 us)
Sparse Core Ops, SparseCore 0:
  86.9 33.0 reduce-scatter.4
  121.9 29.1 all-gather.2
  176.4 38.5 reduce-scatter.2

commit v5 on v4

--- a/solution.py
+++ b/solution.py
@@ -35,8 +35,12 @@
 VMEM_BYTES = 62 * 2**20
 
 
-def params(dims=1):
-    return pltpu.CompilerParams(vmem_limit_bytes=VMEM_BYTES, dimension_semantics=("arbitrary",) * dims)
+def params(spare=0):
+    return pltpu.CompilerParams(vmem_limit_bytes=VMEM_BYTES - spare * 2**20, dimension_semantics=("arbitrary",))
+
+
+def keep(x):
+    return pltpu.with_memory_space_constraint(x, pltpu.VMEM)
 
 
 def cost(us):
@@ -657,12 +661,12 @@
             put(chan_all),
         ],
         out_shape=[
-            jax.ShapeDtypeStruct((chan_all, hidden), F32),
+            pltpu.VMEM((chan_all, hidden), F32),
             jax.ShapeDtypeStruct((1, hidden), F32),
             jax.ShapeDtypeStruct((2, chan_all), F32),
-            jax.ShapeDtypeStruct((bands, area, chan_all), F32),
+            pltpu.VMEM((bands, area, chan_all), F32),
         ],
-        compiler_params=params(),
+        compiler_params=params(4),
         cost_estimate=cost(13),
         name="gather",
     )(own, gout, gains, biases, wt, w_high, w_low, *sums)
@@ -753,6 +757,7 @@
     hidden = wt.shape[1]
     chan_all = nz * chans
     reduced = se_weights[0].shape[0]
+    m, proj = keep(m), keep(proj)
     fixed = [gains, biases, wt, m, s, *se_weights, *ses, *sums]
     grid, tall, put, wide = by_steps(nz, bands, chans, area)
     return pl.pallas_call(
@@ -787,7 +792,7 @@
             jax.ShapeDtypeStruct(x.shape, F32),
             jax.ShapeDtypeStruct(m.shape, F32),
         ],
-        compiler_params=params(),
+        compiler_params=params(4),
         cost_estimate=cost(12),
         name="proj_back",
     )(own, gout, proj, x, *fixed)

time: 311 us -> 309 us (level)
  no operation moved by 1% of the time
where the time goes in v5:
time: 309 us; the launch traced here: 308 us
  Pallas kernels  155 us (50%)
  starting transfers between devices  67.9 us (22%)
  waiting for transfers between devices  56.4 us (18%)
  between operations  14.1 us (5%)
  other arithmetic  8.23 us (3%)
  local copies, waits for them, and re-layouts  6.36 us (2%)
    pallas_call x1, Pallas kernels, spread_back(): pl.pallas_call(partial(spread_back_kernel, len(backs), count), grid=(hidd...  37.4 us
    all_to_all x5, starting transfers between devices, deal(): return lax.all_to_all(x, SPREAD, 0, 0, tiled=True)  34.9 us
    ppermute x33, waiting for transfers between devices, exchange(): return lax.ppermute(x, ALL, [(i, i ^ stride) for i in range(n)])  32.6 us
    ppermute x33, starting transfers between devices, exchange(): return lax.ppermute(x, ALL, [(i, i ^ stride) for i in range(n)])  32.2 us
    all_to_all x5, waiting for transfers between devices, deal(): return lax.all_to_all(x, SPREAD, 0, 0, tiled=True)  23.1 us
    pallas_call x1, Pallas kernels, spread(): pl.pallas_call(partial(spread_kernel, len(sums), count), grid=(hidden //...  21.9 us
    pallas_call x1, Pallas kernels, proj_back(): pl.pallas_call(partial(proj_back_kernel, len(ses), len(sums), count), gri...  13.7 us
    pallas_call x2, Pallas kernels, input_grad(): pl.pallas_call(partial(input_kernel, len(sums), count, start), grid=(band...  13.6 us
  transfers between devices with their start and end apart: 43, of which 16 were waited for; matrix products, arithmetic and copies ran while one was open for 3% of the time, Pallas kernels for 48%

profile of v5, /device:TPU:15, one launch (start us, length us, event | category | flops | bytes accessed | tf_op | source)
XLA Modules:
  0.0 307.8 jit_solution(9967513728504843808)
XLA Ops:
  7.2 1.8 pack_weights.1
  9.1 2.3 collective-permute-start.1
  11.6 5.2 %crop.1 = f32[16,64,512]{2,1,0:T(8,128)} custom-call(s32[4]{0:T(128)} %left_ref.3, s32[4]{0:T(128)} %flip_ref.3, f32[16,64,640]{2,1,0:T(8,128)} %raw_ref.1), custom_call_target="tpu_custom_call" | custom-call | flops 5500000256 | bytes 17500000 | tf_op jit(solution)/shard_map/crop/pallas_call | solution.py:197
  16.8 0.6 collective-permute-done.2
  17.8 8.3 %all-to-all-start = ((f32[16,64,512]{2,1,0:T(8,128)}), f32[16,64,512]{2,1,0:T(8,128)}, u32[]{:S(2)}, u32[]{:S(2)}) async-start(f32[16,64,512]{2,1,0:T(8,128)} %crop.1), calls=%async_computation | async-start | bytes 4194304 | tf_op jit(solution)/shard_map/all_to_all | solution.py:121
  26.1 4.7 %order.1 = f32[16,64,512]{2,1,0:T(8,128)} custom-call(f32[16,64,512]{2,1,0:T(8,128)} %x_ref.1), custom_call_target="tpu_custom_call" | custom-call | flops 27499999232 | bytes 87500000 | tf_op jit(solution)/shard_map/order/pallas_call | solution.py:222
  31.3 14.4 %collective-permute-done.4 = f32[2,72,1024]{2,1,0:T(8,128)S(1)} collective-permute-done((f32[2,72,1024]{2,1,0:T(8,128)S(1)}, f32[2,72,1024]{2,1,0:T(8,128)S(1)}, u32[]{:S(2)}, u32[]{:S(2)}) %collective-permute-start.4) | collective-permute-done | bytes 589856 | tf_op jit(solution)/shard_map/ppermute | solution.py:100
  45.7 1.2 collective-permute-start.5
  47.5 1.9 collective-permute-done.5.refs_1_
  49.4 0.9 select_maximum_fusion
  50.5 4.6 %order_weights.1 = (bf16[256,1024]{1,0:T(8,128)(2,1)}, bf16[256,1024]{1,0:T(8,128)(2,1)}, bf16[1024,256]{1,0:T(8,128)(2,1)}, bf16[1024,256]{1,0:T(8,128)(2,1)}, ...) custom-call(s32[2]{0:T(128)} %pad_add_fusion.base_ref, ...), custom_call_target="tpu_custom_call" | custom-call | flops 3300000000 | bytes 10500000 | tf_op jit(solution)/shard_map/order_weights/pallas_call | solution.py:1285
  55.1 18.6 %all-to-all-done = f32[16,64,512]{2,1,0:T(8,128)} async-done(((f32[16,64,512]{2,1,0:T(8,128)}), f32[16,64,512]{2,1,0:T(8,128)}, u32[]{:S(2)}, u32[]{:S(2)}) %all-to-all-start) | async-done | bytes 2097184 | tf_op jit(solution)/shard_map/all_to_all | solution.py:121
  73.6 4.9 %all-to-all-start.1 = ((f32[16,64,512]{2,1,0:T(8,128)}), f32[16,64,512]{2,1,0:T(8,128)}, u32[]{:S(2)}, u32[]{:S(2)}) async-start(f32[16,64,512]{2,1,0:T(8,128)} %order.1), calls=%async_computation.1 | async-start | bytes 4194304 | tf_op jit(solution)/shard_map/all_to_all | solution.py:121
  78.6 8.2 %expand.1 = (f32[4,512,1024]{2,1,0:T(8,128)}, f32[2,1024]{1,0:T(2,128)}, f32[256,384]{1,0:T(8,128)}) custom-call(f32[4,4,64,512]{3,2,1,0:T(8,128)} %bitcast.5.x_ref, bf16[256,1024]{1,0:T(8,128)(2,1)} %get-tuple-element.120.high_ref, bf16[256,1024]{1,0:T(8,128)(2,1)} %get-tuple-element.121.low_ref.lower_ref), custom_call_target="tpu_custom_call" | custom-call | flops 8800000000 | bytes 28000000 | tf_op jit(solution)/shard_map/expand/pallas_call | solution.py:335
  87.3 1.0 collective-permute-done.6
  88.3 0.7 add.33.rest_0_.rest_4_
  89.0 1.1 slice_select_fusion
  90.4 1.2 collective-permute-start.10
  91.6 1.2 collective-permute-start.8
  94.4 3.7 %collective-permute-done.9.rest_2_.rest_6_ = f32[2,1024]{1,0:T(2,128)S(1)} collective-permute-done((f32[2,1024]{1,0:T(2,128)S(1)}, f32[2,1024]{1,0:T(2,128)S(1)}, u32[]{:S(2)}, u32[]{:S(2)}) %collective-permute-start.9) | collective-permute-done | bytes 8224 | tf_op jit(solution)/shard_map/ppermute | solution.py:100
  98.9 21.9 %spread.1 = (f32[32,8,8,1024]{3,2,1,0:T(8,128)}, f32[2,2,8,8,1024]{4,3,2,1,0:T(8,128)}, f32[2,2,8,8,1024]{4,3,2,1,0:T(8,128)}, f32[2,1024]{1,0:T(2,128)}) custom-call(s32[2]{0:T(128)} %add_convert_fusion.side_ref, f32[4,1,64,256]{3,2,1,0:T(8,128)} %copy-done.16, f32[4,1,64,256]{3,2,1,0:T(8,128)} %copy-done.16, f32[32,8,8,1024]{3,2,1,0:T(8,128)} %bitcast.47, ...), custom_call_target="tpu_custom_call" | custom-call | flops 11000000512 | bytes 35000000 | tf_op jit(solution)/shard_map/spread/pallas_call | solution.py:570
  120.8 1.1 collective-permute-start.11
  122.0 1.0 collective-permute-done.11
  123.0 0.7 add.34.rest_0_.rest_2_.rest_4_
  124.2 2.2 collective-permute-start.14
  126.4 1.0 slice_select_fusion.1
  128.2 11.0 %gather.1 = (f32[256,1024]{1,0:T(8,128)S(1)}, f32[1,1024]{1,0:T(1,128)}, f32[2,256]{1,0:T(2,128)}, f32[4,512,256]{2,1,0:T(8,128)S(1)}) custom-call(f32[4,512,1024]{2,1,0:T(8,128)} %bitcast.49, f32[4,4,64,512]{3,2,1,0:T(8,128)} %bitcast.12.gout_ref, f32[2,1024]{1,0:T(2,128)} %get-tuple-element.125.gain_ref, f32[2,1024]{1,0:T(2,128)} %get-tuple-element.126.bias_ref, ...), custom_call_target="tpu_custom_call" | custom-call | flops 14300000256 | bytes 45500000 | tf_op jit(solution)/shard_map/gather/pallas_call | solution.py:644
  139.2 1.4 collective-permute-start.15
  140.6 0.7 copy.25.down_ref
  142.4 13.7 %proj_back.1 = (f32[4,512,1024]{2,1,0:T(8,128)}, f32[2,1024]{1,0:T(2,128)}, f32[8,256]{1,0:T(8,128)}, f32[16,128]{1,0:T(8,128)}, bf16[256,1024]{1,0:T(8,128)(2,1...) custom-call(f32[4,512,1024]{2,1,0:T(8,128)} %bitcast.50, ...), custom_call_target="tpu_custom_call" | custom-call | flops 13200000000 | bytes 42000000 | tf_op jit(solution)/shard_map/proj_back/pallas_call | solution.py:763
  156.2 3.1 %collective-permute-start.17 = (f32[2,1024]{1,0:T(2,128)}, f32[2,1024]{1,0:T(2,128)S(1)}, u32[]{:S(2)}, u32[]{:S(2)}) collective-permute-start(f32[2,1024]{1,0:T(2,128)} %get-tuple-element.152.two_ref), channel_id=1, source_target_pairs={{0,1},{1,0},{2,3},{3,2},{4,5},{5,4},{6,7},{7,6},{8,9},{9,8},{10,11... | collective-permute-start | bytes 24584 | tf_op jit(solution)/shard_map/ppermute | solution.py:100
  159.3 1.0 collective-permute-done.17
  160.3 0.7 add.35.rest_8_
  161.0 1.2 collective-permute-start.18
  162.2 1.3 collective-permute-start.19
  163.7 6.8 %all-to-all-start.2 = ((f32[16,64,512]{2,1,0:T(8,128)}), f32[16,64,512]{2,1,0:T(8,128)}, u32[]{:S(2)}, u32[]{:S(2)}) async-start(f32[16,64,512]{2,1,0:T(8,128)} %bitcast.33), calls=%async_computation.2 | async-start | bytes 4194304 | tf_op jit(solution)/shard_map/all_to_all | solution.py:121
  171.9 37.4 %spread_back.1 = (f32[32,8,8,1024]{3,2,1,0:T(8,128)}, f32[2,1024]{1,0:T(2,128)}, f32[25,1024]{1,0:T(8,128)}) custom-call(s32[2]{0:T(128)} %add_convert_fusion.side_ref, f32[4,1,64,128]{3,2,1,0:T(8,128)} %copy-done.20, f32[4,1,64,128]{3,2,1,0:T(8,128)} %copy-done.20, f32[32,8,8,1024]{3,2,1,0:T(8,128)} %bitcast.48, ...), custom_call_target="tpu_custom_call" | custom-call | flops 165000003584 | bytes 525000000 | tf_op jit(solution)/shard_map/spread_back/pallas_call | solution.py:933
  210.7 0.7 add.36.rest_4_.rest_8_
  211.7 1.3 collective-permute-start.23
  213.0 1.1 collective-permute-start.24
  214.1 8.0 %weight_grad.1 = (f32[4,40,1024]{2,1,0:T(8,128)}, f32[4,40,1024]{2,1,0:T(8,128)}) custom-call(s32[3]{0:T(128)} %pad_add_fusion.1.ids_ref, f32[4,512,1024]{2,1,0:T(8,128)} %bitcast.51, f32[4,4,64,512]{3,2,1,0:T(8,128)} %bitcast.5.x_ref, f32[25,1024]{1,0:T(8,128)} %get-tuple-element.160.tap_ref, f32[2,1024]{1,0:T(2,128)} %get-tuple-element.153.one_ref, ...), custom_call_target="tpu_custom_call" | custom-call | flops 7699999744 | bytes 24500000 | tf_op jit(solution)/shard_map/weight_grad/pallas_call | solution.py:1058
  222.2 1.3 collective-permute-start.25
  224.0 6.8 %input_grad.2 = f32[4,4,64,256]{3,2,1,0:T(8,128)} custom-call(f32[4,512,1024]{2,1,0:T(8,128)} %bitcast.52, f32[4,512,1024]{2,1,0:T(8,128)} %get-tuple-element.124.hid_ref, f32[4,4,64,512]{3,2,1,0:T(8,128)} %bitcast.12.gout_ref, f32[2,1024]{1,0:T(2,128)} %get-tuple-element.125.gain_ref, bf16[1024,256]{1,0:T(8,128)(2,1)} %get-tuple-element.166.w_high, ...), custom_call_target="tpu_custom_call" | custom-call | flops 13200000000 | bytes 42000000 | tf_op jit(solution)/shard_map/input_grad/pallas_call | solution.py:988
  230.8 5.8 %all-to-all-start.3 = ((f32[16,64,256]{2,1,0:T(8,128)}), f32[16,64,256]{2,1,0:T(8,128)S(1)}, u32[]{:S(2)}, u32[]{:S(2)}) async-start(f32[16,64,256]{2,1,0:T(8,128)} %bitcast.35), calls=%async_computation.5 | async-start | bytes 2097152 | tf_op jit(solution)/shard_map/all_to_all | solution.py:121
  236.6 2.2 merge.1
  239.1 1.3 collective-permute-start.27
  240.4 1.1 collective-permute-start.28
  241.5 6.8 %input_grad.3 = f32[4,4,64,256]{3,2,1,0:T(8,128)} custom-call(f32[4,512,1024]{2,1,0:T(8,128)} %bitcast.53, f32[4,512,1024]{2,1,0:T(8,128)} %get-tuple-element.124.hid_ref, f32[4,4,64,512]{3,2,1,0:T(8,128)} %bitcast.12.gout_ref, f32[2,1024]{1,0:T(2,128)} %get-tuple-element.125.gain_ref, bf16[1024,256]{1,0:T(8,128)(2,1)} %get-tuple-element.166.w_high, ...), custom_call_target="tpu_custom_call" | custom-call | flops 13200000000 | bytes 42000000 | tf_op jit(solution)/shard_map/input_grad/pallas_call | solution.py:988
  248.3 4.8 %restore.1 = f32[16,64,512]{2,1,0:T(8,128)} custom-call(f32[16,64,512]{2,1,0:T(8,128)} %all-to-all-done.2.x_ref), custom_call_target="tpu_custom_call" | custom-call | flops 1100000000 | bytes 3500000 | tf_op jit(solution)/shard_map/restore/pallas_call | solution.py:243
  253.1 0.6 copy-done.17
  253.9 2.6 collect.1
  256.5 3.2 %collective-permute-start.29 = (f32[72,256]{1,0:T(8,128)}, f32[72,256]{1,0:T(8,128)S(1)}, u32[]{:S(2)}, u32[]{:S(2)}) collective-permute-start(f32[72,256]{1,0:T(8,128)} %get-tuple-element.191), channel_id=1, source_target_pairs={{0,8},{1,9},{2,10},{3,11},{4,12},{5,13},{6,14},{7,15},{8,0},{9,1},... | collective-permute-start | bytes 221192 | tf_op jit(solution)/shard_map/ppermute | solution.py:100
  260.1 0.9 collective-permute-start.31
  261.0 0.8 copy.27.col_ref
  261.8 9.0 %all-to-all-start.4 = ((f32[16,64,256]{2,1,0:T(8,128)}), f32[16,64,256]{2,1,0:T(8,128)}, u32[]{:S(2)}, u32[]{:S(2)}) async-start(f32[16,64,256]{2,1,0:T(8,128)} %bitcast.34), calls=%async_computation.6 | async-start | bytes 2097152 | tf_op jit(solution)/shard_map/all_to_all | solution.py:121
  271.2 4.7 %prepare.1 = (f32[138,1024]{1,0:T(8,128)}, f32[138,1024]{1,0:T(8,128)}, f32[138,1024]{1,0:T(8,128)}) custom-call(s32[1]{0:T(128)} %constant.21.clone.1.base_ref, s32[138,1]{1,0:T(8,128)} %copy.27.col_ref, f32[256,256]{1,0:T(8,128)} %we_ref.3, f32[25,256]{1,0:T(8,128)} %dw_ref.3, f32[2,256]{1,0:T(2,128)} %gain_ref.3, f32[2,256]{1,0:T(2,128)} %bias_ref.3, ...), custom_call_target="tpu_custom_call" | custom-call | flops 1100000000 | bytes 3500000 | tf_op jit(solution)/shard_map/prepare/pallas_call | solution.py:1432
  275.9 2.1 collective-permute-done.32
  278.2 4.4 %collective-permute-done.33 = f32[2,72,256]{2,1,0:T(8,128)S(1)} collective-permute-done((f32[2,72,256]{2,1,0:T(8,128)S(1)}, f32[2,72,256]{2,1,0:T(8,128)S(1)}, u32[]{:S(2)}, u32[]{:S(2)}) %collective-permute-start.33) | collective-permute-done | bytes 147488 | tf_op jit(solution)/shard_map/ppermute | solution.py:100
  282.7 1.7 collective-permute-start.34
  285.0 0.6 collective-permute-done.34.rest_1_
  285.6 0.7 copy-done.15
  286.3 4.9 %adam.1 = (f32[26,1,1024]{2,1,0:T(1,128)}, f32[26,1,1024]{2,1,0:T(1,128)}, f32[1,140624]{1,0:T(1,128)}) custom-call(s32[2]{0:T(128)} %pad_add_fusion.2.me_ref, s32[138,1]{1,0:T(8,128)} %copy.27.col_ref, f32[138,1024]{1,0:T(8,128)} %get-tuple-element.200.weight_ref, f32[138,1024]{1,0:T(8,128)} %get-tuple-element.201.old_one_ref, ...), custom_call_target="tpu_custom_call" | custom-call | flops 11000000512 | bytes 35000000 | tf_op jit(solution)/shard_map/adam/pallas_call | solution.py:1530
  291.2 4.5 %all-to-all-done.4.y_ref = f32[16,64,256]{2,1,0:T(8,128)} async-done(((f32[16,64,256]{2,1,0:T(8,128)}), f32[16,64,256]{2,1,0:T(8,128)}, u32[]{:S(2)}, u32[]{:S(2)}) %all-to-all-start.4) | async-done | bytes 1048608 | tf_op jit(solution)/shard_map/all_to_all | solution.py:121
  295.8 5.5 %uncrop.1 = f32[16,64,640]{2,1,0:T(8,128)} custom-call(s32[4]{0:T(128)} %left_ref.3, s32[4]{0:T(128)} %flip_ref.3, f32[16,64,256]{2,1,0:T(8,128)} %copy-done, f32[16,64,256]{2,1,0:T(8,128)} %all-to-all-done.4.y_ref), custom_call_target="tpu_custom_call" | custom-call | flops 1100000000 | bytes 3500000 | tf_op jit(solution)/shard_map/uncrop/pallas_call | solution.py:272
  (133 shorter events, 13.4 us)
Async XLA Ops:
  9.0 8.5 %copy-start.4 = (f32[72,256]{1,0:T(8,128)S(1)}, f32[72,256]{1,0:T(8,128)}, u32[]{:S(2)}) copy-start(f32[72,256]{1,0:T(8,128)} %pack_weights.1) | copy-start | bytes 221188
  9.0 7.9 %collective-permute-start = (f32[72,256]{1,0:T(8,128)}, f32[72,256]{1,0:T(8,128)S(1)}, u32[]{:S(2)}, u32[]{:S(2)}) collective-permute-start(f32[72,256]{1,0:T(8,128)} %pack_weights.1), channel_id=1, source_target_pairs={{0,8},{1,9},{2,10},{3,11},{4,12},{5,13},{6,14},{7,15},{8,0},{9,1},... | collective-permute-start | bytes 221192 | tf_op jit(solution)/shard_map/ppermute | solution.py:100
  9.1 7.7 %collective-permute-start.1 = (f32[72,256]{1,0:T(8,128)}, f32[72,256]{1,0:T(8,128)S(1)}, u32[]{:S(2)}, u32[]{:S(2)}) collective-permute-start(f32[72,256]{1,0:T(8,128)} %pack_weights.1), channel_id=1, source_target_pairs={{0,16},{1,17},{2,18},{3,19},{4,20},{5,21},{6,22},{7,23},{8,24},{9,... | collective-permute-start | bytes 221192 | tf_op jit(solution)/shard_map/ppermute | solution.py:100
  11.4 6.0 %collective-permute-start.2 = (f32[72,256]{1,0:T(8,128)}, f32[72,256]{1,0:T(8,128)S(1)}, u32[]{:S(2)}, u32[]{:S(2)}) collective-permute-start(f32[72,256]{1,0:T(8,128)} %pack_weights.1), channel_id=1, source_target_pairs={{0,24},{1,25},{2,26},{3,27},{4,28},{5,29},{6,30},{7,31},{8,16},{9,... | collective-permute-start | bytes 221192 | tf_op jit(solution)/shard_map/ppermute | solution.py:100
  17.5 13.4 %collective-permute-start.3 = (f32[1,72,1024]{2,1,0:T(8,128)S(1)}, f32[1,72,1024]{2,1,0:T(8,128)S(1)}, u32[]{:S(2)}, u32[]{:S(2)}) collective-permute-start(f32[1,72,1024]{2,1,0:T(8,128)S(1)} %maximum_bitcast_fusion), channel_id=1, source_target_pairs={{0,2},{1,3},{2,0},{3,1},{4,6},{5,7},{6,4},{7,5},{8,10},{9,11},{10,... | collective-permute-start | bytes 884744 | tf_op jit(solution)/shard_map/ppermute | solution.py:100
  17.8 55.9 %all-to-all-start = ((f32[16,64,512]{2,1,0:T(8,128)}), f32[16,64,512]{2,1,0:T(8,128)}, u32[]{:S(2)}, u32[]{:S(2)}) async-start(f32[16,64,512]{2,1,0:T(8,128)} %crop.1), calls=%async_computation | async-start | bytes 4194304 | tf_op jit(solution)/shard_map/all_to_all | solution.py:121
  30.9 18.5 %copy-start.2 = (f32[1,26,1024]{2,0,1:T(1,128)S(1)}, f32[1,26,1024]{2,0,1:T(1,128)}, u32[]{:S(2)}) copy-start(f32[1,26,1024]{2,0,1:T(1,128)} %param.31) | copy-start | bytes 319492
  30.9 18.5 %copy-start.3 = (f32[1,26,1024]{2,0,1:T(1,128)S(1)}, f32[1,26,1024]{2,0,1:T(1,128)}, u32[]{:S(2)}) copy-start(f32[1,26,1024]{2,0,1:T(1,128)} %param.30) | copy-start | bytes 319492
  30.9 14.7 %collective-permute-start.4 = (f32[2,72,1024]{2,1,0:T(8,128)S(1)}, f32[2,72,1024]{2,1,0:T(8,128)S(1)}, u32[]{:S(2)}, u32[]{:S(2)}) collective-permute-start(f32[2,72,1024]{2,1,0:T(8,128)S(1)} %pad_maximum_fusion), channel_id=1, source_target_pairs={{0,4},{1,5},{2,6},{3,7},{4,0},{5,1},{6,2},{7,3},{8,12},{9,13},{10,... | collective-permute-start | bytes 1769480 | tf_op jit(solution)/shard_map/ppermute | solution.py:100
  45.7 4.8 %copy-start.1 = (f32[4,72,1024]{2,1,0:T(8,128)}, f32[4,72,1024]{2,1,0:T(8,128)S(1)}, u32[]{:S(2)}) copy-start(f32[4,72,1024]{2,1,0:T(8,128)S(1)} %constant_dynamic-update-slice_fusion.refs_0_) | copy-start | bytes 3538948
  45.7 3.6 %collective-permute-start.5 = (f32[4,72,1024]{2,1,0:T(8,128)S(1)}, f32[4,72,1024]{2,1,0:T(8,128)S(1)}, u32[]{:S(2)}, u32[]{:S(2)}) collective-permute-start(f32[4,72,1024]{2,1,0:T(8,128)S(1)} %constant_dynamic-update-slice_fusion.refs_0_), channel_id=1, source_target_pairs={{0,1},{1,0},{2,3},{3,2},{4,5},{5,4},{6,7},{7,6},{8,9},{9,8},{10,11... | collective-permute-start | bytes 3538952 | tf_op jit(solution)/shard_map/ppermute | solution.py:100
  49.3 1.1 copy-start.13
  73.6 52.7 %all-to-all-start.1 = ((f32[16,64,512]{2,1,0:T(8,128)}), f32[16,64,512]{2,1,0:T(8,128)}, u32[]{:S(2)}, u32[]{:S(2)}) async-start(f32[16,64,512]{2,1,0:T(8,128)} %order.1), calls=%async_computation.1 | async-start | bytes 4194304 | tf_op jit(solution)/shard_map/all_to_all | solution.py:121
  78.5 143.6 %reduce-scatter.5.cloned.1.call-start = ((), (), s32[]{:S(2)}) async-start(), calls=%async_computation.8 | async-start | bytes 442368 | tf_op jit(solution)/shard_map/reduce_scatter | solution.py:1700
  86.8 135.3 %all-gather.3.cloned.1.call-start = ((), (), s32[]{:S(2)}) async-start(), calls=%async_computation.9 | async-start | bytes 2359296 | tf_op jit(solution)/shard_map/all_gather | solution.py:1640
  86.9 1.5 collective-permute-start.6
  89.0 9.2 %copy-start.7 = (f32[2,1024]{1,0:T(2,128)}, f32[2,1024]{1,0:T(2,128)S(1)}, u32[]{:S(2)}) copy-start(f32[2,1024]{1,0:T(2,128)S(1)} %add.33.rest_0_.rest_4_) | copy-start | bytes 24580
  90.1 8.1 %collective-permute-start.7 = (f32[4,1,64,256]{3,2,1,0:T(8,128)S(1)}, f32[4,1,64,256]{3,2,1,0:T(8,128)S(1)}, u32[]{:S(2)}, u32[]{:S(2)}) collective-permute-start(f32[4,1,64,256]{3,2,1,0:T(8,128)S(1)} %slice_select_fusion), channel_id=1, source_target_pairs={{0,4},{4,0},{1,5},{5,1},{2,6},{6,2},{3,7},{7,3},{8,12},{12,8},{9,1... | collective-permute-start | bytes 786440 | tf_op jit(solution)/shard_map/ppermute | solution.py:136
  90.4 3.6 %collective-permute-start.10 = (f32[2,1024]{1,0:T(2,128)S(1)}, f32[2,1024]{1,0:T(2,128)S(1)}, u32[]{:S(2)}, u32[]{:S(2)}) collective-permute-start(f32[2,1024]{1,0:T(2,128)S(1)} %add.33.rest_0_.rest_4_), channel_id=1, source_target_pairs={{0,6},{1,7},{2,4},{3,5},{4,2},{5,3},{6,0},{7,1},{8,14},{9,15},{10,... | collective-permute-start | bytes 24584 | tf_op jit(solution)/shard_map/ppermute | solution.py:100
  91.6 2.8 collective-permute-start.8
  92.8 5.4 %collective-permute-start.9 = (f32[2,1024]{1,0:T(2,128)S(1)}, f32[2,1024]{1,0:T(2,128)S(1)}, u32[]{:S(2)}, u32[]{:S(2)}) collective-permute-start(f32[2,1024]{1,0:T(2,128)S(1)} %add.33.rest_0_.rest_4_), channel_id=1, source_target_pairs={{0,4},{1,5},{2,6},{3,7},{4,0},{5,1},{6,2},{7,3},{8,12},{9,13},{10,... | collective-permute-start | bytes 24584 | tf_op jit(solution)/shard_map/ppermute | solution.py:100
  94.0 4.2 %copy-start.21 = (f32[2,1024]{1,0:T(2,128)}, f32[2,1024]{1,0:T(2,128)S(1)}, u32[]{:S(2)}) copy-start(f32[2,1024]{1,0:T(2,128)S(1)} %collective-permute-done.10.rest_3_.rest_7_) | copy-start | bytes 24580
  94.4 3.8 %copy-start.22 = (f32[2,1024]{1,0:T(2,128)}, f32[2,1024]{1,0:T(2,128)S(1)}, u32[]{:S(2)}) copy-start(f32[2,1024]{1,0:T(2,128)S(1)} %collective-permute-done.8.rest_1_.rest_5_) | copy-start | bytes 24580
  120.8 2.2 collective-permute-start.11
  123.7 3.9 %copy-start.8 = (f32[2,1024]{1,0:T(2,128)}, f32[2,1024]{1,0:T(2,128)S(1)}, u32[]{:S(2)}) copy-start(f32[2,1024]{1,0:T(2,128)S(1)} %add.34.rest_0_.rest_2_.rest_4_) | copy-start | bytes 24580
  123.7 3.9 %collective-permute-start.12 = (f32[2,1024]{1,0:T(2,128)S(1)}, f32[2,1024]{1,0:T(2,128)S(1)}, u32[]{:S(2)}, u32[]{:S(2)}) collective-permute-start(f32[2,1024]{1,0:T(2,128)S(1)} %add.34.rest_0_.rest_2_.rest_4_), channel_id=1, source_target_pairs={{0,2},{1,3},{2,0},{3,1},{4,6},{5,7},{6,4},{7,5},{8,10},{9,11},{10,... | collective-permute-start | bytes 24584 | tf_op jit(solution)/shard_map/ppermute | solution.py:100
  124.0 3.6 %collective-permute-start.13 = (f32[2,1024]{1,0:T(2,128)S(1)}, f32[2,1024]{1,0:T(2,128)S(1)}, u32[]{:S(2)}, u32[]{:S(2)}) collective-permute-start(f32[2,1024]{1,0:T(2,128)S(1)} %add.34.rest_0_.rest_2_.rest_4_), channel_id=1, source_target_pairs={{0,4},{1,5},{2,6},{3,7},{4,0},{5,1},{6,2},{7,3},{8,12},{9,13},{10,... | collective-permute-start | bytes 24584 | tf_op jit(solution)/shard_map/ppermute | solution.py:100
  124.2 3.5 %collective-permute-start.14 = (f32[2,1024]{1,0:T(2,128)S(1)}, f32[2,1024]{1,0:T(2,128)S(1)}, u32[]{:S(2)}, u32[]{:S(2)}) collective-permute-start(f32[2,1024]{1,0:T(2,128)S(1)} %add.34.rest_0_.rest_2_.rest_4_), channel_id=1, source_target_pairs={{0,6},{1,7},{2,4},{3,5},{4,2},{5,3},{6,0},{7,1},{8,14},{9,15},{10,... | collective-permute-start | bytes 24584 | tf_op jit(solution)/shard_map/ppermute | solution.py:100
  127.4 14.5 %collective-permute-start.16 = (f32[4,1,64,128]{3,2,1,0:T(8,128)S(1)}, f32[4,1,64,128]{3,2,1,0:T(8,128)S(1)}, u32[]{:S(2)}, u32[]{:S(2)}) collective-permute-start(f32[4,1,64,128]{3,2,1,0:T(8,128)S(1)} %slice_select_fusion.1), channel_id=1, source_target_pairs={{0,4},{4,0},{1,5},{5,1},{2,6},{6,2},{3,7},{7,3},{8,12},{12,8},{9,1... | collective-permute-start | bytes 393224 | tf_op jit(solution)/shard_map/ppermute | solution.py:136
  128.2 12.4 %copy-start.12 = (f32[16]{0:T(128)S(1)}, f32[16]{0:T(128)}, u32[]{:S(2)}) copy-start(f32[16]{0:T(128)} %param.27) | copy-start | bytes 196
  139.2 2.6 collective-permute-start.15
  141.9 14.3 %copy-start.20 = (f32[4,1,64,128]{3,2,1,0:T(8,128)}, f32[4,1,64,128]{3,2,1,0:T(8,128)S(1)}, u32[]{:S(2)}) copy-start(f32[4,1,64,128]{3,2,1,0:T(8,128)S(1)} %collective-permute-done.16.top_ref.low_ref) | copy-start | bytes 393220
  156.2 4.1 %collective-permute-start.17 = (f32[2,1024]{1,0:T(2,128)}, f32[2,1024]{1,0:T(2,128)S(1)}, u32[]{:S(2)}, u32[]{:S(2)}) collective-permute-start(f32[2,1024]{1,0:T(2,128)} %get-tuple-element.152.two_ref), channel_id=1, source_target_pairs={{0,1},{1,0},{2,3},{3,2},{4,5},{5,4},{6,7},{7,6},{8,9},{9,8},{10,11... | collective-permute-start | bytes 24584 | tf_op jit(solution)/shard_map/ppermute | solution.py:100
  161.0 2.7 copy-start.10
  161.0 10.2 %collective-permute-start.18 = (f32[2,1024]{1,0:T(2,128)S(1)}, f32[2,1024]{1,0:T(2,128)S(1)}, u32[]{:S(2)}, u32[]{:S(2)}) collective-permute-start(f32[2,1024]{1,0:T(2,128)S(1)} %add.35.rest_8_), channel_id=1, source_target_pairs={{0,2},{1,3},{2,0},{3,1},{4,6},{5,7},{6,4},{7,5},{8,10},{9,11},{10,... | collective-permute-start | bytes 24584 | tf_op jit(solution)/shard_map/ppermute | solution.py:100
  162.2 9.1 %collective-permute-start.19 = (f32[2,1024]{1,0:T(2,128)S(1)}, f32[2,1024]{1,0:T(2,128)S(1)}, u32[]{:S(2)}, u32[]{:S(2)}) collective-permute-start(f32[2,1024]{1,0:T(2,128)S(1)} %add.35.rest_8_), channel_id=1, source_target_pairs={{0,4},{1,5},{2,6},{3,7},{4,0},{5,1},{6,2},{7,3},{8,12},{9,13},{10,... | collective-permute-start | bytes 24584 | tf_op jit(solution)/shard_map/ppermute | solution.py:100
  163.5 7.8 %collective-permute-start.20 = (f32[2,1024]{1,0:T(2,128)S(1)}, f32[2,1024]{1,0:T(2,128)S(1)}, u32[]{:S(2)}, u32[]{:S(2)}) collective-permute-start(f32[2,1024]{1,0:T(2,128)S(1)} %add.35.rest_8_), channel_id=1, source_target_pairs={{0,6},{1,7},{2,4},{3,5},{4,2},{5,3},{6,0},{7,1},{8,14},{9,15},{10,... | collective-permute-start | bytes 24584 | tf_op jit(solution)/shard_map/ppermute | solution.py:100
  163.7 58.5 %all-to-all-start.2 = ((f32[16,64,512]{2,1,0:T(8,128)}), f32[16,64,512]{2,1,0:T(8,128)}, u32[]{:S(2)}, u32[]{:S(2)}) async-start(f32[16,64,512]{2,1,0:T(8,128)} %bitcast.33), calls=%async_computation.2 | async-start | bytes 4194304 | tf_op jit(solution)/shard_map/all_to_all | solution.py:121
  170.5 51.6 %reduce-scatter.3.cloned.1.call-start = ((), (), s32[]{:S(2)}) async-start(), calls=%async_computation.7 | async-start | bytes 1179648 | tf_op jit(solution)/shard_map/reduce_scatter | solution.py:1699
  209.3 1.5 collective-permute-start.21
  211.4 10.7 %copy-start.9 = (f32[2,1024]{1,0:T(2,128)}, f32[2,1024]{1,0:T(2,128)S(1)}, u32[]{:S(2)}) copy-start(f32[2,1024]{1,0:T(2,128)S(1)} %add.36.rest_4_.rest_8_) | copy-start | bytes 24580
  211.4 12.0 %collective-permute-start.22 = (f32[2,1024]{1,0:T(2,128)S(1)}, f32[2,1024]{1,0:T(2,128)S(1)}, u32[]{:S(2)}, u32[]{:S(2)}) collective-permute-start(f32[2,1024]{1,0:T(2,128)S(1)} %add.36.rest_4_.rest_8_), channel_id=1, source_target_pairs={{0,2},{1,3},{2,0},{3,1},{4,6},{5,7},{6,4},{7,5},{8,10},{9,11},{10,... | collective-permute-start | bytes 24584 | tf_op jit(solution)/shard_map/ppermute | solution.py:100
  211.7 11.7 %collective-permute-start.23 = (f32[2,1024]{1,0:T(2,128)S(1)}, f32[2,1024]{1,0:T(2,128)S(1)}, u32[]{:S(2)}, u32[]{:S(2)}) collective-permute-start(f32[2,1024]{1,0:T(2,128)S(1)} %add.36.rest_4_.rest_8_), channel_id=1, source_target_pairs={{0,4},{1,5},{2,6},{3,7},{4,0},{5,1},{6,2},{7,3},{8,12},{9,13},{10,... | collective-permute-start | bytes 24584 | tf_op jit(solution)/shard_map/ppermute | solution.py:100
  213.0 10.4 %collective-permute-start.24 = (f32[2,1024]{1,0:T(2,128)S(1)}, f32[2,1024]{1,0:T(2,128)S(1)}, u32[]{:S(2)}, u32[]{:S(2)}) collective-permute-start(f32[2,1024]{1,0:T(2,128)S(1)} %add.36.rest_4_.rest_8_), channel_id=1, source_target_pairs={{0,6},{1,7},{2,4},{3,5},{4,2},{5,3},{6,0},{7,1},{8,14},{9,15},{10,... | collective-permute-start | bytes 24584 | tf_op jit(solution)/shard_map/ppermute | solution.py:100
  222.2 8.7 %collective-permute-start.25 = (f32[4,40,1024]{2,1,0:T(8,128)}, f32[4,40,1024]{2,1,0:T(8,128)S(1)}, u32[]{:S(2)}, u32[]{:S(2)}) collective-permute-start(f32[4,40,1024]{2,1,0:T(8,128)} %get-tuple-element.170), channel_id=1, source_target_pairs={{0,1},{1,0},{2,3},{3,2},{4,5},{5,4},{6,7},{7,6},{8,9},{9,8},{10,11... | collective-permute-start | bytes 1966088 | tf_op jit(solution)/shard_map/ppermute | solution.py:100
  230.8 5.8 %copy-start.14 = (f32[4,40,1024]{2,1,0:T(8,128)}, f32[4,40,1024]{2,1,0:T(8,128)S(1)}, u32[]{:S(2)}) copy-start(f32[4,40,1024]{2,1,0:T(8,128)S(1)} %collective-permute-done.25.two_ref) | copy-start | bytes 1966084
  230.8 30.9 %all-to-all-start.3 = ((f32[16,64,256]{2,1,0:T(8,128)}), f32[16,64,256]{2,1,0:T(8,128)S(1)}, u32[]{:S(2)}, u32[]{:S(2)}) async-start(f32[16,64,256]{2,1,0:T(8,128)} %bitcast.35), calls=%async_computation.5 | async-start | bytes 2097152 | tf_op jit(solution)/shard_map/all_to_all | solution.py:121
  238.8 14.3 %collective-permute-start.26 = (f32[40,1024]{1,0:T(8,128)}, f32[40,1024]{1,0:T(8,128)S(1)}, u32[]{:S(2)}, u32[]{:S(2)}) collective-permute-start(f32[40,1024]{1,0:T(8,128)} %get-tuple-element.178), channel_id=1, source_target_pairs={{0,2},{1,3},{2,0},{3,1},{4,6},{5,7},{6,4},{7,5},{8,10},{9,11},{10,... | collective-permute-start | bytes 491528 | tf_op jit(solution)/shard_map/ppermute | solution.py:100
  239.1 14.0 %collective-permute-start.27 = (f32[40,1024]{1,0:T(8,128)}, f32[40,1024]{1,0:T(8,128)S(1)}, u32[]{:S(2)}, u32[]{:S(2)}) collective-permute-start(f32[40,1024]{1,0:T(8,128)} %get-tuple-element.179), channel_id=1, source_target_pairs={{0,4},{1,5},{2,6},{3,7},{4,0},{5,1},{6,2},{7,3},{8,12},{9,13},{10,... | collective-permute-start | bytes 491528 | tf_op jit(solution)/shard_map/ppermute | solution.py:100
  240.4 12.7 %collective-permute-start.28 = (f32[40,1024]{1,0:T(8,128)}, f32[40,1024]{1,0:T(8,128)S(1)}, u32[]{:S(2)}, u32[]{:S(2)}) collective-permute-start(f32[40,1024]{1,0:T(8,128)} %get-tuple-element.180), channel_id=1, source_target_pairs={{0,6},{1,7},{2,4},{3,5},{4,2},{5,3},{6,0},{7,1},{8,14},{9,15},{10,... | collective-permute-start | bytes 491528 | tf_op jit(solution)/shard_map/ppermute | solution.py:100
  253.1 0.7 copy-start.18
  253.1 0.8 copy-start.19
  253.9 7.1 %copy-start.11 = (s32[138,1]{0,1:T(1,128)S(1)}, s32[138,1]{0,1:T(1,128)}, u32[]{:S(2)}) copy-start(s32[138,1]{0,1:T(1,128)} %param.20) | copy-start | bytes 1660
  256.5 14.3 %copy-start.6 = (f32[72,256]{1,0:T(8,128)S(1)}, f32[72,256]{1,0:T(8,128)}, u32[]{:S(2)}) copy-start(f32[72,256]{1,0:T(8,128)} %get-tuple-element.190) | copy-start | bytes 221188
  256.5 14.3 %collective-permute-start.29 = (f32[72,256]{1,0:T(8,128)}, f32[72,256]{1,0:T(8,128)S(1)}, u32[]{:S(2)}, u32[]{:S(2)}) collective-permute-start(f32[72,256]{1,0:T(8,128)} %get-tuple-element.191), channel_id=1, source_target_pairs={{0,8},{1,9},{2,10},{3,11},{4,12},{5,13},{6,14},{7,15},{8,0},{9,1},... | collective-permute-start | bytes 221192 | tf_op jit(solution)/shard_map/ppermute | solution.py:100
  259.8 11.1 %collective-permute-start.30 = (f32[72,256]{1,0:T(8,128)}, f32[72,256]{1,0:T(8,128)S(1)}, u32[]{:S(2)}, u32[]{:S(2)}) collective-permute-start(f32[72,256]{1,0:T(8,128)} %get-tuple-element.192), channel_id=1, source_target_pairs={{0,16},{1,17},{2,18},{3,19},{4,20},{5,21},{6,22},{7,23},{8,24},{9,... | collective-permute-start | bytes 221192 | tf_op jit(solution)/shard_map/ppermute | solution.py:100
  260.1 10.7 %collective-permute-start.31 = (f32[72,256]{1,0:T(8,128)}, f32[72,256]{1,0:T(8,128)S(1)}, u32[]{:S(2)}, u32[]{:S(2)}) collective-permute-start(f32[72,256]{1,0:T(8,128)} %get-tuple-element.193), channel_id=1, source_target_pairs={{0,24},{1,25},{2,26},{3,27},{4,28},{5,29},{6,30},{7,31},{8,16},{9,... | collective-permute-start | bytes 221192 | tf_op jit(solution)/shard_map/ppermute | solution.py:100
  261.8 14.1 %copy-start = (f32[16,64,256]{2,1,0:T(8,128)}, f32[16,64,256]{2,1,0:T(8,128)S(1)}, u32[]{:S(2)}) copy-start(f32[16,64,256]{2,1,0:T(8,128)S(1)} %all-to-all-done.3.x_ref) | copy-start | bytes 3145732
  261.8 34.0 %all-to-all-start.4 = ((f32[16,64,256]{2,1,0:T(8,128)}), f32[16,64,256]{2,1,0:T(8,128)}, u32[]{:S(2)}, u32[]{:S(2)}) async-start(f32[16,64,256]{2,1,0:T(8,128)} %bitcast.34), calls=%async_computation.6 | async-start | bytes 2097152 | tf_op jit(solution)/shard_map/all_to_all | solution.py:121
  270.9 7.1 %collective-permute-start.32 = (f32[1,72,256]{2,1,0:T(8,128)S(1)}, f32[1,72,256]{2,1,0:T(8,128)S(1)}, u32[]{:S(2)}, u32[]{:S(2)}) collective-permute-start(f32[1,72,256]{2,1,0:T(8,128)S(1)} %add_bitcast_fusion), channel_id=1, source_target_pairs={{0,2},{1,3},{2,0},{3,1},{4,6},{5,7},{6,4},{7,5},{8,10},{9,11},{10,... | collective-permute-start | bytes 221192 | tf_op jit(solution)/shard_map/ppermute | solution.py:100
  278.0 4.7 %collective-permute-start.33 = (f32[2,72,256]{2,1,0:T(8,128)S(1)}, f32[2,72,256]{2,1,0:T(8,128)S(1)}, u32[]{:S(2)}, u32[]{:S(2)}) collective-permute-start(f32[2,72,256]{2,1,0:T(8,128)S(1)} %pad_maximum_fusion.1), channel_id=1, source_target_pairs={{0,4},{1,5},{2,6},{3,7},{4,0},{5,1},{6,2},{7,3},{8,12},{9,13},{10,... | collective-permute-start | bytes 442376 | tf_op jit(solution)/shard_map/ppermute | solution.py:100
  282.6 2.9 copy-start.5
  282.7 2.9 collective-permute-start.34
  285.6 0.7 copy-start.15
  (13 other events, 7.9 us)
Sparse Core Ops, SparseCore 0:
  86.9 33.0 reduce-scatter.4
  121.9 29.1 all-gather.2
  175.1 38.5 reduce-scatter.2

commit v6 on v5

--- a/solution.py
+++ b/solution.py
@@ -607,7 +607,7 @@
 
 
 def gather_kernel(parts, count, own_ref, gout_ref, gain_ref, bias_ref, wt_ref, high_ref, low_ref, *rest):
-    sums, (m_ref, s_ref, se_ref, proj_ref) = rest[:parts], rest[parts:]
+    sums, (m_ref, s_ref, se_ref, proj_ref, h_ref) = rest[:parts], rest[parts:]
     t = pl.program_id(0)
     chan_all, hidden = wt_ref.shape
 
@@ -621,7 +621,9 @@
     gout = split(gout_ref[:, 0].reshape(chan_all, gout_ref.shape[3]))
     proj = None
     for cut in chunks(hidden):
-        act = swish_half(own_ref[0, :, cut] * scale[:, cut] + shift[:, cut])
+        h = own_ref[0, :, cut] * scale[:, cut] + shift[:, cut]
+        h_ref[0, :, cut] = h
+        act = swish_half(h)
         s_ref[0:1, cut] += jnp.sum(act, axis=0, keepdims=True)
         act = split(act)
         m_ref[:, cut] += dot3(gout, act)
@@ -659,14 +661,16 @@
             whole((1, hidden)),
             whole((2, chan_all)),
             put(chan_all),
+            put(hidden),
         ],
         out_shape=[
             pltpu.VMEM((chan_all, hidden), F32),
             jax.ShapeDtypeStruct((1, hidden), F32),
             jax.ShapeDtypeStruct((2, chan_all), F32),
             pltpu.VMEM((bands, area, chan_all), F32),
+            pltpu.VMEM((bands, area, hidden), F32),
         ],
-        compiler_params=params(4),
+        compiler_params=params(13),
         cost_estimate=cost(13),
         name="gather",
     )(own, gout, gains, biases, wt, w_high, w_low, *sums)
@@ -682,7 +686,7 @@
 
 
 def second_grad(gout, weights, k_row, value, terms, cut):
-    h = value * terms[0][:, cut] + terms[1][:, cut]
+    h = value if terms is None else value * terms[0][:, cut] + terms[1][:, cut]
     return (dot3(gout, (weights[0][:, cut], weights[1][:, cut])) + k_row[:, cut]) * slope_half(h), h
 
 
@@ -714,7 +718,10 @@
         se = total(ses)
         pooled = se[0:1] / (FRAME_ROWS * FRAME_COLUMNS)
         sqt, ex = sqt_ref[...], ex_ref[...]
-        pre = jnp.sum(sqt * pooled, axis=1, keepdims=True) + down_ref[...]
+        n = ex.shape[0]
+        same = lax.broadcasted_iota(jnp.int32, (n, n), 0) == lax.broadcasted_iota(jnp.int32, (n, n), 1)
+        down = jnp.sum(jnp.where(same, down_ref[...], 0.0), axis=1, keepdims=True)
+        pre = jnp.sum(sqt * pooled, axis=1, keepdims=True) + down
         gate = sigmoid(pre)
         squeezed = pre * gate
         excite = sigmoid(jnp.sum(ex * squeezed, axis=0, keepdims=True) + exb_ref[...])
@@ -736,10 +743,9 @@
         grad_ref[...] = tall_excite * m_ref[...] + tall_pool * s_ref[...]
         sum_ref[...] = jnp.zeros_like(sum_ref)
 
-    terms = slope_terms(total(sums), count, gain_ref, bias_ref)
     gout = split(gout_ref[:, 0].reshape(chan_all, gout_ref.shape[3]).T)
     for cut in chunks(hidden):
-        q, h = second_grad(gout, (w_high, w_low), k_row, own_ref[0, :, cut], terms, cut)
+        q, h = second_grad(gout, (w_high, w_low), k_row, own_ref[0, :, cut], None, cut)
         q_ref[0, :, cut] = q
         sum_ref[0:1, cut] += jnp.sum(q, axis=0, keepdims=True)
         sum_ref[1:2, cut] += jnp.sum(q * h, axis=0, keepdims=True)
@@ -757,7 +763,7 @@
     hidden = wt.shape[1]
     chan_all = nz * chans
     reduced = se_weights[0].shape[0]
-    m, proj = keep(m), keep(proj)
+    m, proj, own = keep(m), keep(proj), keep(own)
     fixed = [gains, biases, wt, m, s, *se_weights, *ses, *sums]
     grid, tall, put, wide = by_steps(nz, bands, chans, area)
     return pl.pallas_call(
@@ -792,7 +798,7 @@
             jax.ShapeDtypeStruct(x.shape, F32),
             jax.ShapeDtypeStruct(m.shape, F32),
         ],
-        compiler_params=params(4),
+        compiler_params=params(13),
         cost_estimate=cost(12),
         name="proj_back",
     )(own, gout, proj, x, *fixed)
@@ -1635,7 +1641,7 @@
     ) = order_weights(
         jnp.stack([relative, z_relative]), slabs, orders, nz, chan_in, chans, reduced
     )
-    se_weights = [sq_t, se_down_bias[:, None], ex_all, ex_bias]
+    se_weights = [sq_t, se_down_bias[None], ex_all, ex_bias]
     x, ordered, we_high, we_low, moments = together(x, ordered, we_high, we_low, moments)
     moments = lax.all_gather(moments, PIX, axis=0)
 
@@ -1659,13 +1665,13 @@
         count, side, top, low, as_rows(hid), we_high, we_low, gains, biases, taps, sums_one
     )
     sums_two = shares(sums_two, 1, group)
-    m, s, se_part, proj = gather(
+    m, s, se_part, proj, normed = gather(
         count, as_bands(spatial), gout, gains, biases, w_project_t, wp_high, wp_low, sums_two
     )
     ses = shares(se_part, nlo, nhi)
     ses, g_top, g_low = together(ses, g_top, g_low)
     q, back_two, values, columns, *w4, out, g_project = proj_back(
-        count, as_bands(spatial), gout, proj, x, gains, biases, w_project_t, m, s, se_weights, ses, sums_two
+        count, normed, gout, proj, x, gains, biases, w_project_t, m, s, se_weights, ses, sums_two
     )
     backs_two = shares(back_two, 1, group)
     out = deal(out.reshape(frames, chans, area))

time: 309 us -> 309 us (level)
    all_to_all x5, waiting for transfers between devices: 23.1 us -> 9 us  [deal(): return lax.all_to_all(x, SPREAD, 0, 0, tiled=True)]
    ppermute x33, waiting for transfers between devices: 32.6 us -> 46.6 us  [exchange(): return lax.ppermute(x, ALL, [(i, i ^ stride) for i in range(n)])]
  transfers between devices with their start and end apart: 43 -> 43, of which waited for: 16 -> 16; matrix products, arithmetic and copies ran while one was open for 3% -> 3% of each run, Pallas kernels for 48% -> 47%
where the time goes in v6:
time: 309 us; the launch traced here: 307 us
  Pallas kernels  152 us (49%)
  starting transfers between devices  70.2 us (23%)
  waiting for transfers between devices  56.2 us (18%)
  between operations  14.1 us (5%)
  other arithmetic  8.32 us (3%)
  local copies, waits for them, and re-layouts  5.75 us (2%)
    ppermute x33, waiting for transfers between devices, exchange(): return lax.ppermute(x, ALL, [(i, i ^ stride) for i in range(n)])  46.6 us
    pallas_call x1, Pallas kernels, spread_back(): pl.pallas_call(partial(spread_back_kernel, len(backs), count), grid=(hidd...  37.5 us
    all_to_all x5, starting transfers between devices, deal(): return lax.all_to_all(x, SPREAD, 0, 0, tiled=True)  35.6 us
    ppermute x33, starting transfers between devices, exchange(): return lax.ppermute(x, ALL, [(i, i ^ stride) for i in range(n)])  33.8 us
    pallas_call x1, Pallas kernels, spread(): pl.pallas_call(partial(spread_kernel, len(sums), count), grid=(hidden //...  22.1 us
    pallas_call x2, Pallas kernels, input_grad(): pl.pallas_call(partial(input_kernel, len(sums), count, start), grid=(band...  13.5 us
    pallas_call x1, Pallas kernels, proj_back(): pl.pallas_call(partial(proj_back_kernel, len(ses), len(sums), count), gri...  11.2 us
    pallas_call x1, Pallas kernels, gather(): pl.pallas_call(partial(gather_kernel, len(sums), count), grid=grid, in_sp...  11 us
  transfers between devices with their start and end apart: 43, of which 16 were waited for; matrix products, arithmetic and copies ran while one was open for 3% of the time, Pallas kernels for 47%

profile of v6, /device:TPU:15, one launch (start us, length us, event | category | flops | bytes accessed | tf_op | source)
XLA Modules:
  0.0 307.1 jit_solution(12336471548172619374)
XLA Ops:
  7.2 1.8 pack_weights.1
  9.1 2.3 collective-permute-start.1
  11.6 5.2 %crop.1 = f32[16,64,512]{2,1,0:T(8,128)} custom-call(s32[4]{0:T(128)} %left_ref.3, s32[4]{0:T(128)} %flip_ref.3, f32[16,64,640]{2,1,0:T(8,128)} %raw_ref.1), custom_call_target="tpu_custom_call" | custom-call | flops 5500000256 | bytes 17500000 | tf_op jit(solution)/shard_map/crop/pallas_call | solution.py:197
  17.4 7.8 %all-to-all-start = ((f32[16,64,512]{2,1,0:T(8,128)}), f32[16,64,512]{2,1,0:T(8,128)}, u32[]{:S(2)}, u32[]{:S(2)}) async-start(f32[16,64,512]{2,1,0:T(8,128)} %crop.1), calls=%async_computation | async-start | bytes 4194304 | tf_op jit(solution)/shard_map/all_to_all | solution.py:121
  25.7 4.7 %order.1 = f32[16,64,512]{2,1,0:T(8,128)} custom-call(f32[16,64,512]{2,1,0:T(8,128)} %x_ref.1), custom_call_target="tpu_custom_call" | custom-call | flops 27499999232 | bytes 87500000 | tf_op jit(solution)/shard_map/order/pallas_call | solution.py:222
  30.4 13.8 %collective-permute-done.3 = f32[1,72,1024]{2,1,0:T(8,128)S(1)} collective-permute-done((f32[1,72,1024]{2,1,0:T(8,128)S(1)}, f32[1,72,1024]{2,1,0:T(8,128)S(1)}, u32[]{:S(2)}, u32[]{:S(2)}) %collective-permute-start.3) | collective-permute-done | bytes 294944 | tf_op jit(solution)/shard_map/ppermute | solution.py:100
  44.6 13.8 %collective-permute-done.4 = f32[2,72,1024]{2,1,0:T(8,128)S(1)} collective-permute-done((f32[2,72,1024]{2,1,0:T(8,128)S(1)}, f32[2,72,1024]{2,1,0:T(8,128)S(1)}, u32[]{:S(2)}, u32[]{:S(2)}) %collective-permute-start.4) | collective-permute-done | bytes 589856 | tf_op jit(solution)/shard_map/ppermute | solution.py:100
  58.5 1.7 collective-permute-start.5
  60.8 1.9 collective-permute-done.5.refs_1_
  62.7 0.9 select_maximum_fusion
  63.8 4.6 %order_weights.1 = (bf16[256,1024]{1,0:T(8,128)(2,1)}, bf16[256,1024]{1,0:T(8,128)(2,1)}, bf16[1024,256]{1,0:T(8,128)(2,1)}, bf16[1024,256]{1,0:T(8,128)(2,1)}, ...) custom-call(s32[2]{0:T(128)} %pad_add_fusion.base_ref, ...), custom_call_target="tpu_custom_call" | custom-call | flops 3300000000 | bytes 10500000 | tf_op jit(solution)/shard_map/order_weights/pallas_call | solution.py:1291
  68.4 4.5 %all-to-all-done = f32[16,64,512]{2,1,0:T(8,128)} async-done(((f32[16,64,512]{2,1,0:T(8,128)}), f32[16,64,512]{2,1,0:T(8,128)}, u32[]{:S(2)}, u32[]{:S(2)}) %all-to-all-start) | async-done | bytes 2097184 | tf_op jit(solution)/shard_map/all_to_all | solution.py:121
  72.8 7.1 %all-to-all-start.1 = ((f32[16,64,512]{2,1,0:T(8,128)}), f32[16,64,512]{2,1,0:T(8,128)}, u32[]{:S(2)}, u32[]{:S(2)}) async-start(f32[16,64,512]{2,1,0:T(8,128)} %order.1), calls=%async_computation.1 | async-start | bytes 4194304 | tf_op jit(solution)/shard_map/all_to_all | solution.py:121
  80.0 8.2 %expand.1 = (f32[4,512,1024]{2,1,0:T(8,128)}, f32[2,1024]{1,0:T(2,128)}, f32[256,384]{1,0:T(8,128)}) custom-call(f32[4,4,64,512]{3,2,1,0:T(8,128)} %bitcast.5.x_ref, bf16[256,1024]{1,0:T(8,128)(2,1)} %get-tuple-element.121.high_ref, bf16[256,1024]{1,0:T(8,128)(2,1)} %get-tuple-element.122.low_ref.lower_ref), custom_call_target="tpu_custom_call" | custom-call | flops 8800000000 | bytes 28000000 | tf_op jit(solution)/shard_map/expand/pallas_call | solution.py:335
  88.7 1.0 collective-permute-done.6
  89.8 0.7 add.33.rest_0_.rest_4_
  90.5 1.1 slice_select_fusion
  92.1 1.2 collective-permute-start.9
  93.4 1.1 collective-permute-start.10
  95.1 4.5 %collective-permute-done.9.rest_2_.rest_6_ = f32[2,1024]{1,0:T(2,128)S(1)} collective-permute-done((f32[2,1024]{1,0:T(2,128)S(1)}, f32[2,1024]{1,0:T(2,128)S(1)}, u32[]{:S(2)}, u32[]{:S(2)}) %collective-permute-start.9) | collective-permute-done | bytes 8224 | tf_op jit(solution)/shard_map/ppermute | solution.py:100
  100.3 22.1 %spread.1 = (f32[32,8,8,1024]{3,2,1,0:T(8,128)}, f32[2,2,8,8,1024]{4,3,2,1,0:T(8,128)}, f32[2,2,8,8,1024]{4,3,2,1,0:T(8,128)}, f32[2,1024]{1,0:T(2,128)}) custom-call(s32[2]{0:T(128)} %add_convert_fusion.side_ref, f32[4,1,64,256]{3,2,1,0:T(8,128)} %copy-done.15, f32[4,1,64,256]{3,2,1,0:T(8,128)} %copy-done.15, f32[32,8,8,1024]{3,2,1,0:T(8,128)} %bitcast.46, ...), custom_call_target="tpu_custom_call" | custom-call | flops 11000000512 | bytes 35000000 | tf_op jit(solution)/shard_map/spread/pallas_call | solution.py:570
  122.4 1.1 collective-permute-start.11
  123.5 1.0 collective-permute-done.11
  124.6 0.7 add.34.rest_0_.rest_2_.rest_4_
  125.3 0.7 collective-permute-start.12
  126.0 2.0 collective-permute-start.14
  127.9 1.0 slice_select_fusion.1
  130.0 11.0 %gather.1 = (f32[256,1024]{1,0:T(8,128)S(1)}, f32[1,1024]{1,0:T(1,128)}, f32[2,256]{1,0:T(2,128)}, f32[4,512,256]{2,1,0:T(8,128)S(1)}, f32[4,512,1024]{2,1,0:T(8,128)S(1)}) custom-call(f32[4,512,1024]{2,1,0:T(8,128)} %bitcast.48, f32[4,4,64,512]{3,2,1,0:T(8,128)} %bitcast.12.gout_ref, f32[2,1024]{1,0:T(2,128)} %get-tuple-element.126.gain_ref, ...), custom_call_target="tpu_custom_call" | custom-call | flops 14300000256 | bytes 45500000 | tf_op jit(solution)/shard_map/gather/pallas_call | solution.py:646
  141.0 1.6 collective-permute-start.15
  142.6 1.2 collective-permute-done.15.rest_1_
  144.4 11.2 %proj_back.1 = (f32[4,512,1024]{2,1,0:T(8,128)}, f32[2,1024]{1,0:T(2,128)}, f32[8,256]{1,0:T(8,128)}, f32[16,128]{1,0:T(8,128)}, bf16[256,1024]{1,0:T(8,128)(2,1...) custom-call(f32[4,512,1024]{2,1,0:T(8,128)S(1)} %get-tuple-element.141.own_r, ...), custom_call_target="tpu_custom_call" | custom-call | flops 13200000000 | bytes 42000000 | tf_op jit(solution)/shard_map/proj_back/pallas_call | solution.py:769
  155.6 3.0 collective-permute-start.17
  158.6 1.0 collective-permute-done.17
  159.6 0.7 add.35.rest_8_
  160.3 1.1 collective-permute-start.18
  161.4 1.3 collective-permute-start.19
  163.1 6.6 %all-to-all-start.2 = ((f32[16,64,512]{2,1,0:T(8,128)}), f32[16,64,512]{2,1,0:T(8,128)}, u32[]{:S(2)}, u32[]{:S(2)}) async-start(f32[16,64,512]{2,1,0:T(8,128)} %bitcast.32), calls=%async_computation.2 | async-start | bytes 4194304 | tf_op jit(solution)/shard_map/all_to_all | solution.py:121
  171.1 37.5 %spread_back.1 = (f32[32,8,8,1024]{3,2,1,0:T(8,128)}, f32[2,1024]{1,0:T(2,128)}, f32[25,1024]{1,0:T(8,128)}) custom-call(s32[2]{0:T(128)} %add_convert_fusion.side_ref, f32[4,1,64,128]{3,2,1,0:T(8,128)} %copy-done.19, f32[4,1,64,128]{3,2,1,0:T(8,128)} %copy-done.19, f32[32,8,8,1024]{3,2,1,0:T(8,128)} %bitcast.47, ...), custom_call_target="tpu_custom_call" | custom-call | flops 165000003584 | bytes 525000000 | tf_op jit(solution)/shard_map/spread_back/pallas_call | solution.py:939
  210.1 0.7 add.36.rest_4_.rest_8_
  211.0 1.3 collective-permute-start.23
  212.3 1.1 collective-permute-start.24
  213.4 8.0 %weight_grad.1 = (f32[4,40,1024]{2,1,0:T(8,128)}, f32[4,40,1024]{2,1,0:T(8,128)}) custom-call(s32[3]{0:T(128)} %pad_add_fusion.1.ids_ref, f32[4,512,1024]{2,1,0:T(8,128)} %bitcast.49, f32[4,4,64,512]{3,2,1,0:T(8,128)} %bitcast.5.x_ref, f32[25,1024]{1,0:T(8,128)} %get-tuple-element.162.tap_ref, f32[2,1024]{1,0:T(2,128)} %get-tuple-element.155.one_ref, ...), custom_call_target="tpu_custom_call" | custom-call | flops 7699999744 | bytes 24500000 | tf_op jit(solution)/shard_map/weight_grad/pallas_call | solution.py:1064
  221.5 1.2 collective-permute-start.25
  223.4 6.8 %input_grad.2 = f32[4,4,64,256]{3,2,1,0:T(8,128)} custom-call(f32[4,512,1024]{2,1,0:T(8,128)} %bitcast.50, f32[4,512,1024]{2,1,0:T(8,128)} %get-tuple-element.125.hid_ref, f32[4,4,64,512]{3,2,1,0:T(8,128)} %bitcast.12.gout_ref, f32[2,1024]{1,0:T(2,128)} %get-tuple-element.126.gain_ref, bf16[1024,256]{1,0:T(8,128)(2,1)} %get-tuple-element.168.w_high, ...), custom_call_target="tpu_custom_call" | custom-call | flops 13200000000 | bytes 42000000 | tf_op jit(solution)/shard_map/input_grad/pallas_call | solution.py:994
  230.2 5.8 %all-to-all-start.3 = ((f32[16,64,256]{2,1,0:T(8,128)}), f32[16,64,256]{2,1,0:T(8,128)S(1)}, u32[]{:S(2)}, u32[]{:S(2)}) async-start(f32[16,64,256]{2,1,0:T(8,128)} %bitcast.34), calls=%async_computation.5 | async-start | bytes 2097152 | tf_op jit(solution)/shard_map/all_to_all | solution.py:121
  236.0 2.2 merge.1
  238.4 1.3 collective-permute-start.27
  239.7 1.1 collective-permute-start.28
  240.8 6.8 %input_grad.3 = f32[4,4,64,256]{3,2,1,0:T(8,128)} custom-call(f32[4,512,1024]{2,1,0:T(8,128)} %bitcast.51, f32[4,512,1024]{2,1,0:T(8,128)} %get-tuple-element.125.hid_ref, f32[4,4,64,512]{3,2,1,0:T(8,128)} %bitcast.12.gout_ref, f32[2,1024]{1,0:T(2,128)} %get-tuple-element.126.gain_ref, bf16[1024,256]{1,0:T(8,128)(2,1)} %get-tuple-element.168.w_high, ...), custom_call_target="tpu_custom_call" | custom-call | flops 13200000000 | bytes 42000000 | tf_op jit(solution)/shard_map/input_grad/pallas_call | solution.py:994
  247.5 4.8 %restore.1 = f32[16,64,512]{2,1,0:T(8,128)} custom-call(f32[16,64,512]{2,1,0:T(8,128)} %all-to-all-done.2.x_ref), custom_call_target="tpu_custom_call" | custom-call | flops 1100000000 | bytes 3500000 | tf_op jit(solution)/shard_map/restore/pallas_call | solution.py:243
  253.2 2.6 collect.1
  255.8 2.4 collective-permute-start.31
  258.2 2.9 collective-permute-start.30
  261.1 0.7 copy.25.col_ref
  261.9 8.2 %all-to-all-start.4 = ((f32[16,64,256]{2,1,0:T(8,128)}), f32[16,64,256]{2,1,0:T(8,128)}, u32[]{:S(2)}, u32[]{:S(2)}) async-start(f32[16,64,256]{2,1,0:T(8,128)} %bitcast.33), calls=%async_computation.6 | async-start | bytes 2097152 | tf_op jit(solution)/shard_map/all_to_all | solution.py:121
  270.5 4.7 %prepare.1 = (f32[138,1024]{1,0:T(8,128)}, f32[138,1024]{1,0:T(8,128)}, f32[138,1024]{1,0:T(8,128)}) custom-call(s32[1]{0:T(128)} %constant.21.clone.1.base_ref, s32[138,1]{1,0:T(8,128)} %copy.25.col_ref, f32[256,256]{1,0:T(8,128)} %we_ref.3, f32[25,256]{1,0:T(8,128)} %dw_ref.3, f32[2,256]{1,0:T(2,128)} %gain_ref.3, f32[2,256]{1,0:T(2,128)} %bias_ref.3, ...), custom_call_target="tpu_custom_call" | custom-call | flops 1100000000 | bytes 3500000 | tf_op jit(solution)/shard_map/prepare/pallas_call | solution.py:1438
  275.2 2.1 collective-permute-done.32
  277.5 4.4 %collective-permute-done.33 = f32[2,72,256]{2,1,0:T(8,128)S(1)} collective-permute-done((f32[2,72,256]{2,1,0:T(8,128)S(1)}, f32[2,72,256]{2,1,0:T(8,128)S(1)}, u32[]{:S(2)}, u32[]{:S(2)}) %collective-permute-start.33) | collective-permute-done | bytes 147488 | tf_op jit(solution)/shard_map/ppermute | solution.py:100
  282.0 1.7 collective-permute-start.34
  283.7 0.7 pad_add_fusion.2.me_ref
  284.9 0.7 copy-done.14
  285.7 4.9 %adam.1 = (f32[26,1,1024]{2,1,0:T(1,128)}, f32[26,1,1024]{2,1,0:T(1,128)}, f32[1,140624]{1,0:T(1,128)}) custom-call(s32[2]{0:T(128)} %pad_add_fusion.2.me_ref, s32[138,1]{1,0:T(8,128)} %copy.25.col_ref, f32[138,1024]{1,0:T(8,128)} %get-tuple-element.202.weight_ref, f32[138,1024]{1,0:T(8,128)} %get-tuple-element.203.old_one_ref, ...), custom_call_target="tpu_custom_call" | custom-call | flops 11000000512 | bytes 35000000 | tf_op jit(solution)/shard_map/adam/pallas_call | solution.py:1536
  290.6 4.5 %all-to-all-done.4.y_ref = f32[16,64,256]{2,1,0:T(8,128)} async-done(((f32[16,64,256]{2,1,0:T(8,128)}), f32[16,64,256]{2,1,0:T(8,128)}, u32[]{:S(2)}, u32[]{:S(2)}) %all-to-all-start.4) | async-done | bytes 1048608 | tf_op jit(solution)/shard_map/all_to_all | solution.py:121
  295.1 5.5 %uncrop.1 = f32[16,64,640]{2,1,0:T(8,128)} custom-call(s32[4]{0:T(128)} %left_ref.3, s32[4]{0:T(128)} %flip_ref.3, f32[16,64,256]{2,1,0:T(8,128)} %copy-done, f32[16,64,256]{2,1,0:T(8,128)} %all-to-all-done.4.y_ref), custom_call_target="tpu_custom_call" | custom-call | flops 1100000000 | bytes 3500000 | tf_op jit(solution)/shard_map/uncrop/pallas_call | solution.py:272
  (130 shorter events, 13.1 us)
Async XLA Ops:
  9.0 7.9 %collective-permute-start = (f32[72,256]{1,0:T(8,128)}, f32[72,256]{1,0:T(8,128)S(1)}, u32[]{:S(2)}, u32[]{:S(2)}) collective-permute-start(f32[72,256]{1,0:T(8,128)} %pack_weights.1), channel_id=1, source_target_pairs={{0,8},{1,9},{2,10},{3,11},{4,12},{5,13},{6,14},{7,15},{8,0},{9,1},... | collective-permute-start | bytes 221192 | tf_op jit(solution)/shard_map/ppermute | solution.py:100
  9.1 7.7 %collective-permute-start.1 = (f32[72,256]{1,0:T(8,128)}, f32[72,256]{1,0:T(8,128)S(1)}, u32[]{:S(2)}, u32[]{:S(2)}) collective-permute-start(f32[72,256]{1,0:T(8,128)} %pack_weights.1), channel_id=1, source_target_pairs={{0,16},{1,17},{2,18},{3,19},{4,20},{5,21},{6,22},{7,23},{8,24},{9,... | collective-permute-start | bytes 221192 | tf_op jit(solution)/shard_map/ppermute | solution.py:100
  11.4 6.0 %collective-permute-start.2 = (f32[72,256]{1,0:T(8,128)}, f32[72,256]{1,0:T(8,128)S(1)}, u32[]{:S(2)}, u32[]{:S(2)}) collective-permute-start(f32[72,256]{1,0:T(8,128)} %pack_weights.1), channel_id=1, source_target_pairs={{0,24},{1,25},{2,26},{3,27},{4,28},{5,29},{6,30},{7,31},{8,16},{9,... | collective-permute-start | bytes 221192 | tf_op jit(solution)/shard_map/ppermute | solution.py:100
  16.8 8.5 %copy-start.4 = (f32[72,256]{1,0:T(8,128)S(1)}, f32[72,256]{1,0:T(8,128)}, u32[]{:S(2)}) copy-start(f32[72,256]{1,0:T(8,128)} %pack_weights.1) | copy-start | bytes 221188
  17.4 55.4 %all-to-all-start = ((f32[16,64,512]{2,1,0:T(8,128)}), f32[16,64,512]{2,1,0:T(8,128)}, u32[]{:S(2)}, u32[]{:S(2)}) async-start(f32[16,64,512]{2,1,0:T(8,128)} %crop.1), calls=%async_computation | async-start | bytes 4194304 | tf_op jit(solution)/shard_map/all_to_all | solution.py:121
  25.3 18.9 %collective-permute-start.3 = (f32[1,72,1024]{2,1,0:T(8,128)S(1)}, f32[1,72,1024]{2,1,0:T(8,128)S(1)}, u32[]{:S(2)}, u32[]{:S(2)}) collective-permute-start(f32[1,72,1024]{2,1,0:T(8,128)S(1)} %maximum_bitcast_fusion), channel_id=1, source_target_pairs={{0,2},{1,3},{2,0},{3,1},{4,6},{5,7},{6,4},{7,5},{8,10},{9,11},{10,... | collective-permute-start | bytes 884744 | tf_op jit(solution)/shard_map/ppermute | solution.py:100
  30.4 32.2 %copy-start.2 = (f32[1,26,1024]{2,0,1:T(1,128)S(1)}, f32[1,26,1024]{2,0,1:T(1,128)}, u32[]{:S(2)}) copy-start(f32[1,26,1024]{2,0,1:T(1,128)} %param.31) | copy-start | bytes 319492
  30.4 32.2 %copy-start.3 = (f32[1,26,1024]{2,0,1:T(1,128)S(1)}, f32[1,26,1024]{2,0,1:T(1,128)}, u32[]{:S(2)}) copy-start(f32[1,26,1024]{2,0,1:T(1,128)} %param.30) | copy-start | bytes 319492
  44.2 14.2 %collective-permute-start.4 = (f32[2,72,1024]{2,1,0:T(8,128)S(1)}, f32[2,72,1024]{2,1,0:T(8,128)S(1)}, u32[]{:S(2)}, u32[]{:S(2)}) collective-permute-start(f32[2,72,1024]{2,1,0:T(8,128)S(1)} %pad_maximum_fusion), channel_id=1, source_target_pairs={{0,4},{1,5},{2,6},{3,7},{4,0},{5,1},{6,2},{7,3},{8,12},{9,13},{10,... | collective-permute-start | bytes 1769480 | tf_op jit(solution)/shard_map/ppermute | solution.py:100
  58.5 5.3 %copy-start.1 = (f32[4,72,1024]{2,1,0:T(8,128)}, f32[4,72,1024]{2,1,0:T(8,128)S(1)}, u32[]{:S(2)}) copy-start(f32[4,72,1024]{2,1,0:T(8,128)S(1)} %constant_dynamic-update-slice_fusion.refs_0_) | copy-start | bytes 3538948
  58.5 4.2 %collective-permute-start.5 = (f32[4,72,1024]{2,1,0:T(8,128)S(1)}, f32[4,72,1024]{2,1,0:T(8,128)S(1)}, u32[]{:S(2)}, u32[]{:S(2)}) collective-permute-start(f32[4,72,1024]{2,1,0:T(8,128)S(1)} %constant_dynamic-update-slice_fusion.refs_0_), channel_id=1, source_target_pairs={{0,1},{1,0},{2,3},{3,2},{4,5},{5,4},{6,7},{7,6},{8,9},{9,8},{10,11... | collective-permute-start | bytes 3538952 | tf_op jit(solution)/shard_map/ppermute | solution.py:100
  62.6 1.2 copy-start.12
  72.8 55.1 %all-to-all-start.1 = ((f32[16,64,512]{2,1,0:T(8,128)}), f32[16,64,512]{2,1,0:T(8,128)}, u32[]{:S(2)}, u32[]{:S(2)}) async-start(f32[16,64,512]{2,1,0:T(8,128)} %order.1), calls=%async_computation.1 | async-start | bytes 4194304 | tf_op jit(solution)/shard_map/all_to_all | solution.py:121
  80.0 141.5 %reduce-scatter.5.cloned.1.call-start = ((), (), s32[]{:S(2)}) async-start(), calls=%async_computation.8 | async-start | bytes 442368 | tf_op jit(solution)/shard_map/reduce_scatter | solution.py:1706
  88.2 133.2 %all-gather.3.cloned.1.call-start = ((), (), s32[]{:S(2)}) async-start(), calls=%async_computation.9 | async-start | bytes 2359296 | tf_op jit(solution)/shard_map/all_gather | solution.py:1646
  88.3 1.5 collective-permute-start.6
  90.5 9.2 %copy-start.7 = (f32[2,1024]{1,0:T(2,128)}, f32[2,1024]{1,0:T(2,128)S(1)}, u32[]{:S(2)}) copy-start(f32[2,1024]{1,0:T(2,128)S(1)} %add.33.rest_0_.rest_4_) | copy-start | bytes 24580
  91.5 8.1 %collective-permute-start.7 = (f32[4,1,64,256]{3,2,1,0:T(8,128)S(1)}, f32[4,1,64,256]{3,2,1,0:T(8,128)S(1)}, u32[]{:S(2)}, u32[]{:S(2)}) collective-permute-start(f32[4,1,64,256]{3,2,1,0:T(8,128)S(1)} %slice_select_fusion), channel_id=1, source_target_pairs={{0,4},{4,0},{1,5},{5,1},{2,6},{6,2},{3,7},{7,3},{8,12},{12,8},{9,1... | collective-permute-start | bytes 786440 | tf_op jit(solution)/shard_map/ppermute | solution.py:136
  91.8 3.3 %collective-permute-start.8 = (f32[2,1024]{1,0:T(2,128)S(1)}, f32[2,1024]{1,0:T(2,128)S(1)}, u32[]{:S(2)}, u32[]{:S(2)}) collective-permute-start(f32[2,1024]{1,0:T(2,128)S(1)} %add.33.rest_0_.rest_4_), channel_id=1, source_target_pairs={{0,2},{1,3},{2,0},{3,1},{4,6},{5,7},{6,4},{7,5},{8,10},{9,11},{10,... | collective-permute-start | bytes 24584 | tf_op jit(solution)/shard_map/ppermute | solution.py:100
  92.1 7.5 %collective-permute-start.9 = (f32[2,1024]{1,0:T(2,128)S(1)}, f32[2,1024]{1,0:T(2,128)S(1)}, u32[]{:S(2)}, u32[]{:S(2)}) collective-permute-start(f32[2,1024]{1,0:T(2,128)S(1)} %add.33.rest_0_.rest_4_), channel_id=1, source_target_pairs={{0,4},{1,5},{2,6},{3,7},{4,0},{5,1},{6,2},{7,3},{8,12},{9,13},{10,... | collective-permute-start | bytes 24584 | tf_op jit(solution)/shard_map/ppermute | solution.py:100
  93.4 6.3 %collective-permute-start.10 = (f32[2,1024]{1,0:T(2,128)S(1)}, f32[2,1024]{1,0:T(2,128)S(1)}, u32[]{:S(2)}, u32[]{:S(2)}) collective-permute-start(f32[2,1024]{1,0:T(2,128)S(1)} %add.33.rest_0_.rest_4_), channel_id=1, source_target_pairs={{0,6},{1,7},{2,4},{3,5},{4,2},{5,3},{6,0},{7,1},{8,14},{9,15},{10,... | collective-permute-start | bytes 24584 | tf_op jit(solution)/shard_map/ppermute | solution.py:100
  95.1 4.6 %copy-start.20 = (f32[2,1024]{1,0:T(2,128)}, f32[2,1024]{1,0:T(2,128)S(1)}, u32[]{:S(2)}) copy-start(f32[2,1024]{1,0:T(2,128)S(1)} %collective-permute-done.8.rest_1_.rest_5_) | copy-start | bytes 24580
  99.6 0.7 copy-start.15
  122.4 2.2 collective-permute-start.11
  125.3 4.1 %copy-start.8 = (f32[2,1024]{1,0:T(2,128)}, f32[2,1024]{1,0:T(2,128)S(1)}, u32[]{:S(2)}) copy-start(f32[2,1024]{1,0:T(2,128)S(1)} %add.34.rest_0_.rest_2_.rest_4_) | copy-start | bytes 24580
  125.3 3.9 %collective-permute-start.12 = (f32[2,1024]{1,0:T(2,128)S(1)}, f32[2,1024]{1,0:T(2,128)S(1)}, u32[]{:S(2)}, u32[]{:S(2)}) collective-permute-start(f32[2,1024]{1,0:T(2,128)S(1)} %add.34.rest_0_.rest_2_.rest_4_), channel_id=1, source_target_pairs={{0,2},{1,3},{2,0},{3,1},{4,6},{5,7},{6,4},{7,5},{8,10},{9,11},{10,... | collective-permute-start | bytes 24584 | tf_op jit(solution)/shard_map/ppermute | solution.py:100
  126.0 3.2 %collective-permute-start.13 = (f32[2,1024]{1,0:T(2,128)S(1)}, f32[2,1024]{1,0:T(2,128)S(1)}, u32[]{:S(2)}, u32[]{:S(2)}) collective-permute-start(f32[2,1024]{1,0:T(2,128)S(1)} %add.34.rest_0_.rest_2_.rest_4_), channel_id=1, source_target_pairs={{0,4},{1,5},{2,6},{3,7},{4,0},{5,1},{6,2},{7,3},{8,12},{9,13},{10,... | collective-permute-start | bytes 24584 | tf_op jit(solution)/shard_map/ppermute | solution.py:100
  126.0 3.4 %collective-permute-start.14 = (f32[2,1024]{1,0:T(2,128)S(1)}, f32[2,1024]{1,0:T(2,128)S(1)}, u32[]{:S(2)}, u32[]{:S(2)}) collective-permute-start(f32[2,1024]{1,0:T(2,128)S(1)} %add.34.rest_0_.rest_2_.rest_4_), channel_id=1, source_target_pairs={{0,6},{1,7},{2,4},{3,5},{4,2},{5,3},{6,0},{7,1},{8,14},{9,15},{10,... | collective-permute-start | bytes 24584 | tf_op jit(solution)/shard_map/ppermute | solution.py:100
  128.9 14.9 %collective-permute-start.16 = (f32[4,1,64,128]{3,2,1,0:T(8,128)S(1)}, f32[4,1,64,128]{3,2,1,0:T(8,128)S(1)}, u32[]{:S(2)}, u32[]{:S(2)}) collective-permute-start(f32[4,1,64,128]{3,2,1,0:T(8,128)S(1)} %slice_select_fusion.1), channel_id=1, source_target_pairs={{0,4},{4,0},{1,5},{5,1},{2,6},{6,2},{3,7},{7,3},{8,12},{12,8},{9,1... | collective-permute-start | bytes 393224 | tf_op jit(solution)/shard_map/ppermute | solution.py:136
  141.0 2.8 collective-permute-start.15
  143.8 11.8 %copy-start.19 = (f32[4,1,64,128]{3,2,1,0:T(8,128)}, f32[4,1,64,128]{3,2,1,0:T(8,128)S(1)}, u32[]{:S(2)}) copy-start(f32[4,1,64,128]{3,2,1,0:T(8,128)S(1)} %collective-permute-done.16.top_ref.low_ref) | copy-start | bytes 393220
  155.6 4.0 %collective-permute-start.17 = (f32[2,1024]{1,0:T(2,128)}, f32[2,1024]{1,0:T(2,128)S(1)}, u32[]{:S(2)}, u32[]{:S(2)}) collective-permute-start(f32[2,1024]{1,0:T(2,128)} %get-tuple-element.154.two_ref), channel_id=1, source_target_pairs={{0,1},{1,0},{2,3},{3,2},{4,5},{5,4},{6,7},{7,6},{8,9},{9,8},{10,11... | collective-permute-start | bytes 24584 | tf_op jit(solution)/shard_map/ppermute | solution.py:100
  160.3 2.8 copy-start.10
  160.3 10.1 %collective-permute-start.18 = (f32[2,1024]{1,0:T(2,128)S(1)}, f32[2,1024]{1,0:T(2,128)S(1)}, u32[]{:S(2)}, u32[]{:S(2)}) collective-permute-start(f32[2,1024]{1,0:T(2,128)S(1)} %add.35.rest_8_), channel_id=1, source_target_pairs={{0,2},{1,3},{2,0},{3,1},{4,6},{5,7},{6,4},{7,5},{8,10},{9,11},{10,... | collective-permute-start | bytes 24584 | tf_op jit(solution)/shard_map/ppermute | solution.py:100
  161.4 9.1 %collective-permute-start.19 = (f32[2,1024]{1,0:T(2,128)S(1)}, f32[2,1024]{1,0:T(2,128)S(1)}, u32[]{:S(2)}, u32[]{:S(2)}) collective-permute-start(f32[2,1024]{1,0:T(2,128)S(1)} %add.35.rest_8_), channel_id=1, source_target_pairs={{0,4},{1,5},{2,6},{3,7},{4,0},{5,1},{6,2},{7,3},{8,12},{9,13},{10,... | collective-permute-start | bytes 24584 | tf_op jit(solution)/shard_map/ppermute | solution.py:100
  162.7 7.8 %collective-permute-start.20 = (f32[2,1024]{1,0:T(2,128)S(1)}, f32[2,1024]{1,0:T(2,128)S(1)}, u32[]{:S(2)}, u32[]{:S(2)}) collective-permute-start(f32[2,1024]{1,0:T(2,128)S(1)} %add.35.rest_8_), channel_id=1, source_target_pairs={{0,6},{1,7},{2,4},{3,5},{4,2},{5,3},{6,0},{7,1},{8,14},{9,15},{10,... | collective-permute-start | bytes 24584 | tf_op jit(solution)/shard_map/ppermute | solution.py:100
  163.1 58.4 %all-to-all-start.2 = ((f32[16,64,512]{2,1,0:T(8,128)}), f32[16,64,512]{2,1,0:T(8,128)}, u32[]{:S(2)}, u32[]{:S(2)}) async-start(f32[16,64,512]{2,1,0:T(8,128)} %bitcast.32), calls=%async_computation.2 | async-start | bytes 4194304 | tf_op jit(solution)/shard_map/all_to_all | solution.py:121
  169.7 51.8 %reduce-scatter.3.cloned.1.call-start = ((), (), s32[]{:S(2)}) async-start(), calls=%async_computation.7 | async-start | bytes 1179648 | tf_op jit(solution)/shard_map/reduce_scatter | solution.py:1705
  208.6 1.5 collective-permute-start.21
  210.8 10.7 %copy-start.9 = (f32[2,1024]{1,0:T(2,128)}, f32[2,1024]{1,0:T(2,128)S(1)}, u32[]{:S(2)}) copy-start(f32[2,1024]{1,0:T(2,128)S(1)} %add.36.rest_4_.rest_8_) | copy-start | bytes 24580
  210.8 12.0 %collective-permute-start.22 = (f32[2,1024]{1,0:T(2,128)S(1)}, f32[2,1024]{1,0:T(2,128)S(1)}, u32[]{:S(2)}, u32[]{:S(2)}) collective-permute-start(f32[2,1024]{1,0:T(2,128)S(1)} %add.36.rest_4_.rest_8_), channel_id=1, source_target_pairs={{0,2},{1,3},{2,0},{3,1},{4,6},{5,7},{6,4},{7,5},{8,10},{9,11},{10,... | collective-permute-start | bytes 24584 | tf_op jit(solution)/shard_map/ppermute | solution.py:100
  211.0 11.7 %collective-permute-start.23 = (f32[2,1024]{1,0:T(2,128)S(1)}, f32[2,1024]{1,0:T(2,128)S(1)}, u32[]{:S(2)}, u32[]{:S(2)}) collective-permute-start(f32[2,1024]{1,0:T(2,128)S(1)} %add.36.rest_4_.rest_8_), channel_id=1, source_target_pairs={{0,4},{1,5},{2,6},{3,7},{4,0},{5,1},{6,2},{7,3},{8,12},{9,13},{10,... | collective-permute-start | bytes 24584 | tf_op jit(solution)/shard_map/ppermute | solution.py:100
  212.3 10.4 %collective-permute-start.24 = (f32[2,1024]{1,0:T(2,128)S(1)}, f32[2,1024]{1,0:T(2,128)S(1)}, u32[]{:S(2)}, u32[]{:S(2)}) collective-permute-start(f32[2,1024]{1,0:T(2,128)S(1)} %add.36.rest_4_.rest_8_), channel_id=1, source_target_pairs={{0,6},{1,7},{2,4},{3,5},{4,2},{5,3},{6,0},{7,1},{8,14},{9,15},{10,... | collective-permute-start | bytes 24584 | tf_op jit(solution)/shard_map/ppermute | solution.py:100
  221.5 8.7 %collective-permute-start.25 = (f32[4,40,1024]{2,1,0:T(8,128)}, f32[4,40,1024]{2,1,0:T(8,128)S(1)}, u32[]{:S(2)}, u32[]{:S(2)}) collective-permute-start(f32[4,40,1024]{2,1,0:T(8,128)} %get-tuple-element.172), channel_id=1, source_target_pairs={{0,1},{1,0},{2,3},{3,2},{4,5},{5,4},{6,7},{7,6},{8,9},{9,8},{10,11... | collective-permute-start | bytes 1966088 | tf_op jit(solution)/shard_map/ppermute | solution.py:100
  230.2 5.8 %copy-start.13 = (f32[4,40,1024]{2,1,0:T(8,128)}, f32[4,40,1024]{2,1,0:T(8,128)S(1)}, u32[]{:S(2)}) copy-start(f32[4,40,1024]{2,1,0:T(8,128)S(1)} %collective-permute-done.25.two_ref) | copy-start | bytes 1966084
  230.2 31.7 %all-to-all-start.3 = ((f32[16,64,256]{2,1,0:T(8,128)}), f32[16,64,256]{2,1,0:T(8,128)S(1)}, u32[]{:S(2)}, u32[]{:S(2)}) async-start(f32[16,64,256]{2,1,0:T(8,128)} %bitcast.34), calls=%async_computation.5 | async-start | bytes 2097152 | tf_op jit(solution)/shard_map/all_to_all | solution.py:121
  238.1 14.2 %collective-permute-start.26 = (f32[40,1024]{1,0:T(8,128)}, f32[40,1024]{1,0:T(8,128)S(1)}, u32[]{:S(2)}, u32[]{:S(2)}) collective-permute-start(f32[40,1024]{1,0:T(8,128)} %get-tuple-element.180), channel_id=1, source_target_pairs={{0,2},{1,3},{2,0},{3,1},{4,6},{5,7},{6,4},{7,5},{8,10},{9,11},{10,... | collective-permute-start | bytes 491528 | tf_op jit(solution)/shard_map/ppermute | solution.py:100
  238.4 14.0 %collective-permute-start.27 = (f32[40,1024]{1,0:T(8,128)}, f32[40,1024]{1,0:T(8,128)S(1)}, u32[]{:S(2)}, u32[]{:S(2)}) collective-permute-start(f32[40,1024]{1,0:T(8,128)} %get-tuple-element.181), channel_id=1, source_target_pairs={{0,4},{1,5},{2,6},{3,7},{4,0},{5,1},{6,2},{7,3},{8,12},{9,13},{10,... | collective-permute-start | bytes 491528 | tf_op jit(solution)/shard_map/ppermute | solution.py:100
  239.7 12.7 %collective-permute-start.28 = (f32[40,1024]{1,0:T(8,128)}, f32[40,1024]{1,0:T(8,128)S(1)}, u32[]{:S(2)}, u32[]{:S(2)}) collective-permute-start(f32[40,1024]{1,0:T(8,128)} %get-tuple-element.182), channel_id=1, source_target_pairs={{0,6},{1,7},{2,4},{3,5},{4,2},{5,3},{6,0},{7,1},{8,14},{9,15},{10,... | collective-permute-start | bytes 491528 | tf_op jit(solution)/shard_map/ppermute | solution.py:100
  252.4 0.7 copy-start.16
  252.4 0.7 copy-start.17
  252.4 0.8 copy-start.18
  253.2 7.9 %copy-start.11 = (s32[138,1]{0,1:T(1,128)S(1)}, s32[138,1]{0,1:T(1,128)}, u32[]{:S(2)}) copy-start(s32[138,1]{0,1:T(1,128)} %param.20) | copy-start | bytes 1660
  255.8 14.3 %copy-start.6 = (f32[72,256]{1,0:T(8,128)S(1)}, f32[72,256]{1,0:T(8,128)}, u32[]{:S(2)}) copy-start(f32[72,256]{1,0:T(8,128)} %get-tuple-element.192) | copy-start | bytes 221188
  255.8 14.3 %collective-permute-start.31 = (f32[72,256]{1,0:T(8,128)}, f32[72,256]{1,0:T(8,128)S(1)}, u32[]{:S(2)}, u32[]{:S(2)}) collective-permute-start(f32[72,256]{1,0:T(8,128)} %get-tuple-element.195), channel_id=1, source_target_pairs={{0,24},{1,25},{2,26},{3,27},{4,28},{5,29},{6,30},{7,31},{8,16},{9,... | collective-permute-start | bytes 221192 | tf_op jit(solution)/shard_map/ppermute | solution.py:100
  258.2 11.9 %collective-permute-start.30 = (f32[72,256]{1,0:T(8,128)}, f32[72,256]{1,0:T(8,128)S(1)}, u32[]{:S(2)}, u32[]{:S(2)}) collective-permute-start(f32[72,256]{1,0:T(8,128)} %get-tuple-element.194), channel_id=1, source_target_pairs={{0,16},{1,17},{2,18},{3,19},{4,20},{5,21},{6,22},{7,23},{8,24},{9,... | collective-permute-start | bytes 221192 | tf_op jit(solution)/shard_map/ppermute | solution.py:100
  261.1 9.0 %collective-permute-start.29 = (f32[72,256]{1,0:T(8,128)}, f32[72,256]{1,0:T(8,128)S(1)}, u32[]{:S(2)}, u32[]{:S(2)}) collective-permute-start(f32[72,256]{1,0:T(8,128)} %get-tuple-element.193), channel_id=1, source_target_pairs={{0,8},{1,9},{2,10},{3,11},{4,12},{5,13},{6,14},{7,15},{8,0},{9,1},... | collective-permute-start | bytes 221192 | tf_op jit(solution)/shard_map/ppermute | solution.py:100
  261.9 13.3 %copy-start = (f32[16,64,256]{2,1,0:T(8,128)}, f32[16,64,256]{2,1,0:T(8,128)S(1)}, u32[]{:S(2)}) copy-start(f32[16,64,256]{2,1,0:T(8,128)S(1)} %all-to-all-done.3.x_ref) | copy-start | bytes 3145732
  261.9 33.2 %all-to-all-start.4 = ((f32[16,64,256]{2,1,0:T(8,128)}), f32[16,64,256]{2,1,0:T(8,128)}, u32[]{:S(2)}, u32[]{:S(2)}) async-start(f32[16,64,256]{2,1,0:T(8,128)} %bitcast.33), calls=%async_computation.6 | async-start | bytes 2097152 | tf_op jit(solution)/shard_map/all_to_all | solution.py:121
  270.2 7.1 %collective-permute-start.32 = (f32[1,72,256]{2,1,0:T(8,128)S(1)}, f32[1,72,256]{2,1,0:T(8,128)S(1)}, u32[]{:S(2)}, u32[]{:S(2)}) collective-permute-start(f32[1,72,256]{2,1,0:T(8,128)S(1)} %add_bitcast_fusion), channel_id=1, source_target_pairs={{0,2},{1,3},{2,0},{3,1},{4,6},{5,7},{6,4},{7,5},{8,10},{9,11},{10,... | collective-permute-start | bytes 221192 | tf_op jit(solution)/shard_map/ppermute | solution.py:100
  277.3 4.7 %collective-permute-start.33 = (f32[2,72,256]{2,1,0:T(8,128)S(1)}, f32[2,72,256]{2,1,0:T(8,128)S(1)}, u32[]{:S(2)}, u32[]{:S(2)}) collective-permute-start(f32[2,72,256]{2,1,0:T(8,128)S(1)} %pad_maximum_fusion.1), channel_id=1, source_target_pairs={{0,4},{1,5},{2,6},{3,7},{4,0},{5,1},{6,2},{7,3},{8,12},{9,13},{10,... | collective-permute-start | bytes 442376 | tf_op jit(solution)/shard_map/ppermute | solution.py:100
  282.0 2.9 copy-start.5
  282.0 2.9 collective-permute-start.34
  284.9 0.7 copy-start.14
  (12 other events, 7.1 us)
Sparse Core Ops, SparseCore 0:
  88.4 33.0 reduce-scatter.4
  123.3 29.1 all-gather.2
  174.3 38.5 reduce-scatter.2
